TPU v7x, 32 devices: a whole 2x2x4 slice. The times are simulated.
32 devices in a mesh: dp: 4 (over x, core), table: 8 (over z, y).
Axes of the slice: x: 2, y: 2, z: 4, core: 2. Of those that a mesh axis runs over, the one named last changes fastest.
Arguments:
- features: bfloat16 [4096, 2048], P(('dp', 'table')), may hold values from -6 to 6
- w_first: bfloat16 [2048, 1024], replicated, may hold values from -0.125 to 0.125
- b_first: float32 [1024], replicated, may hold values from -4 to 4
- grad_out: bfloat16 [4096, 1024], P(('dp', 'table')), may hold values from -6 to 6
- admit: int32 [4096, 16], P(('dp', 'table')), may hold values from 0 to 1, as said below
- owner: int32 [4096, 16, 1], P(('dp', 'table')), may hold values from 0 to 3, as said below
- adm_row: int32 [4096, 16], P(('dp', 'table')), may hold values from 0 to 1023
- q_shard: int32 [4096, 16, 1], P(('dp', 'table')), may hold values from 0 to 31, as said below
- q_local: int32 [4096, 16], P(('dp', 'table')), may hold values from 0 to 4095
- r_shard: int32 [4096, 16, 1], P(('dp', 'table')), may hold values from 0 to 31, as said below
- r_local: int32 [4096, 16], P(('dp', 'table')), may hold values from 0 to 4095
Outputs:
- w_grad: float32 [2048, 1024], replicated
- b_grad: float32 [1024], replicated
- adm_grad: float32 [4096, 128], P(('dp', 'table'))
- q_grad: float32 [131072, 128], P(('dp', 'table'))
- r_grad: float32 [131072, 128], P(('dp', 'table'))
Inputs may be any that keep to these rules, and one draw needn't show every extreme that they name: `admit`: on some device every lookup is admitted, and on another device none is. Among the 2048 lookups of one device no owner is named more than 768 times, and on every device some owner exactly 768 times. `q_shard`: among the 2048 lookups of one device no block is named more than 96 times, and on every device some block exactly 96 times. `r_shard`: among the 2048 lookups of one device no block is named more than 96 times, and on every device some block exactly 96 times.
All inputs are finite; a program needn't handle non-finite values.
Results may differ from a plain program's by a relative error of at most 0.0055.
Values may be sent and summed in bfloat16 or wider, within the bound.
No kernel may reach another device: no remote copies, remote signals or barrier semaphores. Data moves between devices by JAX's collectives and lax.ppermute only.
A program may use at most 128 MiB of HBM per device.

v0:
```python
import math

import jax
import jax.numpy as jnp
from jax import lax
from jax.sharding import PartitionSpec as P

E = 128
ADM_DEV = 128
QROWS_DEV = 4096


def row_sums(values, marks, n_rows):
    block = math.gcd(n_rows, 512)

    def one_block(start):
        wanted = start + jnp.arange(block, dtype=jnp.int32)
        picked = (wanted[:, None] == marks[None, :]).astype(jnp.bfloat16)
        return jnp.dot(picked, values, preferred_element_type=jnp.float32)

    starts = jnp.arange(n_rows // block, dtype=jnp.int32) * block
    return lax.map(one_block, starts).reshape(n_rows, values.shape[1])


def make_buckets(lookup, live, dest, labels, n_dest, capacity, empty_label):
    count = lookup.shape[0]
    hits = ((dest[:, None] == jnp.arange(n_dest, dtype=jnp.int32)[None, :]) & live[:, None]).astype(
        jnp.int32
    )
    row_block = math.gcd(count, 512)
    n_blocks = count // row_block
    grouped = hits.reshape(n_blocks, row_block, n_dest)
    totals = jnp.sum(grouped, axis=1)
    earlier = jnp.cumsum(totals, axis=0) - totals
    places = jnp.arange(row_block, dtype=jnp.int32)
    lower = (places[:, None] > places[None, :]).astype(jnp.bfloat16)
    within = jnp.einsum(
        "ij,bjd->bid", lower, grouped.astype(jnp.bfloat16), preferred_element_type=jnp.float32
    )
    before = (within.astype(jnp.int32) + earlier[:, None, :]).reshape(count, n_dest)
    rank = jnp.sum(before * hits, axis=1)
    n_slots = n_dest * capacity
    slot = jnp.where(live, dest * capacity + rank, n_slots)
    slot_block = math.gcd(n_slots, 512)

    def fill_block(start):
        wanted = start + jnp.arange(slot_block, dtype=jnp.int32)
        match = slot[:, None] == wanted[None, :]
        rows_out = lax.dot_general(
            match.astype(jnp.bfloat16),
            lookup,
            (((0,), (0,)), ((), ())),
            preferred_element_type=jnp.float32,
        )
        label_sum = jnp.sum(jnp.where(match, labels[:, None], 0), axis=0)
        filled = jnp.any(match, axis=0)
        return (rows_out.astype(jnp.bfloat16), jnp.where(filled, label_sum, empty_label))

    starts = jnp.arange(n_slots // slot_block, dtype=jnp.int32) * slot_block
    bucket, marks = lax.map(fill_block, starts)
    return (bucket.reshape(n_dest, capacity, lookup.shape[1]), marks.reshape(n_dest, capacity))


def local(
    features, w_first, b_first, grad_out, admit, owner, adm_row, q_shard, q_local, r_shard, r_local
):
    n_owner = lax.axis_size("dp")
    n_table = lax.axis_size("table")
    n_device = n_owner * n_table
    pre = jnp.dot(features, w_first, preferred_element_type=jnp.float32) + b_first
    sig = jax.nn.sigmoid(pre)
    dpre = (grad_out.astype(jnp.float32) * sig * (1.0 + pre * (1.0 - sig))).astype(jnp.bfloat16)
    local_w = lax.dot_general(
        features, dpre, (((0,), (0,)), ((), ())), preferred_element_type=jnp.float32
    )
    local_b = jnp.sum(dpre.astype(jnp.float32), axis=0)
    lookup = lax.dot_general(
        dpre, w_first, (((1,), (1,)), ((), ())), preferred_element_type=jnp.float32
    ).astype(jnp.bfloat16)
    lookup = lookup.reshape(-1, E)
    flag = admit.reshape(-1)
    count = flag.shape[0]
    own_rows = ADM_DEV * n_table
    capacity = max(2, 3 * count // (2 * n_owner))
    bucket, labels = make_buckets(
        lookup, flag == 1, owner.reshape(-1), adm_row.reshape(-1), n_owner, capacity, own_rows
    )
    arrived, arrived_rows = (
        lax.all_to_all(bucket, "dp", split_axis=0, concat_axis=0, tiled=True),
        lax.all_to_all(labels, "dp", split_axis=0, concat_axis=0, tiled=True),
    )
    owner_sums = row_sums(arrived.reshape(-1, E), arrived_rows.reshape(-1), own_rows)
    adm_grad = lax.psum_scatter(owner_sums, "table", scatter_dimension=0, tiled=True)
    q_cap = max(2, 3 * count // (2 * n_device))
    plain = flag == 0
    q_bucket, q_marks = make_buckets(
        lookup, plain, q_shard.reshape(-1), q_local.reshape(-1), n_device, q_cap, QROWS_DEV
    )
    r_bucket, r_marks = make_buckets(
        lookup, plain, r_shard.reshape(-1), r_local.reshape(-1), n_device, q_cap, QROWS_DEV
    )
    q_in, q_rows_in, r_in, r_rows_in = (
        lax.all_to_all(q_bucket, ("dp", "table"), split_axis=0, concat_axis=0, tiled=True),
        lax.all_to_all(q_marks, ("dp", "table"), split_axis=0, concat_axis=0, tiled=True),
        lax.all_to_all(r_bucket, ("dp", "table"), split_axis=0, concat_axis=0, tiled=True),
        lax.all_to_all(r_marks, ("dp", "table"), split_axis=0, concat_axis=0, tiled=True),
    )
    q_grad = row_sums(q_in.reshape(-1, E), q_rows_in.reshape(-1), QROWS_DEV)
    r_grad = row_sums(r_in.reshape(-1, E), r_rows_in.reshape(-1), QROWS_DEV)
    w_grad, b_grad = lax.psum((local_w, local_b), ("dp", "table"))
    return (w_grad, b_grad, adm_grad, q_grad, r_grad)


def solution(mesh):
    in_specs = (
        P(("dp", "table"), None),
        P(),
        P(),
        P(("dp", "table"), None),
        P(("dp", "table"), None),
        P(("dp", "table"), None, None),
        P(("dp", "table"), None),
        P(("dp", "table"), None, None),
        P(("dp", "table"), None),
        P(("dp", "table"), None, None),
        P(("dp", "table"), None),
    )
    out_specs = (
        P(),
        P(),
        P(("dp", "table"), None),
        P(("dp", "table"), None),
        P(("dp", "table"), None),
    )
    return jax.shard_map(local, mesh=mesh, in_specs=in_specs, out_specs=out_specs, check_vma=False)
```

profile of v0, /device:TPU:0, one launch (start us, length us, event | category | flops | bytes accessed | tf_op | source)
XLA Modules:
  0.0 301.2 jit_solution(6946092733897099827)
XLA Ops:
  9.0 3.1 %convert_reduce_fusion = (f32[1024]{0:T(1024)S(1)}, bf16[128,1024]{1,0:T(8,128)(2,1)S(1)}) fusion(f32[1024]{0:T(1024)} %param.25, bf16[128,2048]{1,0:T(8,128)(2,1)S(1)} %copy-done, bf16[2048,1024]{1,0:T(8,128)(2,1)} %param.24, bf16[128,1024]{1,0:T(8,128)(2,1)} %param.26), kind=kOutput, calls=%fused_computation.77 | convolution fusion | flops 538573824 | bytes 5251072 | tf_op jit(solution)/shard_map/dot_general | solution.py:70
  12.2 4.7 %convolution_bitcast_fusion = f32[2048,1024]{0,1:T(8,128)} fusion(bf16[128,1024]{1,0:T(8,128)(2,1)S(1)} %get-tuple-element.371, bf16[128,2048]{1,0:T(8,128)(2,1)S(1)} %copy-done), kind=kOutput, calls=%fused_computation.57 | convolution fusion | flops 536870912 | bytes 9175040 | tf_op jit(solution)/shard_map/dot_general | solution.py:73
  18.0 3.7 %convolution_convert_fusion = bf16[128,2048]{1,0:T(8,128)(2,1)S(1)} fusion(bf16[128,1024]{1,0:T(8,128)(2,1)S(1)} %get-tuple-element.371, bf16[2048,1024]{1,0:T(8,128)(2,1)} %param.24), kind=kOutput, calls=%fused_computation.58 | convolution fusion | flops 537133056 | bytes 4980736 | tf_op jit(solution)/shard_map/dot_general | solution.py:77
  23.5 29.6 %while.72 = (s32[]{:T(128)}, bf16[6,512,128]{2,1,0:T(8,128)(2,1)S(1)}, s32[6,512]{1,0:T(8,128)S(1)}, s32[2048]{0:T(1024)S(1)}, s32[6]{0:T(128)S(1)}, /*index=5*/...) while((s32[]{:T(128)}, ...), condition=%wide.wide.region_9.10_spmd, body=%wide.wide.region_6.9_spmd.sunk | while | flops 274792448 | bytes 707717 | solution.py:60
  53.7 4.2 %all-to-all-start = ((s32[4,1,768]{2,1,0:T(1,128)}), s32[4,1,768]{2,1,0:T(1,128)S(1)}, u32[]{:S(2)}, u32[]{:S(2)}) async-start(s32[4,1,768]{2,1,0:T(1,128)} %all_to_all.33), calls=%async_computation | async-start | bytes 24576 | tf_op jit(solution)/shard_map/all_to_all | solution.py:90
  61.3 33.0 %while.74 = (s32[]{:T(128)}, bf16[6,512,128]{2,1,0:T(8,128)(2,1)}, s32[6,512]{1,0:T(8,128)S(1)}, s32[2048]{0:T(1024)S(1)}, s32[6]{0:T(128)S(1)}, /*index=5*/bf16...) while((s32[]{:T(128)}, bf16[6,512,128]{2,1,0:T(8,128)(2,1)}, ...), condition=%wide.wide.region_19.20_spmd, body=%wide.wide.region_16.19_spmd.sunk | while | flops 274792448 | bytes 707717 | solution.py:60
  62.5 2.3 fusion.161
  68.0 2.3 fusion.161
  73.6 2.3 fusion.161
  79.1 2.3 fusion.161
  84.6 2.3 fusion.161
  90.1 2.3 fusion.161
  95.2 7.0 %all-to-all-start.2 = ((s32[32,1,96]{2,1,0:T(1,128)}), s32[32,1,96]{2,1,0:T(1,128)S(1)}, u32[]{:S(2)}, u32[]{:S(2)}) async-start(s32[32,1,96]{2,1,0:T(1,128)} %all_to_all.37), calls=%async_computation.3 | async-start | bytes 32768 | tf_op jit(solution)/shard_map/all_to_all | solution.py:104
  103.2 32.3 %while.76 = (s32[]{:T(128)}, bf16[6,512,128]{2,1,0:T(8,128)(2,1)}, s32[6,512]{1,0:T(8,128)S(1)}, s32[2048]{0:T(1024)S(1)}, s32[6]{0:T(128)S(1)}, /*index=5*/bf16...) while((s32[]{:T(128)}, bf16[6,512,128]{2,1,0:T(8,128)(2,1)}, ...), condition=%wide.wide.region_28.29_spmd, body=%wide.wide.region_25.28_spmd.sunk | while | flops 274792448 | bytes 707717 | solution.py:60
  135.7 12.6 %all_to_all.51 = s32[32,1,96]{2,1,0:T(1,128)S(1)} all-to-all(s32[32,1,96]{2,1,0:T(1,128)S(1)} %all_to_all.41), channel_id=1, replica_groups=mesh['dp'=4,'table'=8] {'dp','table'}, dimensions={0} | all-to-all | bytes 24576 | tf_op jit(solution)/shard_map/all_to_all | solution.py:106
  148.3 18.8 %all_to_all.52 = bf16[4,768,128]{2,1,0:T(8,128)(2,1)S(1)} all-to-all(bf16[4,768,128]{2,1,0:T(8,128)(2,1)S(1)} %bitcast.165), channel_id=1, replica_groups=mesh['dp'=4,'table'=8] {'dp'}, dimensions={0} | all-to-all | bytes 1572864 | tf_op jit(solution)/shard_map/all_to_all | solution.py:89
  167.1 2.6 all-to-all-start.3
  169.8 49.8 %psum.15 = f32[1024]{0:T(1024)} all-reduce(f32[1024]{0:T(1024)S(1)} %get-tuple-element.370), channel_id=1, replica_groups=mesh['dp'=4,'table'=8] {'dp','table'}, use_global_device_ids=true, to_apply=%region_2.0 | all-reduce | flops 1024 | bytes 8192 | tf_op jit(solution)/shard_map/psum | solution.py:110
  220.2 4.4 %while.73 = (s32[]{:T(128)}, f32[2,512,128]{2,1,0:T(8,128)S(1)}, s32[2]{0:T(128)S(1)}, s32[4,768]{1,0:T(4,128)}, bf16[3072,128]{1,0:T(8,128)(2,1)S(1)}, /*index=5*/s32[3072]{0:T(1024)S(1)}, s32[]{:T(128)}) while((s32[]{:T(128)}, f32[2,512,128]{2,1,0:T(8,128)S(1)}, s32[2]{0:T(128)S(1)}, s32[4,768]{1,0:T(4,128)}, ...), condition=%wide.wide.region_11.12_spmd, body=%wide.wide.region_10.11_spmd.sunk | while | flops 404226560 | bytes 1065065 | solution.py:22
  225.5 5.1 %all-to-all-start.5 = ((bf16[32,96,128]{2,1,0:T(8,128)(2,1)}), bf16[32,96,128]{2,1,0:T(8,128)(2,1)}, u32[]{:S(2)}, u32[]{:S(2)}) async-start(bf16[32,96,128]{2,1,0:T(8,128)(2,1)} %bitcast.28), calls=%async_computation.6 | async-start | bytes 1572864 | tf_op jit(solution)/shard_map/all_to_all | solution.py:105
  230.7 18.3 %while.75 = (s32[]{:T(128)}, f32[8,512,128]{2,1,0:T(8,128)S(1)}, s32[8]{0:T(128)S(1)}, s32[32,96]{1,0:T(8,128)}, bf16[3072,128]{1,0:T(8,128)(2,1)S(1)}, /*index=5*/s32[3072]{0:T(1024)S(1)}, s32[]{:T(128)}) while((s32[]{:T(128)}, f32[8,512,128]{2,1,0:T(8,128)S(1)}, s32[8]{0:T(128)S(1)}, s32[32,96]{1,0:T(8,128)}, ...), condition=%wide.wide.region_21.22_spmd, body=%wide.wide.region_20.21_spmd.sunk | while | flops 404226560 | bytes 1065065 | solution.py:22
  249.1 7.1 %all-to-all-done.5 = bf16[32,96,128]{2,1,0:T(8,128)(2,1)} async-done(((bf16[32,96,128]{2,1,0:T(8,128)(2,1)}), bf16[32,96,128]{2,1,0:T(8,128)(2,1)}, u32[]{:S(2)}, u32[]{:S(2)}) %all-to-all-start.5) | async-done | bytes 786464 | tf_op jit(solution)/shard_map/all_to_all | solution.py:105
  256.3 27.4 %while.77 = (s32[]{:T(128)}, f32[8,512,128]{2,1,0:T(8,128)S(1)}, s32[8]{0:T(128)S(1)}, s32[32,96]{1,0:T(8,128)}, bf16[3072,128]{1,0:T(8,128)(2,1)}, /*index=5*/s32[3072]{0:T(1024)S(1)}, s32[]{:T(128)}) while((s32[]{:T(128)}, f32[8,512,128]{2,1,0:T(8,128)S(1)}, s32[8]{0:T(128)S(1)}, s32[32,96]{1,0:T(8,128)}, ...), condition=%wide.wide.region_30.31_spmd, body=%wide.wide.region_29.30_spmd.sunk | while | flops 404226560 | bytes 1065065 | solution.py:22
  283.7 10.0 %copy.58 = f32[2048,1024]{1,0:T(8,128)} copy(f32[2048,1024]{0,1:T(8,128)} %all-reduce.2.cloned.1.call-done) | data formatting | bytes 16777216
  (281 shorter events, 142.0 us)
Async XLA Ops:
  8.0 1.0 copy-start
  8.0 275.7 %all-reduce.2.cloned.1.call-start = ((), (), s32[]{:S(2)}) async-start(), calls=%async_computation.7 | async-start | bytes 16777216 | tf_op jit(solution)/shard_map/psum | solution.py:110
  16.9 0.7 copy-start.10
  16.9 0.8 copy-start.16
  17.6 5.2 %copy-start.13 = (s32[128,16]{0,1:T(8,128)S(1)}, s32[128,16]{0,1:T(8,128)}, u32[]{:S(2)}) copy-start(s32[128,16]{0,1:T(8,128)} %param.29) | copy-start | bytes 24580
  22.9 0.6 copy-start.6
  23.5 34.4 %copy-start.11 = (s32[128,16,1]{0,2,1:T(1,128)S(1)}, s32[128,16,1]{0,2,1:T(1,128)}, u32[]{:S(2)}) copy-start(s32[128,16,1]{0,2,1:T(1,128)} %param.32) | copy-start | bytes 24580
  23.5 34.8 %copy-start.12 = (s32[128,16,1]{0,2,1:T(1,128)S(1)}, s32[128,16,1]{0,2,1:T(1,128)}, u32[]{:S(2)}) copy-start(s32[128,16,1]{0,2,1:T(1,128)} %param.30) | copy-start | bytes 24580
  23.5 36.5 %copy-start.14 = (s32[128,16]{0,1:T(8,128)S(1)}, s32[128,16]{0,1:T(8,128)}, u32[]{:S(2)}) copy-start(s32[128,16]{0,1:T(8,128)} %param.31) | copy-start | bytes 24580
  53.7 41.5 %all-to-all-start = ((s32[4,1,768]{2,1,0:T(1,128)}), s32[4,1,768]{2,1,0:T(1,128)S(1)}, u32[]{:S(2)}, u32[]{:S(2)}) async-start(s32[4,1,768]{2,1,0:T(1,128)} %all_to_all.33), calls=%async_computation | async-start | bytes 24576 | tf_op jit(solution)/shard_map/all_to_all | solution.py:90
  60.2 1.1 copy-start.5
  61.3 33.7 %copy-start.15 = (s32[128,16]{0,1:T(8,128)S(1)}, s32[128,16]{0,1:T(8,128)}, u32[]{:S(2)}) copy-start(s32[128,16]{0,1:T(8,128)} %param.33) | copy-start | bytes 24580
  95.1 8.1 %copy-start.4 = (s32[128,16]{1,0:T(8,128)}, s32[128,16]{1,0:T(8,128)S(1)}, u32[]{:S(2)}) copy-start(s32[128,16]{1,0:T(8,128)S(1)} %copy.57) | copy-start | bytes 24580
  95.2 40.5 %all-to-all-start.2 = ((s32[32,1,96]{2,1,0:T(1,128)}), s32[32,1,96]{2,1,0:T(1,128)S(1)}, u32[]{:S(2)}, u32[]{:S(2)}) async-start(s32[32,1,96]{2,1,0:T(1,128)} %all_to_all.37), calls=%async_computation.3 | async-start | bytes 32768 | tf_op jit(solution)/shard_map/all_to_all | solution.py:104
  135.7 84.5 %copy-start.7 = (s32[32,1,96]{2,1,0:T(1,128)}, s32[32,1,96]{2,1,0:T(1,128)S(1)}, u32[]{:S(2)}) copy-start(s32[32,1,96]{2,1,0:T(1,128)S(1)} %all-to-all-done.2) | copy-start | bytes 36868
  148.3 71.9 %copy-start.8 = (s32[32,1,96]{2,1,0:T(1,128)}, s32[32,1,96]{2,1,0:T(1,128)S(1)}, u32[]{:S(2)}) copy-start(s32[32,1,96]{2,1,0:T(1,128)S(1)} %all_to_all.51) | copy-start | bytes 36868
  167.1 58.3 %all-to-all-start.3 = ((bf16[32,96,128]{2,1,0:T(8,128)(2,1)}), bf16[32,96,128]{2,1,0:T(8,128)(2,1)S(1)}, u32[]{:S(2)}, u32[]{:S(2)}) async-start(bf16[32,96,128]{2,1,0:T(8,128)(2,1)} %bitcast.23), calls=%async_computation.4 | async-start | bytes 1572864 | tf_op jit(solution)/shard_map/all_to_all | solution.py:103
  169.7 124.0 %reduce-scatter.2.cloned.1.call-start = ((), (), s32[]{:S(2)}) async-start(), calls=%async_computation.8 | async-start | bytes 589824 | tf_op jit(solution)/shard_map/reduce_scatter | solution.py:93
  219.6 0.6 copy-start.9
  224.6 0.8 copy-start.3
  225.5 30.7 %all-to-all-start.5 = ((bf16[32,96,128]{2,1,0:T(8,128)(2,1)}), bf16[32,96,128]{2,1,0:T(8,128)(2,1)}, u32[]{:S(2)}, u32[]{:S(2)}) async-start(bf16[32,96,128]{2,1,0:T(8,128)(2,1)} %bitcast.28), calls=%async_computation.6 | async-start | bytes 1572864 | tf_op jit(solution)/shard_map/all_to_all | solution.py:105
  249.1 7.1 %copy-start.2 = (f32[8,512,128]{2,1,0:T(8,128)}, f32[8,512,128]{2,1,0:T(8,128)S(1)}, u32[]{:S(2)}) copy-start(f32[8,512,128]{2,1,0:T(8,128)S(1)} %get-tuple-element.205) | copy-start | bytes 6291460
  283.7 10.0 %copy-start.1 = (f32[8,512,128]{2,1,0:T(8,128)}, f32[8,512,128]{2,1,0:T(8,128)S(1)}, u32[]{:S(2)}) copy-start(f32[8,512,128]{2,1,0:T(8,128)S(1)} %get-tuple-element.208) | copy-start | bytes 6291460
Sparse Core Ops, SparseCore 0:
  17.0 199.3 all-reduce.1
Sparse Core Ops, SparseCore 1:
  225.5 64.4 reduce-scatter.1
where the time goes:
time: 303 us; the launch traced here: 301 us
  blocking collectives  81.2 us (27%)
  matrix products  77.2 us (25%)
  other arithmetic  57.8 us (19%)
  local copies, waits for them, and re-layouts  41.9 us (14%)
  starting transfers between devices  19 us (6%)
  between operations  15.8 us (5%)
  waiting for transfers between devices  7.12 us (2%)
    psum x1, blocking collectives, local(): w_grad, b_grad = lax.psum((local_w, local_b), ('dp', 'table'))  49.8 us
    dot_general x18, matrix products, fill_block(): lax.dot_general(match.astype(jnp.bfloat16), lookup, (((0,), (0,)), ((), (...  37 us
    dot_general x18, matrix products, one_block(): return jnp.dot(picked, values, preferred_element_type=jnp.float32)  27.7 us
    reduce_sum x18, other arithmetic, fill_block(): label_sum = jnp.sum(jnp.where(match, labels[:, None], 0), axis=0)  21.7 us
    all_to_all x1, blocking collectives, local(): lax.all_to_all(bucket, 'dp', split_axis=0, concat_axis=0, tiled=True)  18.8 us
    unnamed x42, local copies, waits for them, and re-layouts  13.7 us
    reduce_or x18, other arithmetic, fill_block(): filled = jnp.any(match, axis=0)  12.7 us
    all_to_all x1, blocking collectives, local(): lax.all_to_all(r_marks, ('dp', 'table'), split_axis=0, concat_axis=0, til...  12.6 us
  transfers between devices with their start and end apart: 6, of which 1 were waited for; matrix products, arithmetic and copies ran while one was open for 55% of the time, Pallas kernels for 0%

commit v1 on v0

v1 whole, which is shorter than its diff:
```python
import functools

import jax
import jax.numpy as jnp
from jax import lax
from jax.experimental import pallas as pl
from jax.experimental.pallas import tpu as pltpu
from jax.sharding import Mesh, PartitionSpec as P

E = 128
ADM_DEV = 128
QROWS_DEV = 4096
N_Z = 4
GROUPS = 4
VMEM_LIMIT = 48 * 1024 * 1024
BF = jnp.bfloat16
F32 = jnp.float32


def iota(shape, dim):
    return lax.broadcasted_iota(jnp.int32, shape, dim)


def dot(a, b, dims=((1,), (0,))):
    return lax.dot_general(a, b, (dims, ((), ())), preferred_element_type=F32)


def slots_kernel(n_dest, cap, dq_ref, lq_ref, dr_ref, lr_ref, row_ref, slot_ref, labels_ref):
    n_rows, n_feat = dq_ref.shape
    n_s = n_rows // N_Z
    sample = iota((n_s, n_s), 0)
    earlier = (sample < iota((n_s, n_s), 1)).astype(F32).astype(BF)
    ones = jnp.ones((n_s, n_s), BF)
    count = n_dest * n_feat
    at_row, at_col = iota((count, count), 0), iota((count, count), 1)
    before = ((at_row // n_feat == at_col // n_feat) & (at_col < at_row)).astype(F32).astype(BF)
    for table, ref in enumerate((dq_ref, dr_ref)):
        across = ref[...].astype(F32).T
        for z in range(N_Z):
            dest = across[:, z * n_s : (z + 1) * n_s]
            hits = jnp.concatenate([jnp.where(dest == d, 1.0, 0.0) for d in range(n_dest)], axis=0)
            hits_bf = hits.astype(BF)
            rank = dot(hits_bf, earlier) + dot(before, dot(hits_bf, ones).astype(BF))
            rank = rank * hits
            total = rank[0:n_feat, :]
            for d in range(1, n_dest):
                total = total + rank[d * n_feat : (d + 1) * n_feat, :]
            slot = jnp.where(dest >= 0, dest * cap + total, -1.0)
            slot_ref[table, z, :, :] = slot.astype(jnp.int32)
    across = row_ref[...].astype(F32).T.astype(jnp.int32)
    for z in range(N_Z):
        slot_ref[2, z, :, :] = across[:, z * n_s : (z + 1) * n_s]
    lane = iota((n_s, E), 1) % 4
    for z in range(N_Z):
        lq, lr = lq_ref[z * n_s : (z + 1) * n_s, :], lr_ref[z * n_s : (z + 1) * n_s, :]
        for f in range(n_feat):
            q, r = lq[:, f : f + 1], lr[:, f : f + 1]
            one = jnp.where(lane < 2, q, r)
            one = jnp.where(lane % 2 == 0, one >> 8, one & 255)
            labels_ref[z, f * n_s : (f + 1) * n_s, :] = one.astype(F32).astype(BF)


def bucket_kernel(
    n_dest, cap, d_ref, w_ref, slot_ref, labels_ref, out_ref, v_ref, mark_ref
):
    n_rows, depth = d_ref.shape
    n_s = n_rows // N_Z
    n_feat = w_ref.shape[0] // E
    look = n_feat * n_s
    seg = N_Z * cap
    n_mark = -(-seg // E)

    def lookups(step, carry):
        wide = 2 * E
        start = pl.multiple_of(step * wide, wide)
        res = dot(d_ref[...], w_ref[pl.ds(start, wide), :], ((1,), (1,))).astype(BF)
        for z in range(N_Z):
            for h in range(2):
                row = pl.multiple_of((step * 2 + h) * n_s, n_s)
                v_ref[z, pl.ds(row, n_s), 0:E] = res[z * n_s : (z + 1) * n_s, h * E : (h + 1) * E]
        return carry

    lax.fori_loop(0, n_feat // 2, lookups, 0)
    for z in range(N_Z):
        v_ref[z, :, E : 2 * E] = labels_ref[z]

    def picked(which, z, base, n):
        wanted = iota((n, n_s), 0) + base
        parts = [
            jnp.where(wanted == slot_ref[which, z, f : f + 1, :], 1.0, 0.0).astype(BF)
            for f in range(n_feat)
        ]
        return jnp.concatenate(parts, axis=1)

    per = 4
    for which in range(2):
        for z in range(N_Z):

            def fill(block, carry):
                o = dot(picked(which, z, block * (per * cap), per * cap), v_ref[z])
                for g in range(per):
                    d = block * per + g
                    rows = o[g * cap : (g + 1) * cap, :]
                    out_ref[d, which * seg + z * cap : which * seg + (z + 1) * cap, :] = rows[:, 0:E].astype(BF)
                    mark_ref[which, d, z * cap : (z + 1) * cap, :] = rows[:, E : 2 * E]
                return carry

            lax.fori_loop(0, n_dest // per, fill, 0)

    def admitted(block, carry):
        o = jnp.zeros((per * ADM_DEV, E), F32)
        for z in range(N_Z):
            o = o + dot(picked(2, z, block * (per * ADM_DEV), per * ADM_DEV), v_ref[z, :, 0:E])
        for g in range(per):
            out_ref[block * per + g, 2 * seg : 2 * seg + ADM_DEV, :] = o[
                g * ADM_DEV : (g + 1) * ADM_DEV, :
            ].astype(BF)
        return carry

    lax.fori_loop(0, n_dest // per, admitted, 0)

    bias = jnp.sum(d_ref[...].astype(F32), axis=0, keepdims=True)
    high = bias.astype(BF)
    low = (bias - high.astype(F32)).astype(BF)
    n_bias = depth // E
    bias_rows = jnp.concatenate(
        [part[:, i * E : (i + 1) * E].astype(F32) for part in (high, low) for i in range(n_bias)], axis=0
    ).astype(BF)
    at_mark = 2 * seg + ADM_DEV

    def finish(d, carry):
        lane = iota((seg, E), 1) % 4
        mixed = jnp.where(lane < 2, mark_ref[0, d], mark_ref[1, d])
        if seg % E:
            mixed = jnp.concatenate([mixed, jnp.zeros((n_mark * E - seg, E), F32)], axis=0)
        rows = iota((16, E), 0) // 4
        marks = jnp.zeros((16, E), F32)
        for j in range(n_mark):
            across = mixed[j * E : (j + 1) * E, :].T
            marks = jnp.where(rows == j, across[0:16, :], marks)
        out_ref[d, at_mark : at_mark + 16, :] = marks.astype(BF)
        out_ref[d, at_mark + 16 : at_mark + 16 + 2 * n_bias, :] = bias_rows
        return carry

    lax.fori_loop(0, n_dest, finish, 0)


def sums_kernel(n_src, seg, n_bias, in_ref, bias_ref, adm_ref, q_ref, r_ref, v_ref, row_ref):
    n_mark = -(-seg // E)
    at_mark = 2 * seg + ADM_DEV
    adm = jnp.zeros((ADM_DEV, E), F32)
    bias = jnp.zeros((2 * n_bias, E), F32)
    for s in range(n_src):
        adm = adm + in_ref[s, 2 * seg : at_mark, :].astype(F32)
        bias = bias + in_ref[s, at_mark + 16 : at_mark + 16 + 2 * n_bias, :].astype(F32)
    adm_ref[...] = adm
    bias_ref[...] = bias[0:n_bias, :] + bias[n_bias:, :]

    per_group = QROWS_DEV // GROUPS
    tall = n_mark * E
    for table, out in enumerate((q_ref, r_ref)):
        for s in range(n_src):
            marks = in_ref[s, at_mark : at_mark + 16, :].astype(F32)
            down = jnp.concatenate([marks, jnp.zeros((E - 16, E), F32)], axis=0).T
            for j in range(n_mark):
                at = j * 4 + table * 2
                label = marks[at : at + 1, :] * 256.0 + marks[at + 1 : at + 2, :]
                label = label.astype(jnp.int32) % per_group
                if (j + 1) * E > seg:
                    label = jnp.where(iota((1, E), 1) + j * E < seg, label, -1)
                k = s * n_mark + j
                row_ref[k : k + 1, :] = label
                group = (down[:, at : at + 1] * 256.0 + down[:, at + 1 : at + 2]).astype(jnp.int32) // per_group
                rows = in_ref[s, table * seg + j * E : table * seg + (j + 1) * E, :]
                for g in range(GROUPS):
                    v_ref[k * E : (k + 1) * E, g * E : (g + 1) * E] = jnp.where(
                        group == g, rows.astype(F32), 0.0
                    ).astype(BF)
        block = 256

        def add_up(b, carry):
            wanted = iota((block, E), 0) + b * block
            hits = jnp.concatenate(
                [
                    jnp.where(wanted == row_ref[k : k + 1, :], 1.0, 0.0).astype(BF)
                    for k in range(n_src * n_mark)
                ],
                axis=1,
            )
            o = dot(hits, v_ref[...])
            for g in range(GROUPS):
                start = pl.multiple_of(g * per_group + b * block, block)
                out[pl.ds(start, block), :] = o[:, g * E : (g + 1) * E]
            return carry

        lax.fori_loop(0, per_group // block, add_up, 0)


def local(
    features, w_first, b_first, grad_out, admit, owner, adm_row, q_shard, q_local, r_shard, r_local
):
    n_dp = lax.axis_size("dp")
    n_y = lax.axis_size("ty")
    n_table = N_Z * n_y
    n_dev = n_dp * n_table
    n_plane = n_dp * n_y
    n_s, width = features.shape
    hidden = w_first.shape[1]
    n_feat = width // E
    count = n_s * n_feat
    cap = max(2, 3 * count // (2 * n_dev))
    seg = N_Z * cap
    n_bias = hidden // E
    my_z = lax.axis_index("tz")

    plain = admit == 0
    codes = jnp.stack(
        [
            jnp.where(plain, q_shard[:, :, 0] * QROWS_DEV + q_local, -1),
            jnp.where(plain, r_shard[:, :, 0] * QROWS_DEV + r_local, -1),
            jnp.where(admit == 1, owner[:, :, 0] * (ADM_DEV * n_table) + adm_row, -1),
        ]
    )
    codes = lax.all_to_all(
        jnp.broadcast_to(codes[None], (N_Z,) + codes.shape), "tz", split_axis=0, concat_axis=0, tiled=True
    )
    share = width // n_dev * n_y
    cut = features.reshape(n_s, n_dp, N_Z, share).transpose(2, 0, 1, 3).reshape(N_Z, n_s, n_dp * share)
    feat_in = lax.all_to_all(cut, "tz", split_axis=0, concat_axis=0, tiled=True)
    feat_in = feat_in.reshape(N_Z * n_s, n_dp * share)

    pre = jnp.dot(features, w_first, preferred_element_type=F32) + b_first
    sig = jax.nn.sigmoid(pre)
    dpre = (grad_out.astype(F32) * sig * (1.0 + pre * (1.0 - sig))).astype(BF)
    dpre = lax.all_to_all(
        jnp.broadcast_to(dpre[None], (N_Z,) + dpre.shape), "tz", split_axis=0, concat_axis=0, tiled=True
    ).reshape(N_Z * n_s, hidden)

    def in_plane(code, block):
        dev = code // block
        table = dev % n_table
        here = (code >= 0) & (table // n_y == my_z)
        return jnp.where(here, dev // n_table * n_y + table % n_y, -1), code % block

    rows = [codes[:, i].reshape(N_Z * n_s, n_feat) for i in range(3)]
    dq, lq = in_plane(rows[0], QROWS_DEV)
    dr, lr = in_plane(rows[1], QROWS_DEV)
    da, la = in_plane(rows[2], ADM_DEV)
    arow = jnp.where(da >= 0, da * ADM_DEV + la, -1)
    slots, labels = pl.pallas_call(
        functools.partial(slots_kernel, n_plane, cap),
        out_shape=(
            jax.ShapeDtypeStruct((3, N_Z, n_feat, n_s), jnp.int32),
            jax.ShapeDtypeStruct((N_Z, count, E), BF),
        ),
        compiler_params=pltpu.CompilerParams(vmem_limit_bytes=VMEM_LIMIT),
        cost_estimate=pl.CostEstimate(flops=10**9, bytes_accessed=3 * 10**6, transcendentals=0),
        name="slots",
    )(dq, lq, dr, lr, arow)

    w_part = lax.dot_general(feat_in, dpre, (((0,), (0,)), ((), ())), preferred_element_type=F32).astype(BF)
    w_part = lax.all_to_all(
        w_part.reshape(n_plane, width // n_dev, hidden), ("dp", "ty"), split_axis=0, concat_axis=0, tiled=True
    )

    n_rows = 2 * seg + ADM_DEV + 16 + 2 * n_bias
    chunks = pl.pallas_call(
        functools.partial(bucket_kernel, n_plane, cap),
        out_shape=jax.ShapeDtypeStruct((n_plane, n_rows, E), BF),
        scratch_shapes=[
            pltpu.VMEM((N_Z, count, 2 * E), BF),
            pltpu.VMEM((2, n_plane, seg, E), F32),
        ],
        compiler_params=pltpu.CompilerParams(vmem_limit_bytes=VMEM_LIMIT),
        cost_estimate=pl.CostEstimate(flops=13 * 10**9, bytes_accessed=10**7, transcendentals=0),
        name="buckets",
    )(dpre, w_first, slots, labels)
    chunks = lax.all_to_all(chunks, ("dp", "ty"), split_axis=0, concat_axis=0, tiled=True)

    w_own = jnp.sum(w_part.astype(F32), axis=0).astype(BF)
    w_all = lax.all_gather(w_own, ("dp", "tz", "ty"), axis=0, tiled=True)

    n_tall = n_plane * -(-seg // E)
    b_grad, adm_grad, q_grad, r_grad = pl.pallas_call(
        functools.partial(sums_kernel, n_plane, seg, n_bias),
        out_shape=(
            jax.ShapeDtypeStruct((n_bias, E), F32),
            jax.ShapeDtypeStruct((ADM_DEV, E), F32),
            jax.ShapeDtypeStruct((QROWS_DEV, E), F32),
            jax.ShapeDtypeStruct((QROWS_DEV, E), F32),
        ),
        scratch_shapes=[
            pltpu.VMEM((n_tall * E, GROUPS * E), BF),
            pltpu.VMEM((-(-n_tall // 8) * 8, E), jnp.int32),
        ],
        compiler_params=pltpu.CompilerParams(vmem_limit_bytes=VMEM_LIMIT),
        cost_estimate=pl.CostEstimate(flops=7 * 10**9, bytes_accessed=7 * 10**6, transcendentals=0),
        name="sums",
    )(chunks)
    return (w_all.astype(F32), b_grad.reshape(hidden), adm_grad, q_grad, r_grad)


def solution(mesh):
    n_dp, n_table = mesh.devices.shape
    fine = Mesh(mesh.devices.reshape(n_dp, N_Z, n_table // N_Z), ("dp", "tz", "ty"))
    every = ("dp", "tz", "ty")
    two, three = P(every, None), P(every, None, None)
    in_specs = (two, P(), P(), two, two, three, two, three, two, three, two)
    out_specs = (P(), P(), two, two, two)
    return jax.shard_map(local, mesh=fine, in_specs=in_specs, out_specs=out_specs, check_vma=False)
```

time: 303 us -> 179 us (0.59)
  matrix products: 77.2 us -> 3.99 us
  other arithmetic: 57.8 us -> 9.68 us
  Pallas kernels: 0 us -> 39.6 us
  local copies, waits for them, and re-layouts: 41.9 us -> 3.84 us
  waiting for transfers between devices: 7.12 us -> 17 us
  starting transfers between devices: 19 us -> 9.81 us
    dot_general x42 -> x2, matrix products: 77.2 us -> 3.99 us  [the longest x1 3.26 us: local(): pre = jnp.dot(features, w_first, preferred_element_type=F32) + b_first]
    psum x1 -> x0, blocking collectives: 49.8 us -> none  [local(): w_grad, b_grad = lax.psum((local_w, local_b), ('dp', 'table'))]
    all_to_all x2 -> x3, blocking collectives: 31.4 us -> 80 us  [the longest x1 34.2 us: local(): lax.all_to_all(chunks, ('dp', 'ty'), split_axis=0, concat_axis=0, tiled=T...]
    pallas_call x0 -> x3, Pallas kernels: none -> 39.6 us  [the longest x1 21 us: local(): pl.pallas_call(functools.partial(bucket_kernel, n_plane, cap), out_shape=...]
    add x36 -> x0, other arithmetic: 22.7 us -> none  [the longest x18 11.5 us: one_block(): wanted = start + jnp.arange(block, dtype=jnp.int32)]
    reduce_sum x20 -> x1, other arithmetic: 22.1 us -> 0.84 us  [local(): w_own = jnp.sum(w_part.astype(F32), axis=0).astype(BF)]
    dynamic_slice x36 -> x0, local copies, waits for them, and re-layouts: 20.9 us -> none  [the longest x18 10.6 us: row_sums(): return lax.map(one_block, starts).reshape(n_rows, values.shape[1])]
    unnamed x42 -> x14, local copies, waits for them, and re-layouts: 13.7 us -> 0.04 us
  transfers between devices with their start and end apart: 6 -> 3, of which waited for: 1 -> 2; matrix products, arithmetic and copies ran while one was open for 55% -> 4% of each run, Pallas kernels for 0% -> 22%
where the time goes in v1:
time: 179 us; the launch traced here: 178 us
  blocking collectives  80 us (45%)
  Pallas kernels  39.6 us (22%)
  waiting for transfers between devices  17 us (9%)
  between operations  14.2 us (8%)
  starting transfers between devices  9.81 us (5%)
  other arithmetic  9.68 us (5%)
  matrix products  3.99 us (2%)
  local copies, waits for them, and re-layouts  3.84 us (2%)
    all_to_all x1, blocking collectives, local(): lax.all_to_all(chunks, ('dp', 'ty'), split_axis=0, concat_axis=0, tiled=T...  34.2 us
    all_to_all x1, blocking collectives, local(): lax.all_to_all(jnp.broadcast_to(dpre[None], (N_Z,) + dpre.shape), 'tz', s...  27.8 us
    pallas_call x1, Pallas kernels, local(): pl.pallas_call(functools.partial(bucket_kernel, n_plane, cap), out_shape=...  21 us
    all_to_all x1, blocking collectives, local(): lax.all_to_all(w_part.reshape(n_plane, width // n_dev, hidden), ('dp', 't...  18 us
    pallas_call x1, Pallas kernels, local(): pl.pallas_call(functools.partial(sums_kernel, n_plane, seg, n_bias), out_...  15.9 us
    all_to_all x1, waiting for transfers between devices, local(): feat_in = lax.all_to_all(cut, 'tz', split_axis=0, concat_axis=0, tiled=True)  11.2 us
    convert_element_type x1, other arithmetic, local(): return (w_all.astype(F32), b_grad.reshape(hidden), adm_grad, q_grad, r_grad)  6.63 us
    all_to_all x1, starting transfers between devices, local(): feat_in = lax.all_to_all(cut, 'tz', split_axis=0, concat_axis=0, tiled=True)  6.32 us
  transfers between devices with their start and end apart: 3, of which 2 were waited for; matrix products, arithmetic and copies ran while one was open for 4% of the time, Pallas kernels for 22%

profile of v1, /device:TPU:0, one launch (start us, length us, event | category | flops | bytes accessed | tf_op | source)
XLA Modules:
  0.0 178.2 jit_solution(9226413426122921874)
XLA Ops:
  7.2 1.4 reshape.35
  8.6 1.2 copy.21
  9.8 6.3 %all-to-all-start.1 = ((bf16[4,128,512]{1,2,0:T(8,128)(2,1)}), bf16[4,128,512]{1,2,0:T(8,128)(2,1)S(1)}, u32[]{:S(2)}, u32[]{:S(2)}) async-start(bf16[4,128,512]{1,2,0:T(8,128)(2,1)} %bitcast.1), calls=%async_computation.1 | async-start | bytes 1048576 | tf_op jit(solution)/shard_map/all_to_all | solution.py:229
  16.1 3.3 %multiply_convert_fusion = bf16[128,1024]{1,0:T(8,128)(2,1)S(1)} fusion(bf16[128,2048]{1,0:T(8,128)(2,1)} %param.11, bf16[2048,1024]{1,0:T(8,128)(2,1)} %w_ref.1, bf16[128,1024]{1,0:T(8,128)(2,1)} %param.14, f32[1024]{0:T(1024)} %param.13), kind=kOutput, calls=%fused_computation.2 | convolution fusion | flops 538312704 | bytes 5246976 | tf_op jit(solution)/shard_map/dot_general | solution.py:232
  19.4 11.2 %all-to-all-done.1 = bf16[4,128,512]{1,2,0:T(8,128)(2,1)S(1)} async-done(((bf16[4,128,512]{1,2,0:T(8,128)(2,1)}), bf16[4,128,512]{1,2,0:T(8,128)(2,1)S(1)}, u32[]{:S(2)}, u32[]{:S(2)}) %all-to-all-start.1) | async-done | bytes 524320 | tf_op jit(solution)/shard_map/all_to_all | solution.py:229
  30.6 0.1 broadcast_in_dim.24
  30.8 27.8 %all_to_all.25 = bf16[4,128,1024]{2,1,0:T(8,128)(2,1)S(1)} all-to-all(bf16[4,128,1024]{2,1,0:T(8,128)(2,1)S(1)} %broadcast_in_dim.24), channel_id=1, replica_groups=mesh['dp'=4,'tz'=4,'ty'=2] {'tz'}, dimensions={0} | all-to-all | bytes 2097152 | tf_op jit(solution)/shard_map/all_to_all | solution.py:235
  58.7 0.7 bitcast_convert_fusion
  59.4 18.0 %all_to_all.26 = bf16[8,64,1024]{2,1,0:T(8,128)(2,1)S(1)} all-to-all(bf16[8,64,1024]{2,1,0:T(8,128)(2,1)S(1)} %bitcast.133), channel_id=1, replica_groups=mesh['dp'=4,'tz'=4,'ty'=2] {'dp','ty'}, dimensions={0} | all-to-all | bytes 2097152 | tf_op jit(solution)/shard_map/all_to_all | solution.py:262
  77.4 0.8 reduce_sum.12
  78.2 0.0 all-gather.2.cloned.1.call-update
  78.4 0.6 broadcast_in_dim.26
  79.0 3.5 %all-to-all-start.3 = ((s32[4,3,128,16]{2,3,1,0:T(8,128)}), s32[4,3,128,16]{2,3,1,0:T(8,128)S(1)}, u32[]{:S(2)}, u32[]{:S(2)}) async-start(s32[4,3,128,16]{2,3,1,0:T(8,128)} %broadcast_in_dim.26), calls=%async_computation.3 | async-start | bytes 196608 | tf_op jit(solution)/shard_map/all_to_all | solution.py:224
  82.5 5.8 %all-to-all-done.3 = s32[4,3,128,16]{2,3,1,0:T(8,128)S(1)} async-done(((s32[4,3,128,16]{2,3,1,0:T(8,128)}), s32[4,3,128,16]{2,3,1,0:T(8,128)S(1)}, u32[]{:S(2)}, u32[]{:S(2)}) %all-to-all-start.3) | async-done | bytes 98336 | tf_op jit(solution)/shard_map/all_to_all | solution.py:224
  88.3 0.1 copy.26
  88.4 0.1 copy.25
  88.6 0.1 copy.27
  88.7 0.8 fusion.13.row_ref
  89.5 1.4 add_select_fusion.6
  90.9 2.7 %slots.1 = (s32[3,4,16,128]{3,2,1,0:T(8,128)S(1)}, bf16[4,2048,128]{2,1,0:T(8,128)(2,1)S(1)}) custom-call(s32[512,16]{1,0:T(8,128)S(1)} %get-tuple-element.27.dq_ref, s32[512,16]{1,0:T(8,128)S(1)} %get-tuple-element.28.lq_ref, s32[512,16]{1,0:T(8,128)S(1)} %get-tuple-element.20.dr_ref, s32[512,16]{1,0:T(8,128)S(1)} %get-tuple-element.19.lr_ref, ...), custom_call_target="tpu_custom_call" | custom-call | flops 1000000000 | bytes 3000000 | tf_op jit(solution)/shard_map/slots/pallas_call | solution.py:250
  93.6 21.0 %buckets.1 = bf16[8,928,128]{2,1,0:T(8,128)(2,1)S(1)} custom-call(bf16[512,1024]{1,0:T(8,128)(2,1)S(1)} %bitcast.132, bf16[2048,1024]{1,0:T(8,128)(2,1)} %w_ref.1, s32[3,4,16,128]{3,2,1,0:T(8,128)S(1)} %get-tuple-element.11.slot_ref, bf16[4,2048,128]{2,1,0:T(8,128)(2,1)S(1)} %get-tuple-element.12.labels_ref), custom_call_target="tpu_custom_call" | custom-call | flops 12999999488 | bytes 10000000 | tf_op jit(solution)/shard_map/buckets/pallas_call | solution.py:267
  114.6 34.2 %all_to_all.27.in_ref = bf16[8,928,128]{2,1,0:T(8,128)(2,1)S(1)} all-to-all(bf16[8,928,128]{2,1,0:T(8,128)(2,1)S(1)} %buckets.1), channel_id=1, replica_groups=mesh['dp'=4,'tz'=4,'ty'=2] {'dp','ty'}, dimensions={0} | all-to-all | bytes 3801088 | tf_op jit(solution)/shard_map/all_to_all | solution.py:278
  148.8 15.9 %sums.1 = (f32[8,128]{1,0:T(8,128)}, f32[128,128]{1,0:T(8,128)}, f32[4096,128]{1,0:T(8,128)}, f32[4096,128]{1,0:T(8,128)}) custom-call(bf16[8,928,128]{2,1,0:T(8,128)(2,1)S(1)} %all_to_all.27.in_ref), custom_call_target="tpu_custom_call" | custom-call | flops 7000000000 | bytes 7000000 | tf_op jit(solution)/shard_map/sums/pallas_call | solution.py:284
  164.7 6.6 %convert_element_type.21 = f32[2048,1024]{1,0:T(8,128)} convert(bf16[2048,1024]{1,0:T(8,128)(2,1)} %all-gather.2.cloned.1.call-done) | non-fusion elementwise | flops 2097152 | bytes 12582912 | tf_op jit(solution)/shard_map/convert_element_type | solution.py:300
  (20 shorter events, 0.1 us)
Async XLA Ops:
  9.8 20.8 %all-to-all-start.1 = ((bf16[4,128,512]{1,2,0:T(8,128)(2,1)}), bf16[4,128,512]{1,2,0:T(8,128)(2,1)S(1)}, u32[]{:S(2)}, u32[]{:S(2)}) async-start(bf16[4,128,512]{1,2,0:T(8,128)(2,1)} %bitcast.1), calls=%async_computation.1 | async-start | bytes 1048576 | tf_op jit(solution)/shard_map/all_to_all | solution.py:229
  16.1 148.6 %all-gather.2.cloned.1.call-start = ((), (), s32[]{:S(2)}) async-start(), calls=%async_computation.5 | async-start | bytes 4325376 | tf_op jit(solution)/shard_map/all_gather | solution.py:281
  30.7 47.5 %copy-start.2 = (s32[128,16]{0,1:T(8,128)S(1)}, s32[128,16]{0,1:T(8,128)}, u32[]{:S(2)}) copy-start(s32[128,16]{0,1:T(8,128)} %param.19) | copy-start | bytes 24580
  30.8 47.5 %copy-start.3 = (s32[128,16,1]{0,2,1:T(1,128)S(1)}, s32[128,16,1]{0,2,1:T(1,128)}, u32[]{:S(2)}) copy-start(s32[128,16,1]{0,2,1:T(1,128)} %param.18) | copy-start | bytes 24580
  30.8 47.5 %copy-start.4 = (s32[128,16]{0,1:T(8,128)S(1)}, s32[128,16]{0,1:T(8,128)}, u32[]{:S(2)}) copy-start(s32[128,16]{0,1:T(8,128)} %param.15) | copy-start | bytes 24580
  30.8 47.5 %copy-start.5 = (s32[128,16]{0,1:T(8,128)S(1)}, s32[128,16]{0,1:T(8,128)}, u32[]{:S(2)}) copy-start(s32[128,16]{0,1:T(8,128)} %param.17) | copy-start | bytes 24580
  30.8 47.5 %copy-start.6 = (s32[128,16,1]{0,2,1:T(1,128)S(1)}, s32[128,16,1]{0,2,1:T(1,128)}, u32[]{:S(2)}) copy-start(s32[128,16,1]{0,2,1:T(1,128)} %param.16) | copy-start | bytes 24580
  30.8 47.5 %copy-start = (s32[128,16]{0,1:T(8,128)S(1)}, s32[128,16]{0,1:T(8,128)}, u32[]{:S(2)}) copy-start(s32[128,16]{0,1:T(8,128)} %param.21) | copy-start | bytes 24580
  30.8 47.5 %copy-start.1 = (s32[128,16,1]{0,2,1:T(1,128)S(1)}, s32[128,16,1]{0,2,1:T(1,128)}, u32[]{:S(2)}) copy-start(s32[128,16,1]{0,2,1:T(1,128)} %param.20) | copy-start | bytes 24580
  79.0 9.3 %all-to-all-start.3 = ((s32[4,3,128,16]{2,3,1,0:T(8,128)}), s32[4,3,128,16]{2,3,1,0:T(8,128)S(1)}, u32[]{:S(2)}, u32[]{:S(2)}) async-start(s32[4,3,128,16]{2,3,1,0:T(8,128)} %broadcast_in_dim.26), calls=%async_computation.3 | async-start | bytes 196608 | tf_op jit(solution)/shard_map/all_to_all | solution.py:224
Sparse Core Ops, SparseCore 0:
  78.4 74.6 all-gather.1

commit v2 on v1

--- a/solution.py
+++ b/solution.py
@@ -199,7 +199,8 @@
 def local(
     features, w_first, b_first, grad_out, admit, owner, adm_row, q_shard, q_local, r_shard, r_local
 ):
-    n_dp = lax.axis_size("dp")
+    n_dp = lax.axis_size("x") * lax.axis_size("core")
+    n_core = lax.axis_size("core")
     n_y = lax.axis_size("ty")
     n_table = N_Z * n_y
     n_dev = n_dp * n_table
@@ -221,20 +222,25 @@
             jnp.where(admit == 1, owner[:, :, 0] * (ADM_DEV * n_table) + adm_row, -1),
         ]
     )
-    codes = lax.all_to_all(
-        jnp.broadcast_to(codes[None], (N_Z,) + codes.shape), "tz", split_axis=0, concat_axis=0, tiled=True
+    codes = lax.all_gather(codes, "tz", axis=0)
+
+    share = width // n_dev
+    wide = width // (n_core * N_Z)
+    cut = jnp.stack(
+        [
+            jnp.concatenate(
+                [features[:, (c * N_Z + z) * wide : (c * N_Z + z + 1) * wide] for c in range(n_core)], axis=1
+            )
+            for z in range(N_Z)
+        ]
     )
-    share = width // n_dev * n_y
-    cut = features.reshape(n_s, n_dp, N_Z, share).transpose(2, 0, 1, 3).reshape(N_Z, n_s, n_dp * share)
     feat_in = lax.all_to_all(cut, "tz", split_axis=0, concat_axis=0, tiled=True)
-    feat_in = feat_in.reshape(N_Z * n_s, n_dp * share)
+    feat_in = feat_in.reshape(N_Z * n_s, n_core * wide)
 
     pre = jnp.dot(features, w_first, preferred_element_type=F32) + b_first
     sig = jax.nn.sigmoid(pre)
     dpre = (grad_out.astype(F32) * sig * (1.0 + pre * (1.0 - sig))).astype(BF)
-    dpre = lax.all_to_all(
-        jnp.broadcast_to(dpre[None], (N_Z,) + dpre.shape), "tz", split_axis=0, concat_axis=0, tiled=True
-    ).reshape(N_Z * n_s, hidden)
+    dpre = lax.all_gather(dpre, "tz", axis=0, tiled=True)
 
     def in_plane(code, block):
         dev = code // block
@@ -260,7 +266,7 @@
 
     w_part = lax.dot_general(feat_in, dpre, (((0,), (0,)), ((), ())), preferred_element_type=F32).astype(BF)
     w_part = lax.all_to_all(
-        w_part.reshape(n_plane, width // n_dev, hidden), ("dp", "ty"), split_axis=0, concat_axis=0, tiled=True
+        w_part.reshape(n_plane, share, hidden), ("core", "x", "ty"), split_axis=0, concat_axis=0, tiled=True
     )
 
     n_rows = 2 * seg + ADM_DEV + 16 + 2 * n_bias
@@ -272,13 +278,18 @@
             pltpu.VMEM((2, n_plane, seg, E), F32),
         ],
         compiler_params=pltpu.CompilerParams(vmem_limit_bytes=VMEM_LIMIT),
-        cost_estimate=pl.CostEstimate(flops=13 * 10**9, bytes_accessed=10**7, transcendentals=0),
+        cost_estimate=pl.CostEstimate(flops=20 * 10**9, bytes_accessed=4 * 10**7, transcendentals=0),
         name="buckets",
     )(dpre, w_first, slots, labels)
-    chunks = lax.all_to_all(chunks, ("dp", "ty"), split_axis=0, concat_axis=0, tiled=True)
-
+
+    w_part, chunks = lax.optimization_barrier((w_part, chunks))
     w_own = jnp.sum(w_part.astype(F32), axis=0).astype(BF)
-    w_all = lax.all_gather(w_own, ("dp", "tz", "ty"), axis=0, tiled=True)
+    w_own, chunks = lax.optimization_barrier((w_own, chunks))
+    chunks = lax.all_to_all(chunks, ("x", "core", "ty"), split_axis=0, concat_axis=0, tiled=True)
+    w_own = lax.all_gather(w_own, ("x", "ty"), axis=0, tiled=True)
+    w_own, chunks = lax.optimization_barrier((w_own, chunks))
+    w_own = lax.all_gather(w_own, "tz", axis=0, tiled=True)
+    w_all = lax.all_gather(w_own, "core", axis=0, tiled=True)
 
     n_tall = n_plane * -(-seg // E)
     b_grad, adm_grad, q_grad, r_grad = pl.pallas_call(
@@ -302,8 +313,8 @@
 
 def solution(mesh):
     n_dp, n_table = mesh.devices.shape
-    fine = Mesh(mesh.devices.reshape(n_dp, N_Z, n_table // N_Z), ("dp", "tz", "ty"))
-    every = ("dp", "tz", "ty")
+    every = ("x", "core", "tz", "ty")
+    fine = Mesh(mesh.devices.reshape(n_dp // 2, 2, N_Z, n_table // N_Z), every)
     two, three = P(every, None), P(every, None, None)
     in_specs = (two, P(), P(), two, two, three, two, three, two, three, two)
     out_specs = (P(), P(), two, two, two)

time: 179 us -> 199 us (1.11)
  waiting for transfers between devices: 17 us -> 46.3 us
  blocking collectives: 80 us -> 62.7 us
  starting transfers between devices: 9.81 us -> 15.3 us
  matrix products: 3.99 us -> 7.19 us
    all_to_all x3 -> x0, blocking collectives: 80 us -> none  [the longest x1 34.2 us: local(): lax.all_to_all(chunks, ('dp', 'ty'), split_axis=0, concat_axis=0, tiled=T...]
    all_gather x0 -> x2, blocking collectives: none -> 62.7 us  [the longest x1 32.1 us: local(): codes = lax.all_gather(codes, 'tz', axis=0)]
    all_gather x1 -> x3, waiting for transfers between devices: 0.01 us -> 46.2 us  [the longest x1 46.2 us: local(): w_own = lax.all_gather(w_own, 'tz', axis=0, tiled=True)]
    all_to_all x1, waiting for transfers between devices: 11.2 us -> 0.01 us  [local(): feat_in = lax.all_to_all(cut, 'tz', split_axis=0, concat_axis=0, tiled=True)]
    all_to_all x1 -> x2, waiting for transfers between devices: 5.8 us -> 0.01 us  [the longest x1 0.01 us: local(): lax.all_to_all(chunks, ('x', 'core', 'ty'), split_axis=0, concat_axis=0,...]
    all_to_all x1 -> x2, starting transfers between devices: 3.49 us -> 8.6 us  [the longest x1 4.43 us: local(): lax.all_to_all(w_part.reshape(n_plane, share, hidden), ('core', 'x', 'ty'...]
    reshape x2 -> x0, local copies, waits for them, and re-layouts: 2.64 us -> none  [local(): features.reshape(n_s, n_dp, N_Z, share).transpose(2, 0, 1, 3)]
    dot_general x1, matrix products: 0.73 us -> 3.17 us  [local(): lax.dot_general(feat_in, dpre, (((0,), (0,)), ((), ())), preferred_elemen...]
  transfers between devices with their start and end apart: 3 -> 6, of which waited for: 2 -> 1; matrix products, arithmetic and copies ran while one was open for 4% -> 2% of each run, Pallas kernels for 22% -> 20%
where the time goes in v2:
time: 199 us
  blocking collectives  62.7 us (32%)
  waiting for transfers between devices  46.3 us (23%)
  Pallas kernels  39.6 us (20%)
  starting transfers between devices  15.3 us (8%)
  between operations  14 us (7%)
  other arithmetic  11.1 us (6%)
  matrix products  7.19 us (4%)
  local copies, waits for them, and re-layouts  2.5 us (1%)
    all_gather x1, waiting for transfers between devices, local(): w_own = lax.all_gather(w_own, 'tz', axis=0, tiled=True)  46.2 us
    all_gather x1, blocking collectives, local(): codes = lax.all_gather(codes, 'tz', axis=0)  32.1 us
    all_gather x1, blocking collectives, local(): w_own = lax.all_gather(w_own, ('x', 'ty'), axis=0, tiled=True)  30.6 us
    pallas_call x1, Pallas kernels, local(): pl.pallas_call(functools.partial(bucket_kernel, n_plane, cap), out_shape=...  21 us
    pallas_call x1, Pallas kernels, local(): pl.pallas_call(functools.partial(sums_kernel, n_plane, seg, n_bias), out_...  15.9 us
    convert_element_type x1, other arithmetic, local(): return (w_all.astype(F32), b_grad.reshape(hidden), adm_grad, q_grad, r_grad)  6.63 us
    all_to_all x1, starting transfers between devices, local(): feat_in = lax.all_to_all(cut, 'tz', split_axis=0, concat_axis=0, tiled=True)  6.32 us
    all_to_all x1, starting transfers between devices, local(): lax.all_to_all(w_part.reshape(n_plane, share, hidden), ('core', 'x', 'ty'...  4.43 us
  transfers between devices with their start and end apart: 6, of which 1 were waited for; matrix products, arithmetic and copies ran while one was open for 2% of the time, Pallas kernels for 20%

profile of v2, /device:TPU:0, one launch (start us, length us, event | category | flops | bytes accessed | tf_op | source)
XLA Modules:
  0.0 198.6 jit_solution(15938654460878480372)
XLA Ops:
  7.2 0.0 all-gather.5.cloned.1.call-start
  7.2 4.0 %multiply_convert_fusion = bf16[128,1024]{1,0:T(8,128)(2,1)} fusion(bf16[128,2048]{1,0:T(8,128)(2,1)} %param.11, bf16[2048,1024]{1,0:T(8,128)(2,1)} %w_ref.1, bf16[128,1024]{1,0:T(8,128)(2,1)} %param.14, f32[1024]{0:T(1024)} %param.13), kind=kOutput, calls=%fused_computation.3 | convolution fusion | flops 538312704 | bytes 5246976 | tf_op jit(solution)/shard_map/dot_general | solution.py:240
  11.5 0.9 pad_maximum_fusion
  12.3 6.3 %all-to-all-start = ((bf16[4,128,512]{2,1,0:T(8,128)(2,1)}), bf16[4,128,512]{2,1,0:T(8,128)(2,1)S(1)}, u32[]{:S(2)}, u32[]{:S(2)}) async-start(bf16[4,128,512]{2,1,0:T(8,128)(2,1)} %pad_maximum_fusion), calls=%async_computation | async-start | bytes 1048576 | tf_op jit(solution)/shard_map/all_to_all | solution.py:237
  18.7 32.1 %all-gather = s32[12,128,16]{1,2,0:T(8,128)S(1)} all-gather(s32[3,128,16]{1,2,0:T(8,128)S(1)} %pad_add_fusion), channel_id=2, replica_groups=mesh['x'=2,'core'=2,'tz'=4,'ty'=2] {'tz'}, dimensions={0}, use_global_device_ids=true | all-gather | bytes 122880 | tf_op jit(solution)/shard_map/all_gather | solution.py:225
  50.9 0.1 copy.30
  51.0 0.1 copy.29
  51.2 0.1 copy.28
  51.3 0.8 fusion.13.row_ref
  52.1 1.4 add_select_fusion.6
  53.5 2.7 %slots.1 = (s32[3,4,16,128]{3,2,1,0:T(8,128)S(1)}, bf16[4,2048,128]{2,1,0:T(8,128)(2,1)S(1)}) custom-call(s32[512,16]{1,0:T(8,128)S(1)} %get-tuple-element.51.dq_ref, s32[512,16]{1,0:T(8,128)S(1)} %get-tuple-element.52.lq_ref, s32[512,16]{1,0:T(8,128)S(1)} %get-tuple-element.40.dr_ref, s32[512,16]{1,0:T(8,128)S(1)} %get-tuple-element.39.lr_ref, ...), custom_call_target="tpu_custom_call" | custom-call | flops 1000000000 | bytes 3000000 | tf_op jit(solution)/shard_map/slots/pallas_call | solution.py:256
  56.2 0.8 copy-done.3
  57.0 3.2 %convolution_convert_fusion = bf16[512,1024]{1,0:T(8,128)(2,1)} fusion(bf16[512,512]{1,0:T(8,128)(2,1)} %bitcast.135, bf16[512,1024]{1,0:T(8,128)(2,1)} %all-gather.5.cloned.1.call-done.d_ref), kind=kOutput, calls=%fused_computation | convolution fusion | flops 537395200 | bytes 2621440 | tf_op jit(solution)/shard_map/dot_general | solution.py:267
  60.1 4.4 %all-to-all-start.1 = ((bf16[8,64,1024]{2,1,0:T(8,128)(2,1)}), bf16[8,64,1024]{2,1,0:T(8,128)(2,1)}, u32[]{:S(2)}, u32[]{:S(2)}) async-start(bf16[8,64,1024]{2,1,0:T(8,128)(2,1)} %bitcast.134), calls=%async_computation.1 | async-start | bytes 2097152 | tf_op jit(solution)/shard_map/all_to_all | solution.py:268
  64.6 21.0 %buckets.1 = bf16[8,928,128]{2,1,0:T(8,128)(2,1)S(1)} custom-call(bf16[512,1024]{1,0:T(8,128)(2,1)S(1)} %copy-done.1, bf16[2048,1024]{1,0:T(8,128)(2,1)} %w_ref.1, s32[3,4,16,128]{3,2,1,0:T(8,128)S(1)} %get-tuple-element.17.slot_ref, bf16[4,2048,128]{2,1,0:T(8,128)(2,1)S(1)} %get-tuple-element.18.labels_ref), custom_call_target="tpu_custom_call" | custom-call | flops 20000000000 | bytes 40000000 | tf_op jit(solution)/shard_map/buckets/pallas_call | solution.py:273
  85.6 1.3 copy-done
  86.9 1.4 reduce_sum.12
  88.3 4.2 %all-to-all-start.2 = ((bf16[8,928,128]{2,1,0:T(8,128)(2,1)}), bf16[8,928,128]{2,1,0:T(8,128)(2,1)S(1)}, u32[]{:S(2)}, u32[]{:S(2)}) async-start(bf16[8,928,128]{2,1,0:T(8,128)(2,1)} %copy-done), calls=%async_computation.2 | async-start | bytes 3801088 | tf_op jit(solution)/shard_map/all_to_all | solution.py:288
  92.5 0.0 all-gather.7.cloned.1.call-start
  92.5 30.6 %all_gather.21 = bf16[256,1024]{1,0:T(8,128)(2,1)} all-gather(bf16[64,1024]{1,0:T(8,128)(2,1)S(1)} %reduce_sum.12), channel_id=1, replica_groups=mesh['x'=2,'core'=2,'tz'=4,'ty'=2] {'x','ty'}, dimensions={0}, use_global_device_ids=true | all-gather | bytes 655360 | tf_op jit(solution)/shard_map/all_gather | solution.py:289
  123.1 0.3 all-gather.9.cloned.1.call-start
  123.4 46.2 %all-gather.7.cloned.1.call-done = bf16[1024,1024]{1,0:T(8,128)(2,1)} async-done(((bf16[256,1024]{1,0:T(8,128)(2,1)}), bf16[1024,1024]{1,0:T(8,128)(2,1)}) %all-gather.7.cloned.1.call-update) | async-done | bytes 2097168 | tf_op jit(solution)/shard_map/all_gather | solution.py:291
  169.6 15.9 %sums.1 = (f32[8,128]{1,0:T(8,128)}, f32[128,128]{1,0:T(8,128)}, f32[4096,128]{1,0:T(8,128)}, f32[4096,128]{1,0:T(8,128)}) custom-call(bf16[8,928,128]{2,1,0:T(8,128)(2,1)S(1)} %all-to-all-done.2.in_ref), custom_call_target="tpu_custom_call" | custom-call | flops 7000000000 | bytes 7000000 | tf_op jit(solution)/shard_map/sums/pallas_call | solution.py:295
  185.5 6.6 %convert_element_type.17 = f32[2048,1024]{1,0:T(8,128)} convert(bf16[2048,1024]{1,0:T(8,128)(2,1)} %all-gather.9.cloned.1.call-done) | non-fusion elementwise | flops 2097152 | bytes 12582912 | tf_op jit(solution)/shard_map/convert_element_type | solution.py:311
  (35 shorter events, 0.2 us)
Async XLA Ops:
  7.2 4.1 %copy-start.2 = (bf16[128,2048]{1,0:T(8,128)(2,1)S(1)}, bf16[128,2048]{1,0:T(8,128)(2,1)}, u32[]{:S(2)}) copy-start(bf16[128,2048]{1,0:T(8,128)(2,1)} %param.11) | copy-start | bytes 1572868
  7.2 49.0 %all-gather.5.cloned.1.call-start = ((), (), s32[]{:S(2)}) async-start(), calls=%async_computation.3 | async-start | bytes 1310720 | tf_op jit(solution)/shard_map/all_gather | solution.py:243
  11.3 7.4 %copy-start.6 = (s32[128,16]{0,1:T(8,128)S(1)}, s32[128,16]{0,1:T(8,128)}, u32[]{:S(2)}) copy-start(s32[128,16]{0,1:T(8,128)} %param.19) | copy-start | bytes 24580
  11.3 7.4 %copy-start.7 = (s32[128,16,1]{0,2,1:T(1,128)S(1)}, s32[128,16,1]{0,2,1:T(1,128)}, u32[]{:S(2)}) copy-start(s32[128,16,1]{0,2,1:T(1,128)} %param.18) | copy-start | bytes 24580
  11.3 7.4 %copy-start.8 = (s32[128,16]{0,1:T(8,128)S(1)}, s32[128,16]{0,1:T(8,128)}, u32[]{:S(2)}) copy-start(s32[128,16]{0,1:T(8,128)} %param.15) | copy-start | bytes 24580
  11.3 7.3 %copy-start.9 = (s32[128,16]{0,1:T(8,128)S(1)}, s32[128,16]{0,1:T(8,128)}, u32[]{:S(2)}) copy-start(s32[128,16]{0,1:T(8,128)} %param.17) | copy-start | bytes 24580
  11.3 7.3 %copy-start.10 = (s32[128,16,1]{0,2,1:T(1,128)S(1)}, s32[128,16,1]{0,2,1:T(1,128)}, u32[]{:S(2)}) copy-start(s32[128,16,1]{0,2,1:T(1,128)} %param.16) | copy-start | bytes 24580
  11.3 7.4 %copy-start.4 = (s32[128,16]{0,1:T(8,128)S(1)}, s32[128,16]{0,1:T(8,128)}, u32[]{:S(2)}) copy-start(s32[128,16]{0,1:T(8,128)} %param.21) | copy-start | bytes 24580
  11.4 7.4 %copy-start.5 = (s32[128,16,1]{0,2,1:T(1,128)S(1)}, s32[128,16,1]{0,2,1:T(1,128)}, u32[]{:S(2)}) copy-start(s32[128,16,1]{0,2,1:T(1,128)} %param.20) | copy-start | bytes 24580
  12.3 43.8 %all-to-all-start = ((bf16[4,128,512]{2,1,0:T(8,128)(2,1)}), bf16[4,128,512]{2,1,0:T(8,128)(2,1)S(1)}, u32[]{:S(2)}, u32[]{:S(2)}) async-start(bf16[4,128,512]{2,1,0:T(8,128)(2,1)} %pad_maximum_fusion), calls=%async_computation | async-start | bytes 1048576 | tf_op jit(solution)/shard_map/all_to_all | solution.py:237
  56.2 0.8 copy-start.3
  57.0 7.6 %copy-start.1 = (bf16[512,1024]{1,0:T(8,128)(2,1)S(1)}, bf16[512,1024]{1,0:T(8,128)(2,1)}, u32[]{:S(2)}) copy-start(bf16[512,1024]{1,0:T(8,128)(2,1)} %all-gather.5.cloned.1.call-done.d_ref) | copy-start | bytes 3145732
  60.1 26.8 %all-to-all-start.1 = ((bf16[8,64,1024]{2,1,0:T(8,128)(2,1)}), bf16[8,64,1024]{2,1,0:T(8,128)(2,1)}, u32[]{:S(2)}, u32[]{:S(2)}) async-start(bf16[8,64,1024]{2,1,0:T(8,128)(2,1)} %bitcast.134), calls=%async_computation.1 | async-start | bytes 2097152 | tf_op jit(solution)/shard_map/all_to_all | solution.py:268
  85.6 1.3 copy-start
  88.3 34.8 %all-to-all-start.2 = ((bf16[8,928,128]{2,1,0:T(8,128)(2,1)}), bf16[8,928,128]{2,1,0:T(8,128)(2,1)S(1)}, u32[]{:S(2)}, u32[]{:S(2)}) async-start(bf16[8,928,128]{2,1,0:T(8,128)(2,1)} %copy-done), calls=%async_computation.2 | async-start | bytes 3801088 | tf_op jit(solution)/shard_map/all_to_all | solution.py:288
  92.5 77.1 %all-gather.7.cloned.1.call-start = ((), (), s32[]{:S(2)}) async-start(), calls=%async_computation.4 | async-start | bytes 2621440 | tf_op jit(solution)/shard_map/all_gather | solution.py:291
  123.1 62.4 %all-gather.9.cloned.1.call-start = ((), (), s32[]{:S(2)}) async-start(), calls=%async_computation.5 | async-start | bytes 6291456 | tf_op jit(solution)/shard_map/all_gather | solution.py:292
Sparse Core Ops, SparseCore 0:
  11.4 40.4 all-gather.4
  123.2 46.2 all-gather.6
  171.1 12.3 all-gather.8

commit v3 on v1

v3 whole, which is shorter than its diff:
```python
import functools

import jax
import jax.numpy as jnp
from jax import lax
from jax.experimental import pallas as pl
from jax.experimental.pallas import tpu as pltpu
from jax.sharding import Mesh, PartitionSpec as P

E = 128
ADM_DEV = 128
QROWS_DEV = 4096
N_Z = 4
N_CODE = 8
GROUPS = 4
VMEM_LIMIT = 50 * 1024 * 1024
BF = jnp.bfloat16
F32 = jnp.float32


def iota(shape, dim):
    return lax.broadcasted_iota(jnp.int32, shape, dim)


def dot(a, b, dims=((1,), (0,))):
    return lax.dot_general(a, b, (dims, ((), ())), preferred_element_type=F32)


def one_hot(wanted, row):
    row = jnp.broadcast_to(row, (16, E)).astype(jnp.int16)
    hit = jnp.where(wanted == row[None], jnp.ones((), BF), jnp.zeros((), BF))
    return hit.reshape(wanted.shape[0] * 16, E)


def rows_from(n, base=0):
    return (iota((n, E), 0) + base).astype(jnp.int16).reshape(n // 16, 16, E)


def call(kernel, name, out_shape, flops, traffic, **kwargs):
    return pl.pallas_call(
        kernel,
        out_shape=out_shape,
        compiler_params=pltpu.CompilerParams(vmem_limit_bytes=VMEM_LIMIT),
        cost_estimate=pl.CostEstimate(flops=flops, bytes_accessed=traffic, transcendentals=0),
        name=name,
        **kwargs,
    )


def cut_kernel(n_dp, n_y, n_table, x_ref, admit, owner, adm_row, q_shard, q_local, r_shard, r_local, out_ref):
    piece = x_ref.shape[1] // (n_dp * N_Z)
    wide = n_dp * piece
    plain = admit[...] == 0
    a_row = owner[...] * (ADM_DEV * n_table) + adm_row[...]
    a_dev = a_row // ADM_DEV

    def in_plane(dev, live, z):
        table = dev % n_table
        here = live & (table // n_y == z)
        return here, dev // n_table * n_y + table % n_y

    for z in range(N_Z):
        for d in range(n_dp):
            at = (d * N_Z + z) * piece
            out_ref[z, :, d * piece : (d + 1) * piece] = x_ref[:, at : at + piece]
        codes = []
        for shard, low in ((q_shard, q_local), (r_shard, r_local)):
            here, dest = in_plane(shard[...], plain, z)
            codes += [jnp.where(here, dest, -1), low[...] // 256, low[...] % 256]
        here, dest = in_plane(a_dev, jnp.logical_not(plain), z)
        codes += [jnp.where(here, dest, -1), a_row % ADM_DEV]
        block = jnp.concatenate(codes, axis=0).astype(F32).astype(BF)
        out_ref[z, :, wide : wide + block.shape[1]] = block


def dpre_kernel(x_ref, w_ref, b_ref, g_ref, out_ref):
    pre = dot(x_ref[...], w_ref[...]) + b_ref[...]
    sig = jax.nn.sigmoid(pre)
    dpre = (g_ref[...].astype(F32) * sig * (1.0 + pre * (1.0 - sig))).astype(BF)
    for z in range(N_Z):
        out_ref[z] = dpre


def slots_kernel(n_dest, cap, wide, in_ref, slot_ref, labels_ref, group_ref):
    n_s = in_ref.shape[1]
    n_feat = n_s // N_CODE
    sample = iota((n_s, n_s), 0)
    earlier = (sample < iota((n_s, n_s), 1)).astype(F32).astype(BF)
    ones = jnp.ones((n_s, n_s), BF)
    count = n_dest * n_feat
    at_row, at_col = iota((count, count), 0), iota((count, count), 1)
    before = ((at_row // n_feat == at_col // n_feat) & (at_col < at_row)).astype(F32).astype(BF)
    half = n_dest // 2
    lane = iota((n_s, E), 1) % 4
    for z in range(N_Z):
        codes = in_ref[z, :, wide : wide + n_s].astype(F32)
        plane = [codes[i * n_feat : (i + 1) * n_feat, :] for i in range(N_CODE)]
        for table in range(2):
            dest = plane[table * 3]
            hits = jnp.concatenate([jnp.where(dest == d, 1.0, 0.0) for d in range(n_dest)], axis=0)
            hits_bf = hits.astype(BF)
            rank = dot(hits_bf, earlier) + dot(before, dot(hits_bf, ones).astype(BF))
            rank = rank * hits
            total = rank[0:n_feat, :]
            for d in range(1, n_dest):
                total = total + rank[d * n_feat : (d + 1) * n_feat, :]
            slot = jnp.where(dest >= 0, dest * cap + total, -1.0)
            slot_ref[table, z, :, :] = slot.astype(jnp.int32)
        dest = plane[6]
        folded = jnp.where(dest >= half, dest - half, dest)
        slot_ref[2, z, :, :] = jnp.where(dest >= 0, folded * ADM_DEV + plane[7], -1.0).astype(jnp.int32)
        down = codes.T
        group_ref[z] = down[:, 6 * n_feat : 7 * n_feat]
        for f in range(n_feat):
            col = [down[:, i * n_feat + f : i * n_feat + f + 1] for i in (1, 2, 4, 5)]
            one = jnp.where(lane == 0, col[0], jnp.where(lane == 1, col[1], jnp.where(lane == 2, col[2], col[3])))
            labels_ref[z, f * n_s : (f + 1) * n_s, :] = one.astype(BF)


def w_kernel(n_plane, x_ref, d_ref, out_ref):
    wide = x_ref.shape[2] - E
    share = wide // n_plane
    x = jnp.concatenate([x_ref[z, :, 0:wide] for z in range(N_Z)], axis=0)
    res = dot(x, d_ref[...], ((0,), (0,))).astype(BF)
    for p in range(n_plane):
        out_ref[p] = res[p * share : (p + 1) * share, :]


def bucket_kernel(n_dest, cap, d_ref, w_ref, slot_ref, labels_ref, group_ref, out_ref, v_ref, a_ref, p_ref, mark_ref):
    n_rows, depth = d_ref.shape
    n_s = n_rows // N_Z
    n_feat = w_ref.shape[0] // E
    seg = N_Z * cap
    n_mark = -(-seg // E)
    half = n_dest // 2

    def lookups(step, carry):
        wide = 2 * E
        start = pl.multiple_of(step * wide, wide)
        res = dot(d_ref[...], w_ref[pl.ds(start, wide), :], ((1,), (1,)))
        for z in range(N_Z):
            for h in range(2):
                row = pl.multiple_of((step * 2 + h) * n_s, n_s)
                v_ref[z, pl.ds(row, n_s), 0:E] = res[z * n_s : (z + 1) * n_s, h * E : (h + 1) * E].astype(BF)
        return carry

    lax.fori_loop(0, n_feat // 2, lookups, 0)
    for z in range(N_Z):
        v_ref[z, :, E : 2 * E] = labels_ref[z]

    slots = n_dest * cap
    wanted = rows_from(slots)
    for z in range(N_Z):
        for which in range(2):
            for f in range(n_feat):
                p_ref[which * slots : (which + 1) * slots, f * n_s : (f + 1) * n_s] = one_hot(
                    wanted, slot_ref[which, z, f : f + 1, :]
                )
        for which in range(2):
            o = dot(p_ref[which * slots : (which + 1) * slots, :], v_ref[z])
            for d in range(n_dest):
                rows = o[d * cap : (d + 1) * cap, :]
                out_ref[d, which * seg + z * cap : which * seg + (z + 1) * cap, :] = rows[:, 0:E].astype(BF)
                mark_ref[which, d, z * cap : (z + 1) * cap, :] = rows[:, E : 2 * E]

    tall = half * ADM_DEV
    wanted = rows_from(tall)
    o = jnp.zeros((tall, 2 * E), F32)
    for z in range(N_Z):
        for f in range(n_feat):
            at = f * n_s
            p_ref[0:tall, at : at + n_s] = one_hot(wanted, slot_ref[2, z, f : f + 1, :])
            upper = group_ref[z, :, f : f + 1] >= half
            v = v_ref[z, at : at + n_s, 0:E].astype(F32)
            a_ref[at : at + n_s, 0:E] = jnp.where(upper, 0.0, v).astype(BF)
            a_ref[at : at + n_s, E : 2 * E] = jnp.where(upper, v, 0.0).astype(BF)
        o = o + dot(p_ref[0:tall, :], a_ref[...])
    for d in range(n_dest):
        at = d % half * ADM_DEV
        side = d // half * E
        out_ref[d, 2 * seg : 2 * seg + ADM_DEV, :] = o[at : at + ADM_DEV, side : side + E].astype(BF)

    bias = jnp.sum(d_ref[...].astype(F32), axis=0, keepdims=True)
    high = bias.astype(BF)
    low = (bias - high.astype(F32)).astype(BF)
    n_bias = depth // E
    bias_rows = jnp.concatenate(
        [part[:, i * E : (i + 1) * E].astype(F32) for part in (high, low) for i in range(n_bias)], axis=0
    ).astype(BF)
    at_mark = 2 * seg + ADM_DEV

    def finish(d, carry):
        lane = iota((seg, E), 1) % 4
        mixed = jnp.where(lane < 2, mark_ref[0, d], mark_ref[1, d])
        if seg % E:
            mixed = jnp.concatenate([mixed, jnp.zeros((n_mark * E - seg, E), F32)], axis=0)
        rows = iota((16, E), 0) // 4
        marks = jnp.zeros((16, E), F32)
        for j in range(n_mark):
            across = mixed[j * E : (j + 1) * E, :].T
            marks = jnp.where(rows == j, across[0:16, :], marks)
        out_ref[d, at_mark : at_mark + 16, :] = marks.astype(BF)
        out_ref[d, at_mark + 16 : at_mark + 16 + 2 * n_bias, :] = bias_rows
        return carry

    lax.fori_loop(0, n_dest, finish, 0)


def sums_kernel(n_src, seg, n_bias, in_ref, bias_ref, adm_ref, q_ref, r_ref, v_ref, p_ref):
    n_mark = -(-seg // E)
    at_mark = 2 * seg + ADM_DEV
    adm = jnp.zeros((ADM_DEV, E), F32)
    bias = jnp.zeros((2 * n_bias, E), F32)
    for s in range(n_src):
        adm = adm + in_ref[s, 2 * seg : at_mark, :].astype(F32)
        bias = bias + in_ref[s, at_mark + 16 : at_mark + 16 + 2 * n_bias, :].astype(F32)
    adm_ref[...] = adm
    bias_ref[...] = bias[0:n_bias, :] + bias[n_bias:, :]

    per_group = QROWS_DEV // GROUPS
    wanted = rows_from(per_group)
    for table, out in enumerate((q_ref, r_ref)):

        def spread(s, carry):
            marks = in_ref[s, at_mark : at_mark + 16, :].astype(F32)
            down = jnp.concatenate([marks, jnp.zeros((E - 16, E), F32)], axis=0).T
            for j in range(n_mark):
                at = j * 4 + table * 2
                label = marks[at : at + 1, :] * 256.0 + marks[at + 1 : at + 2, :]
                label = label.astype(jnp.int32) % per_group
                if (j + 1) * E > seg:
                    label = jnp.where(iota((1, E), 1) + j * E < seg, label, -1)
                start = pl.multiple_of((s * n_mark + j) * E, E)
                p_ref[:, pl.ds(start, E)] = one_hot(wanted, label)
                group = (down[:, at : at + 1] * 256.0 + down[:, at + 1 : at + 2]).astype(jnp.int32) // per_group
                rows = in_ref[s, table * seg + j * E : table * seg + (j + 1) * E, :].astype(F32)
                for g in range(GROUPS):
                    v_ref[pl.ds(start, E), g * E : (g + 1) * E] = jnp.where(group == g, rows, 0.0).astype(BF)
            return carry

        lax.fori_loop(0, n_src, spread, 0)
        block = 512
        for b in range(per_group // block):
            o = dot(p_ref[b * block : (b + 1) * block, :], v_ref[...])
            for g in range(GROUPS):
                start = g * per_group + b * block
                out[start : start + block, :] = o[:, g * E : (g + 1) * E]


def widen_kernel(x_ref, *refs):
    refs[-1][...] = x_ref[...].astype(F32)


def widen(x, half, hidden, so_far):
    rows, cols = x.shape
    block = 256
    spec = pl.BlockSpec((block, cols), lambda i: (i, 0))
    more = {} if so_far is None else {"input_output_aliases": {1: 0}}
    args = (x,) if so_far is None else (x, so_far)
    return call(
        widen_kernel,
        "widen",
        jax.ShapeDtypeStruct((rows, hidden), F32),
        rows * cols,
        rows * cols * 6,
        grid=(rows // block,),
        in_specs=[spec] + [pl.BlockSpec(memory_space=pl.ANY)] * (len(args) - 1),
        out_specs=pl.BlockSpec((block, cols), lambda i: (i, half)),
        **more,
    )(*args)


def after(x, *others):
    return lax.optimization_barrier((x,) + others)[0]


def local(
    features, w_first, b_first, grad_out, admit, owner, adm_row, q_shard, q_local, r_shard, r_local
):
    n_dp = lax.axis_size("dp")
    n_y = lax.axis_size("ty")
    n_table = N_Z * n_y
    n_dev = n_dp * n_table
    n_plane = n_dp * n_y
    n_s, width = features.shape
    hidden = w_first.shape[1]
    n_feat = width // E
    count = n_s * n_feat
    cap = max(2, 3 * count // (2 * n_dev))
    seg = N_Z * cap
    n_bias = hidden // E
    share = width // n_dev
    wide = width // N_Z
    shape = jax.ShapeDtypeStruct

    lookup_args = [a.reshape(n_s, n_feat).T for a in (admit, owner, adm_row, q_shard, q_local, r_shard, r_local)]
    cut = call(
        functools.partial(cut_kernel, n_dp, n_y, n_table),
        "cut",
        shape((N_Z, n_s, wide + E), BF),
        10**7,
        2 * 10**6,
    )(features, *lookup_args)
    feat_in = lax.all_to_all(cut, "tz", split_axis=0, concat_axis=0, tiled=True)

    block = min(256, hidden)
    dpre = call(
        dpre_kernel,
        "dpre",
        shape((N_Z, n_s, hidden), BF),
        2 * n_s * width * hidden,
        6 * 10**6,
        grid=(hidden // block,),
        in_specs=[
            pl.BlockSpec((n_s, width), lambda i: (0, 0)),
            pl.BlockSpec((width, block), lambda i: (0, i)),
            pl.BlockSpec((1, block), lambda i: (0, i)),
            pl.BlockSpec((n_s, block), lambda i: (0, i)),
        ],
        out_specs=pl.BlockSpec((N_Z, n_s, block), lambda i: (0, 0, i)),
    )(after(features, cut), w_first, b_first.reshape(1, hidden), grad_out)
    feat_in = after(feat_in, dpre)
    dpre = lax.all_to_all(dpre, "tz", split_axis=0, concat_axis=0, tiled=True).reshape(N_Z * n_s, hidden)

    slots, labels, group = call(
        functools.partial(slots_kernel, n_plane, cap, wide),
        "slots",
        (
            shape((3, N_Z, n_feat, n_s), jnp.int32),
            shape((N_Z, count, E), BF),
            shape((N_Z, n_s, n_feat), F32),
        ),
        10**9,
        3 * 10**6,
    )(feat_in)
    dpre = after(dpre, slots)

    w_part = call(
        functools.partial(w_kernel, n_plane),
        "w_part",
        shape((n_plane, share, hidden), BF),
        2 * N_Z * n_s * wide * hidden,
        3 * 10**6,
    )(feat_in, dpre)
    dpre = after(dpre, w_part)
    w_part = lax.all_to_all(w_part, ("dp", "ty"), split_axis=0, concat_axis=0, tiled=True)

    n_rows = 2 * seg + ADM_DEV + 16 + 2 * n_bias
    tallest = max(2 * n_plane * cap, n_plane // 2 * ADM_DEV)
    chunks = call(
        functools.partial(bucket_kernel, n_plane, cap),
        "buckets",
        shape((n_plane, n_rows, E), BF),
        15 * 10**9,
        4 * 10**7,
        scratch_shapes=[
            pltpu.VMEM((N_Z, count, 2 * E), BF),
            pltpu.VMEM((count, 2 * E), BF),
            pltpu.VMEM((tallest, count), BF),
            pltpu.VMEM((2, n_plane, seg, E), F32),
        ],
    )(dpre, w_first, slots, labels, group)

    w_part = after(w_part, chunks)
    w_own = jnp.sum(w_part.astype(F32), axis=0).astype(BF)
    w_own, chunks = lax.optimization_barrier((w_own, chunks))
    halves = [
        lax.all_gather(w_own[:, h * (hidden // 2) : (h + 1) * (hidden // 2)], ("dp", "tz", "ty"), axis=0, tiled=True)
        for h in range(2)
    ]
    chunks = lax.all_to_all(chunks, ("dp", "ty"), split_axis=0, concat_axis=0, tiled=True)

    tall = n_plane * -(-seg // E) * E
    b_grad, adm_grad, q_grad, r_grad = call(
        functools.partial(sums_kernel, n_plane, seg, n_bias),
        "sums",
        (
            shape((n_bias, E), F32),
            shape((ADM_DEV, E), F32),
            shape((QROWS_DEV, E), F32),
            shape((QROWS_DEV, E), F32),
        ),
        7 * 10**9,
        7 * 10**6,
        scratch_shapes=[
            pltpu.VMEM((tall, GROUPS * E), BF),
            pltpu.VMEM((QROWS_DEV // GROUPS, tall), BF),
        ],
    )(chunks)
    w_grad = widen(after(halves[0], b_grad), 0, hidden, None)
    w_grad = widen(halves[1], 1, hidden, w_grad)
    return (w_grad, b_grad.reshape(hidden), adm_grad, q_grad, r_grad)


def solution(mesh):
    n_dp, n_table = mesh.devices.shape
    every = ("dp", "tz", "ty")
    fine = Mesh(mesh.devices.reshape(n_dp, N_Z, n_table // N_Z), every)
    two, three = P(every, None), P(every, None, None)
    in_specs = (two, P(), P(), two, two, three, two, three, two, three, two)
    out_specs = (P(), P(), two, two, two)
    return jax.shard_map(local, mesh=fine, in_specs=in_specs, out_specs=out_specs, check_vma=False)
```

time: 179 us -> 222 us (1.24)
  waiting for transfers between devices: 17 us -> 95.4 us
  blocking collectives: 80 us -> 30 us
  Pallas kernels: 39.6 us -> 54.6 us
  other arithmetic: 9.68 us -> 1.43 us
  local copies, waits for them, and re-layouts: 3.84 us -> 11.1 us
  starting transfers between devices: 9.81 us -> 14.3 us
  matrix products: 3.99 us -> 0 us
    all_gather x1 -> x2, waiting for transfers between devices: 0.01 us -> 61.1 us  [local(): lax.all_gather(w_own[:, h * (hidden // 2):(h + 1) * (hidden // 2)], ('dp'...]
    all_to_all x2 -> x0, blocking collectives: 45.8 us -> none  [the longest x1 27.8 us: local(): lax.all_to_all(jnp.broadcast_to(dpre[None], (N_Z,) + dpre.shape), 'tz', s...]
    all_to_all x1 -> x2, waiting for transfers between devices: 5.8 us -> 20.9 us  [the longest x1 20.9 us: local(): lax.all_to_all(dpre, 'tz', split_axis=0, concat_axis=0, tiled=True)]
    pallas_call x3 -> x8, Pallas kernels: 39.6 us -> 54.6 us  [the longest x1 19.9 us: local(): call(functools.partial(bucket_kernel, n_plane, cap), 'buckets', shape((n_...]
    unnamed x14 -> x28, local copies, waits for them, and re-layouts: 0.04 us -> 10.4 us
    convert_element_type x1 -> x0, other arithmetic: 6.63 us -> none  [local(): return (w_all.astype(F32), b_grad.reshape(hidden), adm_grad, q_grad, r_grad)]
    all_to_all x1 -> x2, starting transfers between devices: 3.49 us -> 7.77 us  [the longest x1 4.25 us: local(): lax.all_to_all(w_part, ('dp', 'ty'), split_axis=0, concat_axis=0, tiled=T...]
    all_to_all x1, blocking collectives: 34.2 us -> 30 us  [local(): lax.all_to_all(chunks, ('dp', 'ty'), split_axis=0, concat_axis=0, tiled=T...]
  transfers between devices with their start and end apart: 3 -> 5, of which waited for: 2 -> 4; matrix products, arithmetic and copies ran while one was open for 4% -> 0% of each run, Pallas kernels for 22% -> 22%
where the time goes in v3:
time: 222 us; the launch traced here: 221 us
  waiting for transfers between devices  95.4 us (43%)
  Pallas kernels  54.6 us (25%)
  blocking collectives  30 us (14%)
  starting transfers between devices  14.3 us (6%)
  between operations  14.1 us (6%)
  local copies, waits for them, and re-layouts  11.1 us (5%)
    all_gather x2, waiting for transfers between devices, local(): lax.all_gather(w_own[:, h * (hidden // 2):(h + 1) * (hidden // 2)], ('dp'...  61.1 us
    all_to_all x1, blocking collectives, local(): lax.all_to_all(chunks, ('dp', 'ty'), split_axis=0, concat_axis=0, tiled=T...  30 us
    all_to_all x1, waiting for transfers between devices, local(): lax.all_to_all(dpre, 'tz', split_axis=0, concat_axis=0, tiled=True)  20.9 us
    pallas_call x1, Pallas kernels, local(): call(functools.partial(bucket_kernel, n_plane, cap), 'buckets', shape((n_...  19.9 us
    pallas_call x1, Pallas kernels, local(): call(functools.partial(sums_kernel, n_plane, seg, n_bias), 'sums', (shape...  17.5 us
    all_to_all x1, waiting for transfers between devices, local(): feat_in = lax.all_to_all(cut, 'tz', split_axis=0, concat_axis=0, tiled=True)  12.7 us
    unnamed x28, local copies, waits for them, and re-layouts  10.4 us
    pallas_call x2, Pallas kernels, widen(): call(widen_kernel, 'widen', jax.ShapeDtypeStruct((rows, hidden), F32), ro...  6.96 us
  transfers between devices with their start and end apart: 5, of which 4 were waited for; matrix products, arithmetic and copies ran while one was open for 0% of the time, Pallas kernels for 22%

profile of v3, /device:TPU:0, one launch (start us, length us, event | category | flops | bytes accessed | tf_op | source)
XLA Modules:
  0.0 221.1 jit_solution(1036817564798932880)
XLA Ops:
  7.2 1.0 copy-done.2
  8.2 0.7 copy-done.5
  8.9 0.7 copy-done.6
  13.1 1.0 cut.1
  14.2 6.3 %all-to-all-start = ((bf16[4,128,640]{2,1,0:T(8,128)(2,1)}), bf16[4,128,640]{2,1,0:T(8,128)(2,1)S(1)}, u32[]{:S(2)}, u32[]{:S(2)}) async-start(bf16[4,128,640]{2,1,0:T(8,128)(2,1)} %cut.1), calls=%async_computation | async-start | bytes 1310720 | tf_op jit(solution)/shard_map/all_to_all | solution.py:304
  20.5 4.6 %dpre.1 = bf16[4,128,1024]{2,1,0:T(8,128)(2,1)} custom-call(bf16[128,2048]{1,0:T(8,128)(2,1)S(1)} %copy-done.3, bf16[2048,1024]{1,0:T(8,128)(2,1)} %w_ref.3, f32[1,1024]{1,0:T(1,128)S(1)} %bitcast.25, bf16[128,1024]{1,0:T(8,128)(2,1)S(1)} %copy-done.4), custom_call_target="tpu_custom_call" | custom-call | flops 536870912 | bytes 6000000 | tf_op jit(solution)/shard_map/dpre/pallas_call | solution.py:307
  25.1 12.7 %all-to-all-done.in_ref.x_ref = bf16[4,128,640]{2,1,0:T(8,128)(2,1)S(1)} async-done(((bf16[4,128,640]{2,1,0:T(8,128)(2,1)}), bf16[4,128,640]{2,1,0:T(8,128)(2,1)S(1)}, u32[]{:S(2)}, u32[]{:S(2)}) %all-to-all-start) | async-done | bytes 655392 | tf_op jit(solution)/shard_map/all_to_all | solution.py:304
  37.8 3.5 %all-to-all-start.1 = ((bf16[4,128,1024]{2,1,0:T(8,128)(2,1)}), bf16[4,128,1024]{2,1,0:T(8,128)(2,1)S(1)}, u32[]{:S(2)}, u32[]{:S(2)}) async-start(bf16[4,128,1024]{2,1,0:T(8,128)(2,1)} %dpre.1), calls=%async_computation.1 | async-start | bytes 2097152 | tf_op jit(solution)/shard_map/all_to_all | solution.py:323
  41.3 3.0 %slots.1 = (s32[3,4,16,128]{3,2,1,0:T(8,128)S(1)}, bf16[4,2048,128]{2,1,0:T(8,128)(2,1)S(1)}, f32[4,128,16]{2,1,0:T(8,128)S(1)}) custom-call(bf16[4,128,640]{2,1,0:T(8,128)(2,1)S(1)} %all-to-all-done.in_ref.x_ref), custom_call_target="tpu_custom_call" | custom-call | flops 1000000000 | bytes 3000000 | tf_op jit(solution)/shard_map/slots/pallas_call | solution.py:325
  44.3 1.3 copy-done.13
  45.6 20.9 %all-to-all-done.1 = bf16[4,128,1024]{2,1,0:T(8,128)(2,1)S(1)} async-done(((bf16[4,128,1024]{2,1,0:T(8,128)(2,1)}), bf16[4,128,1024]{2,1,0:T(8,128)(2,1)S(1)}, u32[]{:S(2)}, u32[]{:S(2)}) %all-to-all-start.1) | async-done | bytes 1048608 | tf_op jit(solution)/shard_map/all_to_all | solution.py:323
  66.5 1.7 w_part.1
  68.2 4.2 %all-to-all-start.2 = ((bf16[8,64,1024]{2,1,0:T(8,128)(2,1)}), bf16[8,64,1024]{2,1,0:T(8,128)(2,1)}, u32[]{:S(2)}, u32[]{:S(2)}) async-start(bf16[8,64,1024]{2,1,0:T(8,128)(2,1)} %w_part.1), calls=%async_computation.2 | async-start | bytes 2097152 | tf_op jit(solution)/shard_map/all_to_all | solution.py:346
  72.7 19.9 %buckets.1 = bf16[8,928,128]{2,1,0:T(8,128)(2,1)S(1)} custom-call(bf16[512,1024]{1,0:T(8,128)(2,1)S(1)} %bitcast.17, bf16[2048,1024]{1,0:T(8,128)(2,1)} %w_ref.3, s32[3,4,16,128]{3,2,1,0:T(8,128)S(1)} %get-tuple-element.22.slot_ref, bf16[4,2048,128]{2,1,0:T(8,128)(2,1)} %copy-done.13, f32[4,128,16]{2,1,0:T(8,128)S(1)} %get-tuple-element.26.group_ref), custom_call_target="tpu_custom_call" | custom-call | flops 15000000512 | bytes 40000000 | tf_op jit(solution)/shard_map/buckets/pallas_call | solution.py:350
  92.6 1.4 reduce_sum.12
  94.7 0.7 all-gather.3.cloned.1.call-update
  95.4 30.0 %all_to_all.20.in_ref = bf16[8,928,128]{2,1,0:T(8,128)(2,1)S(1)} all-to-all(bf16[8,928,128]{2,1,0:T(8,128)(2,1)S(1)} %buckets.1), channel_id=1, replica_groups=mesh['dp'=4,'tz'=4,'ty'=2] {'dp','ty'}, dimensions={0} | all-to-all | bytes 3801088 | tf_op jit(solution)/shard_map/all_to_all | solution.py:371
  125.5 17.5 %sums.1 = (f32[8,128]{1,0:T(8,128)}, f32[128,128]{1,0:T(8,128)}, f32[4096,128]{1,0:T(8,128)}, f32[4096,128]{1,0:T(8,128)}) custom-call(bf16[8,928,128]{2,1,0:T(8,128)(2,1)S(1)} %all_to_all.20.in_ref), custom_call_target="tpu_custom_call" | custom-call | flops 7000000000 | bytes 7000000 | tf_op jit(solution)/shard_map/sums/pallas_call | solution.py:374
  142.9 7.8 %all-gather.5.cloned.1.call-done.x_ref = bf16[2048,512]{1,0:T(8,128)(2,1)} async-done(((bf16[64,512]{1,0:T(8,128)(2,1)}), bf16[2048,512]{1,0:T(8,128)(2,1)}) %all-gather.5.cloned.1.call-update) | async-done | bytes 2097168 | tf_op jit(solution)/shard_map/all_gather | solution.py:368
  150.8 1.6 copy-done
  152.3 3.5 %widen.2.refs_0_ = f32[2048,1024]{1,0:T(8,128)} custom-call(bf16[2048,512]{1,0:T(8,128)(2,1)S(1)} %copy-done), custom_call_target="tpu_custom_call" | custom-call | flops 1048576 | bytes 6291456 | tf_op jit(solution)/shard_map/widen/pallas_call | solution.py:260
  155.8 53.3 %all-gather.3.cloned.1.call-done.x_ref = bf16[2048,512]{1,0:T(8,128)(2,1)} async-done(((bf16[64,512]{1,0:T(8,128)(2,1)}), bf16[2048,512]{1,0:T(8,128)(2,1)}) %all-gather.3.cloned.1.call-update) | async-done | bytes 2097168 | tf_op jit(solution)/shard_map/all_gather | solution.py:368
  209.2 1.6 copy-done.1
  210.7 3.5 %widen.3 = f32[2048,1024]{1,0:T(8,128)} custom-call(bf16[2048,512]{1,0:T(8,128)(2,1)S(1)} %copy-done.1, f32[2048,1024]{1,0:T(8,128)} %widen.2.refs_0_), custom_call_target="tpu_custom_call", output_to_operand_aliasing={{}: (1, {})} | custom-call | flops 1048576 | bytes 6291456 | tf_op jit(solution)/shard_map/widen/pallas_call | solution.py:260
  (27 shorter events, 4.5 us)
Async XLA Ops:
  7.2 13.3 %copy-start.12 = (f32[1024]{0:T(1024)S(1)}, f32[1024]{0:T(1024)}, u32[]{:S(2)}) copy-start(f32[1024]{0:T(1024)} %param.13) | copy-start | bytes 12292
  7.2 1.0 copy-start.2
  8.2 0.7 copy-start.5
  8.9 0.7 copy-start.6
  9.6 0.7 copy-start.7
  10.3 0.7 copy-start.8
  11.0 0.7 copy-start.9
  11.7 0.7 copy-start.10
  12.4 0.7 copy-start.11
  13.1 7.4 %copy-start.3 = (bf16[128,2048]{1,0:T(8,128)(2,1)S(1)}, bf16[128,2048]{1,0:T(8,128)(2,1)}, u32[]{:S(2)}) copy-start(bf16[128,2048]{1,0:T(8,128)(2,1)} %x_ref.2) | copy-start | bytes 1572868
  13.1 7.4 %copy-start.4 = (bf16[128,1024]{1,0:T(8,128)(2,1)S(1)}, bf16[128,1024]{1,0:T(8,128)(2,1)}, u32[]{:S(2)}) copy-start(bf16[128,1024]{1,0:T(8,128)(2,1)} %g_ref.1) | copy-start | bytes 786436
  14.2 23.6 %all-to-all-start = ((bf16[4,128,640]{2,1,0:T(8,128)(2,1)}), bf16[4,128,640]{2,1,0:T(8,128)(2,1)S(1)}, u32[]{:S(2)}, u32[]{:S(2)}) async-start(bf16[4,128,640]{2,1,0:T(8,128)(2,1)} %cut.1), calls=%async_computation | async-start | bytes 1310720 | tf_op jit(solution)/shard_map/all_to_all | solution.py:304
  37.8 28.7 %all-to-all-start.1 = ((bf16[4,128,1024]{2,1,0:T(8,128)(2,1)}), bf16[4,128,1024]{2,1,0:T(8,128)(2,1)S(1)}, u32[]{:S(2)}, u32[]{:S(2)}) async-start(bf16[4,128,1024]{2,1,0:T(8,128)(2,1)} %dpre.1), calls=%async_computation.1 | async-start | bytes 2097152 | tf_op jit(solution)/shard_map/all_to_all | solution.py:323
  44.3 1.3 copy-start.13
  68.2 24.4 %all-to-all-start.2 = ((bf16[8,64,1024]{2,1,0:T(8,128)(2,1)}), bf16[8,64,1024]{2,1,0:T(8,128)(2,1)}, u32[]{:S(2)}, u32[]{:S(2)}) async-start(bf16[8,64,1024]{2,1,0:T(8,128)(2,1)} %w_part.1), calls=%async_computation.2 | async-start | bytes 2097152 | tf_op jit(solution)/shard_map/all_to_all | solution.py:346
  72.5 78.3 %all-gather.5.cloned.1.call-start = ((), (), s32[]{:S(2)}) async-start(), calls=%async_computation.5 | async-start | bytes 2162688 | tf_op jit(solution)/shard_map/all_gather | solution.py:368
  94.7 114.5 %all-gather.3.cloned.1.call-start = ((), (), s32[]{:S(2)}) async-start(), calls=%async_computation.4 | async-start | bytes 2162688 | tf_op jit(solution)/shard_map/all_gather | solution.py:368
  150.8 1.6 copy-start
  209.2 1.6 copy-start.1
Sparse Core Ops, SparseCore 0:
  94.8 55.9 all-gather.4
  153.7 55.3 all-gather.2

commit v4 on v3

--- a/solution.py
+++ b/solution.py
@@ -13,6 +13,8 @@
 N_Z = 4
 N_CODE = 8
 GROUPS = 4
+LOG_ADM = 7
+LOG_GROUP = 10
 VMEM_LIMIT = 50 * 1024 * 1024
 BF = jnp.bfloat16
 F32 = jnp.float32
@@ -47,28 +49,34 @@
     )
 
 
-def cut_kernel(n_dp, n_y, n_table, x_ref, admit, owner, adm_row, q_shard, q_local, r_shard, r_local, out_ref):
+def cut_kernel(n_dp, n_y, n_table, x_ref, *refs):
+    labels, (out_ref, held, sems) = refs[:-3], refs[-3:]
+    copies = [pltpu.make_async_copy(ref, held.at[i], sems.at[i]) for i, ref in enumerate(labels)]
+    for copy in copies:
+        copy.start()
     piece = x_ref.shape[1] // (n_dp * N_Z)
     wide = n_dp * piece
-    plain = admit[...] == 0
-    a_row = owner[...] * (ADM_DEV * n_table) + adm_row[...]
-    a_dev = a_row // ADM_DEV
-
-    def in_plane(dev, live, z):
-        table = dev % n_table
-        here = live & (table // n_y == z)
-        return here, dev // n_table * n_y + table % n_y
-
     for z in range(N_Z):
         for d in range(n_dp):
             at = (d * N_Z + z) * piece
             out_ref[z, :, d * piece : (d + 1) * piece] = x_ref[:, at : at + piece]
+    for copy in copies:
+        copy.wait()
+    admit, owner, adm_row, q_shard, q_local, r_shard, r_local = [held[i] for i in range(len(labels))]
+    plain = admit == 0
+    a_row = owner * (ADM_DEV * n_table) + adm_row
+    a_dev = a_row >> LOG_ADM
+    y_bits, table_bits = n_y.bit_length() - 1, n_table.bit_length() - 1
+
+    def in_plane(dev, live, z):
+        here = live & (((dev & (n_table - 1)) >> y_bits) == z)
+        return jnp.where(here, ((dev >> table_bits) << y_bits) + (dev & (n_y - 1)), -1)
+
+    for z in range(N_Z):
         codes = []
         for shard, low in ((q_shard, q_local), (r_shard, r_local)):
-            here, dest = in_plane(shard[...], plain, z)
-            codes += [jnp.where(here, dest, -1), low[...] // 256, low[...] % 256]
-        here, dest = in_plane(a_dev, jnp.logical_not(plain), z)
-        codes += [jnp.where(here, dest, -1), a_row % ADM_DEV]
+            codes += [in_plane(shard, plain, z), low >> 8, low & 255]
+        codes += [in_plane(a_dev, jnp.logical_not(plain), z), a_row & (ADM_DEV - 1)]
         block = jnp.concatenate(codes, axis=0).astype(F32).astype(BF)
         out_ref[z, :, wide : wide + block.shape[1]] = block
 
@@ -77,23 +85,23 @@
     pre = dot(x_ref[...], w_ref[...]) + b_ref[...]
     sig = jax.nn.sigmoid(pre)
     dpre = (g_ref[...].astype(F32) * sig * (1.0 + pre * (1.0 - sig))).astype(BF)
-    for z in range(N_Z):
-        out_ref[z] = dpre
-
-
-def slots_kernel(n_dest, cap, wide, in_ref, slot_ref, labels_ref, group_ref):
+    out_ref[...] = dpre
+
+
+def slots_kernel(n_dest, cap, wide, z_ref, in_ref, slot_ref, labels_ref, group_ref):
     n_s = in_ref.shape[1]
     n_feat = n_s // N_CODE
     sample = iota((n_s, n_s), 0)
     earlier = (sample < iota((n_s, n_s), 1)).astype(F32).astype(BF)
     ones = jnp.ones((n_s, n_s), BF)
     count = n_dest * n_feat
+    feat_bits = n_feat.bit_length() - 1
     at_row, at_col = iota((count, count), 0), iota((count, count), 1)
-    before = ((at_row // n_feat == at_col // n_feat) & (at_col < at_row)).astype(F32).astype(BF)
+    before = ((at_row >> feat_bits == at_col >> feat_bits) & (at_col < at_row)).astype(F32).astype(BF)
     half = n_dest // 2
-    lane = iota((n_s, E), 1) % 4
-    for z in range(N_Z):
-        codes = in_ref[z, :, wide : wide + n_s].astype(F32)
+    lane = iota((n_s, E), 1) & 3
+    for z in range(N_Z):
+        codes = in_ref[z_ref[0] ^ z, :, wide : wide + n_s].astype(F32)
         plane = [codes[i * n_feat : (i + 1) * n_feat, :] for i in range(N_CODE)]
         for table in range(2):
             dest = plane[table * 3]
@@ -117,16 +125,22 @@
             labels_ref[z, f * n_s : (f + 1) * n_s, :] = one.astype(BF)
 
 
-def w_kernel(n_plane, x_ref, d_ref, out_ref):
+def w_kernel(n_plane, z_ref, x_ref, d0_ref, d1_ref, d2_ref, d3_ref, out_ref):
     wide = x_ref.shape[2] - E
     share = wide // n_plane
-    x = jnp.concatenate([x_ref[z, :, 0:wide] for z in range(N_Z)], axis=0)
-    res = dot(x, d_ref[...], ((0,), (0,))).astype(BF)
+    x = jnp.concatenate([x_ref[z_ref[0] ^ z, :, 0:wide] for z in range(N_Z)], axis=0)
+    d = jnp.concatenate([ref[...] for ref in (d0_ref, d1_ref, d2_ref, d3_ref)], axis=0)
+    res = dot(x, d, ((0,), (0,))).astype(BF)
     for p in range(n_plane):
         out_ref[p] = res[p * share : (p + 1) * share, :]
 
 
-def bucket_kernel(n_dest, cap, d_ref, w_ref, slot_ref, labels_ref, group_ref, out_ref, v_ref, a_ref, p_ref, mark_ref):
+def bucket_kernel(
+    n_dest, cap, d0_ref, d1_ref, d2_ref, d3_ref, w_ref, slot_ref, labels_ref, group_ref, out_ref, d_ref, v_ref, a_ref,
+    p_ref, mark_ref,
+):
+    for z, ref in enumerate((d0_ref, d1_ref, d2_ref, d3_ref)):
+        d_ref[z * ref.shape[0] : (z + 1) * ref.shape[0], :] = ref[...]
     n_rows, depth = d_ref.shape
     n_s = n_rows // N_Z
     n_feat = w_ref.shape[0] // E
@@ -190,11 +204,11 @@
     at_mark = 2 * seg + ADM_DEV
 
     def finish(d, carry):
-        lane = iota((seg, E), 1) % 4
+        lane = iota((seg, E), 1) & 3
         mixed = jnp.where(lane < 2, mark_ref[0, d], mark_ref[1, d])
         if seg % E:
             mixed = jnp.concatenate([mixed, jnp.zeros((n_mark * E - seg, E), F32)], axis=0)
-        rows = iota((16, E), 0) // 4
+        rows = iota((16, E), 0) >> 2
         marks = jnp.zeros((16, E), F32)
         for j in range(n_mark):
             across = mixed[j * E : (j + 1) * E, :].T
@@ -227,12 +241,12 @@
             for j in range(n_mark):
                 at = j * 4 + table * 2
                 label = marks[at : at + 1, :] * 256.0 + marks[at + 1 : at + 2, :]
-                label = label.astype(jnp.int32) % per_group
+                label = label.astype(jnp.int32) & (per_group - 1)
                 if (j + 1) * E > seg:
                     label = jnp.where(iota((1, E), 1) + j * E < seg, label, -1)
                 start = pl.multiple_of((s * n_mark + j) * E, E)
                 p_ref[:, pl.ds(start, E)] = one_hot(wanted, label)
-                group = (down[:, at : at + 1] * 256.0 + down[:, at + 1 : at + 2]).astype(jnp.int32) // per_group
+                group = down[:, at : at + 1].astype(jnp.int32) >> (LOG_GROUP - 8)
                 rows = in_ref[s, table * seg + j * E : table * seg + (j + 1) * E, :].astype(F32)
                 for g in range(GROUPS):
                     v_ref[pl.ds(start, E), g * E : (g + 1) * E] = jnp.where(group == g, rows, 0.0).astype(BF)
@@ -247,26 +261,30 @@
                 out[start : start + block, :] = o[:, g * E : (g + 1) * E]
 
 
-def widen_kernel(x_ref, *refs):
+def widen_kernel(core_ref, x_ref, *refs):
     refs[-1][...] = x_ref[...].astype(F32)
 
 
-def widen(x, half, hidden, so_far):
-    rows, cols = x.shape
-    block = 256
-    spec = pl.BlockSpec((block, cols), lambda i: (i, 0))
-    more = {} if so_far is None else {"input_output_aliases": {1: 0}}
-    args = (x,) if so_far is None else (x, so_far)
+def widen(core, x, tall, so_far):
+    rows, hidden = x.shape
+    block = tall // 2
+    alias = {} if so_far is None else {"input_output_aliases": {2: 0}}
+    args = (core, x) if so_far is None else (core, x, so_far)
+    grid_spec = pltpu.PrefetchScalarGridSpec(
+        num_scalar_prefetch=1,
+        grid=(rows // block,),
+        in_specs=[pl.BlockSpec((block, hidden), lambda i, core: (i, 0))]
+        + [pl.BlockSpec(memory_space=pl.ANY)] * (len(args) - 2),
+        out_specs=pl.BlockSpec((block, hidden), lambda i, core: ((i // 2 * 2 + core[0]) * 2 + i % 2, 0)),
+    )
     return call(
         widen_kernel,
         "widen",
-        jax.ShapeDtypeStruct((rows, hidden), F32),
-        rows * cols,
-        rows * cols * 6,
-        grid=(rows // block,),
-        in_specs=[spec] + [pl.BlockSpec(memory_space=pl.ANY)] * (len(args) - 1),
-        out_specs=pl.BlockSpec((block, cols), lambda i: (i, half)),
-        **more,
+        jax.ShapeDtypeStruct((2 * rows, hidden), F32),
+        rows * hidden,
+        rows * hidden * 6,
+        grid_spec=grid_spec,
+        **alias,
     )(*args)
 
 
@@ -277,7 +295,8 @@
 def local(
     features, w_first, b_first, grad_out, admit, owner, adm_row, q_shard, q_local, r_shard, r_local
 ):
-    n_dp = lax.axis_size("dp")
+    n_core = lax.axis_size("core")
+    n_dp = lax.axis_size("x") * n_core
     n_y = lax.axis_size("ty")
     n_table = N_Z * n_y
     n_dev = n_dp * n_table
@@ -291,7 +310,12 @@
     n_bias = hidden // E
     share = width // n_dev
     wide = width // N_Z
+    plane = ("x", "core", "ty")
     shape = jax.ShapeDtypeStruct
+    my_z = lax.axis_index("tz").astype(jnp.int32).reshape(1)
+    my_core = lax.axis_index("core").astype(jnp.int32).reshape(1)
+    scalar = pl.BlockSpec(memory_space=pltpu.SMEM)
+    array = pl.BlockSpec(memory_space=pltpu.VMEM)
 
     lookup_args = [a.reshape(n_s, n_feat).T for a in (admit, owner, adm_row, q_shard, q_local, r_shard, r_local)]
     cut = call(
@@ -300,6 +324,11 @@
         shape((N_Z, n_s, wide + E), BF),
         10**7,
         2 * 10**6,
+        in_specs=[array] + [pl.BlockSpec(memory_space=pl.ANY)] * len(lookup_args),
+        scratch_shapes=[
+            pltpu.VMEM((len(lookup_args), n_feat, n_s), jnp.int32),
+            pltpu.SemaphoreType.DMA((len(lookup_args),)),
+        ],
     )(features, *lookup_args)
     feat_in = lax.all_to_all(cut, "tz", split_axis=0, concat_axis=0, tiled=True)
 
@@ -307,7 +336,7 @@
     dpre = call(
         dpre_kernel,
         "dpre",
-        shape((N_Z, n_s, hidden), BF),
+        shape((n_s, hidden), BF),
         2 * n_s * width * hidden,
         6 * 10**6,
         grid=(hidden // block,),
@@ -317,10 +346,16 @@
             pl.BlockSpec((1, block), lambda i: (0, i)),
             pl.BlockSpec((n_s, block), lambda i: (0, i)),
         ],
-        out_specs=pl.BlockSpec((N_Z, n_s, block), lambda i: (0, 0, i)),
+        out_specs=pl.BlockSpec((n_s, block), lambda i: (0, i)),
     )(after(features, cut), w_first, b_first.reshape(1, hidden), grad_out)
+
+    def swap(x, k):
+        return lax.ppermute(x, "tz", [(z, z ^ k) for z in range(N_Z)])
+
+    far = swap(dpre, 2)
+    near = swap(dpre, 1)
+    sources = [dpre, near, far, swap(far, 1)]
     feat_in = after(feat_in, dpre)
-    dpre = lax.all_to_all(dpre, "tz", split_axis=0, concat_axis=0, tiled=True).reshape(N_Z * n_s, hidden)
 
     slots, labels, group = call(
         functools.partial(slots_kernel, n_plane, cap, wide),
@@ -332,8 +367,9 @@
         ),
         10**9,
         3 * 10**6,
-    )(feat_in)
-    dpre = after(dpre, slots)
+        in_specs=[scalar, array],
+    )(my_z, feat_in)
+    sources[3] = after(sources[3], slots)
 
     w_part = call(
         functools.partial(w_kernel, n_plane),
@@ -341,9 +377,10 @@
         shape((n_plane, share, hidden), BF),
         2 * N_Z * n_s * wide * hidden,
         3 * 10**6,
-    )(feat_in, dpre)
-    dpre = after(dpre, w_part)
-    w_part = lax.all_to_all(w_part, ("dp", "ty"), split_axis=0, concat_axis=0, tiled=True)
+        in_specs=[scalar] + [array] * 5,
+    )(my_z, feat_in, *sources)
+    sources[3] = after(sources[3], w_part)
+    w_part = lax.all_to_all(w_part, plane, split_axis=0, concat_axis=0, tiled=True)
 
     n_rows = 2 * seg + ADM_DEV + 16 + 2 * n_bias
     tallest = max(2 * n_plane * cap, n_plane // 2 * ADM_DEV)
@@ -354,21 +391,19 @@
         15 * 10**9,
         4 * 10**7,
         scratch_shapes=[
+            pltpu.VMEM((N_Z * n_s, hidden), BF),
             pltpu.VMEM((N_Z, count, 2 * E), BF),
             pltpu.VMEM((count, 2 * E), BF),
             pltpu.VMEM((tallest, count), BF),
             pltpu.VMEM((2, n_plane, seg, E), F32),
         ],
-    )(dpre, w_first, slots, labels, group)
+    )(*sources, w_first, slots, labels, group)
 
     w_part = after(w_part, chunks)
     w_own = jnp.sum(w_part.astype(F32), axis=0).astype(BF)
     w_own, chunks = lax.optimization_barrier((w_own, chunks))
-    halves = [
-        lax.all_gather(w_own[:, h * (hidden // 2) : (h + 1) * (hidden // 2)], ("dp", "tz", "ty"), axis=0, tiled=True)
-        for h in range(2)
-    ]
-    chunks = lax.all_to_all(chunks, ("dp", "ty"), split_axis=0, concat_axis=0, tiled=True)
+    w_half = lax.all_gather(w_own, ("x", "tz", "ty"), axis=0, tiled=True)
+    chunks = lax.all_to_all(chunks, plane, split_axis=0, concat_axis=0, tiled=True)
 
     tall = n_plane * -(-seg // E) * E
     b_grad, adm_grad, q_grad, r_grad = call(
@@ -387,15 +422,17 @@
             pltpu.VMEM((QROWS_DEV // GROUPS, tall), BF),
         ],
     )(chunks)
-    w_grad = widen(after(halves[0], b_grad), 0, hidden, None)
-    w_grad = widen(halves[1], 1, hidden, w_grad)
+    w_half = after(w_half, b_grad)
+    w_other = lax.ppermute(w_half, "core", [(c, n_core - 1 - c) for c in range(n_core)])
+    w_grad = widen(my_core, w_half, n_table * share, None)
+    w_grad = widen(1 - my_core, w_other, n_table * share, w_grad)
     return (w_grad, b_grad.reshape(hidden), adm_grad, q_grad, r_grad)
 
 
 def solution(mesh):
     n_dp, n_table = mesh.devices.shape
-    every = ("dp", "tz", "ty")
-    fine = Mesh(mesh.devices.reshape(n_dp, N_Z, n_table // N_Z), every)
+    every = ("x", "core", "tz", "ty")
+    fine = Mesh(mesh.devices.reshape(n_dp // 2, 2, N_Z, n_table // N_Z), every)
     two, three = P(every, None), P(every, None, None)
     in_specs = (two, P(), P(), two, two, three, two, three, two, three, two)
     out_specs = (P(), P(), two, two, two)

time: 222 us -> 166 us (0.75)
  waiting for transfers between devices: 95.4 us -> 44.7 us
  Pallas kernels: 54.6 us -> 51 us
  local copies, waits for them, and re-layouts: 11.1 us -> 8.83 us
    all_gather x2 -> x1, waiting for transfers between devices: 61.1 us -> 15.8 us  [local(): w_half = lax.all_gather(w_own, ('x', 'tz', 'ty'), axis=0, tiled=True)]
    ppermute x0 -> x4, waiting for transfers between devices: none -> 28.8 us  [the longest x3 28.5 us: swap(): return lax.ppermute(x, 'tz', [(z, z ^ k) for z in range(N_Z)])]
    all_to_all x2 -> x1, waiting for transfers between devices: 20.9 us -> 0.01 us  [local(): lax.all_to_all(w_part, plane, split_axis=0, concat_axis=0, tiled=True)]
    all_to_all x1, waiting for transfers between devices: 12.7 us -> 0.01 us  [local(): feat_in = lax.all_to_all(cut, 'tz', split_axis=0, concat_axis=0, tiled=True)]
    ppermute x0 -> x4, starting transfers between devices: none -> 5.02 us  [the longest x3 5.02 us: swap(): return lax.ppermute(x, 'tz', [(z, z ^ k) for z in range(N_Z)])]
    all_to_all x2 -> x1, starting transfers between devices: 7.77 us -> 4.25 us  [local(): lax.all_to_all(w_part, plane, split_axis=0, concat_axis=0, tiled=True)]
    pallas_call x3, Pallas kernels: 11.6 us -> 8.43 us  [the longest x2 4.84 us: widen(): call(widen_kernel, 'widen', jax.ShapeDtypeStruct((2 * rows, hidden), F32)...]
    unnamed x28 -> x26, local copies, waits for them, and re-layouts: 10.4 us -> 8.83 us
  transfers between devices with their start and end apart: 5 -> 7, of which waited for: 4 -> 5; matrix products, arithmetic and copies ran while one was open for 0% -> 0% of each run, Pallas kernels for 22% -> 28%
where the time goes in v4:
time: 166 us; the launch traced here: 165 us
  Pallas kernels  51 us (31%)
  waiting for transfers between devices  44.7 us (27%)
  blocking collectives  28.8 us (17%)
  starting transfers between devices  15.8 us (10%)
  between operations  14.1 us (8%)
  local copies, waits for them, and re-layouts  8.83 us (5%)
  other arithmetic  2.1 us (1%)
    all_to_all x1, blocking collectives, local(): lax.all_to_all(chunks, plane, split_axis=0, concat_axis=0, tiled=True)  28.8 us
    ppermute x3, waiting for transfers between devices, swap(): return lax.ppermute(x, 'tz', [(z, z ^ k) for z in range(N_Z)])  28.5 us
    pallas_call x1, Pallas kernels, local(): call(functools.partial(bucket_kernel, n_plane, cap), 'buckets', shape((n_...  19.9 us
    pallas_call x1, Pallas kernels, local(): call(functools.partial(sums_kernel, n_plane, seg, n_bias), 'sums', (shape...  16.8 us
    all_gather x1, waiting for transfers between devices, local(): w_half = lax.all_gather(w_own, ('x', 'tz', 'ty'), axis=0, tiled=True)  15.8 us
    unnamed x26, local copies, waits for them, and re-layouts  8.83 us
    all_to_all x1, starting transfers between devices, local(): feat_in = lax.all_to_all(cut, 'tz', split_axis=0, concat_axis=0, tiled=True)  6.33 us
    ppermute x3, starting transfers between devices, swap(): return lax.ppermute(x, 'tz', [(z, z ^ k) for z in range(N_Z)])  5.02 us
  transfers between devices with their start and end apart: 7, of which 5 were waited for; matrix products, arithmetic and copies ran while one was open for 0% of the time, Pallas kernels for 28%

profile of v4, /device:TPU:0, one launch (start us, length us, event | category | flops | bytes accessed | tf_op | source)
XLA Modules:
  0.0 165.4 jit_solution(9741412886656776928)
XLA Ops:
  7.2 1.0 copy-done
  8.2 0.7 copy-done.4
  8.9 0.7 copy-done.5
  9.6 0.7 copy-done.6
  13.1 1.1 cut.1
  14.2 6.3 %all-to-all-start = ((bf16[4,128,640]{2,1,0:T(8,128)(2,1)}), bf16[4,128,640]{2,1,0:T(8,128)(2,1)S(1)}, u32[]{:S(2)}, u32[]{:S(2)}) async-start(bf16[4,128,640]{2,1,0:T(8,128)(2,1)} %cut.1), calls=%async_computation | async-start | bytes 1310720 | tf_op jit(solution)/shard_map/all_to_all | solution.py:333
  20.6 3.6 %dpre.1.d0_ref = bf16[128,1024]{1,0:T(8,128)(2,1)S(1)} custom-call(bf16[128,2048]{1,0:T(8,128)(2,1)S(1)} %copy-done.1, bf16[2048,1024]{1,0:T(8,128)(2,1)} %w_ref.3, f32[1,1024]{1,0:T(1,128)S(1)} %bitcast.24, bf16[128,1024]{1,0:T(8,128)(2,1)S(1)} %copy-done.3), custom_call_target="tpu_custom_call" | custom-call | flops 536870912 | bytes 6000000 | tf_op jit(solution)/shard_map/dpre/pallas_call | solution.py:336
  24.2 3.0 %collective-permute-start.1 = (bf16[128,1024]{1,0:T(8,128)(2,1)S(1)}, bf16[128,1024]{1,0:T(8,128)(2,1)S(1)}, u32[]{:S(2)}, u32[]{:S(2)}) collective-permute-start(bf16[128,1024]{1,0:T(8,128)(2,1)S(1)} %dpre.1.d0_ref), channel_id=1, source_target_pairs={{0,4},{2,6},{4,0},{6,2},{1,5},{3,7},{5,1},{7,3},{8,12},{10,14},{12... | collective-permute-start | bytes 786440 | tf_op jit(solution)/shard_map/ppermute | solution.py:353
  27.1 21.9 %collective-permute-done.1.d2_ref = bf16[128,1024]{1,0:T(8,128)(2,1)S(1)} collective-permute-done((bf16[128,1024]{1,0:T(8,128)(2,1)S(1)}, bf16[128,1024]{1,0:T(8,128)(2,1)S(1)}, u32[]{:S(2)}, u32[]{:S(2)}) %collective-permute-start.1) | collective-permute-done | bytes 262176 | tf_op jit(solution)/shard_map/ppermute | solution.py:353
  49.1 2.0 %collective-permute-start = (bf16[128,1024]{1,0:T(8,128)(2,1)S(1)}, bf16[128,1024]{1,0:T(8,128)(2,1)S(1)}, u32[]{:S(2)}, u32[]{:S(2)}) collective-permute-start(bf16[128,1024]{1,0:T(8,128)(2,1)S(1)} %dpre.1.d0_ref), channel_id=1, source_target_pairs={{0,2},{2,0},{4,6},{6,4},{1,3},{3,1},{5,7},{7,5},{8,10},{10,8},{12,... | collective-permute-start | bytes 786440 | tf_op jit(solution)/shard_map/ppermute | solution.py:353
  51.1 3.0 %slots.1 = (s32[3,4,16,128]{3,2,1,0:T(8,128)S(1)}, bf16[4,2048,128]{2,1,0:T(8,128)(2,1)S(1)}, f32[4,128,16]{2,1,0:T(8,128)S(1)}) custom-call(s32[1]{0:T(128)} %bitcast.1.z_ref, bf16[4,128,640]{2,1,0:T(8,128)(2,1)S(1)} %all-to-all-done.in_ref.x_ref), custom_call_target="tpu_custom_call" | custom-call | flops 1000000000 | bytes 3000000 | tf_op jit(solution)/shard_map/slots/pallas_call | solution.py:360
  54.1 1.3 copy-done.12
  55.4 2.9 %collective-permute-done.2.d3_ref = bf16[128,1024]{1,0:T(8,128)(2,1)S(1)} collective-permute-done((bf16[128,1024]{1,0:T(8,128)(2,1)S(1)}, bf16[128,1024]{1,0:T(8,128)(2,1)S(1)}, u32[]{:S(2)}, u32[]{:S(2)}) %collective-permute-start.2) | collective-permute-done | bytes 262176 | tf_op jit(solution)/shard_map/ppermute | solution.py:353
  58.3 3.6 %collective-permute-done.d1_ref = bf16[128,1024]{1,0:T(8,128)(2,1)S(1)} collective-permute-done((bf16[128,1024]{1,0:T(8,128)(2,1)S(1)}, bf16[128,1024]{1,0:T(8,128)(2,1)S(1)}, u32[]{:S(2)}, u32[]{:S(2)}) %collective-permute-start) | collective-permute-done | bytes 262176 | tf_op jit(solution)/shard_map/ppermute | solution.py:353
  62.0 1.7 %w_part.1 = bf16[8,64,1024]{2,1,0:T(8,128)(2,1)} custom-call(s32[1]{0:T(128)} %bitcast.1.z_ref, bf16[4,128,640]{2,1,0:T(8,128)(2,1)S(1)} %all-to-all-done.in_ref.x_ref, bf16[128,1024]{1,0:T(8,128)(2,1)S(1)} %dpre.1.d0_ref, bf16[128,1024]{1,0:T(8,128)(2,1)S(1)} %collective-permute-done.d1_ref, bf16[128,1024]{1,0:T(8,128)(2,1)S(1)} %collective-permute-done.1.d2_ref, ...), custom_call_target="tpu_custom_call" | custom-call | flops 536870912 | bytes 3000000 | tf_op jit(solution)/shard_map/w_part/pallas_call | solution.py:374
  63.7 4.2 %all-to-all-start.1 = ((bf16[8,64,1024]{2,1,0:T(8,128)(2,1)}), bf16[8,64,1024]{2,1,0:T(8,128)(2,1)}, u32[]{:S(2)}, u32[]{:S(2)}) async-start(bf16[8,64,1024]{2,1,0:T(8,128)(2,1)} %w_part.1), calls=%async_computation.1 | async-start | bytes 2097152 | tf_op jit(solution)/shard_map/all_to_all | solution.py:383
  68.2 19.9 %buckets.1 = bf16[8,928,128]{2,1,0:T(8,128)(2,1)S(1)} custom-call(bf16[128,1024]{1,0:T(8,128)(2,1)S(1)} %dpre.1.d0_ref, bf16[128,1024]{1,0:T(8,128)(2,1)S(1)} %collective-permute-done.d1_ref, bf16[128,1024]{1,0:T(8,128)(2,1)S(1)} %collective-permute-done.1.d2_ref, bf16[128,1024]{1,0:T(8,128)(2,1)S(1)} %collective-permute-done.2.d3_ref, ...), custom_call_target="tpu_custom_call" | custom-call | flops 15000000512 | bytes 40000000 | tf_op jit(solution)/shard_map/buckets/pallas_call | solution.py:387
  88.1 2.1 %reduce_sum.12 = bf16[64,1024]{1,0:T(8,128)(2,1)} reduce(bf16[8,64,1024]{2,1,0:T(8,128)(2,1)} %all-to-all-done.1, bf16[]{:T(256)} %constant.13.clone.1), dimensions={0}, to_apply=%region_0.0 | reduce | flops 458752 | bytes 1179650 | tf_op jit(solution)/shard_map/reduce_sum | solution.py:403
  90.2 28.8 %all_to_all.15.in_ref = bf16[8,928,128]{2,1,0:T(8,128)(2,1)S(1)} all-to-all(bf16[8,928,128]{2,1,0:T(8,128)(2,1)S(1)} %buckets.1), channel_id=1, replica_groups=mesh['x'=2,'core'=2,'tz'=4,'ty'=2] {'x','core','ty'}, dimensions={0} | all-to-all | bytes 3801088 | tf_op jit(solution)/shard_map/all_to_all | solution.py:406
  119.1 16.8 %sums.1 = (f32[8,128]{1,0:T(8,128)}, f32[128,128]{1,0:T(8,128)}, f32[4096,128]{1,0:T(8,128)}, f32[4096,128]{1,0:T(8,128)}) custom-call(bf16[8,928,128]{2,1,0:T(8,128)(2,1)S(1)} %all_to_all.15.in_ref), custom_call_target="tpu_custom_call" | custom-call | flops 7000000000 | bytes 7000000 | tf_op jit(solution)/shard_map/sums/pallas_call | solution.py:409
  135.9 15.8 %all-gather.2.cloned.1.call-done.x_ref = bf16[1024,1024]{1,0:T(8,128)(2,1)} async-done(((bf16[64,1024]{1,0:T(8,128)(2,1)}), bf16[1024,1024]{1,0:T(8,128)(2,1)}) %all-gather.2.cloned.1.call-update) | async-done | bytes 2097168 | tf_op jit(solution)/shard_map/all_gather | solution.py:405
  151.8 1.6 copy-done.2
  153.4 2.4 %widen.2.refs_0_ = f32[2048,1024]{1,0:T(8,128)} custom-call(s32[1]{0:T(128)} %bitcast.core_ref, bf16[1024,1024]{1,0:T(8,128)(2,1)S(1)} %copy-done.2), custom_call_target="tpu_custom_call" | custom-call | flops 1048576 | bytes 6291456 | tf_op jit(solution)/shard_map/widen/pallas_call | solution.py:280
  156.1 2.4 %widen.3 = f32[2048,1024]{1,0:T(8,128)} custom-call(s32[1]{0:T(128)S(6)} %sub.3.core_ref, bf16[1024,1024]{1,0:T(8,128)(2,1)S(1)} %collective-permute-done.3.x_ref, f32[2048,1024]{1,0:T(8,128)} %widen.2.refs_0_), custom_call_target="tpu_custom_call", output_to_operand_aliasing={{}: (2, {})} | custom-call | flops 1048576 | bytes 6291456 | tf_op jit(solution)/shard_map/widen/pallas_call | solution.py:280
  (27 shorter events, 3.4 us)
Async XLA Ops:
  7.2 13.4 %copy-start.11 = (f32[1024]{0:T(1024)S(1)}, f32[1024]{0:T(1024)}, u32[]{:S(2)}) copy-start(f32[1024]{0:T(1024)} %param.13) | copy-start | bytes 12292
  7.2 1.0 copy-start
  8.2 0.7 copy-start.4
  8.9 0.7 copy-start.5
  9.6 0.7 copy-start.6
  10.3 0.7 copy-start.7
  11.0 0.7 copy-start.8
  11.7 0.7 copy-start.9
  12.4 0.7 copy-start.10
  13.1 7.4 %copy-start.1 = (bf16[128,2048]{1,0:T(8,128)(2,1)S(1)}, bf16[128,2048]{1,0:T(8,128)(2,1)}, u32[]{:S(2)}) copy-start(bf16[128,2048]{1,0:T(8,128)(2,1)} %x_ref.2) | copy-start | bytes 1572868
  13.1 7.4 %copy-start.3 = (bf16[128,1024]{1,0:T(8,128)(2,1)S(1)}, bf16[128,1024]{1,0:T(8,128)(2,1)}, u32[]{:S(2)}) copy-start(bf16[128,1024]{1,0:T(8,128)(2,1)} %g_ref.1) | copy-start | bytes 786436
  14.2 36.9 %all-to-all-start = ((bf16[4,128,640]{2,1,0:T(8,128)(2,1)}), bf16[4,128,640]{2,1,0:T(8,128)(2,1)S(1)}, u32[]{:S(2)}, u32[]{:S(2)}) async-start(bf16[4,128,640]{2,1,0:T(8,128)(2,1)} %cut.1), calls=%async_computation | async-start | bytes 1310720 | tf_op jit(solution)/shard_map/all_to_all | solution.py:333
  24.2 24.9 %collective-permute-start.1 = (bf16[128,1024]{1,0:T(8,128)(2,1)S(1)}, bf16[128,1024]{1,0:T(8,128)(2,1)S(1)}, u32[]{:S(2)}, u32[]{:S(2)}) collective-permute-start(bf16[128,1024]{1,0:T(8,128)(2,1)S(1)} %dpre.1.d0_ref), channel_id=1, source_target_pairs={{0,4},{2,6},{4,0},{6,2},{1,5},{3,7},{5,1},{7,3},{8,12},{10,14},{12... | collective-permute-start | bytes 786440 | tf_op jit(solution)/shard_map/ppermute | solution.py:353
  49.1 9.2 %collective-permute-start.2 = (bf16[128,1024]{1,0:T(8,128)(2,1)S(1)}, bf16[128,1024]{1,0:T(8,128)(2,1)S(1)}, u32[]{:S(2)}, u32[]{:S(2)}) collective-permute-start(bf16[128,1024]{1,0:T(8,128)(2,1)S(1)} %collective-permute-done.1.d2_ref), channel_id=1, source_target_pairs={{0,2},{2,0},{4,6},{6,4},{1,3},{3,1},{5,7},{7,5},{8,10},{10,8},{12,... | collective-permute-start | bytes 786440 | tf_op jit(solution)/shard_map/ppermute | solution.py:353
  49.1 12.9 %collective-permute-start = (bf16[128,1024]{1,0:T(8,128)(2,1)S(1)}, bf16[128,1024]{1,0:T(8,128)(2,1)S(1)}, u32[]{:S(2)}, u32[]{:S(2)}) collective-permute-start(bf16[128,1024]{1,0:T(8,128)(2,1)S(1)} %dpre.1.d0_ref), channel_id=1, source_target_pairs={{0,2},{2,0},{4,6},{6,4},{1,3},{3,1},{5,7},{7,5},{8,10},{10,8},{12,... | collective-permute-start | bytes 786440 | tf_op jit(solution)/shard_map/ppermute | solution.py:353
  54.1 1.3 copy-start.12
  63.7 24.4 %all-to-all-start.1 = ((bf16[8,64,1024]{2,1,0:T(8,128)(2,1)}), bf16[8,64,1024]{2,1,0:T(8,128)(2,1)}, u32[]{:S(2)}, u32[]{:S(2)}) async-start(bf16[8,64,1024]{2,1,0:T(8,128)(2,1)} %w_part.1), calls=%async_computation.1 | async-start | bytes 2097152 | tf_op jit(solution)/shard_map/all_to_all | solution.py:383
  67.9 83.8 %all-gather.2.cloned.1.call-start = ((), (), s32[]{:S(2)}) async-start(), calls=%async_computation.3 | async-start | bytes 2228224 | tf_op jit(solution)/shard_map/all_gather | solution.py:405
  151.8 4.4 %collective-permute-start.3 = (bf16[1024,1024]{1,0:T(8,128)(2,1)}, bf16[1024,1024]{1,0:T(8,128)(2,1)S(1)}, u32[]{:S(2)}, u32[]{:S(2)}) collective-permute-start(bf16[1024,1024]{1,0:T(8,128)(2,1)} %all-gather.2.cloned.1.call-done.x_ref), channel_id=1, source_target_pairs={{0,8},{8,0},{1,9},{9,1},{2,10},{10,2},{3,11},{11,3},{4,12},{12,4},... | collective-permute-start | bytes 6291464 | tf_op jit(solution)/shard_map/ppermute | solution.py:426
  151.8 1.6 copy-start.2
Sparse Core Ops, SparseCore 0:
  90.4 61.3 all-gather.1

commit v5 on v4

--- a/solution.py
+++ b/solution.py
@@ -15,7 +15,7 @@
 GROUPS = 4
 LOG_ADM = 7
 LOG_GROUP = 10
-VMEM_LIMIT = 50 * 1024 * 1024
+MIB = 1024 * 1024
 BF = jnp.bfloat16
 F32 = jnp.float32
 
@@ -38,11 +38,11 @@
     return (iota((n, E), 0) + base).astype(jnp.int16).reshape(n // 16, 16, E)
 
 
-def call(kernel, name, out_shape, flops, traffic, **kwargs):
+def call(kernel, name, out_shape, flops, traffic, vmem=24, **kwargs):
     return pl.pallas_call(
         kernel,
         out_shape=out_shape,
-        compiler_params=pltpu.CompilerParams(vmem_limit_bytes=VMEM_LIMIT),
+        compiler_params=pltpu.CompilerParams(vmem_limit_bytes=vmem * MIB),
         cost_estimate=pl.CostEstimate(flops=flops, bytes_accessed=traffic, transcendentals=0),
         name=name,
         **kwargs,
@@ -136,8 +136,8 @@
 
 
 def bucket_kernel(
-    n_dest, cap, d0_ref, d1_ref, d2_ref, d3_ref, w_ref, slot_ref, labels_ref, group_ref, out_ref, d_ref, v_ref, a_ref,
-    p_ref, mark_ref,
+    n_dest, cap, d0_ref, d1_ref, d2_ref, d3_ref, w_ref, slot_ref, labels_ref, group_ref, out_ref, d_ref, v_ref,
+    mark_ref,
 ):
     for z, ref in enumerate((d0_ref, d1_ref, d2_ref, d3_ref)):
         d_ref[z * ref.shape[0] : (z + 1) * ref.shape[0], :] = ref[...]
@@ -166,12 +166,8 @@
     wanted = rows_from(slots)
     for z in range(N_Z):
         for which in range(2):
-            for f in range(n_feat):
-                p_ref[which * slots : (which + 1) * slots, f * n_s : (f + 1) * n_s] = one_hot(
-                    wanted, slot_ref[which, z, f : f + 1, :]
-                )
-        for which in range(2):
-            o = dot(p_ref[which * slots : (which + 1) * slots, :], v_ref[z])
+            hits = [one_hot(wanted, slot_ref[which, z, f : f + 1, :]) for f in range(n_feat)]
+            o = dot(jnp.concatenate(hits, axis=1), v_ref[z])
             for d in range(n_dest):
                 rows = o[d * cap : (d + 1) * cap, :]
                 out_ref[d, which * seg + z * cap : which * seg + (z + 1) * cap, :] = rows[:, 0:E].astype(BF)
@@ -181,14 +177,13 @@
     wanted = rows_from(tall)
     o = jnp.zeros((tall, 2 * E), F32)
     for z in range(N_Z):
+        hits = [one_hot(wanted, slot_ref[2, z, f : f + 1, :]) for f in range(n_feat)]
+        sides = []
         for f in range(n_feat):
-            at = f * n_s
-            p_ref[0:tall, at : at + n_s] = one_hot(wanted, slot_ref[2, z, f : f + 1, :])
             upper = group_ref[z, :, f : f + 1] >= half
-            v = v_ref[z, at : at + n_s, 0:E].astype(F32)
-            a_ref[at : at + n_s, 0:E] = jnp.where(upper, 0.0, v).astype(BF)
-            a_ref[at : at + n_s, E : 2 * E] = jnp.where(upper, v, 0.0).astype(BF)
-        o = o + dot(p_ref[0:tall, :], a_ref[...])
+            v = v_ref[z, f * n_s : (f + 1) * n_s, 0:E].astype(F32)
+            sides.append(jnp.concatenate([jnp.where(upper, 0.0, v), jnp.where(upper, v, 0.0)], axis=1).astype(BF))
+        o = o + dot(jnp.concatenate(hits, axis=1), jnp.concatenate(sides, axis=0))
     for d in range(n_dest):
         at = d % half * ADM_DEV
         side = d // half * E
@@ -220,72 +215,95 @@
     lax.fori_loop(0, n_dest, finish, 0)
 
 
-def sums_kernel(n_src, seg, n_bias, in_ref, bias_ref, adm_ref, q_ref, r_ref, v_ref, p_ref):
+def sums_kernel(n_src, seg, n_bias, table, in_ref, *outs):
     n_mark = -(-seg // E)
     at_mark = 2 * seg + ADM_DEV
-    adm = jnp.zeros((ADM_DEV, E), F32)
-    bias = jnp.zeros((2 * n_bias, E), F32)
+    if table == 0:
+        adm = jnp.zeros((ADM_DEV, E), F32)
+        bias = jnp.zeros((2 * n_bias, E), F32)
+        for s in range(n_src):
+            adm = adm + in_ref[s, 2 * seg : at_mark, :].astype(F32)
+            bias = bias + in_ref[s, at_mark + 16 : at_mark + 16 + 2 * n_bias, :].astype(F32)
+        outs[1][...] = bias[0:n_bias, :] + bias[n_bias:, :]
+        outs[2][...] = adm
+
+    per_group = QROWS_DEV // GROUPS
+    labels, sides = [], []
     for s in range(n_src):
-        adm = adm + in_ref[s, 2 * seg : at_mark, :].astype(F32)
-        bias = bias + in_ref[s, at_mark + 16 : at_mark + 16 + 2 * n_bias, :].astype(F32)
-    adm_ref[...] = adm
-    bias_ref[...] = bias[0:n_bias, :] + bias[n_bias:, :]
-
-    per_group = QROWS_DEV // GROUPS
-    wanted = rows_from(per_group)
-    for table, out in enumerate((q_ref, r_ref)):
-
-        def spread(s, carry):
-            marks = in_ref[s, at_mark : at_mark + 16, :].astype(F32)
-            down = jnp.concatenate([marks, jnp.zeros((E - 16, E), F32)], axis=0).T
-            for j in range(n_mark):
-                at = j * 4 + table * 2
-                label = marks[at : at + 1, :] * 256.0 + marks[at + 1 : at + 2, :]
-                label = label.astype(jnp.int32) & (per_group - 1)
-                if (j + 1) * E > seg:
-                    label = jnp.where(iota((1, E), 1) + j * E < seg, label, -1)
-                start = pl.multiple_of((s * n_mark + j) * E, E)
-                p_ref[:, pl.ds(start, E)] = one_hot(wanted, label)
-                group = down[:, at : at + 1].astype(jnp.int32) >> (LOG_GROUP - 8)
-                rows = in_ref[s, table * seg + j * E : table * seg + (j + 1) * E, :].astype(F32)
-                for g in range(GROUPS):
-                    v_ref[pl.ds(start, E), g * E : (g + 1) * E] = jnp.where(group == g, rows, 0.0).astype(BF)
-            return carry
-
-        lax.fori_loop(0, n_src, spread, 0)
-        block = 512
-        for b in range(per_group // block):
-            o = dot(p_ref[b * block : (b + 1) * block, :], v_ref[...])
-            for g in range(GROUPS):
-                start = g * per_group + b * block
-                out[start : start + block, :] = o[:, g * E : (g + 1) * E]
-
-
-def widen_kernel(core_ref, x_ref, *refs):
-    refs[-1][...] = x_ref[...].astype(F32)
-
-
-def widen(core, x, tall, so_far):
-    rows, hidden = x.shape
-    block = tall // 2
-    alias = {} if so_far is None else {"input_output_aliases": {2: 0}}
-    args = (core, x) if so_far is None else (core, x, so_far)
-    grid_spec = pltpu.PrefetchScalarGridSpec(
-        num_scalar_prefetch=1,
-        grid=(rows // block,),
-        in_specs=[pl.BlockSpec((block, hidden), lambda i, core: (i, 0))]
-        + [pl.BlockSpec(memory_space=pl.ANY)] * (len(args) - 2),
-        out_specs=pl.BlockSpec((block, hidden), lambda i, core: ((i // 2 * 2 + core[0]) * 2 + i % 2, 0)),
-    )
+        marks = in_ref[s, at_mark : at_mark + 16, :].astype(F32)
+        down = jnp.concatenate([marks, jnp.zeros((E - 16, E), F32)], axis=0).T
+        for j in range(n_mark):
+            at = j * 4 + table * 2
+            label = marks[at : at + 1, :] * 256.0 + marks[at + 1 : at + 2, :]
+            label = label.astype(jnp.int32) & (per_group - 1)
+            if (j + 1) * E > seg:
+                label = jnp.where(iota((1, E), 1) + j * E < seg, label, -1)
+            labels.append(label)
+            group = down[:, at : at + 1].astype(jnp.int32) >> (LOG_GROUP - 8)
+            rows = in_ref[s, table * seg + j * E : table * seg + (j + 1) * E, :].astype(F32)
+            sides.append(
+                jnp.concatenate([jnp.where(group == g, rows, 0.0) for g in range(GROUPS)], axis=1).astype(BF)
+            )
+    spread = jnp.concatenate(sides, axis=0)
+    block = 512
+    for b in range(per_group // block):
+        wanted = rows_from(block, b * block)
+        o = dot(jnp.concatenate([one_hot(wanted, label) for label in labels], axis=1), spread)
+        for g in range(GROUPS):
+            start = g * per_group + b * block
+            outs[0][start : start + block, :] = o[:, g * E : (g + 1) * E]
+
+
+def doubling(n):
+    return [1 << i for i in range(n.bit_length() - 1)]
+
+
+def swap(x, axis, k):
+    n = lax.axis_size(axis)
+    return lax.ppermute(x, axis, [(i, i ^ k) for i in range(n)])
+
+
+def widen_kernel(n_x, n_y, share, at_ref, a_ref, b_ref, *refs):
+    out_ref, held_ref, sems = refs[-3:]
+    half = a_ref.shape[1]
+    copies = []
+    for b in range(a_ref.shape[0] // share):
+        z = at_ref[2] ^ (((b & 1) << 1) | ((b >> 1) & 1))
+        rest = b >> 2
+        rows = slice(b * share, (b + 1) * share)
+        for side, ref in enumerate((a_ref, b_ref)):
+            y, x = (rest % n_y, rest // n_y) if side == 0 else (rest // n_x, rest % n_x)
+            row = ((((at_ref[0] ^ x) * 2 + at_ref[1]) * N_Z + z) * n_y + (at_ref[3] ^ y)) * share
+            cols = slice(side * half, (side + 1) * half)
+            held_ref[rows, cols] = ref[rows, :].astype(F32)
+            copy = pltpu.make_async_copy(
+                held_ref.at[rows, cols], out_ref.at[pl.ds(pl.multiple_of(row, share), share), cols], sems.at[len(copies)]
+            )
+            copy.start()
+            copies.append(copy)
+    for copy in copies:
+        copy.wait()
+
+
+def widen(n_x, n_y, share, at, sides, so_far):
+    rows, half = sides[0].shape
+    array = pl.BlockSpec(memory_space=pltpu.VMEM)
+    more = () if so_far is None else (so_far,)
+    alias = {} if so_far is None else {"input_output_aliases": {3: 0}}
     return call(
-        widen_kernel,
+        functools.partial(widen_kernel, n_x, n_y, share),
         "widen",
-        jax.ShapeDtypeStruct((2 * rows, hidden), F32),
-        rows * hidden,
-        rows * hidden * 6,
-        grid_spec=grid_spec,
+        jax.ShapeDtypeStruct((2 * rows, 2 * half), F32),
+        rows * half * 2,
+        rows * half * 12,
+        in_specs=[pl.BlockSpec(memory_space=pltpu.SMEM), array, array] + [pl.BlockSpec(memory_space=pltpu.HBM)] * len(more),
+        out_specs=pl.BlockSpec(memory_space=pltpu.HBM),
+        scratch_shapes=[
+            pltpu.VMEM((rows, 2 * half), F32),
+            pltpu.SemaphoreType.DMA((2 * (rows // share),)),
+        ],
         **alias,
-    )(*args)
+    )(at, *sides, *more)
 
 
 def after(x, *others):
@@ -313,7 +331,6 @@
     plane = ("x", "core", "ty")
     shape = jax.ShapeDtypeStruct
     my_z = lax.axis_index("tz").astype(jnp.int32).reshape(1)
-    my_core = lax.axis_index("core").astype(jnp.int32).reshape(1)
     scalar = pl.BlockSpec(memory_space=pltpu.SMEM)
     array = pl.BlockSpec(memory_space=pltpu.VMEM)
 
@@ -324,7 +341,7 @@
         shape((N_Z, n_s, wide + E), BF),
         10**7,
         2 * 10**6,
-        in_specs=[array] + [pl.BlockSpec(memory_space=pl.ANY)] * len(lookup_args),
+        in_specs=[array] + [pl.BlockSpec(memory_space=pltpu.HBM)] * len(lookup_args),
         scratch_shapes=[
             pltpu.VMEM((len(lookup_args), n_feat, n_s), jnp.int32),
             pltpu.SemaphoreType.DMA((len(lookup_args),)),
@@ -349,12 +366,10 @@
         out_specs=pl.BlockSpec((n_s, block), lambda i: (0, i)),
     )(after(features, cut), w_first, b_first.reshape(1, hidden), grad_out)
 
-    def swap(x, k):
-        return lax.ppermute(x, "tz", [(z, z ^ k) for z in range(N_Z)])
-
-    far = swap(dpre, 2)
-    near = swap(dpre, 1)
-    sources = [dpre, near, far, swap(far, 1)]
+    far = swap(dpre, "tz", 2)
+    near = swap(dpre, "tz", 1)
+    far = after(far, near)
+    sources = [dpre, near, far, swap(far, "tz", 1)]
     feat_in = after(feat_in, dpre)
 
     slots, labels, group = call(
@@ -383,7 +398,6 @@
     w_part = lax.all_to_all(w_part, plane, split_axis=0, concat_axis=0, tiled=True)
 
     n_rows = 2 * seg + ADM_DEV + 16 + 2 * n_bias
-    tallest = max(2 * n_plane * cap, n_plane // 2 * ADM_DEV)
     chunks = call(
         functools.partial(bucket_kernel, n_plane, cap),
         "buckets",
@@ -393,39 +407,47 @@
         scratch_shapes=[
             pltpu.VMEM((N_Z * n_s, hidden), BF),
             pltpu.VMEM((N_Z, count, 2 * E), BF),
-            pltpu.VMEM((count, 2 * E), BF),
-            pltpu.VMEM((tallest, count), BF),
             pltpu.VMEM((2, n_plane, seg, E), F32),
         ],
+        vmem=44,
     )(*sources, w_first, slots, labels, group)
 
     w_part = after(w_part, chunks)
     w_own = jnp.sum(w_part.astype(F32), axis=0).astype(BF)
     w_own, chunks = lax.optimization_barrier((w_own, chunks))
-    w_half = lax.all_gather(w_own, ("x", "tz", "ty"), axis=0, tiled=True)
     chunks = lax.all_to_all(chunks, plane, split_axis=0, concat_axis=0, tiled=True)
 
-    tall = n_plane * -(-seg // E) * E
-    b_grad, adm_grad, q_grad, r_grad = call(
-        functools.partial(sums_kernel, n_plane, seg, n_bias),
-        "sums",
-        (
-            shape((n_bias, E), F32),
-            shape((ADM_DEV, E), F32),
-            shape((QROWS_DEV, E), F32),
-            shape((QROWS_DEV, E), F32),
-        ),
-        7 * 10**9,
-        7 * 10**6,
-        scratch_shapes=[
-            pltpu.VMEM((tall, GROUPS * E), BF),
-            pltpu.VMEM((QROWS_DEV // GROUPS, tall), BF),
-        ],
-    )(chunks)
-    w_half = after(w_half, b_grad)
-    w_other = lax.ppermute(w_half, "core", [(c, n_core - 1 - c) for c in range(n_core)])
-    w_grad = widen(my_core, w_half, n_table * share, None)
-    w_grad = widen(1 - my_core, w_other, n_table * share, w_grad)
+    w_two = jnp.concatenate([w_own, swap(w_own, "tz", 2)], axis=0)
+    w_four = jnp.concatenate([w_two, swap(w_two, "tz", 1)], axis=0)
+    sides = [w_four[:, : hidden // 2], w_four[:, hidden // 2 :]]
+    over_y = [("ty", k) for k in doubling(n_y)]
+    over_x = [("x", k) for k in doubling(n_dp // n_core)]
+    before = sides
+    for steps in zip(over_y + over_x, over_x + over_y):
+        before = sides
+        sides = [jnp.concatenate([side, swap(side, *step)], axis=0) for side, step in zip(sides, steps)]
+    chunks = after(chunks, *before)
+
+    def sums(table, chunks):
+        outs = (shape((QROWS_DEV, E), F32), shape((n_bias, E), F32), shape((ADM_DEV, E), F32))
+        return call(
+            functools.partial(sums_kernel, n_plane, seg, n_bias, table),
+            ("q_sums", "r_sums")[table],
+            outs if table == 0 else outs[:1],
+            4 * 10**9,
+            4 * 10**6,
+            vmem=40,
+        )(chunks)
+
+    q_grad, b_grad, adm_grad = sums(0, chunks)
+    sides = [after(side, q_grad) for side in sides]
+    (r_grad,) = sums(1, after(chunks, *sides))
+    others = [swap(side, "core", 1) for side in sides]
+    at = jnp.stack([lax.axis_index(name) for name in ("x", "core", "tz", "ty")]).astype(jnp.int32)
+    n_x = n_dp // n_core
+    w_grad = widen(n_x, n_y, share, at, [after(side, r_grad) for side in sides], None)
+    flip = at ^ jnp.array([0, 1, 0, 0], jnp.int32)
+    w_grad = widen(n_x, n_y, share, flip, others, w_grad)
     return (w_grad, b_grad.reshape(hidden), adm_grad, q_grad, r_grad)
 
 

time: 166 us -> 154 us (0.928)
  blocking collectives: 28.8 us -> 0 us
  waiting for transfers between devices: 44.7 us -> 70.5 us
  between operations: 14.1 us -> 1 us
  starting transfers between devices: 15.8 us -> 25 us
  Pallas kernels: 51 us -> 43 us
  local copies, waits for them, and re-layouts: 8.83 us -> 13.3 us
    ppermute x4 -> x11, waiting for transfers between devices: 28.8 us -> 70.5 us  [swap(): return lax.ppermute(x, axis, [(i, i ^ k) for i in range(n)])]
    all_to_all x1 -> x0, blocking collectives: 28.8 us -> none  [local(): lax.all_to_all(chunks, plane, split_axis=0, concat_axis=0, tiled=True)]
    all_gather x1 -> x0, waiting for transfers between devices: 15.8 us -> none  [local(): w_half = lax.all_gather(w_own, ('x', 'tz', 'ty'), axis=0, tiled=True)]
    ppermute x4 -> x11, starting transfers between devices: 5.02 us -> 10.4 us  [swap(): return lax.ppermute(x, axis, [(i, i ^ k) for i in range(n)])]
    pallas_call x1, Pallas kernels: 19.9 us -> 15 us  [local(): call(functools.partial(bucket_kernel, n_plane, cap), 'buckets', shape((n_...]
    all_to_all x0 -> x1, starting transfers between devices: none -> 4.51 us  [local(): lax.all_to_all(chunks, plane, split_axis=0, concat_axis=0, tiled=True)]
    unnamed x26 -> x34, local copies, waits for them, and re-layouts: 8.83 us -> 13.2 us
    reduce_sum x1, other arithmetic: 2.1 us -> 0.18 us  [local(): w_own = jnp.sum(w_part.astype(F32), axis=0).astype(BF)]
  transfers between devices with their start and end apart: 7 -> 14, of which waited for: 5 -> 7; matrix products, arithmetic and copies ran while one was open for 0% -> 0% of each run, Pallas kernels for 28% -> 19%
where the time goes in v5:
time: 154 us; the launch traced here: 153 us
  waiting for transfers between devices  70.5 us (46%)
  Pallas kernels  43 us (28%)
  starting transfers between devices  25 us (16%)
  local copies, waits for them, and re-layouts  13.3 us (9%)
    ppermute x11, waiting for transfers between devices, swap(): return lax.ppermute(x, axis, [(i, i ^ k) for i in range(n)])  70.5 us
    pallas_call x1, Pallas kernels, local(): call(functools.partial(bucket_kernel, n_plane, cap), 'buckets', shape((n_...  15 us
    pallas_call x2, Pallas kernels, sums(): call(functools.partial(sums_kernel, n_plane, seg, n_bias, table), ('q_sum...  13.8 us
    unnamed x34, local copies, waits for them, and re-layouts  13.2 us
    ppermute x11, starting transfers between devices, swap(): return lax.ppermute(x, axis, [(i, i ^ k) for i in range(n)])  10.4 us
    all_to_all x1, starting transfers between devices, local(): feat_in = lax.all_to_all(cut, 'tz', split_axis=0, concat_axis=0, tiled=True)  6.33 us
    pallas_call x2, Pallas kernels, widen(): call(functools.partial(widen_kernel, n_x, n_y, share), 'widen', jax.Shape...  6.32 us
    all_to_all x1, starting transfers between devices, local(): lax.all_to_all(chunks, plane, split_axis=0, concat_axis=0, tiled=True)  4.51 us
  transfers between devices with their start and end apart: 14, of which 7 were waited for; matrix products, arithmetic and copies ran while one was open for 0% of the time, Pallas kernels for 19%

profile of v5, /device:TPU:0, one launch (start us, length us, event | category | flops | bytes accessed | tf_op | source)
XLA Modules:
  0.0 153.2 jit_solution(1571100858710706460)
XLA Ops:
  7.7 6.3 %all-to-all-start = ((bf16[4,128,640]{2,1,0:T(8,128)(2,1)}), bf16[4,128,640]{2,1,0:T(8,128)(2,1)S(1)}, u32[]{:S(2)}, u32[]{:S(2)}) async-start(bf16[4,128,640]{2,1,0:T(8,128)(2,1)} %cut.1), calls=%async_computation | async-start | bytes 1310720 | tf_op jit(solution)/shard_map/all_to_all | solution.py:350
  14.0 2.2 %copy-done = bf16[2048,1024]{1,0:T(8,128)(2,1)S(1)} copy-done((bf16[2048,1024]{1,0:T(8,128)(2,1)S(1)}, bf16[2048,1024]{1,0:T(8,128)(2,1)}, u32[]{:S(2)}) %copy-start) | copy-done | bytes 4194328
  16.2 2.0 %dpre.1.d0_ref = bf16[128,1024]{1,0:T(8,128)(2,1)S(1)} custom-call(bf16[128,2048]{1,0:T(8,128)(2,1)S(1)} %copy-done.3, bf16[2048,1024]{1,0:T(8,128)(2,1)S(1)} %copy-done, f32[1,1024]{1,0:T(1,128)S(1)} %bitcast.26, bf16[128,1024]{1,0:T(8,128)(2,1)S(1)} %copy-done.4), custom_call_target="tpu_custom_call" | custom-call | flops 536870912 | bytes 6000000 | tf_op jit(solution)/shard_map/dpre/pallas_call | solution.py:353
  18.2 3.0 %collective-permute-start.1 = (bf16[128,1024]{1,0:T(8,128)(2,1)S(1)}, bf16[128,1024]{1,0:T(8,128)(2,1)S(1)}, u32[]{:S(2)}, u32[]{:S(2)}) collective-permute-start(bf16[128,1024]{1,0:T(8,128)(2,1)S(1)} %dpre.1.d0_ref), channel_id=1, source_target_pairs={{0,4},{2,6},{4,0},{6,2},{1,5},{3,7},{5,1},{7,3},{8,12},{10,14},{12... | collective-permute-start | bytes 786440 | tf_op jit(solution)/shard_map/ppermute | solution.py:263
  21.2 1.5 collective-permute-start
  22.7 19.9 %collective-permute-done.1.d2_ref = bf16[128,1024]{1,0:T(8,128)(2,1)S(1)} collective-permute-done((bf16[128,1024]{1,0:T(8,128)(2,1)S(1)}, bf16[128,1024]{1,0:T(8,128)(2,1)S(1)}, u32[]{:S(2)}, u32[]{:S(2)}) %collective-permute-start.1) | collective-permute-done | bytes 262176 | tf_op jit(solution)/shard_map/ppermute | solution.py:263
  42.6 3.0 %slots.1 = (s32[3,4,16,128]{3,2,1,0:T(8,128)S(1)}, bf16[4,2048,128]{2,1,0:T(8,128)(2,1)S(1)}, f32[4,128,16]{2,1,0:T(8,128)S(1)}) custom-call(s32[1]{0:T(128)} %bitcast.2.z_ref, bf16[4,128,640]{2,1,0:T(8,128)(2,1)S(1)} %all-to-all-done.in_ref.x_ref), custom_call_target="tpu_custom_call" | custom-call | flops 1000000000 | bytes 3000000 | tf_op jit(solution)/shard_map/slots/pallas_call | solution.py:375
  46.9 3.0 %collective-permute-done.2.d3_ref = bf16[128,1024]{1,0:T(8,128)(2,1)S(1)} collective-permute-done((bf16[128,1024]{1,0:T(8,128)(2,1)S(1)}, bf16[128,1024]{1,0:T(8,128)(2,1)S(1)}, u32[]{:S(2)}, u32[]{:S(2)}) %collective-permute-start.2) | collective-permute-done | bytes 262176 | tf_op jit(solution)/shard_map/ppermute | solution.py:263
  49.8 1.7 %w_part.1 = bf16[8,64,1024]{2,1,0:T(8,128)(2,1)} custom-call(s32[1]{0:T(128)} %bitcast.2.z_ref, bf16[4,128,640]{2,1,0:T(8,128)(2,1)S(1)} %all-to-all-done.in_ref.x_ref, bf16[128,1024]{1,0:T(8,128)(2,1)S(1)} %dpre.1.d0_ref, bf16[128,1024]{1,0:T(8,128)(2,1)S(1)} %collective-permute-done.d1_ref, bf16[128,1024]{1,0:T(8,128)(2,1)S(1)} %collective-permute-done.1.d2_ref, ...), custom_call_target="tpu_custom_call" | custom-call | flops 536870912 | bytes 3000000 | tf_op jit(solution)/shard_map/w_part/pallas_call | solution.py:389
  51.5 3.7 %all-to-all-start.1 = ((bf16[8,64,1024]{2,1,0:T(8,128)(2,1)}), bf16[8,64,1024]{2,1,0:T(8,128)(2,1)S(1)}, u32[]{:S(2)}, u32[]{:S(2)}) async-start(bf16[8,64,1024]{2,1,0:T(8,128)(2,1)} %w_part.1), calls=%async_computation.1 | async-start | bytes 2097152 | tf_op jit(solution)/shard_map/all_to_all | solution.py:398
  55.3 2.2 %copy-done.1 = bf16[2048,1024]{1,0:T(8,128)(2,1)S(1)} copy-done((bf16[2048,1024]{1,0:T(8,128)(2,1)S(1)}, bf16[2048,1024]{1,0:T(8,128)(2,1)}, u32[]{:S(2)}) %copy-start.1) | copy-done | bytes 4194328
  57.4 1.6 %copy-done.14 = bf16[4,2048,128]{2,1,0:T(8,128)(2,1)S(1)} copy-done((bf16[4,2048,128]{2,1,0:T(8,128)(2,1)S(1)}, bf16[4,2048,128]{2,1,0:T(8,128)(2,1)}, u32[]{:S(2)}) %copy-start.14) | copy-done | bytes 2097176
  59.0 15.0 %buckets.1 = bf16[8,928,128]{2,1,0:T(8,128)(2,1)} custom-call(bf16[128,1024]{1,0:T(8,128)(2,1)S(1)} %dpre.1.d0_ref, bf16[128,1024]{1,0:T(8,128)(2,1)S(1)} %collective-permute-done.d1_ref, bf16[128,1024]{1,0:T(8,128)(2,1)S(1)} %collective-permute-done.1.d2_ref, bf16[128,1024]{1,0:T(8,128)(2,1)S(1)} %collective-permute-done.2.d3_ref, ...), custom_call_target="tpu_custom_call" | custom-call | flops 15000000512 | bytes 40000000 | tf_op jit(solution)/shard_map/buckets/pallas_call | solution.py:401
  74.3 9.3 %collective-permute-done.3 = bf16[64,1024]{1,0:T(8,128)(2,1)S(1)} collective-permute-done((bf16[64,1024]{1,0:T(8,128)(2,1)S(1)}, bf16[64,1024]{1,0:T(8,128)(2,1)S(1)}, u32[]{:S(2)}, u32[]{:S(2)}) %collective-permute-start.3) | collective-permute-done | bytes 131104 | tf_op jit(solution)/shard_map/ppermute | solution.py:263
  83.7 4.5 %all-to-all-start.2 = ((bf16[8,928,128]{2,1,0:T(8,128)(2,1)}), bf16[8,928,128]{2,1,0:T(8,128)(2,1)}, u32[]{:S(2)}, u32[]{:S(2)}) async-start(bf16[8,928,128]{2,1,0:T(8,128)(2,1)} %buckets.1), calls=%async_computation.2 | async-start | bytes 3801088 | tf_op jit(solution)/shard_map/all_to_all | solution.py:418
  88.3 3.7 %collective-permute-done.4 = bf16[128,1024]{1,0:T(8,128)(2,1)S(1)} collective-permute-done((bf16[128,1024]{1,0:T(8,128)(2,1)S(1)}, bf16[128,1024]{1,0:T(8,128)(2,1)S(1)}, u32[]{:S(2)}, u32[]{:S(2)}) %collective-permute-start.4) | collective-permute-done | bytes 262176 | tf_op jit(solution)/shard_map/ppermute | solution.py:263
  92.1 1.7 %collective-permute-start.7 = (bf16[256,512]{1,0:T(8,128)(2,1)S(1)}, bf16[256,512]{1,0:T(8,128)(2,1)S(1)}, u32[]{:S(2)}, u32[]{:S(2)}) collective-permute-start(bf16[256,512]{1,0:T(8,128)(2,1)S(1)} %get-tuple-element.47), channel_id=1, source_target_pairs={{0,16},{16,0},{1,17},{17,1},{2,18},{18,2},{3,19},{19,3},{4,20},{20... | collective-permute-start | bytes 786440 | tf_op jit(solution)/shard_map/ppermute | solution.py:263
  95.2 22.0 %collective-permute-done.7 = bf16[256,512]{1,0:T(8,128)(2,1)S(1)} collective-permute-done((bf16[256,512]{1,0:T(8,128)(2,1)S(1)}, bf16[256,512]{1,0:T(8,128)(2,1)S(1)}, u32[]{:S(2)}, u32[]{:S(2)}) %collective-permute-start.7) | collective-permute-done | bytes 262176 | tf_op jit(solution)/shard_map/ppermute | solution.py:263
  117.3 1.5 collective-permute-start.9
  119.5 11.4 %collective-permute-done.9 = bf16[512,512]{1,0:T(8,128)(2,1)S(1)} collective-permute-done((bf16[512,512]{1,0:T(8,128)(2,1)S(1)}, bf16[512,512]{1,0:T(8,128)(2,1)S(1)}, u32[]{:S(2)}, u32[]{:S(2)}) %collective-permute-start.9) | collective-permute-done | bytes 524320 | tf_op jit(solution)/shard_map/ppermute | solution.py:263
  132.2 6.9 %q_sums.1 = (f32[4096,128]{1,0:T(8,128)}, f32[8,128]{1,0:T(8,128)}, f32[128,128]{1,0:T(8,128)}) custom-call(bf16[8,928,128]{2,1,0:T(8,128)(2,1)} %all-to-all-done.2.in_ref), custom_call_target="tpu_custom_call" | custom-call | flops 4000000000 | bytes 4000000 | tf_op jit(solution)/shard_map/q_sums/pallas_call | solution.py:433
  139.7 6.9 %r_sums.1 = f32[4096,128]{1,0:T(8,128)} custom-call(bf16[8,928,128]{2,1,0:T(8,128)(2,1)} %all-to-all-done.2.in_ref), custom_call_target="tpu_custom_call" | custom-call | flops 4000000000 | bytes 4000000 | tf_op jit(solution)/shard_map/r_sums/pallas_call | solution.py:433
  146.7 2.8 %widen.2.refs_0_ = f32[2048,1024]{1,0:T(8,128)} custom-call(s32[4]{0:T(128)S(1)} %get-tuple-element.46.at_ref, bf16[1024,512]{1,0:T(8,128)(2,1)S(1)} %pad_maximum_fusion.a_ref, bf16[1024,512]{1,0:T(8,128)(2,1)S(1)} %pad_maximum_fusion.1.b_ref), custom_call_target="tpu_custom_call" | custom-call | flops 1048576 | bytes 6291456 | tf_op jit(solution)/shard_map/widen/pallas_call | solution.py:293
  149.5 3.5 %widen.3 = f32[2048,1024]{1,0:T(8,128)} custom-call(s32[4]{0:T(128)S(1)} %get-tuple-element.45.at_ref, bf16[1024,512]{1,0:T(8,128)(2,1)S(1)} %collective-permute-done.8.a_ref, bf16[1024,512]{1,0:T(8,128)(2,1)} %collective-permute-done.10.b_ref, f32[2048,1024]{1,0:T(8,128)} %widen.2.refs_0_), custom_call_target="tpu_custom_call", output_to_operand_aliasing={{}: (3, {})} | custom-call | flops 1048576 | bytes 6291456 | tf_op jit(solution)/shard_map/widen/pallas_call | solution.py:293
  (56 shorter events, 12.9 us)
Async XLA Ops:
  0.6 13.4 %copy-start.12 = (f32[1024]{0:T(1024)S(1)}, f32[1024]{0:T(1024)}, u32[]{:S(2)}) copy-start(f32[1024]{0:T(1024)} %param.14) | copy-start | bytes 12292
  0.6 1.0 copy-start.2
  5.2 0.7 copy-start.10
  6.6 7.4 %copy-start.3 = (bf16[128,2048]{1,0:T(8,128)(2,1)S(1)}, bf16[128,2048]{1,0:T(8,128)(2,1)}, u32[]{:S(2)}) copy-start(bf16[128,2048]{1,0:T(8,128)(2,1)} %x_ref.2) | copy-start | bytes 1572868
  6.6 7.4 %copy-start.4 = (bf16[128,1024]{1,0:T(8,128)(2,1)S(1)}, bf16[128,1024]{1,0:T(8,128)(2,1)}, u32[]{:S(2)}) copy-start(bf16[128,1024]{1,0:T(8,128)(2,1)} %g_ref.1) | copy-start | bytes 786436
  7.7 34.9 %all-to-all-start = ((bf16[4,128,640]{2,1,0:T(8,128)(2,1)}), bf16[4,128,640]{2,1,0:T(8,128)(2,1)S(1)}, u32[]{:S(2)}, u32[]{:S(2)}) async-start(bf16[4,128,640]{2,1,0:T(8,128)(2,1)} %cut.1), calls=%async_computation | async-start | bytes 1310720 | tf_op jit(solution)/shard_map/all_to_all | solution.py:350
  14.0 2.2 %copy-start = (bf16[2048,1024]{1,0:T(8,128)(2,1)S(1)}, bf16[2048,1024]{1,0:T(8,128)(2,1)}, u32[]{:S(2)}) copy-start(bf16[2048,1024]{1,0:T(8,128)(2,1)} %w_ref.3) | copy-start | bytes 12582916
  18.2 24.3 %collective-permute-start.1 = (bf16[128,1024]{1,0:T(8,128)(2,1)S(1)}, bf16[128,1024]{1,0:T(8,128)(2,1)S(1)}, u32[]{:S(2)}, u32[]{:S(2)}) collective-permute-start(bf16[128,1024]{1,0:T(8,128)(2,1)S(1)} %dpre.1.d0_ref), channel_id=1, source_target_pairs={{0,4},{2,6},{4,0},{6,2},{1,5},{3,7},{5,1},{7,3},{8,12},{10,14},{12... | collective-permute-start | bytes 786440 | tf_op jit(solution)/shard_map/ppermute | solution.py:263
  21.2 21.3 %collective-permute-start = (bf16[128,1024]{1,0:T(8,128)(2,1)S(1)}, bf16[128,1024]{1,0:T(8,128)(2,1)S(1)}, u32[]{:S(2)}, u32[]{:S(2)}) collective-permute-start(bf16[128,1024]{1,0:T(8,128)(2,1)S(1)} %dpre.1.d0_ref), channel_id=1, source_target_pairs={{0,2},{2,0},{4,6},{6,4},{1,3},{3,1},{5,7},{7,5},{8,10},{10,8},{12,... | collective-permute-start | bytes 786440 | tf_op jit(solution)/shard_map/ppermute | solution.py:263
  42.5 7.3 %collective-permute-start.2 = (bf16[128,1024]{1,0:T(8,128)(2,1)S(1)}, bf16[128,1024]{1,0:T(8,128)(2,1)S(1)}, u32[]{:S(2)}, u32[]{:S(2)}) collective-permute-start(bf16[128,1024]{1,0:T(8,128)(2,1)S(1)} %collective-permute-done.1.d2_ref), channel_id=1, source_target_pairs={{0,2},{2,0},{4,6},{6,4},{1,3},{3,1},{5,7},{7,5},{8,10},{10,8},{12,... | collective-permute-start | bytes 786440 | tf_op jit(solution)/shard_map/ppermute | solution.py:263
  45.5 1.3 copy-start.13
  51.5 22.5 %all-to-all-start.1 = ((bf16[8,64,1024]{2,1,0:T(8,128)(2,1)}), bf16[8,64,1024]{2,1,0:T(8,128)(2,1)S(1)}, u32[]{:S(2)}, u32[]{:S(2)}) async-start(bf16[8,64,1024]{2,1,0:T(8,128)(2,1)} %w_part.1), calls=%async_computation.1 | async-start | bytes 2097152 | tf_op jit(solution)/shard_map/all_to_all | solution.py:398
  55.3 2.2 %copy-start.1 = (bf16[2048,1024]{1,0:T(8,128)(2,1)S(1)}, bf16[2048,1024]{1,0:T(8,128)(2,1)}, u32[]{:S(2)}) copy-start(bf16[2048,1024]{1,0:T(8,128)(2,1)} %w_ref.3) | copy-start | bytes 12582916
  57.4 1.6 %copy-start.14 = (bf16[4,2048,128]{2,1,0:T(8,128)(2,1)S(1)}, bf16[4,2048,128]{2,1,0:T(8,128)(2,1)}, u32[]{:S(2)}) copy-start(bf16[4,2048,128]{2,1,0:T(8,128)(2,1)} %copy-done.13) | copy-start | bytes 6291460
  74.2 9.4 %collective-permute-start.3 = (bf16[64,1024]{1,0:T(8,128)(2,1)S(1)}, bf16[64,1024]{1,0:T(8,128)(2,1)S(1)}, u32[]{:S(2)}, u32[]{:S(2)}) collective-permute-start(bf16[64,1024]{1,0:T(8,128)(2,1)S(1)} %reduce_sum.12), channel_id=1, source_target_pairs={{0,4},{2,6},{4,0},{6,2},{1,5},{3,7},{5,1},{7,3},{8,12},{10,14},{12... | collective-permute-start | bytes 393224 | tf_op jit(solution)/shard_map/ppermute | solution.py:263
  83.7 8.3 %collective-permute-start.4 = (bf16[128,1024]{1,0:T(8,128)(2,1)S(1)}, bf16[128,1024]{1,0:T(8,128)(2,1)S(1)}, u32[]{:S(2)}, u32[]{:S(2)}) collective-permute-start(bf16[128,1024]{1,0:T(8,128)(2,1)S(1)} %pad_maximum_fusion.4), channel_id=1, source_target_pairs={{0,2},{2,0},{4,6},{6,4},{1,3},{3,1},{5,7},{7,5},{8,10},{10,8},{12,... | collective-permute-start | bytes 786440 | tf_op jit(solution)/shard_map/ppermute | solution.py:263
  83.7 48.5 %all-to-all-start.2 = ((bf16[8,928,128]{2,1,0:T(8,128)(2,1)}), bf16[8,928,128]{2,1,0:T(8,128)(2,1)}, u32[]{:S(2)}, u32[]{:S(2)}) async-start(bf16[8,928,128]{2,1,0:T(8,128)(2,1)} %buckets.1), calls=%async_computation.2 | async-start | bytes 3801088 | tf_op jit(solution)/shard_map/all_to_all | solution.py:418
  92.1 25.2 %collective-permute-start.7 = (bf16[256,512]{1,0:T(8,128)(2,1)S(1)}, bf16[256,512]{1,0:T(8,128)(2,1)S(1)}, u32[]{:S(2)}, u32[]{:S(2)}) collective-permute-start(bf16[256,512]{1,0:T(8,128)(2,1)S(1)} %get-tuple-element.47), channel_id=1, source_target_pairs={{0,16},{16,0},{1,17},{17,1},{2,18},{18,2},{3,19},{19,3},{4,20},{20... | collective-permute-start | bytes 786440 | tf_op jit(solution)/shard_map/ppermute | solution.py:263
  93.8 25.1 %collective-permute-start.5 = (bf16[256,512]{1,0:T(8,128)(2,1)S(1)}, bf16[256,512]{1,0:T(8,128)(2,1)S(1)}, u32[]{:S(2)}, u32[]{:S(2)}) collective-permute-start(bf16[256,512]{1,0:T(8,128)(2,1)S(1)} %get-tuple-element.48), channel_id=1, source_target_pairs={{0,1},{1,0},{2,3},{3,2},{4,5},{5,4},{6,7},{7,6},{8,9},{9,8},{10,11... | collective-permute-start | bytes 786440 | tf_op jit(solution)/shard_map/ppermute | solution.py:263
  117.3 13.5 %collective-permute-start.9 = (bf16[512,512]{1,0:T(8,128)(2,1)S(1)}, bf16[512,512]{1,0:T(8,128)(2,1)S(1)}, u32[]{:S(2)}, u32[]{:S(2)}) collective-permute-start(bf16[512,512]{1,0:T(8,128)(2,1)S(1)} %pad_maximum_fusion.3), channel_id=1, source_target_pairs={{0,1},{1,0},{2,3},{3,2},{4,5},{5,4},{6,7},{7,6},{8,9},{9,8},{10,11... | collective-permute-start | bytes 1572872 | tf_op jit(solution)/shard_map/ppermute | solution.py:263
  118.9 13.3 %collective-permute-start.6 = (bf16[512,512]{1,0:T(8,128)(2,1)S(1)}, bf16[512,512]{1,0:T(8,128)(2,1)S(1)}, u32[]{:S(2)}, u32[]{:S(2)}) collective-permute-start(bf16[512,512]{1,0:T(8,128)(2,1)S(1)} %pad_maximum_fusion.2), channel_id=1, source_target_pairs={{0,16},{16,0},{1,17},{17,1},{2,18},{18,2},{3,19},{19,3},{4,20},{20... | collective-permute-start | bytes 1572872 | tf_op jit(solution)/shard_map/ppermute | solution.py:263
  132.2 7.5 %copy-start.15 = (s32[4]{0:T(128)S(1)}, s32[4]{0:T(128)}, u32[]{:S(2)}) copy-start(s32[4]{0:T(128)} %constant.20.clone) | copy-start | bytes 52
  139.1 10.3 %collective-permute-start.8 = (bf16[1024,512]{1,0:T(8,128)(2,1)S(1)}, bf16[1024,512]{1,0:T(8,128)(2,1)S(1)}, u32[]{:S(2)}, u32[]{:S(2)}) collective-permute-start(bf16[1024,512]{1,0:T(8,128)(2,1)S(1)} %pad_maximum_fusion.a_ref), channel_id=1, source_target_pairs={{0,8},{8,0},{1,9},{9,1},{2,10},{10,2},{3,11},{11,3},{4,12},{12,4},... | collective-permute-start | bytes 3145736 | tf_op jit(solution)/shard_map/ppermute | solution.py:263
  139.1 10.3 %collective-permute-start.10 = (bf16[1024,512]{1,0:T(8,128)(2,1)S(1)}, bf16[1024,512]{1,0:T(8,128)(2,1)}, u32[]{:S(2)}, u32[]{:S(2)}) collective-permute-start(bf16[1024,512]{1,0:T(8,128)(2,1)S(1)} %pad_maximum_fusion.1.b_ref), channel_id=1, source_target_pairs={{0,8},{8,0},{1,9},{9,1},{2,10},{10,2},{3,11},{11,3},{4,12},{12,4},... | collective-permute-start | bytes 3145736 | tf_op jit(solution)/shard_map/ppermute | solution.py:263
  (6 other events, 4.2 us)

commit v6 on v5

--- a/solution.py
+++ b/solution.py
@@ -14,6 +14,7 @@
 N_CODE = 8
 GROUPS = 4
 LOG_ADM = 7
+LOG_QROWS = 12
 LOG_GROUP = 10
 MIB = 1024 * 1024
 BF = jnp.bfloat16
@@ -49,34 +50,25 @@
     )
 
 
-def cut_kernel(n_dp, n_y, n_table, x_ref, *refs):
-    labels, (out_ref, held, sems) = refs[:-3], refs[-3:]
-    copies = [pltpu.make_async_copy(ref, held.at[i], sems.at[i]) for i, ref in enumerate(labels)]
-    for copy in copies:
-        copy.start()
+def cut_kernel(n_dp, n_y, n_table, x_ref, q_ref, r_ref, a_ref, out_ref):
     piece = x_ref.shape[1] // (n_dp * N_Z)
     wide = n_dp * piece
+    y_bits, table_bits = n_y.bit_length() - 1, n_table.bit_length() - 1
+
+    def in_plane(code, bits, z):
+        dev = code >> bits
+        here = (code >= 0) & (((dev & (n_table - 1)) >> y_bits) == z)
+        return jnp.where(here, ((dev >> table_bits) << y_bits) + (dev & (n_y - 1)), -1)
+
     for z in range(N_Z):
         for d in range(n_dp):
             at = (d * N_Z + z) * piece
             out_ref[z, :, d * piece : (d + 1) * piece] = x_ref[:, at : at + piece]
-    for copy in copies:
-        copy.wait()
-    admit, owner, adm_row, q_shard, q_local, r_shard, r_local = [held[i] for i in range(len(labels))]
-    plain = admit == 0
-    a_row = owner * (ADM_DEV * n_table) + adm_row
-    a_dev = a_row >> LOG_ADM
-    y_bits, table_bits = n_y.bit_length() - 1, n_table.bit_length() - 1
-
-    def in_plane(dev, live, z):
-        here = live & (((dev & (n_table - 1)) >> y_bits) == z)
-        return jnp.where(here, ((dev >> table_bits) << y_bits) + (dev & (n_y - 1)), -1)
-
-    for z in range(N_Z):
         codes = []
-        for shard, low in ((q_shard, q_local), (r_shard, r_local)):
-            codes += [in_plane(shard, plain, z), low >> 8, low & 255]
-        codes += [in_plane(a_dev, jnp.logical_not(plain), z), a_row & (ADM_DEV - 1)]
+        for ref in (q_ref, r_ref):
+            low = ref[...] & (QROWS_DEV - 1)
+            codes += [in_plane(ref[...], LOG_QROWS, z), low >> 8, low & 255]
+        codes += [in_plane(a_ref[...], LOG_ADM, z), a_ref[...] & (ADM_DEV - 1)]
         block = jnp.concatenate(codes, axis=0).astype(F32).astype(BF)
         out_ref[z, :, wide : wide + block.shape[1]] = block
 
@@ -135,39 +127,36 @@
         out_ref[p] = res[p * share : (p + 1) * share, :]
 
 
-def bucket_kernel(
-    n_dest, cap, d0_ref, d1_ref, d2_ref, d3_ref, w_ref, slot_ref, labels_ref, group_ref, out_ref, d_ref, v_ref,
-    mark_ref,
-):
+def lookup_kernel(d0_ref, d1_ref, d2_ref, d3_ref, w_ref, out_ref, bias_ref, d_ref):
+    n_s, depth = d0_ref.shape
     for z, ref in enumerate((d0_ref, d1_ref, d2_ref, d3_ref)):
-        d_ref[z * ref.shape[0] : (z + 1) * ref.shape[0], :] = ref[...]
-    n_rows, depth = d_ref.shape
-    n_s = n_rows // N_Z
-    n_feat = w_ref.shape[0] // E
+        d_ref[z * n_s : (z + 1) * n_s, :] = ref[...]
+    for step in range(w_ref.shape[0] // (2 * E)):
+        res = dot(d_ref[...], w_ref[step * 2 * E : (step + 1) * 2 * E, :], ((1,), (1,))).astype(BF)
+        for z in range(N_Z):
+            for h in range(2):
+                row = (step * 2 + h) * n_s
+                out_ref[z, row : row + n_s, :] = res[z * n_s : (z + 1) * n_s, h * E : (h + 1) * E]
+    bias = jnp.sum(d_ref[...].astype(F32), axis=0, keepdims=True)
+    high = bias.astype(BF)
+    low = (bias - high.astype(F32)).astype(BF)
+    bias_ref[...] = jnp.concatenate(
+        [part[:, i * E : (i + 1) * E].astype(F32) for part in (high, low) for i in range(depth // E)], axis=0
+    ).astype(BF)
+
+
+def bucket_kernel(n_dest, cap, look_ref, slot_ref, labels_ref, group_ref, bias_ref, out_ref, mark_ref):
+    n_feat, n_s = slot_ref.shape[2:]
     seg = N_Z * cap
     n_mark = -(-seg // E)
     half = n_dest // 2
-
-    def lookups(step, carry):
-        wide = 2 * E
-        start = pl.multiple_of(step * wide, wide)
-        res = dot(d_ref[...], w_ref[pl.ds(start, wide), :], ((1,), (1,)))
-        for z in range(N_Z):
-            for h in range(2):
-                row = pl.multiple_of((step * 2 + h) * n_s, n_s)
-                v_ref[z, pl.ds(row, n_s), 0:E] = res[z * n_s : (z + 1) * n_s, h * E : (h + 1) * E].astype(BF)
-        return carry
-
-    lax.fori_loop(0, n_feat // 2, lookups, 0)
-    for z in range(N_Z):
-        v_ref[z, :, E : 2 * E] = labels_ref[z]
 
     slots = n_dest * cap
     wanted = rows_from(slots)
     for z in range(N_Z):
         for which in range(2):
             hits = [one_hot(wanted, slot_ref[which, z, f : f + 1, :]) for f in range(n_feat)]
-            o = dot(jnp.concatenate(hits, axis=1), v_ref[z])
+            o = dot(jnp.concatenate(hits, axis=1), jnp.concatenate([look_ref[z], labels_ref[z]], axis=1))
             for d in range(n_dest):
                 rows = o[d * cap : (d + 1) * cap, :]
                 out_ref[d, which * seg + z * cap : which * seg + (z + 1) * cap, :] = rows[:, 0:E].astype(BF)
@@ -181,7 +170,7 @@
         sides = []
         for f in range(n_feat):
             upper = group_ref[z, :, f : f + 1] >= half
-            v = v_ref[z, f * n_s : (f + 1) * n_s, 0:E].astype(F32)
+            v = look_ref[z, f * n_s : (f + 1) * n_s, :].astype(F32)
             sides.append(jnp.concatenate([jnp.where(upper, 0.0, v), jnp.where(upper, v, 0.0)], axis=1).astype(BF))
         o = o + dot(jnp.concatenate(hits, axis=1), jnp.concatenate(sides, axis=0))
     for d in range(n_dest):
@@ -189,13 +178,6 @@
         side = d // half * E
         out_ref[d, 2 * seg : 2 * seg + ADM_DEV, :] = o[at : at + ADM_DEV, side : side + E].astype(BF)
 
-    bias = jnp.sum(d_ref[...].astype(F32), axis=0, keepdims=True)
-    high = bias.astype(BF)
-    low = (bias - high.astype(F32)).astype(BF)
-    n_bias = depth // E
-    bias_rows = jnp.concatenate(
-        [part[:, i * E : (i + 1) * E].astype(F32) for part in (high, low) for i in range(n_bias)], axis=0
-    ).astype(BF)
     at_mark = 2 * seg + ADM_DEV
 
     def finish(d, carry):
@@ -209,7 +191,7 @@
             across = mixed[j * E : (j + 1) * E, :].T
             marks = jnp.where(rows == j, across[0:16, :], marks)
         out_ref[d, at_mark : at_mark + 16, :] = marks.astype(BF)
-        out_ref[d, at_mark + 16 : at_mark + 16 + 2 * n_bias, :] = bias_rows
+        out_ref[d, at_mark + 16 : at_mark + 16 + bias_ref.shape[0], :] = bias_ref[...]
         return carry
 
     lax.fori_loop(0, n_dest, finish, 0)
@@ -334,21 +316,6 @@
     scalar = pl.BlockSpec(memory_space=pltpu.SMEM)
     array = pl.BlockSpec(memory_space=pltpu.VMEM)
 
-    lookup_args = [a.reshape(n_s, n_feat).T for a in (admit, owner, adm_row, q_shard, q_local, r_shard, r_local)]
-    cut = call(
-        functools.partial(cut_kernel, n_dp, n_y, n_table),
-        "cut",
-        shape((N_Z, n_s, wide + E), BF),
-        10**7,
-        2 * 10**6,
-        in_specs=[array] + [pl.BlockSpec(memory_space=pltpu.HBM)] * len(lookup_args),
-        scratch_shapes=[
-            pltpu.VMEM((len(lookup_args), n_feat, n_s), jnp.int32),
-            pltpu.SemaphoreType.DMA((len(lookup_args),)),
-        ],
-    )(features, *lookup_args)
-    feat_in = lax.all_to_all(cut, "tz", split_axis=0, concat_axis=0, tiled=True)
-
     block = min(256, hidden)
     dpre = call(
         dpre_kernel,
@@ -364,14 +331,47 @@
             pl.BlockSpec((n_s, block), lambda i: (0, i)),
         ],
         out_specs=pl.BlockSpec((n_s, block), lambda i: (0, i)),
-    )(after(features, cut), w_first, b_first.reshape(1, hidden), grad_out)
+    )(features, w_first, b_first.reshape(1, hidden), grad_out)
 
     far = swap(dpre, "tz", 2)
     near = swap(dpre, "tz", 1)
     far = after(far, near)
     sources = [dpre, near, far, swap(far, "tz", 1)]
-    feat_in = after(feat_in, dpre)
-
+    admit, owner, adm_row, q_shard, q_local, r_shard, r_local = [
+        a.reshape(n_s, n_feat).T for a in (admit, owner, adm_row, q_shard, q_local, r_shard, r_local)
+    ]
+    cut = call(
+        functools.partial(cut_kernel, n_dp, n_y, n_table),
+        "cut",
+        shape((N_Z, n_s, wide + E), BF),
+        10**7,
+        2 * 10**6,
+    )(
+        after(features, dpre),
+        jnp.where(admit == 0, q_shard * QROWS_DEV + q_local, -1),
+        jnp.where(admit == 0, r_shard * QROWS_DEV + r_local, -1),
+        jnp.where(admit == 1, owner * (ADM_DEV * n_table) + adm_row, -1),
+    )
+    feat_in = lax.all_to_all(cut, "tz", split_axis=0, concat_axis=0, tiled=True)
+
+    look, bias = call(
+        lookup_kernel,
+        "lookups",
+        (shape((N_Z, count, E), BF), shape((2 * n_bias, E), BF)),
+        2 * N_Z * n_s * width * hidden,
+        7 * 10**6,
+        scratch_shapes=[pltpu.VMEM((N_Z * n_s, hidden), BF)],
+    )(*sources, w_first)
+    feat_in = after(feat_in, look)
+
+    w_part = call(
+        functools.partial(w_kernel, n_plane),
+        "w_part",
+        shape((n_plane, share, hidden), BF),
+        2 * N_Z * n_s * wide * hidden,
+        3 * 10**6,
+        in_specs=[scalar] + [array] * 5,
+    )(my_z, feat_in, *sources)
     slots, labels, group = call(
         functools.partial(slots_kernel, n_plane, cap, wide),
         "slots",
@@ -383,18 +383,7 @@
         10**9,
         3 * 10**6,
         in_specs=[scalar, array],
-    )(my_z, feat_in)
-    sources[3] = after(sources[3], slots)
-
-    w_part = call(
-        functools.partial(w_kernel, n_plane),
-        "w_part",
-        shape((n_plane, share, hidden), BF),
-        2 * N_Z * n_s * wide * hidden,
-        3 * 10**6,
-        in_specs=[scalar] + [array] * 5,
-    )(my_z, feat_in, *sources)
-    sources[3] = after(sources[3], w_part)
+    )(my_z, after(feat_in, w_part))
     w_part = lax.all_to_all(w_part, plane, split_axis=0, concat_axis=0, tiled=True)
 
     n_rows = 2 * seg + ADM_DEV + 16 + 2 * n_bias
@@ -404,13 +393,9 @@
         shape((n_plane, n_rows, E), BF),
         15 * 10**9,
         4 * 10**7,
-        scratch_shapes=[
-            pltpu.VMEM((N_Z * n_s, hidden), BF),
-            pltpu.VMEM((N_Z, count, 2 * E), BF),
-            pltpu.VMEM((2, n_plane, seg, E), F32),
-        ],
-        vmem=44,
-    )(*sources, w_first, slots, labels, group)
+        scratch_shapes=[pltpu.VMEM((2, n_plane, seg, E), F32)],
+        vmem=36,
+    )(look, slots, labels, group, bias)
 
     w_part = after(w_part, chunks)
     w_own = jnp.sum(w_part.astype(F32), axis=0).astype(BF)
@@ -419,14 +404,11 @@
 
     w_two = jnp.concatenate([w_own, swap(w_own, "tz", 2)], axis=0)
     w_four = jnp.concatenate([w_two, swap(w_two, "tz", 1)], axis=0)
+    w_four = after(w_four, chunks)
     sides = [w_four[:, : hidden // 2], w_four[:, hidden // 2 :]]
     over_y = [("ty", k) for k in doubling(n_y)]
     over_x = [("x", k) for k in doubling(n_dp // n_core)]
-    before = sides
-    for steps in zip(over_y + over_x, over_x + over_y):
-        before = sides
-        sides = [jnp.concatenate([side, swap(side, *step)], axis=0) for side, step in zip(sides, steps)]
-    chunks = after(chunks, *before)
+    last = sides
 
     def sums(table, chunks):
         outs = (shape((QROWS_DEV, E), F32), shape((n_bias, E), F32), shape((ADM_DEV, E), F32))
@@ -439,9 +421,15 @@
             vmem=40,
         )(chunks)
 
-    q_grad, b_grad, adm_grad = sums(0, chunks)
-    sides = [after(side, q_grad) for side in sides]
-    (r_grad,) = sums(1, after(chunks, *sides))
+    q_grad, b_grad, adm_grad = sums(0, after(chunks, w_four))
+    for i, steps in enumerate(zip(over_y + over_x, over_x + over_y)):
+        moved = [swap(side, *step) for side, step in zip(sides, steps)]
+        if i == 0:
+            moved = [after(part, q_grad) for part in moved]
+        sides = [jnp.concatenate(pair, axis=0) for pair in zip(sides, moved)]
+        last = sides if i == len(over_x + over_y) - 2 else last
+    (r_grad,) = sums(1, after(chunks, *last))
+    sides = [after(side, r_grad) for side in sides]
     others = [swap(side, "core", 1) for side in sides]
     at = jnp.stack([lax.axis_index(name) for name in ("x", "core", "tz", "ty")]).astype(jnp.int32)
     n_x = n_dp // n_core

time: 154 us -> 135 us (0.88)
  waiting for transfers between devices: 70.5 us -> 63.6 us
  Pallas kernels: 43 us -> 36.6 us
  local copies, waits for them, and re-layouts: 13.3 us -> 9.7 us
  starting transfers between devices: 25 us -> 23 us
    ppermute x11, waiting for transfers between devices: 70.5 us -> 56.8 us  [swap(): return lax.ppermute(x, axis, [(i, i ^ k) for i in range(n)])]
    all_to_all x1, waiting for transfers between devices: 0.01 us -> 5.98 us  [local(): lax.all_to_all(chunks, plane, split_axis=0, concat_axis=0, tiled=True)]
    pallas_call x1, Pallas kernels: 15 us -> 9.44 us  [local(): call(functools.partial(bucket_kernel, n_plane, cap), 'buckets', shape((n_...]
    unnamed x34 -> x32, local copies, waits for them, and re-layouts: 13.2 us -> 9.66 us
    pallas_call x2, Pallas kernels: 13.8 us -> 10.8 us  [sums(): call(functools.partial(sums_kernel, n_plane, seg, n_bias, table), ('q_sum...]
    pallas_call x0 -> x1, Pallas kernels: none -> 2.37 us  [local(): call(lookup_kernel, 'lookups', (shape((N_Z, count, E), BF), shape((2 * n_...]
  transfers between devices with their start and end apart: 14 -> 14, of which waited for: 7 -> 10; matrix products, arithmetic and copies ran while one was open for 0% -> 0% of each run, Pallas kernels for 19% -> 21%
where the time goes in v6:
time: 135 us
  waiting for transfers between devices  63.6 us (47%)
  Pallas kernels  36.6 us (27%)
  starting transfers between devices  23 us (17%)
  local copies, waits for them, and re-layouts  9.7 us (7%)
    ppermute x11, waiting for transfers between devices, swap(): return lax.ppermute(x, axis, [(i, i ^ k) for i in range(n)])  56.8 us
    pallas_call x2, Pallas kernels, sums(): call(functools.partial(sums_kernel, n_plane, seg, n_bias, table), ('q_sum...  10.8 us
    unnamed x32, local copies, waits for them, and re-layouts  9.66 us
    pallas_call x1, Pallas kernels, local(): call(functools.partial(bucket_kernel, n_plane, cap), 'buckets', shape((n_...  9.44 us
    ppermute x11, starting transfers between devices, swap(): return lax.ppermute(x, axis, [(i, i ^ k) for i in range(n)])  9.08 us
    pallas_call x2, Pallas kernels, widen(): call(functools.partial(widen_kernel, n_x, n_y, share), 'widen', jax.Shape...  6.32 us
    all_to_all x1, starting transfers between devices, local(): feat_in = lax.all_to_all(cut, 'tz', split_axis=0, concat_axis=0, tiled=True)  6.31 us
    all_to_all x1, waiting for transfers between devices, local(): lax.all_to_all(chunks, plane, split_axis=0, concat_axis=0, tiled=True)  5.98 us
  transfers between devices with their start and end apart: 14, of which 10 were waited for; matrix products, arithmetic and copies ran while one was open for 0% of the time, Pallas kernels for 21%

profile of v6, /device:TPU:0, one launch (start us, length us, event | category | flops | bytes accessed | tf_op | source)
XLA Modules:
  0.0 134.5 jit_solution(18266771531742055049)
XLA Ops:
  0.6 2.2 %copy-done = bf16[2048,1024]{1,0:T(8,128)(2,1)S(1)} copy-done((bf16[2048,1024]{1,0:T(8,128)(2,1)S(1)}, bf16[2048,1024]{1,0:T(8,128)(2,1)}, u32[]{:S(2)}) %copy-start) | copy-done | bytes 4194328
  5.5 2.0 %dpre.1.d0_ref = bf16[128,1024]{1,0:T(8,128)(2,1)S(1)} custom-call(bf16[128,2048]{1,0:T(8,128)(2,1)S(1)} %copy-done.2, bf16[2048,1024]{1,0:T(8,128)(2,1)S(1)} %copy-done, f32[1,1024]{1,0:T(1,128)S(1)} %bitcast.33, bf16[128,1024]{1,0:T(8,128)(2,1)S(1)} %copy-done.4), custom_call_target="tpu_custom_call" | custom-call | flops 536870912 | bytes 6000000 | tf_op jit(solution)/shard_map/dpre/pallas_call | solution.py:320
  8.6 6.3 %all-to-all-start = ((bf16[4,128,640]{2,1,0:T(8,128)(2,1)}), bf16[4,128,640]{2,1,0:T(8,128)(2,1)S(1)}, u32[]{:S(2)}, u32[]{:S(2)}) async-start(bf16[4,128,640]{2,1,0:T(8,128)(2,1)} %cut.1), calls=%async_computation | async-start | bytes 1310720 | tf_op jit(solution)/shard_map/all_to_all | solution.py:355
  15.0 2.9 %collective-permute-start.1 = (bf16[128,1024]{1,0:T(8,128)(2,1)S(1)}, bf16[128,1024]{1,0:T(8,128)(2,1)S(1)}, u32[]{:S(2)}, u32[]{:S(2)}) collective-permute-start(bf16[128,1024]{1,0:T(8,128)(2,1)S(1)} %dpre.1.d0_ref), channel_id=1, source_target_pairs={{0,4},{2,6},{4,0},{6,2},{1,5},{3,7},{5,1},{7,3},{8,12},{10,14},{12... | collective-permute-start | bytes 786440 | tf_op jit(solution)/shard_map/ppermute | solution.py:245
  17.9 1.5 %collective-permute-start = (bf16[128,1024]{1,0:T(8,128)(2,1)S(1)}, bf16[128,1024]{1,0:T(8,128)(2,1)S(1)}, u32[]{:S(2)}, u32[]{:S(2)}) collective-permute-start(bf16[128,1024]{1,0:T(8,128)(2,1)S(1)} %dpre.1.d0_ref), channel_id=1, source_target_pairs={{0,2},{2,0},{4,6},{6,4},{1,3},{3,1},{5,7},{7,5},{8,10},{10,8},{12,... | collective-permute-start | bytes 786440 | tf_op jit(solution)/shard_map/ppermute | solution.py:245
  19.3 24.1 %collective-permute-done.1.d2_ref = bf16[128,1024]{1,0:T(8,128)(2,1)S(1)} collective-permute-done((bf16[128,1024]{1,0:T(8,128)(2,1)S(1)}, bf16[128,1024]{1,0:T(8,128)(2,1)S(1)}, u32[]{:S(2)}, u32[]{:S(2)}) %collective-permute-start.1) | collective-permute-done | bytes 262176 | tf_op jit(solution)/shard_map/ppermute | solution.py:245
  43.5 7.3 %collective-permute-done.2.d3_ref = bf16[128,1024]{1,0:T(8,128)(2,1)S(1)} collective-permute-done((bf16[128,1024]{1,0:T(8,128)(2,1)S(1)}, bf16[128,1024]{1,0:T(8,128)(2,1)S(1)}, u32[]{:S(2)}, u32[]{:S(2)}) %collective-permute-start.2) | collective-permute-done | bytes 262176 | tf_op jit(solution)/shard_map/ppermute | solution.py:245
  50.8 2.2 %copy-done.1 = bf16[2048,1024]{1,0:T(8,128)(2,1)S(1)} copy-done((bf16[2048,1024]{1,0:T(8,128)(2,1)S(1)}, bf16[2048,1024]{1,0:T(8,128)(2,1)}, u32[]{:S(2)}) %copy-start.1) | copy-done | bytes 4194328
  53.0 2.4 %lookups.1 = (bf16[4,2048,128]{2,1,0:T(8,128)(2,1)S(1)}, bf16[16,128]{1,0:T(8,128)(2,1)S(1)}) custom-call(bf16[128,1024]{1,0:T(8,128)(2,1)S(1)} %dpre.1.d0_ref, bf16[128,1024]{1,0:T(8,128)(2,1)S(1)} %collective-permute-done.d1_ref, bf16[128,1024]{1,0:T(8,128)(2,1)S(1)} %collective-permute-done.1.d2_ref, bf16[128,1024]{1,0:T(8,128)(2,1)S(1)} %collective-permute-done.2.d3_ref, ...), custom_call_target="tpu_custom_call" | custom-call | flops 2147483648 | bytes 7000000 | tf_op jit(solution)/shard_map/lookups/pallas_call | solution.py:357
  55.3 1.3 copy-done.6
  56.7 1.7 %w_part.1 = bf16[8,64,1024]{2,1,0:T(8,128)(2,1)} custom-call(s32[1]{0:T(128)} %bitcast.2.z_ref, bf16[4,128,640]{2,1,0:T(8,128)(2,1)S(1)} %all-to-all-done.x_ref.in_ref, bf16[128,1024]{1,0:T(8,128)(2,1)S(1)} %dpre.1.d0_ref, bf16[128,1024]{1,0:T(8,128)(2,1)S(1)} %collective-permute-done.d1_ref, bf16[128,1024]{1,0:T(8,128)(2,1)S(1)} %collective-permute-done.1.d2_ref, ...), custom_call_target="tpu_custom_call" | custom-call | flops 536870912 | bytes 3000000 | tf_op jit(solution)/shard_map/w_part/pallas_call | solution.py:367
  58.4 3.7 %all-to-all-start.1 = ((bf16[8,64,1024]{2,1,0:T(8,128)(2,1)}), bf16[8,64,1024]{2,1,0:T(8,128)(2,1)S(1)}, u32[]{:S(2)}, u32[]{:S(2)}) async-start(bf16[8,64,1024]{2,1,0:T(8,128)(2,1)} %w_part.1), calls=%async_computation.1 | async-start | bytes 2097152 | tf_op jit(solution)/shard_map/all_to_all | solution.py:387
  62.1 3.0 %slots.1 = (s32[3,4,16,128]{3,2,1,0:T(8,128)S(1)}, bf16[4,2048,128]{2,1,0:T(8,128)(2,1)S(1)}, f32[4,128,16]{2,1,0:T(8,128)S(1)}) custom-call(s32[1]{0:T(128)} %bitcast.2.z_ref, bf16[4,128,640]{2,1,0:T(8,128)(2,1)S(1)} %all-to-all-done.x_ref.in_ref), custom_call_target="tpu_custom_call" | custom-call | flops 1000000000 | bytes 3000000 | tf_op jit(solution)/shard_map/slots/pallas_call | solution.py:375
  65.1 9.4 %buckets.1 = bf16[8,928,128]{2,1,0:T(8,128)(2,1)S(1)} custom-call(bf16[4,2048,128]{2,1,0:T(8,128)(2,1)S(1)} %copy-done.7, s32[3,4,16,128]{3,2,1,0:T(8,128)S(1)} %get-tuple-element.34.slot_ref, bf16[4,2048,128]{2,1,0:T(8,128)(2,1)S(1)} %get-tuple-element.35.labels_ref, f32[4,128,16]{2,1,0:T(8,128)S(1)} %get-tuple-element.36.group_ref, ...), custom_call_target="tpu_custom_call" | custom-call | flops 15000000512 | bytes 40000000 | tf_op jit(solution)/shard_map/buckets/pallas_call | solution.py:390
  76.8 3.8 %all-to-all-start.2 = ((bf16[8,928,128]{2,1,0:T(8,128)(2,1)}), bf16[8,928,128]{2,1,0:T(8,128)(2,1)S(1)}, u32[]{:S(2)}, u32[]{:S(2)}) async-start(bf16[8,928,128]{2,1,0:T(8,128)(2,1)} %copy-done.3), calls=%async_computation.2 | async-start | bytes 3801088 | tf_op jit(solution)/shard_map/all_to_all | solution.py:403
  80.7 8.9 %collective-permute-done.3 = bf16[64,1024]{1,0:T(8,128)(2,1)S(1)} collective-permute-done((bf16[64,1024]{1,0:T(8,128)(2,1)S(1)}, bf16[64,1024]{1,0:T(8,128)(2,1)S(1)}, u32[]{:S(2)}, u32[]{:S(2)}) %collective-permute-start.3) | collective-permute-done | bytes 131104 | tf_op jit(solution)/shard_map/ppermute | solution.py:245
  89.8 8.2 %collective-permute-done.4 = bf16[128,1024]{1,0:T(8,128)(2,1)S(1)} collective-permute-done((bf16[128,1024]{1,0:T(8,128)(2,1)S(1)}, bf16[128,1024]{1,0:T(8,128)(2,1)S(1)}, u32[]{:S(2)}, u32[]{:S(2)}) %collective-permute-start.4) | collective-permute-done | bytes 262176 | tf_op jit(solution)/shard_map/ppermute | solution.py:245
  98.1 6.0 %all-to-all-done.2.in_ref = bf16[8,928,128]{2,1,0:T(8,128)(2,1)S(1)} async-done(((bf16[8,928,128]{2,1,0:T(8,128)(2,1)}), bf16[8,928,128]{2,1,0:T(8,128)(2,1)S(1)}, u32[]{:S(2)}, u32[]{:S(2)}) %all-to-all-start.2) | async-done | bytes 1900576 | tf_op jit(solution)/shard_map/all_to_all | solution.py:403
  104.1 1.4 %collective-permute-start.7 = (bf16[256,512]{1,0:T(8,128)(2,1)S(1)}, bf16[256,512]{1,0:T(8,128)(2,1)S(1)}, u32[]{:S(2)}, u32[]{:S(2)}) collective-permute-start(bf16[256,512]{1,0:T(8,128)(2,1)S(1)} %get-tuple-element.57), channel_id=1, source_target_pairs={{0,16},{16,0},{1,17},{17,1},{2,18},{18,2},{3,19},{19,3},{4,20},{20... | collective-permute-start | bytes 786440 | tf_op jit(solution)/shard_map/ppermute | solution.py:245
  106.2 5.4 %q_sums.1 = (f32[4096,128]{1,0:T(8,128)}, f32[8,128]{1,0:T(8,128)}, f32[128,128]{1,0:T(8,128)}) custom-call(bf16[8,928,128]{2,1,0:T(8,128)(2,1)S(1)} %all-to-all-done.2.in_ref), custom_call_target="tpu_custom_call" | custom-call | flops 4000000000 | bytes 4000000 | tf_op jit(solution)/shard_map/q_sums/pallas_call | solution.py:415
  114.4 5.4 %r_sums.1 = f32[4096,128]{1,0:T(8,128)} custom-call(bf16[8,928,128]{2,1,0:T(8,128)(2,1)S(1)} %all-to-all-done.2.in_ref), custom_call_target="tpu_custom_call" | custom-call | flops 4000000000 | bytes 4000000 | tf_op jit(solution)/shard_map/r_sums/pallas_call | solution.py:415
  119.8 5.7 %collective-permute-done.9 = bf16[512,512]{1,0:T(8,128)(2,1)S(1)} collective-permute-done((bf16[512,512]{1,0:T(8,128)(2,1)S(1)}, bf16[512,512]{1,0:T(8,128)(2,1)S(1)}, u32[]{:S(2)}, u32[]{:S(2)}) %collective-permute-start.9) | collective-permute-done | bytes 524320 | tf_op jit(solution)/shard_map/ppermute | solution.py:245
  127.1 2.8 %widen.2.refs_0_ = f32[2048,1024]{1,0:T(8,128)} custom-call(s32[4]{0:T(128)S(1)} %get-tuple-element.56.at_ref, bf16[1024,512]{1,0:T(8,128)(2,1)S(1)} %pad_maximum_fusion.a_ref, bf16[1024,512]{1,0:T(8,128)(2,1)S(1)} %pad_maximum_fusion.1.b_ref), custom_call_target="tpu_custom_call" | custom-call | flops 1048576 | bytes 6291456 | tf_op jit(solution)/shard_map/widen/pallas_call | solution.py:275
  130.8 3.5 %widen.3 = f32[2048,1024]{1,0:T(8,128)} custom-call(s32[4]{0:T(128)S(1)} %get-tuple-element.55.at_ref, bf16[1024,512]{1,0:T(8,128)(2,1)S(1)} %collective-permute-done.8.a_ref, bf16[1024,512]{1,0:T(8,128)(2,1)} %collective-permute-done.10.b_ref, f32[2048,1024]{1,0:T(8,128)} %widen.2.refs_0_), custom_call_target="tpu_custom_call", output_to_operand_aliasing={{}: (3, {})} | custom-call | flops 1048576 | bytes 6291456 | tf_op jit(solution)/shard_map/widen/pallas_call | solution.py:275
  (57 shorter events, 12.2 us)
Async XLA Ops:
  0.6 2.2 %copy-start = (bf16[2048,1024]{1,0:T(8,128)(2,1)S(1)}, bf16[2048,1024]{1,0:T(8,128)(2,1)}, u32[]{:S(2)}) copy-start(bf16[2048,1024]{1,0:T(8,128)(2,1)} %w_ref.3) | copy-start | bytes 12582916
  5.5 2.1 %copy-start.11 = (s32[128,16,1]{0,2,1:T(1,128)S(1)}, s32[128,16,1]{0,2,1:T(1,128)}, u32[]{:S(2)}) copy-start(s32[128,16,1]{0,2,1:T(1,128)} %param.21) | copy-start | bytes 24580
  5.5 2.1 %copy-start.12 = (s32[128,16]{0,1:T(8,128)S(1)}, s32[128,16]{0,1:T(8,128)}, u32[]{:S(2)}) copy-start(s32[128,16]{0,1:T(8,128)} %param.16) | copy-start | bytes 24580
  5.5 2.1 %copy-start.13 = (s32[128,16]{0,1:T(8,128)S(1)}, s32[128,16]{0,1:T(8,128)}, u32[]{:S(2)}) copy-start(s32[128,16]{0,1:T(8,128)} %param.18) | copy-start | bytes 24580
  5.5 2.1 %copy-start.14 = (s32[128,16,1]{0,2,1:T(1,128)S(1)}, s32[128,16,1]{0,2,1:T(1,128)}, u32[]{:S(2)}) copy-start(s32[128,16,1]{0,2,1:T(1,128)} %param.17) | copy-start | bytes 24580
  5.5 2.1 %copy-start.8 = (s32[128,16]{0,1:T(8,128)S(1)}, s32[128,16]{0,1:T(8,128)}, u32[]{:S(2)}) copy-start(s32[128,16]{0,1:T(8,128)} %param.20) | copy-start | bytes 24580
  5.5 2.1 %copy-start.9 = (s32[128,16,1]{0,2,1:T(1,128)S(1)}, s32[128,16,1]{0,2,1:T(1,128)}, u32[]{:S(2)}) copy-start(s32[128,16,1]{0,2,1:T(1,128)} %param.19) | copy-start | bytes 24580
  8.6 48.0 %all-to-all-start = ((bf16[4,128,640]{2,1,0:T(8,128)(2,1)}), bf16[4,128,640]{2,1,0:T(8,128)(2,1)S(1)}, u32[]{:S(2)}, u32[]{:S(2)}) async-start(bf16[4,128,640]{2,1,0:T(8,128)(2,1)} %cut.1), calls=%async_computation | async-start | bytes 1310720 | tf_op jit(solution)/shard_map/all_to_all | solution.py:355
  15.0 28.5 %collective-permute-start.1 = (bf16[128,1024]{1,0:T(8,128)(2,1)S(1)}, bf16[128,1024]{1,0:T(8,128)(2,1)S(1)}, u32[]{:S(2)}, u32[]{:S(2)}) collective-permute-start(bf16[128,1024]{1,0:T(8,128)(2,1)S(1)} %dpre.1.d0_ref), channel_id=1, source_target_pairs={{0,4},{2,6},{4,0},{6,2},{1,5},{3,7},{5,1},{7,3},{8,12},{10,14},{12... | collective-permute-start | bytes 786440 | tf_op jit(solution)/shard_map/ppermute | solution.py:245
  17.9 25.6 %collective-permute-start = (bf16[128,1024]{1,0:T(8,128)(2,1)S(1)}, bf16[128,1024]{1,0:T(8,128)(2,1)S(1)}, u32[]{:S(2)}, u32[]{:S(2)}) collective-permute-start(bf16[128,1024]{1,0:T(8,128)(2,1)S(1)} %dpre.1.d0_ref), channel_id=1, source_target_pairs={{0,2},{2,0},{4,6},{6,4},{1,3},{3,1},{5,7},{7,5},{8,10},{10,8},{12,... | collective-permute-start | bytes 786440 | tf_op jit(solution)/shard_map/ppermute | solution.py:245
  43.5 7.3 %collective-permute-start.2 = (bf16[128,1024]{1,0:T(8,128)(2,1)S(1)}, bf16[128,1024]{1,0:T(8,128)(2,1)S(1)}, u32[]{:S(2)}, u32[]{:S(2)}) collective-permute-start(bf16[128,1024]{1,0:T(8,128)(2,1)S(1)} %collective-permute-done.1.d2_ref), channel_id=1, source_target_pairs={{0,2},{2,0},{4,6},{6,4},{1,3},{3,1},{5,7},{7,5},{8,10},{10,8},{12,... | collective-permute-start | bytes 786440 | tf_op jit(solution)/shard_map/ppermute | solution.py:245
  50.8 2.2 %copy-start.1 = (bf16[2048,1024]{1,0:T(8,128)(2,1)S(1)}, bf16[2048,1024]{1,0:T(8,128)(2,1)}, u32[]{:S(2)}) copy-start(bf16[2048,1024]{1,0:T(8,128)(2,1)} %w_ref.3) | copy-start | bytes 12582916
  58.4 18.3 %all-to-all-start.1 = ((bf16[8,64,1024]{2,1,0:T(8,128)(2,1)}), bf16[8,64,1024]{2,1,0:T(8,128)(2,1)S(1)}, u32[]{:S(2)}, u32[]{:S(2)}) async-start(bf16[8,64,1024]{2,1,0:T(8,128)(2,1)} %w_part.1), calls=%async_computation.1 | async-start | bytes 2097152 | tf_op jit(solution)/shard_map/all_to_all | solution.py:387
  62.1 3.0 %copy-start.7 = (bf16[4,2048,128]{2,1,0:T(8,128)(2,1)S(1)}, bf16[4,2048,128]{2,1,0:T(8,128)(2,1)}, u32[]{:S(2)}) copy-start(bf16[4,2048,128]{2,1,0:T(8,128)(2,1)} %copy-done.6) | copy-start | bytes 6291460
  76.8 27.2 %all-to-all-start.2 = ((bf16[8,928,128]{2,1,0:T(8,128)(2,1)}), bf16[8,928,128]{2,1,0:T(8,128)(2,1)S(1)}, u32[]{:S(2)}, u32[]{:S(2)}) async-start(bf16[8,928,128]{2,1,0:T(8,128)(2,1)} %copy-done.3), calls=%async_computation.2 | async-start | bytes 3801088 | tf_op jit(solution)/shard_map/all_to_all | solution.py:403
  80.7 9.0 %collective-permute-start.3 = (bf16[64,1024]{1,0:T(8,128)(2,1)S(1)}, bf16[64,1024]{1,0:T(8,128)(2,1)S(1)}, u32[]{:S(2)}, u32[]{:S(2)}) collective-permute-start(bf16[64,1024]{1,0:T(8,128)(2,1)S(1)} %reduce_sum.12), channel_id=1, source_target_pairs={{0,4},{2,6},{4,0},{6,2},{1,5},{3,7},{5,1},{7,3},{8,12},{10,14},{12... | collective-permute-start | bytes 393224 | tf_op jit(solution)/shard_map/ppermute | solution.py:245
  89.7 8.3 %collective-permute-start.4 = (bf16[128,1024]{1,0:T(8,128)(2,1)S(1)}, bf16[128,1024]{1,0:T(8,128)(2,1)S(1)}, u32[]{:S(2)}, u32[]{:S(2)}) collective-permute-start(bf16[128,1024]{1,0:T(8,128)(2,1)S(1)} %pad_maximum_fusion.5), channel_id=1, source_target_pairs={{0,2},{2,0},{4,6},{6,4},{1,3},{3,1},{5,7},{7,5},{8,10},{10,8},{12,... | collective-permute-start | bytes 786440 | tf_op jit(solution)/shard_map/ppermute | solution.py:245
  104.1 8.3 %collective-permute-start.7 = (bf16[256,512]{1,0:T(8,128)(2,1)S(1)}, bf16[256,512]{1,0:T(8,128)(2,1)S(1)}, u32[]{:S(2)}, u32[]{:S(2)}) collective-permute-start(bf16[256,512]{1,0:T(8,128)(2,1)S(1)} %get-tuple-element.57), channel_id=1, source_target_pairs={{0,16},{16,0},{1,17},{17,1},{2,18},{18,2},{3,19},{19,3},{4,20},{20... | collective-permute-start | bytes 786440 | tf_op jit(solution)/shard_map/ppermute | solution.py:245
  105.5 8.1 %collective-permute-start.5 = (bf16[256,512]{1,0:T(8,128)(2,1)S(1)}, bf16[256,512]{1,0:T(8,128)(2,1)S(1)}, u32[]{:S(2)}, u32[]{:S(2)}) collective-permute-start(bf16[256,512]{1,0:T(8,128)(2,1)S(1)} %get-tuple-element.58), channel_id=1, source_target_pairs={{0,1},{1,0},{2,3},{3,2},{4,5},{5,4},{6,7},{7,6},{8,9},{9,8},{10,11... | collective-permute-start | bytes 786440 | tf_op jit(solution)/shard_map/ppermute | solution.py:245
  112.4 13.0 %collective-permute-start.9 = (bf16[512,512]{1,0:T(8,128)(2,1)S(1)}, bf16[512,512]{1,0:T(8,128)(2,1)S(1)}, u32[]{:S(2)}, u32[]{:S(2)}) collective-permute-start(bf16[512,512]{1,0:T(8,128)(2,1)S(1)} %pad_maximum_fusion.4), channel_id=1, source_target_pairs={{0,1},{1,0},{2,3},{3,2},{4,5},{5,4},{6,7},{7,6},{8,9},{9,8},{10,11... | collective-permute-start | bytes 1572872 | tf_op jit(solution)/shard_map/ppermute | solution.py:245
  113.6 12.8 %collective-permute-start.6 = (bf16[512,512]{1,0:T(8,128)(2,1)S(1)}, bf16[512,512]{1,0:T(8,128)(2,1)S(1)}, u32[]{:S(2)}, u32[]{:S(2)}) collective-permute-start(bf16[512,512]{1,0:T(8,128)(2,1)S(1)} %pad_maximum_fusion.3), channel_id=1, source_target_pairs={{0,16},{16,0},{1,17},{17,1},{2,18},{18,2},{3,19},{19,3},{4,20},{20... | collective-permute-start | bytes 1572872 | tf_op jit(solution)/shard_map/ppermute | solution.py:245
  119.8 7.3 %copy-start.15 = (s32[4]{0:T(128)S(1)}, s32[4]{0:T(128)}, u32[]{:S(2)}) copy-start(s32[4]{0:T(128)} %constant.30.clone) | copy-start | bytes 52
  126.5 3.5 %collective-permute-start.8 = (bf16[1024,512]{1,0:T(8,128)(2,1)S(1)}, bf16[1024,512]{1,0:T(8,128)(2,1)S(1)}, u32[]{:S(2)}, u32[]{:S(2)}) collective-permute-start(bf16[1024,512]{1,0:T(8,128)(2,1)S(1)} %pad_maximum_fusion.a_ref), channel_id=1, source_target_pairs={{0,8},{8,0},{1,9},{9,1},{2,10},{10,2},{3,11},{11,3},{4,12},{12,4},... | collective-permute-start | bytes 3145736 | tf_op jit(solution)/shard_map/ppermute | solution.py:245
  126.5 4.3 %collective-permute-start.10 = (bf16[1024,512]{1,0:T(8,128)(2,1)S(1)}, bf16[1024,512]{1,0:T(8,128)(2,1)}, u32[]{:S(2)}, u32[]{:S(2)}) collective-permute-start(bf16[1024,512]{1,0:T(8,128)(2,1)S(1)} %pad_maximum_fusion.1.b_ref), channel_id=1, source_target_pairs={{0,8},{8,0},{1,9},{9,1},{2,10},{10,2},{3,11},{11,3},{4,12},{12,4},... | collective-permute-start | bytes 3145736 | tf_op jit(solution)/shard_map/ppermute | solution.py:245
  (6 other events, 7.3 us)

commit v7 on v6

--- a/solution.py
+++ b/solution.py
@@ -250,11 +250,11 @@
     half = a_ref.shape[1]
     copies = []
     for b in range(a_ref.shape[0] // share):
-        z = at_ref[2] ^ (((b & 1) << 1) | ((b >> 1) & 1))
-        rest = b >> 2
         rows = slice(b * share, (b + 1) * share)
-        for side, ref in enumerate((a_ref, b_ref)):
-            y, x = (rest % n_y, rest // n_y) if side == 0 else (rest // n_x, rest % n_x)
+        for side, (ref, first) in enumerate(((a_ref, n_y), (b_ref, n_x))):
+            low, mid, high = b % first, b // first % N_Z, b // (first * N_Z)
+            y, x = (low, high) if side == 0 else (high, low)
+            z = at_ref[2] ^ (((mid & 1) << 1) | (mid >> 1))
             row = ((((at_ref[0] ^ x) * 2 + at_ref[1]) * N_Z + z) * n_y + (at_ref[3] ^ y)) * share
             cols = slice(side * half, (side + 1) * half)
             held_ref[rows, cols] = ref[rows, :].astype(F32)
@@ -331,6 +331,7 @@
             pl.BlockSpec((n_s, block), lambda i: (0, i)),
         ],
         out_specs=pl.BlockSpec((n_s, block), lambda i: (0, i)),
+        vmem=58,
     )(features, w_first, b_first.reshape(1, hidden), grad_out)
 
     far = swap(dpre, "tz", 2)
@@ -352,17 +353,7 @@
         jnp.where(admit == 0, r_shard * QROWS_DEV + r_local, -1),
         jnp.where(admit == 1, owner * (ADM_DEV * n_table) + adm_row, -1),
     )
-    feat_in = lax.all_to_all(cut, "tz", split_axis=0, concat_axis=0, tiled=True)
-
-    look, bias = call(
-        lookup_kernel,
-        "lookups",
-        (shape((N_Z, count, E), BF), shape((2 * n_bias, E), BF)),
-        2 * N_Z * n_s * width * hidden,
-        7 * 10**6,
-        scratch_shapes=[pltpu.VMEM((N_Z * n_s, hidden), BF)],
-    )(*sources, w_first)
-    feat_in = after(feat_in, look)
+    feat_in = lax.all_to_all(after(cut, near), "tz", split_axis=0, concat_axis=0, tiled=True)
 
     w_part = call(
         functools.partial(w_kernel, n_plane),
@@ -372,6 +363,14 @@
         3 * 10**6,
         in_specs=[scalar] + [array] * 5,
     )(my_z, feat_in, *sources)
+    look, bias = call(
+        lookup_kernel,
+        "lookups",
+        (shape((N_Z, count, E), BF), shape((2 * n_bias, E), BF)),
+        2 * N_Z * n_s * width * hidden,
+        7 * 10**6,
+        scratch_shapes=[pltpu.VMEM((N_Z * n_s, hidden), BF)],
+    )(*sources[:3], after(sources[3], w_part), w_first)
     slots, labels, group = call(
         functools.partial(slots_kernel, n_plane, cap, wide),
         "slots",
@@ -394,7 +393,7 @@
         15 * 10**9,
         4 * 10**7,
         scratch_shapes=[pltpu.VMEM((2, n_plane, seg, E), F32)],
-        vmem=36,
+        vmem=28,
     )(look, slots, labels, group, bias)
 
     w_part = after(w_part, chunks)
@@ -402,13 +401,16 @@
     w_own, chunks = lax.optimization_barrier((w_own, chunks))
     chunks = lax.all_to_all(chunks, plane, split_axis=0, concat_axis=0, tiled=True)
 
-    w_two = jnp.concatenate([w_own, swap(w_own, "tz", 2)], axis=0)
-    w_four = jnp.concatenate([w_two, swap(w_two, "tz", 1)], axis=0)
-    w_four = after(w_four, chunks)
-    sides = [w_four[:, : hidden // 2], w_four[:, hidden // 2 :]]
+    def spread(x, steps):
+        for step in steps:
+            x = jnp.concatenate([x, swap(x, *step)], axis=0)
+        return x
+
     over_y = [("ty", k) for k in doubling(n_y)]
     over_x = [("x", k) for k in doubling(n_dp // n_core)]
-    last = sides
+    side = hidden // 2
+    w_rows = jnp.concatenate([spread(w_own[:, :side], over_y), spread(w_own[:, side:], over_x)], axis=1)
+    w_rows = after(spread(w_rows, [("tz", 2), ("tz", 1)]), chunks)
 
     def sums(table, chunks):
         outs = (shape((QROWS_DEV, E), F32), shape((n_bias, E), F32), shape((ADM_DEV, E), F32))
@@ -421,19 +423,16 @@
             vmem=40,
         )(chunks)
 
-    q_grad, b_grad, adm_grad = sums(0, after(chunks, w_four))
-    for i, steps in enumerate(zip(over_y + over_x, over_x + over_y)):
-        moved = [swap(side, *step) for side, step in zip(sides, steps)]
-        if i == 0:
-            moved = [after(part, q_grad) for part in moved]
-        sides = [jnp.concatenate(pair, axis=0) for pair in zip(sides, moved)]
-        last = sides if i == len(over_x + over_y) - 2 else last
-    (r_grad,) = sums(1, after(chunks, *last))
-    sides = [after(side, r_grad) for side in sides]
-    others = [swap(side, "core", 1) for side in sides]
+    q_grad, b_grad, adm_grad = sums(0, after(chunks, w_rows))
+    (r_grad,) = sums(1, after(chunks, q_grad))
+    sides = []
+    for x, steps in ((w_rows[:, :side], over_x), (w_rows[:, side:], over_y)):
+        x = spread(x, steps[:-1])
+        sides.append(jnp.concatenate([x, after(swap(x, *steps[-1]), r_grad)], axis=0))
+    others = [swap(x, "core", 1) for x in sides]
     at = jnp.stack([lax.axis_index(name) for name in ("x", "core", "tz", "ty")]).astype(jnp.int32)
     n_x = n_dp // n_core
-    w_grad = widen(n_x, n_y, share, at, [after(side, r_grad) for side in sides], None)
+    w_grad = widen(n_x, n_y, share, at, sides, None)
     flip = at ^ jnp.array([0, 1, 0, 0], jnp.int32)
     w_grad = widen(n_x, n_y, share, flip, others, w_grad)
     return (w_grad, b_grad.reshape(hidden), adm_grad, q_grad, r_grad)

time: 135 us -> 159 us (1.18)
  waiting for transfers between devices: 63.6 us -> 88.9 us
  local copies, waits for them, and re-layouts: 9.7 us -> 3.57 us
  Pallas kernels: 36.6 us -> 39.5 us
  starting transfers between devices: 23 us -> 25.4 us
    ppermute x11, waiting for transfers between devices: 56.8 us -> 88.9 us  [swap(): return lax.ppermute(x, axis, [(i, i ^ k) for i in range(n)])]
    unnamed x32 -> x24, local copies, waits for them, and re-layouts: 9.66 us -> 3.49 us
    all_to_all x1, waiting for transfers between devices: 5.98 us -> 0.01 us  [local(): lax.all_to_all(chunks, plane, split_axis=0, concat_axis=0, tiled=True)]
    ppermute x11, starting transfers between devices: 9.08 us -> 12.4 us  [swap(): return lax.ppermute(x, axis, [(i, i ^ k) for i in range(n)])]
    pallas_call x1, Pallas kernels: 2.03 us -> 4.86 us  [local(): call(dpre_kernel, 'dpre', shape((n_s, hidden), BF), 2 * n_s * width * hid...]
  transfers between devices with their start and end apart: 14 -> 14, of which waited for: 10 -> 9; matrix products, arithmetic and copies ran while one was open for 0% -> 0% of each run, Pallas kernels for 21% -> 19%
where the time goes in v7:
time: 159 us
  waiting for transfers between devices  88.9 us (56%)
  Pallas kernels  39.5 us (25%)
  starting transfers between devices  25.4 us (16%)
  local copies, waits for them, and re-layouts  3.57 us (2%)
    ppermute x11, waiting for transfers between devices, swap(): return lax.ppermute(x, axis, [(i, i ^ k) for i in range(n)])  88.9 us
    ppermute x11, starting transfers between devices, swap(): return lax.ppermute(x, axis, [(i, i ^ k) for i in range(n)])  12.4 us
    pallas_call x2, Pallas kernels, sums(): call(functools.partial(sums_kernel, n_plane, seg, n_bias, table), ('q_sum...  10.8 us
    pallas_call x1, Pallas kernels, local(): call(functools.partial(bucket_kernel, n_plane, cap), 'buckets', shape((n_...  9.46 us
    pallas_call x2, Pallas kernels, widen(): call(functools.partial(widen_kernel, n_x, n_y, share), 'widen', jax.Shape...  6.32 us
    all_to_all x1, starting transfers between devices, local(): lax.all_to_all(after(cut, near), 'tz', split_axis=0, concat_axis=0, tiled...  4.96 us
    pallas_call x1, Pallas kernels, local(): call(dpre_kernel, 'dpre', shape((n_s, hidden), BF), 2 * n_s * width * hid...  4.86 us
    all_to_all x1, starting transfers between devices, local(): lax.all_to_all(chunks, plane, split_axis=0, concat_axis=0, tiled=True)  4.21 us
  transfers between devices with their start and end apart: 14, of which 9 were waited for; matrix products, arithmetic and copies ran while one was open for 0% of the time, Pallas kernels for 19%

profile of v7, /device:TPU:0, one launch (start us, length us, event | category | flops | bytes accessed | tf_op | source)
XLA Modules:
  0.0 158.9 jit_solution(9525267304696052655)
XLA Ops:
  0.7 4.9 %dpre.1.d0_ref = bf16[128,1024]{1,0:T(8,128)(2,1)} custom-call(bf16[128,2048]{1,0:T(8,128)(2,1)} %x_ref.2, bf16[2048,1024]{1,0:T(8,128)(2,1)} %w_ref.3, f32[1,1024]{1,0:T(1,128)} %bitcast.36, bf16[128,1024]{1,0:T(8,128)(2,1)} %g_ref.1), custom_call_target="tpu_custom_call" | custom-call | flops 536870912 | bytes 6000000 | tf_op jit(solution)/shard_map/dpre/pallas_call | solution.py:320
  5.6 3.0 %collective-permute-start = (bf16[128,1024]{1,0:T(8,128)(2,1)}, bf16[128,1024]{1,0:T(8,128)(2,1)S(1)}, u32[]{:S(2)}, u32[]{:S(2)}) collective-permute-start(bf16[128,1024]{1,0:T(8,128)(2,1)} %dpre.1.d0_ref), channel_id=1, source_target_pairs={{0,2},{2,0},{4,6},{6,4},{1,3},{3,1},{5,7},{7,5},{8,10},{10,8},{12,... | collective-permute-start | bytes 786440 | tf_op jit(solution)/shard_map/ppermute | solution.py:245
  9.6 5.5 %collective-permute-done.d1_ref = bf16[128,1024]{1,0:T(8,128)(2,1)S(1)} collective-permute-done((bf16[128,1024]{1,0:T(8,128)(2,1)}, bf16[128,1024]{1,0:T(8,128)(2,1)S(1)}, u32[]{:S(2)}, u32[]{:S(2)}) %collective-permute-start) | collective-permute-done | bytes 262176 | tf_op jit(solution)/shard_map/ppermute | solution.py:245
  15.2 5.0 %all-to-all-start = ((bf16[4,128,640]{2,1,0:T(8,128)(2,1)}), bf16[4,128,640]{2,1,0:T(8,128)(2,1)S(1)}, u32[]{:S(2)}, u32[]{:S(2)}) async-start(bf16[4,128,640]{2,1,0:T(8,128)(2,1)} %cut.1), calls=%async_computation | async-start | bytes 1310720 | tf_op jit(solution)/shard_map/all_to_all | solution.py:356
  20.1 2.9 %collective-permute-start.1 = (bf16[128,1024]{1,0:T(8,128)(2,1)S(1)}, bf16[128,1024]{1,0:T(8,128)(2,1)S(1)}, u32[]{:S(2)}, u32[]{:S(2)}) collective-permute-start(bf16[128,1024]{1,0:T(8,128)(2,1)S(1)} %copy-done.3), channel_id=1, source_target_pairs={{0,4},{2,6},{4,0},{6,2},{1,5},{3,7},{5,1},{7,3},{8,12},{10,14},{12... | collective-permute-start | bytes 786440 | tf_op jit(solution)/shard_map/ppermute | solution.py:245
  23.1 24.7 %collective-permute-done.1.d2_ref = bf16[128,1024]{1,0:T(8,128)(2,1)S(1)} collective-permute-done((bf16[128,1024]{1,0:T(8,128)(2,1)S(1)}, bf16[128,1024]{1,0:T(8,128)(2,1)S(1)}, u32[]{:S(2)}, u32[]{:S(2)}) %collective-permute-start.1) | collective-permute-done | bytes 262176 | tf_op jit(solution)/shard_map/ppermute | solution.py:245
  47.8 7.3 %collective-permute-done.2.d3_ref = bf16[128,1024]{1,0:T(8,128)(2,1)S(1)} collective-permute-done((bf16[128,1024]{1,0:T(8,128)(2,1)S(1)}, bf16[128,1024]{1,0:T(8,128)(2,1)S(1)}, u32[]{:S(2)}, u32[]{:S(2)}) %collective-permute-start.2) | collective-permute-done | bytes 262176 | tf_op jit(solution)/shard_map/ppermute | solution.py:245
  55.1 1.7 %w_part.1 = bf16[8,64,1024]{2,1,0:T(8,128)(2,1)} custom-call(s32[1]{0:T(128)} %bitcast.2.z_ref, bf16[4,128,640]{2,1,0:T(8,128)(2,1)S(1)} %all-to-all-done.x_ref.in_ref, bf16[128,1024]{1,0:T(8,128)(2,1)S(1)} %copy-done.3, bf16[128,1024]{1,0:T(8,128)(2,1)S(1)} %collective-permute-done.d1_ref, bf16[128,1024]{1,0:T(8,128)(2,1)S(1)} %collective-permute-done.1.d2_ref, ...), custom_call_target="tpu_custom_call" | custom-call | flops 536870912 | bytes 3000000 | tf_op jit(solution)/shard_map/w_part/pallas_call | solution.py:358
  56.8 3.7 %all-to-all-start.1 = ((bf16[8,64,1024]{2,1,0:T(8,128)(2,1)}), bf16[8,64,1024]{2,1,0:T(8,128)(2,1)S(1)}, u32[]{:S(2)}, u32[]{:S(2)}) async-start(bf16[8,64,1024]{2,1,0:T(8,128)(2,1)} %w_part.1), calls=%async_computation.1 | async-start | bytes 2097152 | tf_op jit(solution)/shard_map/all_to_all | solution.py:386
  60.5 3.0 %slots.1 = (s32[3,4,16,128]{3,2,1,0:T(8,128)S(1)}, bf16[4,2048,128]{2,1,0:T(8,128)(2,1)S(1)}, f32[4,128,16]{2,1,0:T(8,128)S(1)}) custom-call(s32[1]{0:T(128)} %bitcast.2.z_ref, bf16[4,128,640]{2,1,0:T(8,128)(2,1)S(1)} %all-to-all-done.x_ref.in_ref), custom_call_target="tpu_custom_call" | custom-call | flops 1000000000 | bytes 3000000 | tf_op jit(solution)/shard_map/slots/pallas_call | solution.py:374
  63.5 2.2 %copy-done = bf16[2048,1024]{1,0:T(8,128)(2,1)S(1)} copy-done((bf16[2048,1024]{1,0:T(8,128)(2,1)S(1)}, bf16[2048,1024]{1,0:T(8,128)(2,1)}, u32[]{:S(2)}) %copy-start) | copy-done | bytes 4194328
  65.7 2.4 %lookups.1 = (bf16[4,2048,128]{2,1,0:T(8,128)(2,1)S(1)}, bf16[16,128]{1,0:T(8,128)(2,1)S(1)}) custom-call(bf16[128,1024]{1,0:T(8,128)(2,1)S(1)} %copy-done.3, bf16[128,1024]{1,0:T(8,128)(2,1)S(1)} %collective-permute-done.d1_ref, bf16[128,1024]{1,0:T(8,128)(2,1)S(1)} %collective-permute-done.1.d2_ref, bf16[128,1024]{1,0:T(8,128)(2,1)S(1)} %collective-permute-done.2.d3_ref, ...), custom_call_target="tpu_custom_call" | custom-call | flops 2147483648 | bytes 7000000 | tf_op jit(solution)/shard_map/lookups/pallas_call | solution.py:366
  68.1 9.5 %buckets.1 = bf16[8,928,128]{2,1,0:T(8,128)(2,1)S(1)} custom-call(bf16[4,2048,128]{2,1,0:T(8,128)(2,1)S(1)} %get-tuple-element.30.look_ref, s32[3,4,16,128]{3,2,1,0:T(8,128)S(1)} %get-tuple-element.32.slot_ref, bf16[4,2048,128]{2,1,0:T(8,128)(2,1)S(1)} %get-tuple-element.33.labels_ref, f32[4,128,16]{2,1,0:T(8,128)S(1)} %get-tuple-element.34.group_ref, ...), custom_call_target="tpu_custom_call" | custom-call | flops 15000000512 | bytes 40000000 | tf_op jit(solution)/shard_map/buckets/pallas_call | solution.py:389
  79.0 4.2 %all-to-all-start.2 = ((bf16[8,928,128]{2,1,0:T(8,128)(2,1)}), bf16[8,928,128]{2,1,0:T(8,128)(2,1)S(1)}, u32[]{:S(2)}, u32[]{:S(2)}) async-start(bf16[8,928,128]{2,1,0:T(8,128)(2,1)} %copy-done.2), calls=%async_computation.2 | async-start | bytes 3801088 | tf_op jit(solution)/shard_map/all_to_all | solution.py:402
  83.2 2.1 %collective-permute-start.3 = (bf16[64,512]{1,0:T(8,128)(2,1)S(1)}, bf16[64,512]{1,0:T(8,128)(2,1)S(1)}, u32[]{:S(2)}, u32[]{:S(2)}) collective-permute-start(bf16[64,512]{1,0:T(8,128)(2,1)S(1)} %get-tuple-element.53), channel_id=1, source_target_pairs={{0,1},{1,0},{2,3},{3,2},{4,5},{5,4},{6,7},{7,6},{8,9},{9,8},{10,11... | collective-permute-start | bytes 196616 | tf_op jit(solution)/shard_map/ppermute | solution.py:245
  85.3 1.5 collective-permute-start.4
  86.8 21.4 %collective-permute-done.3 = bf16[64,512]{1,0:T(8,128)(2,1)S(1)} collective-permute-done((bf16[64,512]{1,0:T(8,128)(2,1)S(1)}, bf16[64,512]{1,0:T(8,128)(2,1)S(1)}, u32[]{:S(2)}, u32[]{:S(2)}) %collective-permute-start.3) | collective-permute-done | bytes 65568 | tf_op jit(solution)/shard_map/ppermute | solution.py:245
  108.4 14.1 %collective-permute-done.5 = bf16[128,1024]{1,0:T(8,128)(2,1)S(1)} collective-permute-done((bf16[128,1024]{1,0:T(8,128)(2,1)S(1)}, bf16[128,1024]{1,0:T(8,128)(2,1)S(1)}, u32[]{:S(2)}, u32[]{:S(2)}) %collective-permute-start.5) | collective-permute-done | bytes 262176 | tf_op jit(solution)/shard_map/ppermute | solution.py:245
  122.6 13.8 %collective-permute-done.6 = bf16[256,1024]{1,0:T(8,128)(2,1)S(1)} collective-permute-done((bf16[256,1024]{1,0:T(8,128)(2,1)S(1)}, bf16[256,1024]{1,0:T(8,128)(2,1)S(1)}, u32[]{:S(2)}, u32[]{:S(2)}) %collective-permute-start.6) | collective-permute-done | bytes 524320 | tf_op jit(solution)/shard_map/ppermute | solution.py:245
  136.6 1.5 collective-permute-start.9
  138.8 5.4 %q_sums.1 = (f32[4096,128]{1,0:T(8,128)}, f32[8,128]{1,0:T(8,128)}, f32[128,128]{1,0:T(8,128)}) custom-call(bf16[8,928,128]{2,1,0:T(8,128)(2,1)S(1)} %all-to-all-done.2.in_ref), custom_call_target="tpu_custom_call" | custom-call | flops 4000000000 | bytes 4000000 | tf_op jit(solution)/shard_map/q_sums/pallas_call | solution.py:417
  144.2 5.4 %r_sums.1 = f32[4096,128]{1,0:T(8,128)} custom-call(bf16[8,928,128]{2,1,0:T(8,128)(2,1)S(1)} %all-to-all-done.2.in_ref), custom_call_target="tpu_custom_call" | custom-call | flops 4000000000 | bytes 4000000 | tf_op jit(solution)/shard_map/r_sums/pallas_call | solution.py:417
  151.6 2.8 %widen.2.refs_0_ = f32[2048,1024]{1,0:T(8,128)} custom-call(s32[4]{0:T(128)S(1)} %get-tuple-element.50.at_ref, bf16[1024,512]{1,0:T(8,128)(2,1)S(1)} %pad_maximum_fusion.1.a_ref, bf16[1024,512]{1,0:T(8,128)(2,1)S(1)} %pad_maximum_fusion.2.b_ref), custom_call_target="tpu_custom_call" | custom-call | flops 1048576 | bytes 6291456 | tf_op jit(solution)/shard_map/widen/pallas_call | solution.py:275
  155.3 3.5 %widen.3 = f32[2048,1024]{1,0:T(8,128)} custom-call(s32[4]{0:T(128)S(1)} %get-tuple-element.49.at_ref, bf16[1024,512]{1,0:T(8,128)(2,1)S(1)} %collective-permute-done.8.a_ref, bf16[1024,512]{1,0:T(8,128)(2,1)} %collective-permute-done.10.b_ref, f32[2048,1024]{1,0:T(8,128)} %widen.2.refs_0_), custom_call_target="tpu_custom_call", output_to_operand_aliasing={{}: (3, {})} | custom-call | flops 1048576 | bytes 6291456 | tf_op jit(solution)/shard_map/widen/pallas_call | solution.py:275
  (49 shorter events, 6.4 us)
Async XLA Ops:
  0.6 8.0 %copy-start.6 = (s32[128,16]{0,1:T(8,128)S(1)}, s32[128,16]{0,1:T(8,128)}, u32[]{:S(2)}) copy-start(s32[128,16]{0,1:T(8,128)} %param.22) | copy-start | bytes 24580
  0.6 8.0 %copy-start.7 = (s32[128,16,1]{0,2,1:T(1,128)S(1)}, s32[128,16,1]{0,2,1:T(1,128)}, u32[]{:S(2)}) copy-start(s32[128,16,1]{0,2,1:T(1,128)} %param.21) | copy-start | bytes 24580
  0.7 8.0 %copy-start.8 = (s32[128,16]{0,1:T(8,128)S(1)}, s32[128,16]{0,1:T(8,128)}, u32[]{:S(2)}) copy-start(s32[128,16]{0,1:T(8,128)} %param.16) | copy-start | bytes 24580
  0.7 7.9 %copy-start.9 = (s32[128,16]{0,1:T(8,128)S(1)}, s32[128,16]{0,1:T(8,128)}, u32[]{:S(2)}) copy-start(s32[128,16]{0,1:T(8,128)} %param.18) | copy-start | bytes 24580
  0.7 7.9 %copy-start.10 = (s32[128,16,1]{0,2,1:T(1,128)S(1)}, s32[128,16,1]{0,2,1:T(1,128)}, u32[]{:S(2)}) copy-start(s32[128,16,1]{0,2,1:T(1,128)} %param.17) | copy-start | bytes 24580
  0.7 8.0 %copy-start.4 = (s32[128,16]{0,1:T(8,128)S(1)}, s32[128,16]{0,1:T(8,128)}, u32[]{:S(2)}) copy-start(s32[128,16]{0,1:T(8,128)} %param.20) | copy-start | bytes 24580
  0.7 8.0 %copy-start.5 = (s32[128,16,1]{0,2,1:T(1,128)S(1)}, s32[128,16,1]{0,2,1:T(1,128)}, u32[]{:S(2)}) copy-start(s32[128,16,1]{0,2,1:T(1,128)} %param.19) | copy-start | bytes 24580
  0.7 8.0 %copy-start.1 = (bf16[128,2048]{1,0:T(8,128)(2,1)S(1)}, bf16[128,2048]{1,0:T(8,128)(2,1)}, u32[]{:S(2)}) copy-start(bf16[128,2048]{1,0:T(8,128)(2,1)} %x_ref.2) | copy-start | bytes 1572868
  5.6 14.6 %copy-start.3 = (bf16[128,1024]{1,0:T(8,128)(2,1)S(1)}, bf16[128,1024]{1,0:T(8,128)(2,1)}, u32[]{:S(2)}) copy-start(bf16[128,1024]{1,0:T(8,128)(2,1)} %dpre.1.d0_ref) | copy-start | bytes 786436
  5.6 9.6 %collective-permute-start = (bf16[128,1024]{1,0:T(8,128)(2,1)}, bf16[128,1024]{1,0:T(8,128)(2,1)S(1)}, u32[]{:S(2)}, u32[]{:S(2)}) collective-permute-start(bf16[128,1024]{1,0:T(8,128)(2,1)} %dpre.1.d0_ref), channel_id=1, source_target_pairs={{0,2},{2,0},{4,6},{6,4},{1,3},{3,1},{5,7},{7,5},{8,10},{10,8},{12,... | collective-permute-start | bytes 786440 | tf_op jit(solution)/shard_map/ppermute | solution.py:245
  15.2 39.9 %all-to-all-start = ((bf16[4,128,640]{2,1,0:T(8,128)(2,1)}), bf16[4,128,640]{2,1,0:T(8,128)(2,1)S(1)}, u32[]{:S(2)}, u32[]{:S(2)}) async-start(bf16[4,128,640]{2,1,0:T(8,128)(2,1)} %cut.1), calls=%async_computation | async-start | bytes 1310720 | tf_op jit(solution)/shard_map/all_to_all | solution.py:356
  20.1 27.7 %collective-permute-start.1 = (bf16[128,1024]{1,0:T(8,128)(2,1)S(1)}, bf16[128,1024]{1,0:T(8,128)(2,1)S(1)}, u32[]{:S(2)}, u32[]{:S(2)}) collective-permute-start(bf16[128,1024]{1,0:T(8,128)(2,1)S(1)} %copy-done.3), channel_id=1, source_target_pairs={{0,4},{2,6},{4,0},{6,2},{1,5},{3,7},{5,1},{7,3},{8,12},{10,14},{12... | collective-permute-start | bytes 786440 | tf_op jit(solution)/shard_map/ppermute | solution.py:245
  47.8 7.3 %collective-permute-start.2 = (bf16[128,1024]{1,0:T(8,128)(2,1)S(1)}, bf16[128,1024]{1,0:T(8,128)(2,1)S(1)}, u32[]{:S(2)}, u32[]{:S(2)}) collective-permute-start(bf16[128,1024]{1,0:T(8,128)(2,1)S(1)} %collective-permute-done.1.d2_ref), channel_id=1, source_target_pairs={{0,2},{2,0},{4,6},{6,4},{1,3},{3,1},{5,7},{7,5},{8,10},{10,8},{12,... | collective-permute-start | bytes 786440 | tf_op jit(solution)/shard_map/ppermute | solution.py:245
  56.8 22.0 %all-to-all-start.1 = ((bf16[8,64,1024]{2,1,0:T(8,128)(2,1)}), bf16[8,64,1024]{2,1,0:T(8,128)(2,1)S(1)}, u32[]{:S(2)}, u32[]{:S(2)}) async-start(bf16[8,64,1024]{2,1,0:T(8,128)(2,1)} %w_part.1), calls=%async_computation.1 | async-start | bytes 2097152 | tf_op jit(solution)/shard_map/all_to_all | solution.py:386
  63.5 2.2 %copy-start = (bf16[2048,1024]{1,0:T(8,128)(2,1)S(1)}, bf16[2048,1024]{1,0:T(8,128)(2,1)}, u32[]{:S(2)}) copy-start(bf16[2048,1024]{1,0:T(8,128)(2,1)} %w_ref.3) | copy-start | bytes 12582916
  79.0 57.5 %all-to-all-start.2 = ((bf16[8,928,128]{2,1,0:T(8,128)(2,1)}), bf16[8,928,128]{2,1,0:T(8,128)(2,1)S(1)}, u32[]{:S(2)}, u32[]{:S(2)}) async-start(bf16[8,928,128]{2,1,0:T(8,128)(2,1)} %copy-done.2), calls=%async_computation.2 | async-start | bytes 3801088 | tf_op jit(solution)/shard_map/all_to_all | solution.py:402
  83.2 25.0 %collective-permute-start.3 = (bf16[64,512]{1,0:T(8,128)(2,1)S(1)}, bf16[64,512]{1,0:T(8,128)(2,1)S(1)}, u32[]{:S(2)}, u32[]{:S(2)}) collective-permute-start(bf16[64,512]{1,0:T(8,128)(2,1)S(1)} %get-tuple-element.53), channel_id=1, source_target_pairs={{0,1},{1,0},{2,3},{3,2},{4,5},{5,4},{6,7},{7,6},{8,9},{9,8},{10,11... | collective-permute-start | bytes 196616 | tf_op jit(solution)/shard_map/ppermute | solution.py:245
  85.3 23.0 %collective-permute-start.4 = (bf16[64,512]{1,0:T(8,128)(2,1)S(1)}, bf16[64,512]{1,0:T(8,128)(2,1)S(1)}, u32[]{:S(2)}, u32[]{:S(2)}) collective-permute-start(bf16[64,512]{1,0:T(8,128)(2,1)S(1)} %get-tuple-element.54), channel_id=1, source_target_pairs={{0,16},{16,0},{1,17},{17,1},{2,18},{18,2},{3,19},{19,3},{4,20},{20... | collective-permute-start | bytes 196616 | tf_op jit(solution)/shard_map/ppermute | solution.py:245
  108.3 14.1 %collective-permute-start.5 = (bf16[128,1024]{1,0:T(8,128)(2,1)S(1)}, bf16[128,1024]{1,0:T(8,128)(2,1)S(1)}, u32[]{:S(2)}, u32[]{:S(2)}) collective-permute-start(bf16[128,1024]{1,0:T(8,128)(2,1)S(1)} %maximum_maximum_fusion), channel_id=1, source_target_pairs={{0,4},{2,6},{4,0},{6,2},{1,5},{3,7},{5,1},{7,3},{8,12},{10,14},{12... | collective-permute-start | bytes 786440 | tf_op jit(solution)/shard_map/ppermute | solution.py:245
  122.5 13.9 %collective-permute-start.6 = (bf16[256,1024]{1,0:T(8,128)(2,1)S(1)}, bf16[256,1024]{1,0:T(8,128)(2,1)S(1)}, u32[]{:S(2)}, u32[]{:S(2)}) collective-permute-start(bf16[256,1024]{1,0:T(8,128)(2,1)S(1)} %pad_maximum_fusion.3), channel_id=1, source_target_pairs={{0,2},{2,0},{4,6},{6,4},{1,3},{3,1},{5,7},{7,5},{8,10},{10,8},{12,... | collective-permute-start | bytes 1572872 | tf_op jit(solution)/shard_map/ppermute | solution.py:245
  136.6 13.1 %collective-permute-start.9 = (bf16[512,512]{1,0:T(8,128)(2,1)S(1)}, bf16[512,512]{1,0:T(8,128)(2,1)S(1)}, u32[]{:S(2)}, u32[]{:S(2)}) collective-permute-start(bf16[512,512]{1,0:T(8,128)(2,1)S(1)} %get-tuple-element.51), channel_id=1, source_target_pairs={{0,1},{1,0},{2,3},{3,2},{4,5},{5,4},{6,7},{7,6},{8,9},{9,8},{10,11... | collective-permute-start | bytes 1572872 | tf_op jit(solution)/shard_map/ppermute | solution.py:245
  138.1 12.7 %collective-permute-start.7 = (bf16[512,512]{1,0:T(8,128)(2,1)S(1)}, bf16[512,512]{1,0:T(8,128)(2,1)S(1)}, u32[]{:S(2)}, u32[]{:S(2)}) collective-permute-start(bf16[512,512]{1,0:T(8,128)(2,1)S(1)} %get-tuple-element.52), channel_id=1, source_target_pairs={{0,16},{16,0},{1,17},{17,1},{2,18},{18,2},{3,19},{19,3},{4,20},{20... | collective-permute-start | bytes 1572872 | tf_op jit(solution)/shard_map/ppermute | solution.py:245
  150.9 3.5 %collective-permute-start.8 = (bf16[1024,512]{1,0:T(8,128)(2,1)S(1)}, bf16[1024,512]{1,0:T(8,128)(2,1)S(1)}, u32[]{:S(2)}, u32[]{:S(2)}) collective-permute-start(bf16[1024,512]{1,0:T(8,128)(2,1)S(1)} %pad_maximum_fusion.1.a_ref), channel_id=1, source_target_pairs={{0,8},{8,0},{1,9},{9,1},{2,10},{10,2},{3,11},{11,3},{4,12},{12,4},... | collective-permute-start | bytes 3145736 | tf_op jit(solution)/shard_map/ppermute | solution.py:245
  151.0 4.3 %collective-permute-start.10 = (bf16[1024,512]{1,0:T(8,128)(2,1)S(1)}, bf16[1024,512]{1,0:T(8,128)(2,1)}, u32[]{:S(2)}, u32[]{:S(2)}) collective-permute-start(bf16[1024,512]{1,0:T(8,128)(2,1)S(1)} %pad_maximum_fusion.2.b_ref), channel_id=1, source_target_pairs={{0,8},{8,0},{1,9},{9,1},{2,10},{10,2},{3,11},{11,3},{4,12},{12,4},... | collective-permute-start | bytes 3145736 | tf_op jit(solution)/shard_map/ppermute | solution.py:245
  (2 other events, 3.1 us)

commit v8 on v6

--- a/solution.py
+++ b/solution.py
@@ -50,9 +50,7 @@
     )
 
 
-def cut_kernel(n_dp, n_y, n_table, x_ref, q_ref, r_ref, a_ref, out_ref):
-    piece = x_ref.shape[1] // (n_dp * N_Z)
-    wide = n_dp * piece
+def codes_kernel(n_y, n_table, z_ref, q_ref, r_ref, a_ref, own_ref, near_ref, far_ref):
     y_bits, table_bits = n_y.bit_length() - 1, n_table.bit_length() - 1
 
     def in_plane(code, bits, z):
@@ -60,29 +58,50 @@
         here = (code >= 0) & (((dev & (n_table - 1)) >> y_bits) == z)
         return jnp.where(here, ((dev >> table_bits) << y_bits) + (dev & (n_y - 1)), -1)
 
-    for z in range(N_Z):
-        for d in range(n_dp):
-            at = (d * N_Z + z) * piece
-            out_ref[z, :, d * piece : (d + 1) * piece] = x_ref[:, at : at + piece]
+    for k in range(N_Z):
+        z = z_ref[0] ^ k
         codes = []
         for ref in (q_ref, r_ref):
             low = ref[...] & (QROWS_DEV - 1)
             codes += [in_plane(ref[...], LOG_QROWS, z), low >> 8, low & 255]
         codes += [in_plane(a_ref[...], LOG_ADM, z), a_ref[...] & (ADM_DEV - 1)]
         block = jnp.concatenate(codes, axis=0).astype(F32).astype(BF)
-        out_ref[z, :, wide : wide + block.shape[1]] = block
-
-
-def dpre_kernel(x_ref, w_ref, b_ref, g_ref, out_ref):
-    pre = dot(x_ref[...], w_ref[...]) + b_ref[...]
-    sig = jax.nn.sigmoid(pre)
-    dpre = (g_ref[...].astype(F32) * sig * (1.0 + pre * (1.0 - sig))).astype(BF)
-    out_ref[...] = dpre
-
-
-def slots_kernel(n_dest, cap, wide, z_ref, in_ref, slot_ref, labels_ref, group_ref):
-    n_s = in_ref.shape[1]
-    n_feat = n_s // N_CODE
+        if k < 2:
+            (own_ref, near_ref)[k][...] = block
+        else:
+            far_ref[k - 2] = block
+
+
+def cut_kernel(n_dp, x_ref, out_ref):
+    piece = x_ref.shape[1] // (n_dp * N_Z)
+    for z in range(N_Z):
+        for d in range(n_dp):
+            at = (d * N_Z + z) * piece
+            out_ref[z, :, d * piece : (d + 1) * piece] = x_ref[:, at : at + piece]
+
+
+def dpre_kernel(x_ref, w_ref, b_ref, g_ref, out_ref, acc_ref):
+    step = pl.program_id(0)
+    part = dot(x_ref[...], w_ref[...])
+
+    @pl.when(step == 0)
+    def _():
+        acc_ref[...] = part
+
+    @pl.when(step > 0)
+    def _():
+        acc_ref[...] += part
+
+    @pl.when(step == pl.num_programs(0) - 1)
+    def _():
+        pre = acc_ref[...] + b_ref[...]
+        sig = jax.nn.sigmoid(pre)
+        out_ref[...] = (g_ref[...].astype(F32) * sig * (1.0 + pre * (1.0 - sig))).astype(BF)
+
+
+def slots_kernel(n_dest, cap, own_ref, near_ref, far_ref, last_ref, slot_ref, labels_ref, group_ref):
+    n_s = own_ref.shape[1]
+    n_feat = own_ref.shape[0] // N_CODE
     sample = iota((n_s, n_s), 0)
     earlier = (sample < iota((n_s, n_s), 1)).astype(F32).astype(BF)
     ones = jnp.ones((n_s, n_s), BF)
@@ -93,7 +112,7 @@
     half = n_dest // 2
     lane = iota((n_s, E), 1) & 3
     for z in range(N_Z):
-        codes = in_ref[z_ref[0] ^ z, :, wide : wide + n_s].astype(F32)
+        codes = (own_ref[...], near_ref[...], far_ref[0], last_ref[...])[z].astype(F32)
         plane = [codes[i * n_feat : (i + 1) * n_feat, :] for i in range(N_CODE)]
         for table in range(2):
             dest = plane[table * 3]
@@ -118,7 +137,7 @@
 
 
 def w_kernel(n_plane, z_ref, x_ref, d0_ref, d1_ref, d2_ref, d3_ref, out_ref):
-    wide = x_ref.shape[2] - E
+    wide = x_ref.shape[2]
     share = wide // n_plane
     x = jnp.concatenate([x_ref[z_ref[0] ^ z, :, 0:wide] for z in range(N_Z)], axis=0)
     d = jnp.concatenate([ref[...] for ref in (d0_ref, d1_ref, d2_ref, d3_ref)], axis=0)
@@ -316,44 +335,67 @@
     scalar = pl.BlockSpec(memory_space=pltpu.SMEM)
     array = pl.BlockSpec(memory_space=pltpu.VMEM)
 
-    block = min(256, hidden)
+    admit, owner, adm_row, q_shard, q_local, r_shard, r_local = [
+        a.reshape(n_s, n_feat).T for a in (admit, owner, adm_row, q_shard, q_local, r_shard, r_local)
+    ]
+    n_code = N_CODE * n_feat
+    own_codes, near_codes, far_codes = call(
+        functools.partial(codes_kernel, n_y, n_table),
+        "codes",
+        (shape((n_code, n_s), BF), shape((n_code, n_s), BF), shape((2, n_code, n_s), BF)),
+        10**6,
+        2 * 10**5,
+        in_specs=[scalar] + [array] * 3,
+    )(
+        my_z,
+        jnp.where(admit == 0, q_shard * QROWS_DEV + q_local, -1),
+        jnp.where(admit == 0, r_shard * QROWS_DEV + r_local, -1),
+        jnp.where(admit == 1, owner * (ADM_DEV * n_table) + adm_row, -1),
+    )
+    far_codes = swap(far_codes, "tz", 2)
+    near_codes = swap(near_codes, "tz", 1)
+    last_codes = swap(after(far_codes[1], near_codes), "tz", 1)
+
+    block = width // 4
     dpre = call(
         dpre_kernel,
         "dpre",
         shape((n_s, hidden), BF),
         2 * n_s * width * hidden,
         6 * 10**6,
-        grid=(hidden // block,),
+        grid=(width // block,),
         in_specs=[
-            pl.BlockSpec((n_s, width), lambda i: (0, 0)),
-            pl.BlockSpec((width, block), lambda i: (0, i)),
-            pl.BlockSpec((1, block), lambda i: (0, i)),
             pl.BlockSpec((n_s, block), lambda i: (0, i)),
+            pl.BlockSpec((block, hidden), lambda i: (i, 0)),
+            pl.BlockSpec((1, hidden), lambda i: (0, 0)),
+            pl.BlockSpec((n_s, hidden), lambda i: (0, 0)),
         ],
-        out_specs=pl.BlockSpec((n_s, block), lambda i: (0, i)),
-    )(features, w_first, b_first.reshape(1, hidden), grad_out)
+        out_specs=pl.BlockSpec((n_s, hidden), lambda i: (0, 0)),
+        scratch_shapes=[pltpu.VMEM((n_s, hidden), F32)],
+        vmem=56,
+    )(after(features, own_codes), w_first, b_first.reshape(1, hidden), grad_out)
 
     far = swap(dpre, "tz", 2)
     near = swap(dpre, "tz", 1)
     far = after(far, near)
     sources = [dpre, near, far, swap(far, "tz", 1)]
-    admit, owner, adm_row, q_shard, q_local, r_shard, r_local = [
-        a.reshape(n_s, n_feat).T for a in (admit, owner, adm_row, q_shard, q_local, r_shard, r_local)
-    ]
+
     cut = call(
-        functools.partial(cut_kernel, n_dp, n_y, n_table),
-        "cut",
-        shape((N_Z, n_s, wide + E), BF),
-        10**7,
-        2 * 10**6,
-    )(
-        after(features, dpre),
-        jnp.where(admit == 0, q_shard * QROWS_DEV + q_local, -1),
-        jnp.where(admit == 0, r_shard * QROWS_DEV + r_local, -1),
-        jnp.where(admit == 1, owner * (ADM_DEV * n_table) + adm_row, -1),
-    )
-    feat_in = lax.all_to_all(cut, "tz", split_axis=0, concat_axis=0, tiled=True)
-
+        functools.partial(cut_kernel, n_dp), "cut", shape((N_Z, n_s, wide), BF), 10**6, 2 * 10**6
+    )(after(features, dpre))
+    feat_in = lax.all_to_all(after(cut, far), "tz", split_axis=0, concat_axis=0, tiled=True)
+
+    slots, labels, group = call(
+        functools.partial(slots_kernel, n_plane, cap),
+        "slots",
+        (
+            shape((3, N_Z, n_feat, n_s), jnp.int32),
+            shape((N_Z, count, E), BF),
+            shape((N_Z, n_s, n_feat), F32),
+        ),
+        10**9,
+        3 * 10**6,
+    )(own_codes, near_codes, far_codes, last_codes)
     look, bias = call(
         lookup_kernel,
         "lookups",
@@ -362,7 +404,7 @@
         7 * 10**6,
         scratch_shapes=[pltpu.VMEM((N_Z * n_s, hidden), BF)],
     )(*sources, w_first)
-    feat_in = after(feat_in, look)
+    feat_in = after(feat_in, look, slots)
 
     w_part = call(
         functools.partial(w_kernel, n_plane),
@@ -372,18 +414,7 @@
         3 * 10**6,
         in_specs=[scalar] + [array] * 5,
     )(my_z, feat_in, *sources)
-    slots, labels, group = call(
-        functools.partial(slots_kernel, n_plane, cap, wide),
-        "slots",
-        (
-            shape((3, N_Z, n_feat, n_s), jnp.int32),
-            shape((N_Z, count, E), BF),
-            shape((N_Z, n_s, n_feat), F32),
-        ),
-        10**9,
-        3 * 10**6,
-        in_specs=[scalar, array],
-    )(my_z, after(feat_in, w_part))
+    look = after(look, w_part)
     w_part = lax.all_to_all(w_part, plane, split_axis=0, concat_axis=0, tiled=True)
 
     n_rows = 2 * seg + ADM_DEV + 16 + 2 * n_bias
@@ -394,12 +425,11 @@
         15 * 10**9,
         4 * 10**7,
         scratch_shapes=[pltpu.VMEM((2, n_plane, seg, E), F32)],
-        vmem=36,
+        vmem=28,
     )(look, slots, labels, group, bias)
 
     w_part = after(w_part, chunks)
     w_own = jnp.sum(w_part.astype(F32), axis=0).astype(BF)
-    w_own, chunks = lax.optimization_barrier((w_own, chunks))
     chunks = lax.all_to_all(chunks, plane, split_axis=0, concat_axis=0, tiled=True)
 
     w_two = jnp.concatenate([w_own, swap(w_own, "tz", 2)], axis=0)

time: 135 us -> 134 us (level)
  waiting for transfers between devices: 63.6 us -> 51.9 us
  starting transfers between devices: 23 us -> 30.5 us
  Pallas kernels: 36.6 us -> 39.3 us
  other arithmetic: 0.53 us -> 2.91 us
  local copies, waits for them, and re-layouts: 9.7 us -> 7.73 us
    ppermute x11 -> x14, waiting for transfers between devices: 56.8 us -> 44.5 us  [swap(): return lax.ppermute(x, axis, [(i, i ^ k) for i in range(n)])]
    ppermute x11 -> x14, starting transfers between devices: 9.08 us -> 19.1 us  [swap(): return lax.ppermute(x, axis, [(i, i ^ k) for i in range(n)])]
    pallas_call x1, Pallas kernels: 2.03 us -> 4.8 us  [local(): call(dpre_kernel, 'dpre', shape((n_s, hidden), BF), 2 * n_s * width * hid...]
    all_to_all x1, starting transfers between devices: 6.31 us -> 3.72 us  [local(): lax.all_to_all(after(cut, far), 'tz', split_axis=0, concat_axis=0, tiled=...]
    unnamed x32 -> x20, local copies, waits for them, and re-layouts: 9.66 us -> 7.69 us
    all_to_all x1, waiting for transfers between devices: 0.81 us -> 2.22 us  [local(): lax.all_to_all(w_part, plane, split_axis=0, concat_axis=0, tiled=True)]
    pallas_call x2 -> x3, Pallas kernels: 3.94 us -> 3.88 us  [the longest x1 2.97 us: local(): call(functools.partial(slots_kernel, n_plane, cap), 'slots', (shape((3, N...]
  transfers between devices with their start and end apart: 14 -> 17, of which waited for: 10 -> 12; matrix products, arithmetic and copies ran while one was open for 0% -> 1% of each run, Pallas kernels for 21% -> 22%
where the time goes in v8:
time: 134 us; the launch traced here: 133 us
  waiting for transfers between devices  51.9 us (39%)
  Pallas kernels  39.3 us (29%)
  starting transfers between devices  30.5 us (23%)
  local copies, waits for them, and re-layouts  7.73 us (6%)
  other arithmetic  2.91 us (2%)
    ppermute x14, waiting for transfers between devices, swap(): return lax.ppermute(x, axis, [(i, i ^ k) for i in range(n)])  44.5 us
    ppermute x14, starting transfers between devices, swap(): return lax.ppermute(x, axis, [(i, i ^ k) for i in range(n)])  19.1 us
    pallas_call x2, Pallas kernels, sums(): call(functools.partial(sums_kernel, n_plane, seg, n_bias, table), ('q_sum...  10.8 us
    pallas_call x1, Pallas kernels, local(): call(functools.partial(bucket_kernel, n_plane, cap), 'buckets', shape((n_...  9.44 us
    unnamed x20, local copies, waits for them, and re-layouts  7.69 us
    pallas_call x2, Pallas kernels, widen(): call(functools.partial(widen_kernel, n_x, n_y, share), 'widen', jax.Shape...  6.32 us
    all_to_all x1, waiting for transfers between devices, local(): lax.all_to_all(chunks, plane, split_axis=0, concat_axis=0, tiled=True)  5.21 us
    pallas_call x1, Pallas kernels, local(): call(dpre_kernel, 'dpre', shape((n_s, hidden), BF), 2 * n_s * width * hid...  4.8 us
  transfers between devices with their start and end apart: 17, of which 12 were waited for; matrix products, arithmetic and copies ran while one was open for 1% of the time, Pallas kernels for 22%

profile of v8, /device:TPU:0, one launch (start us, length us, event | category | flops | bytes accessed | tf_op | source)
XLA Modules:
  0.0 133.4 jit_solution(6165307851133116907)
XLA Ops:
  2.2 4.8 %dpre.1.d0_ref = bf16[128,1024]{1,0:T(8,128)(2,1)} custom-call(bf16[128,2048]{1,0:T(8,128)(2,1)} %x_ref.1, bf16[2048,1024]{1,0:T(8,128)(2,1)} %w_ref.3, f32[1,1024]{1,0:T(1,128)} %bitcast.38, bf16[128,1024]{1,0:T(8,128)(2,1)} %g_ref.1), custom_call_target="tpu_custom_call" | custom-call | flops 536870912 | bytes 6000000 | tf_op jit(solution)/shard_map/dpre/pallas_call | solution.py:360
  7.0 3.0 %collective-permute-start.1 = (bf16[128,1024]{1,0:T(8,128)(2,1)}, bf16[128,1024]{1,0:T(8,128)(2,1)S(1)}, u32[]{:S(2)}, u32[]{:S(2)}) collective-permute-start(bf16[128,1024]{1,0:T(8,128)(2,1)} %dpre.1.d0_ref), channel_id=1, source_target_pairs={{0,2},{2,0},{4,6},{6,4},{1,3},{3,1},{5,7},{7,5},{8,10},{10,8},{12,... | collective-permute-start | bytes 786440 | tf_op jit(solution)/shard_map/ppermute | solution.py:264
  10.0 2.6 %collective-permute-start = (bf16[128,1024]{1,0:T(8,128)(2,1)}, bf16[128,1024]{1,0:T(8,128)(2,1)S(1)}, u32[]{:S(2)}, u32[]{:S(2)}) collective-permute-start(bf16[128,1024]{1,0:T(8,128)(2,1)} %dpre.1.d0_ref), channel_id=1, source_target_pairs={{0,4},{2,6},{4,0},{6,2},{1,5},{3,7},{5,1},{7,3},{8,12},{10,14},{12... | collective-permute-start | bytes 786440 | tf_op jit(solution)/shard_map/ppermute | solution.py:264
  13.5 8.5 %collective-permute-done.1.d1_ref = bf16[128,1024]{1,0:T(8,128)(2,1)S(1)} collective-permute-done((bf16[128,1024]{1,0:T(8,128)(2,1)}, bf16[128,1024]{1,0:T(8,128)(2,1)S(1)}, u32[]{:S(2)}, u32[]{:S(2)}) %collective-permute-start.1) | collective-permute-done | bytes 262176 | tf_op jit(solution)/shard_map/ppermute | solution.py:264
  22.0 2.6 %collective-permute-done.d2_ref = bf16[128,1024]{1,0:T(8,128)(2,1)S(1)} collective-permute-done((bf16[128,1024]{1,0:T(8,128)(2,1)}, bf16[128,1024]{1,0:T(8,128)(2,1)S(1)}, u32[]{:S(2)}, u32[]{:S(2)}) %collective-permute-start) | collective-permute-done | bytes 262176 | tf_op jit(solution)/shard_map/ppermute | solution.py:264
  24.5 3.7 %all-to-all-start = ((bf16[4,128,512]{2,1,0:T(8,128)(2,1)}), bf16[4,128,512]{2,1,0:T(8,128)(2,1)S(1)}, u32[]{:S(2)}, u32[]{:S(2)}) async-start(bf16[4,128,512]{2,1,0:T(8,128)(2,1)} %cut.1), calls=%async_computation | async-start | bytes 1048576 | tf_op jit(solution)/shard_map/all_to_all | solution.py:386
  28.3 2.9 %collective-permute-start.4 = (bf16[2,128,128]{2,1,0:T(8,128)(2,1)S(1)}, bf16[2,128,128]{2,1,0:T(8,128)(2,1)S(1)}, u32[]{:S(2)}, u32[]{:S(2)}) collective-permute-start(bf16[2,128,128]{2,1,0:T(8,128)(2,1)S(1)} %get-tuple-element.40), channel_id=1, source_target_pairs={{0,4},{2,6},{4,0},{6,2},{1,5},{3,7},{5,1},{7,3},{8,12},{10,14},{12... | collective-permute-start | bytes 196616 | tf_op jit(solution)/shard_map/ppermute | solution.py:264
  33.2 8.2 %collective-permute-done.4.far_ref = bf16[2,128,128]{2,1,0:T(8,128)(2,1)S(1)} collective-permute-done((bf16[2,128,128]{2,1,0:T(8,128)(2,1)S(1)}, bf16[2,128,128]{2,1,0:T(8,128)(2,1)S(1)}, u32[]{:S(2)}, u32[]{:S(2)}) %collective-permute-start.4) | collective-permute-done | bytes 65568 | tf_op jit(solution)/shard_map/ppermute | solution.py:264
  43.2 2.2 %collective-permute-done.5.last_ref = bf16[128,128]{1,0:T(8,128)(2,1)S(1)} collective-permute-done((bf16[128,128]{1,0:T(8,128)(2,1)S(1)}, bf16[128,128]{1,0:T(8,128)(2,1)S(1)}, u32[]{:S(2)}, u32[]{:S(2)}) %collective-permute-start.5) | collective-permute-done | bytes 32800 | tf_op jit(solution)/shard_map/ppermute | solution.py:264
  45.4 3.0 %slots.1 = (s32[3,4,16,128]{3,2,1,0:T(8,128)S(1)}, bf16[4,2048,128]{2,1,0:T(8,128)(2,1)S(1)}, f32[4,128,16]{2,1,0:T(8,128)S(1)}) custom-call(bf16[128,128]{1,0:T(8,128)(2,1)S(1)} %get-tuple-element.33.own_ref, bf16[128,128]{1,0:T(8,128)(2,1)S(1)} %collective-permute-done.3.near_ref, bf16[2,128,128]{2,1,0:T(8,128)(2,1)S(1)} %collective-permute-done.4.far_ref, ...), custom_call_target="tpu_custom_call" | custom-call | flops 1000000000 | bytes 3000000 | tf_op jit(solution)/shard_map/slots/pallas_call | solution.py:388
  49.7 2.2 %copy-done = bf16[2048,1024]{1,0:T(8,128)(2,1)S(1)} copy-done((bf16[2048,1024]{1,0:T(8,128)(2,1)S(1)}, bf16[2048,1024]{1,0:T(8,128)(2,1)}, u32[]{:S(2)}) %copy-start) | copy-done | bytes 4194328
  51.9 2.4 %lookups.1 = (bf16[4,2048,128]{2,1,0:T(8,128)(2,1)S(1)}, bf16[16,128]{1,0:T(8,128)(2,1)S(1)}) custom-call(bf16[128,1024]{1,0:T(8,128)(2,1)S(1)} %copy-done.3, bf16[128,1024]{1,0:T(8,128)(2,1)S(1)} %collective-permute-done.1.d1_ref, bf16[128,1024]{1,0:T(8,128)(2,1)S(1)} %collective-permute-done.d2_ref, bf16[128,1024]{1,0:T(8,128)(2,1)S(1)} %collective-permute-done.2.d3_ref, ...), custom_call_target="tpu_custom_call" | custom-call | flops 2147483648 | bytes 7000000 | tf_op jit(solution)/shard_map/lookups/pallas_call | solution.py:399
  57.3 3.9 %all-to-all-start.1 = ((bf16[8,64,1024]{2,1,0:T(8,128)(2,1)}), bf16[8,64,1024]{2,1,0:T(8,128)(2,1)S(1)}, u32[]{:S(2)}, u32[]{:S(2)}) async-start(bf16[8,64,1024]{2,1,0:T(8,128)(2,1)} %w_part.1), calls=%async_computation.1 | async-start | bytes 2097152 | tf_op jit(solution)/shard_map/all_to_all | solution.py:418
  62.8 9.4 %buckets.1 = bf16[8,928,128]{2,1,0:T(8,128)(2,1)S(1)} custom-call(bf16[4,2048,128]{2,1,0:T(8,128)(2,1)S(1)} %copy-done.5, s32[3,4,16,128]{3,2,1,0:T(8,128)S(1)} %get-tuple-element.42.slot_ref, bf16[4,2048,128]{2,1,0:T(8,128)(2,1)S(1)} %copy-done.7, f32[4,128,16]{2,1,0:T(8,128)S(1)} %get-tuple-element.46.group_ref, bf16[16,128]{1,0:T(8,128)(2,1)S(1)} %get-tuple-element.47.bias_ref), custom_call_target="tpu_custom_call" | custom-call | flops 15000000512 | bytes 40000000 | tf_op jit(solution)/shard_map/buckets/pallas_call | solution.py:421
  73.5 2.2 %all-to-all-done.1 = bf16[8,64,1024]{2,1,0:T(8,128)(2,1)S(1)} async-done(((bf16[8,64,1024]{2,1,0:T(8,128)(2,1)}), bf16[8,64,1024]{2,1,0:T(8,128)(2,1)S(1)}, u32[]{:S(2)}, u32[]{:S(2)}) %all-to-all-start.1) | async-done | bytes 1048608 | tf_op jit(solution)/shard_map/all_to_all | solution.py:418
  75.7 3.8 %all-to-all-start.2 = ((bf16[8,928,128]{2,1,0:T(8,128)(2,1)}), bf16[8,928,128]{2,1,0:T(8,128)(2,1)S(1)}, u32[]{:S(2)}, u32[]{:S(2)}) async-start(bf16[8,928,128]{2,1,0:T(8,128)(2,1)} %copy-done.2), calls=%async_computation.2 | async-start | bytes 3801088 | tf_op jit(solution)/shard_map/all_to_all | solution.py:433
  81.8 7.3 %collective-permute-done.6 = bf16[64,1024]{1,0:T(8,128)(2,1)S(1)} collective-permute-done((bf16[64,1024]{1,0:T(8,128)(2,1)S(1)}, bf16[64,1024]{1,0:T(8,128)(2,1)S(1)}, u32[]{:S(2)}, u32[]{:S(2)}) %collective-permute-start.6) | collective-permute-done | bytes 131104 | tf_op jit(solution)/shard_map/ppermute | solution.py:264
  89.3 7.5 %collective-permute-done.7 = bf16[128,1024]{1,0:T(8,128)(2,1)S(1)} collective-permute-done((bf16[128,1024]{1,0:T(8,128)(2,1)S(1)}, bf16[128,1024]{1,0:T(8,128)(2,1)S(1)}, u32[]{:S(2)}, u32[]{:S(2)}) %collective-permute-start.7) | collective-permute-done | bytes 262176 | tf_op jit(solution)/shard_map/ppermute | solution.py:264
  97.7 5.2 %all-to-all-done.2.in_ref = bf16[8,928,128]{2,1,0:T(8,128)(2,1)S(1)} async-done(((bf16[8,928,128]{2,1,0:T(8,128)(2,1)}), bf16[8,928,128]{2,1,0:T(8,128)(2,1)S(1)}, u32[]{:S(2)}, u32[]{:S(2)}) %all-to-all-start.2) | async-done | bytes 1900576 | tf_op jit(solution)/shard_map/all_to_all | solution.py:433
  105.0 5.4 %q_sums.1 = (f32[4096,128]{1,0:T(8,128)}, f32[8,128]{1,0:T(8,128)}, f32[128,128]{1,0:T(8,128)}) custom-call(bf16[8,928,128]{2,1,0:T(8,128)(2,1)S(1)} %all-to-all-done.2.in_ref), custom_call_target="tpu_custom_call" | custom-call | flops 4000000000 | bytes 4000000 | tf_op jit(solution)/shard_map/q_sums/pallas_call | solution.py:445
  113.2 5.4 %r_sums.1 = f32[4096,128]{1,0:T(8,128)} custom-call(bf16[8,928,128]{2,1,0:T(8,128)(2,1)S(1)} %all-to-all-done.2.in_ref), custom_call_target="tpu_custom_call" | custom-call | flops 4000000000 | bytes 4000000 | tf_op jit(solution)/shard_map/r_sums/pallas_call | solution.py:445
  118.6 5.7 %collective-permute-done.12 = bf16[512,512]{1,0:T(8,128)(2,1)S(1)} collective-permute-done((bf16[512,512]{1,0:T(8,128)(2,1)S(1)}, bf16[512,512]{1,0:T(8,128)(2,1)S(1)}, u32[]{:S(2)}, u32[]{:S(2)}) %collective-permute-start.12) | collective-permute-done | bytes 524320 | tf_op jit(solution)/shard_map/ppermute | solution.py:264
  126.0 2.8 %widen.2.refs_0_ = f32[2048,1024]{1,0:T(8,128)} custom-call(s32[4]{0:T(128)S(1)} %get-tuple-element.64.at_ref, bf16[1024,512]{1,0:T(8,128)(2,1)S(1)} %pad_maximum_fusion.a_ref, bf16[1024,512]{1,0:T(8,128)(2,1)S(1)} %pad_maximum_fusion.1.b_ref), custom_call_target="tpu_custom_call" | custom-call | flops 1048576 | bytes 6291456 | tf_op jit(solution)/shard_map/widen/pallas_call | solution.py:294
  129.7 3.5 %widen.3 = f32[2048,1024]{1,0:T(8,128)} custom-call(s32[4]{0:T(128)S(1)} %get-tuple-element.63.at_ref, bf16[1024,512]{1,0:T(8,128)(2,1)S(1)} %collective-permute-done.11.a_ref, bf16[1024,512]{1,0:T(8,128)(2,1)} %collective-permute-done.13.b_ref, f32[2048,1024]{1,0:T(8,128)} %widen.2.refs_0_), custom_call_target="tpu_custom_call", output_to_operand_aliasing={{}: (3, {})} | custom-call | flops 1048576 | bytes 6291456 | tf_op jit(solution)/shard_map/widen/pallas_call | solution.py:294
  (53 shorter events, 24.2 us)
Async XLA Ops:
  2.2 10.4 %copy-start.1 = (bf16[128,2048]{1,0:T(8,128)(2,1)S(1)}, bf16[128,2048]{1,0:T(8,128)(2,1)}, u32[]{:S(2)}) copy-start(bf16[128,2048]{1,0:T(8,128)(2,1)} %x_ref.1) | copy-start | bytes 1572868
  7.0 15.0 %collective-permute-start.1 = (bf16[128,1024]{1,0:T(8,128)(2,1)}, bf16[128,1024]{1,0:T(8,128)(2,1)S(1)}, u32[]{:S(2)}, u32[]{:S(2)}) collective-permute-start(bf16[128,1024]{1,0:T(8,128)(2,1)} %dpre.1.d0_ref), channel_id=1, source_target_pairs={{0,2},{2,0},{4,6},{6,4},{1,3},{3,1},{5,7},{7,5},{8,10},{10,8},{12,... | collective-permute-start | bytes 786440 | tf_op jit(solution)/shard_map/ppermute | solution.py:264
  10.0 14.6 %collective-permute-start = (bf16[128,1024]{1,0:T(8,128)(2,1)}, bf16[128,1024]{1,0:T(8,128)(2,1)S(1)}, u32[]{:S(2)}, u32[]{:S(2)}) collective-permute-start(bf16[128,1024]{1,0:T(8,128)(2,1)} %dpre.1.d0_ref), channel_id=1, source_target_pairs={{0,4},{2,6},{4,0},{6,2},{1,5},{3,7},{5,1},{7,3},{8,12},{10,14},{12... | collective-permute-start | bytes 786440 | tf_op jit(solution)/shard_map/ppermute | solution.py:264
  24.5 31.0 %all-to-all-start = ((bf16[4,128,512]{2,1,0:T(8,128)(2,1)}), bf16[4,128,512]{2,1,0:T(8,128)(2,1)S(1)}, u32[]{:S(2)}, u32[]{:S(2)}) async-start(bf16[4,128,512]{2,1,0:T(8,128)(2,1)} %cut.1), calls=%async_computation | async-start | bytes 1048576 | tf_op jit(solution)/shard_map/all_to_all | solution.py:386
  28.3 21.4 %copy-start.3 = (bf16[128,1024]{1,0:T(8,128)(2,1)S(1)}, bf16[128,1024]{1,0:T(8,128)(2,1)}, u32[]{:S(2)}) copy-start(bf16[128,1024]{1,0:T(8,128)(2,1)} %dpre.1.d0_ref) | copy-start | bytes 786436
  28.3 13.2 %collective-permute-start.4 = (bf16[2,128,128]{2,1,0:T(8,128)(2,1)S(1)}, bf16[2,128,128]{2,1,0:T(8,128)(2,1)S(1)}, u32[]{:S(2)}, u32[]{:S(2)}) collective-permute-start(bf16[2,128,128]{2,1,0:T(8,128)(2,1)S(1)} %get-tuple-element.40), channel_id=1, source_target_pairs={{0,4},{2,6},{4,0},{6,2},{1,5},{3,7},{5,1},{7,3},{8,12},{10,14},{12... | collective-permute-start | bytes 196616 | tf_op jit(solution)/shard_map/ppermute | solution.py:264
  31.2 10.3 %collective-permute-start.3 = (bf16[128,128]{1,0:T(8,128)(2,1)S(1)}, bf16[128,128]{1,0:T(8,128)(2,1)S(1)}, u32[]{:S(2)}, u32[]{:S(2)}) collective-permute-start(bf16[128,128]{1,0:T(8,128)(2,1)S(1)} %get-tuple-element.39), channel_id=1, source_target_pairs={{0,2},{2,0},{4,6},{6,4},{1,3},{3,1},{5,7},{7,5},{8,10},{10,8},{12,... | collective-permute-start | bytes 98312 | tf_op jit(solution)/shard_map/ppermute | solution.py:264
  32.7 17.0 %collective-permute-start.2 = (bf16[128,1024]{1,0:T(8,128)(2,1)S(1)}, bf16[128,1024]{1,0:T(8,128)(2,1)S(1)}, u32[]{:S(2)}, u32[]{:S(2)}) collective-permute-start(bf16[128,1024]{1,0:T(8,128)(2,1)S(1)} %collective-permute-done.d2_ref), channel_id=1, source_target_pairs={{0,2},{2,0},{4,6},{6,4},{1,3},{3,1},{5,7},{7,5},{8,10},{10,8},{12,... | collective-permute-start | bytes 786440 | tf_op jit(solution)/shard_map/ppermute | solution.py:264
  41.5 3.9 %collective-permute-start.5 = (bf16[128,128]{1,0:T(8,128)(2,1)S(1)}, bf16[128,128]{1,0:T(8,128)(2,1)S(1)}, u32[]{:S(2)}, u32[]{:S(2)}) collective-permute-start(bf16[128,128]{1,0:T(8,128)(2,1)S(1)} %slice_bitcast_fusion), channel_id=1, source_target_pairs={{0,2},{2,0},{4,6},{6,4},{1,3},{3,1},{5,7},{7,5},{8,10},{10,8},{12,... | collective-permute-start | bytes 98312 | tf_op jit(solution)/shard_map/ppermute | solution.py:264
  49.7 2.2 %copy-start = (bf16[2048,1024]{1,0:T(8,128)(2,1)S(1)}, bf16[2048,1024]{1,0:T(8,128)(2,1)}, u32[]{:S(2)}) copy-start(bf16[2048,1024]{1,0:T(8,128)(2,1)} %w_ref.3) | copy-start | bytes 12582916
  57.3 3.9 %copy-start.5 = (bf16[4,2048,128]{2,1,0:T(8,128)(2,1)S(1)}, bf16[4,2048,128]{2,1,0:T(8,128)(2,1)}, u32[]{:S(2)}) copy-start(bf16[4,2048,128]{2,1,0:T(8,128)(2,1)} %copy-done.4) | copy-start | bytes 6291460
  57.3 18.4 %all-to-all-start.1 = ((bf16[8,64,1024]{2,1,0:T(8,128)(2,1)}), bf16[8,64,1024]{2,1,0:T(8,128)(2,1)S(1)}, u32[]{:S(2)}, u32[]{:S(2)}) async-start(bf16[8,64,1024]{2,1,0:T(8,128)(2,1)} %w_part.1), calls=%async_computation.1 | async-start | bytes 2097152 | tf_op jit(solution)/shard_map/all_to_all | solution.py:418
  61.2 1.6 %copy-start.7 = (bf16[4,2048,128]{2,1,0:T(8,128)(2,1)S(1)}, bf16[4,2048,128]{2,1,0:T(8,128)(2,1)}, u32[]{:S(2)}) copy-start(bf16[4,2048,128]{2,1,0:T(8,128)(2,1)} %copy-done.6) | copy-start | bytes 6291460
  75.7 27.2 %all-to-all-start.2 = ((bf16[8,928,128]{2,1,0:T(8,128)(2,1)}), bf16[8,928,128]{2,1,0:T(8,128)(2,1)S(1)}, u32[]{:S(2)}, u32[]{:S(2)}) async-start(bf16[8,928,128]{2,1,0:T(8,128)(2,1)} %copy-done.2), calls=%async_computation.2 | async-start | bytes 3801088 | tf_op jit(solution)/shard_map/all_to_all | solution.py:433
  79.7 9.6 %copy-start.8 = (bf16[64,1024]{1,0:T(8,128)(2,1)}, bf16[64,1024]{1,0:T(8,128)(2,1)S(1)}, u32[]{:S(2)}) copy-start(bf16[64,1024]{1,0:T(8,128)(2,1)S(1)} %reduce_sum.12) | copy-start | bytes 393220
  79.7 9.4 %collective-permute-start.6 = (bf16[64,1024]{1,0:T(8,128)(2,1)S(1)}, bf16[64,1024]{1,0:T(8,128)(2,1)S(1)}, u32[]{:S(2)}, u32[]{:S(2)}) collective-permute-start(bf16[64,1024]{1,0:T(8,128)(2,1)S(1)} %reduce_sum.12), channel_id=1, source_target_pairs={{0,4},{2,6},{4,0},{6,2},{1,5},{3,7},{5,1},{7,3},{8,12},{10,14},{12... | collective-permute-start | bytes 393224 | tf_op jit(solution)/shard_map/ppermute | solution.py:264
  89.1 7.6 %collective-permute-start.7 = (bf16[128,1024]{1,0:T(8,128)(2,1)S(1)}, bf16[128,1024]{1,0:T(8,128)(2,1)S(1)}, u32[]{:S(2)}, u32[]{:S(2)}) collective-permute-start(bf16[128,1024]{1,0:T(8,128)(2,1)S(1)} %pad_maximum_fusion.5), channel_id=1, source_target_pairs={{0,2},{2,0},{4,6},{6,4},{1,3},{3,1},{5,7},{7,5},{8,10},{10,8},{12,... | collective-permute-start | bytes 786440 | tf_op jit(solution)/shard_map/ppermute | solution.py:264
  102.9 8.3 %collective-permute-start.10 = (bf16[256,512]{1,0:T(8,128)(2,1)S(1)}, bf16[256,512]{1,0:T(8,128)(2,1)S(1)}, u32[]{:S(2)}, u32[]{:S(2)}) collective-permute-start(bf16[256,512]{1,0:T(8,128)(2,1)S(1)} %get-tuple-element.65), channel_id=1, source_target_pairs={{0,16},{16,0},{1,17},{17,1},{2,18},{18,2},{3,19},{19,3},{4,20},{20... | collective-permute-start | bytes 786440 | tf_op jit(solution)/shard_map/ppermute | solution.py:264
  104.3 8.1 %collective-permute-start.8 = (bf16[256,512]{1,0:T(8,128)(2,1)S(1)}, bf16[256,512]{1,0:T(8,128)(2,1)S(1)}, u32[]{:S(2)}, u32[]{:S(2)}) collective-permute-start(bf16[256,512]{1,0:T(8,128)(2,1)S(1)} %get-tuple-element.66), channel_id=1, source_target_pairs={{0,1},{1,0},{2,3},{3,2},{4,5},{5,4},{6,7},{7,6},{8,9},{9,8},{10,11... | collective-permute-start | bytes 786440 | tf_op jit(solution)/shard_map/ppermute | solution.py:264
  111.3 13.0 %collective-permute-start.12 = (bf16[512,512]{1,0:T(8,128)(2,1)S(1)}, bf16[512,512]{1,0:T(8,128)(2,1)S(1)}, u32[]{:S(2)}, u32[]{:S(2)}) collective-permute-start(bf16[512,512]{1,0:T(8,128)(2,1)S(1)} %pad_maximum_fusion.4), channel_id=1, source_target_pairs={{0,1},{1,0},{2,3},{3,2},{4,5},{5,4},{6,7},{7,6},{8,9},{9,8},{10,11... | collective-permute-start | bytes 1572872 | tf_op jit(solution)/shard_map/ppermute | solution.py:264
  112.5 12.8 %collective-permute-start.9 = (bf16[512,512]{1,0:T(8,128)(2,1)S(1)}, bf16[512,512]{1,0:T(8,128)(2,1)S(1)}, u32[]{:S(2)}, u32[]{:S(2)}) collective-permute-start(bf16[512,512]{1,0:T(8,128)(2,1)S(1)} %pad_maximum_fusion.3), channel_id=1, source_target_pairs={{0,16},{16,0},{1,17},{17,1},{2,18},{18,2},{3,19},{19,3},{4,20},{20... | collective-permute-start | bytes 1572872 | tf_op jit(solution)/shard_map/ppermute | solution.py:264
  118.6 7.3 %copy-start.9 = (s32[4]{0:T(128)S(1)}, s32[4]{0:T(128)}, u32[]{:S(2)}) copy-start(s32[4]{0:T(128)} %constant.30.clone) | copy-start | bytes 52
  125.3 3.5 %collective-permute-start.11 = (bf16[1024,512]{1,0:T(8,128)(2,1)S(1)}, bf16[1024,512]{1,0:T(8,128)(2,1)S(1)}, u32[]{:S(2)}, u32[]{:S(2)}) collective-permute-start(bf16[1024,512]{1,0:T(8,128)(2,1)S(1)} %pad_maximum_fusion.a_ref), channel_id=1, source_target_pairs={{0,8},{8,0},{1,9},{9,1},{2,10},{10,2},{3,11},{11,3},{4,12},{12,4},... | collective-permute-start | bytes 3145736 | tf_op jit(solution)/shard_map/ppermute | solution.py:264
  125.4 4.3 %collective-permute-start.13 = (bf16[1024,512]{1,0:T(8,128)(2,1)S(1)}, bf16[1024,512]{1,0:T(8,128)(2,1)}, u32[]{:S(2)}, u32[]{:S(2)}) collective-permute-start(bf16[1024,512]{1,0:T(8,128)(2,1)S(1)} %pad_maximum_fusion.1.b_ref), channel_id=1, source_target_pairs={{0,8},{8,0},{1,9},{9,1},{2,10},{10,2},{3,11},{11,3},{4,12},{12,4},... | collective-permute-start | bytes 3145736 | tf_op jit(solution)/shard_map/ppermute | solution.py:264
  (3 other events, 3.9 us)

commit v9 on v8

--- a/solution.py
+++ b/solution.py
@@ -99,7 +99,7 @@
         out_ref[...] = (g_ref[...].astype(F32) * sig * (1.0 + pre * (1.0 - sig))).astype(BF)
 
 
-def slots_kernel(n_dest, cap, own_ref, near_ref, far_ref, last_ref, slot_ref, labels_ref, group_ref):
+def slots_kernel(n_dest, cap, own_ref, near_ref, far_ref, last_ref, slot_ref, down_ref):
     n_s = own_ref.shape[1]
     n_feat = own_ref.shape[0] // N_CODE
     sample = iota((n_s, n_s), 0)
@@ -110,7 +110,6 @@
     at_row, at_col = iota((count, count), 0), iota((count, count), 1)
     before = ((at_row >> feat_bits == at_col >> feat_bits) & (at_col < at_row)).astype(F32).astype(BF)
     half = n_dest // 2
-    lane = iota((n_s, E), 1) & 3
     for z in range(N_Z):
         codes = (own_ref[...], near_ref[...], far_ref[0], last_ref[...])[z].astype(F32)
         plane = [codes[i * n_feat : (i + 1) * n_feat, :] for i in range(N_CODE)]
@@ -128,12 +127,7 @@
         dest = plane[6]
         folded = jnp.where(dest >= half, dest - half, dest)
         slot_ref[2, z, :, :] = jnp.where(dest >= 0, folded * ADM_DEV + plane[7], -1.0).astype(jnp.int32)
-        down = codes.T
-        group_ref[z] = down[:, 6 * n_feat : 7 * n_feat]
-        for f in range(n_feat):
-            col = [down[:, i * n_feat + f : i * n_feat + f + 1] for i in (1, 2, 4, 5)]
-            one = jnp.where(lane == 0, col[0], jnp.where(lane == 1, col[1], jnp.where(lane == 2, col[2], col[3])))
-            labels_ref[z, f * n_s : (f + 1) * n_s, :] = one.astype(BF)
+        down_ref[z] = codes.T
 
 
 def w_kernel(n_plane, z_ref, x_ref, d0_ref, d1_ref, d2_ref, d3_ref, out_ref):
@@ -164,7 +158,7 @@
     ).astype(BF)
 
 
-def bucket_kernel(n_dest, cap, look_ref, slot_ref, labels_ref, group_ref, bias_ref, out_ref, mark_ref):
+def bucket_kernel(n_dest, cap, look_ref, slot_ref, down_ref, bias_ref, all_ref, mark_ref, out_ref, sems):
     n_feat, n_s = slot_ref.shape[2:]
     seg = N_Z * cap
     n_mark = -(-seg // E)
@@ -172,10 +166,17 @@
 
     slots = n_dest * cap
     wanted = rows_from(slots)
+    kind = iota((n_s, E), 1) & 3
     for z in range(N_Z):
+        labels = []
+        for f in range(n_feat):
+            col = [down_ref[z, :, i * n_feat + f : i * n_feat + f + 1] for i in (1, 2, 4, 5)]
+            one = jnp.where(kind < 2, jnp.where(kind == 0, col[0], col[1]), jnp.where(kind == 2, col[2], col[3]))
+            labels.append(one.astype(BF))
+        values = jnp.concatenate([look_ref[z], jnp.concatenate(labels, axis=0)], axis=1)
         for which in range(2):
             hits = [one_hot(wanted, slot_ref[which, z, f : f + 1, :]) for f in range(n_feat)]
-            o = dot(jnp.concatenate(hits, axis=1), jnp.concatenate([look_ref[z], labels_ref[z]], axis=1))
+            o = dot(jnp.concatenate(hits, axis=1), values)
             for d in range(n_dest):
                 rows = o[d * cap : (d + 1) * cap, :]
                 out_ref[d, which * seg + z * cap : which * seg + (z + 1) * cap, :] = rows[:, 0:E].astype(BF)
@@ -188,7 +189,7 @@
         hits = [one_hot(wanted, slot_ref[2, z, f : f + 1, :]) for f in range(n_feat)]
         sides = []
         for f in range(n_feat):
-            upper = group_ref[z, :, f : f + 1] >= half
+            upper = down_ref[z, :, 6 * n_feat + f : 6 * n_feat + f + 1] >= half
             v = look_ref[z, f * n_s : (f + 1) * n_s, :].astype(F32)
             sides.append(jnp.concatenate([jnp.where(upper, 0.0, v), jnp.where(upper, v, 0.0)], axis=1).astype(BF))
         o = o + dot(jnp.concatenate(hits, axis=1), jnp.concatenate(sides, axis=0))
@@ -199,21 +200,23 @@
 
     at_mark = 2 * seg + ADM_DEV
 
-    def finish(d, carry):
-        lane = iota((seg, E), 1) & 3
+    lane = iota((seg, E), 1) & 3
+    rows = iota((16, E), 0) >> 2
+    copies = []
+    for d in range(n_dest):
         mixed = jnp.where(lane < 2, mark_ref[0, d], mark_ref[1, d])
         if seg % E:
             mixed = jnp.concatenate([mixed, jnp.zeros((n_mark * E - seg, E), F32)], axis=0)
-        rows = iota((16, E), 0) >> 2
         marks = jnp.zeros((16, E), F32)
         for j in range(n_mark):
             across = mixed[j * E : (j + 1) * E, :].T
             marks = jnp.where(rows == j, across[0:16, :], marks)
         out_ref[d, at_mark : at_mark + 16, :] = marks.astype(BF)
         out_ref[d, at_mark + 16 : at_mark + 16 + bias_ref.shape[0], :] = bias_ref[...]
-        return carry
-
-    lax.fori_loop(0, n_dest, finish, 0)
+        copies.append(pltpu.make_async_copy(out_ref.at[d], all_ref.at[d], sems.at[d]))
+        copies[-1].start()
+    for copy in copies:
+        copy.wait()
 
 
 def sums_kernel(n_src, seg, n_bias, table, in_ref, *outs):
@@ -303,6 +306,7 @@
             pltpu.VMEM((rows, 2 * half), F32),
             pltpu.SemaphoreType.DMA((2 * (rows // share),)),
         ],
+        vmem=16,
         **alias,
     )(at, *sides, *more)
 
@@ -374,28 +378,26 @@
         scratch_shapes=[pltpu.VMEM((n_s, hidden), F32)],
         vmem=56,
     )(after(features, own_codes), w_first, b_first.reshape(1, hidden), grad_out)
+    dpre = after(dpre, far_codes, near_codes)
 
     far = swap(dpre, "tz", 2)
     near = swap(dpre, "tz", 1)
-    far = after(far, near)
+    slots, down = call(
+        functools.partial(slots_kernel, n_plane, cap),
+        "slots",
+        (shape((3, N_Z, n_feat, n_s), jnp.int32), shape((N_Z, n_s, n_code), F32)),
+        10**9,
+        10**6,
+        vmem=12,
+    )(after(own_codes, dpre), near_codes, far_codes, last_codes)
+    far = after(far, near, slots)
     sources = [dpre, near, far, swap(far, "tz", 1)]
 
     cut = call(
-        functools.partial(cut_kernel, n_dp), "cut", shape((N_Z, n_s, wide), BF), 10**6, 2 * 10**6
+        functools.partial(cut_kernel, n_dp), "cut", shape((N_Z, n_s, wide), BF), 10**6, 2 * 10**6, vmem=8
     )(after(features, dpre))
     feat_in = lax.all_to_all(after(cut, far), "tz", split_axis=0, concat_axis=0, tiled=True)
 
-    slots, labels, group = call(
-        functools.partial(slots_kernel, n_plane, cap),
-        "slots",
-        (
-            shape((3, N_Z, n_feat, n_s), jnp.int32),
-            shape((N_Z, count, E), BF),
-            shape((N_Z, n_s, n_feat), F32),
-        ),
-        10**9,
-        3 * 10**6,
-    )(own_codes, near_codes, far_codes, last_codes)
     look, bias = call(
         lookup_kernel,
         "lookups",
@@ -403,8 +405,9 @@
         2 * N_Z * n_s * width * hidden,
         7 * 10**6,
         scratch_shapes=[pltpu.VMEM((N_Z * n_s, hidden), BF)],
+        vmem=16,
     )(*sources, w_first)
-    feat_in = after(feat_in, look, slots)
+    feat_in = after(feat_in, look)
 
     w_part = call(
         functools.partial(w_kernel, n_plane),
@@ -413,6 +416,7 @@
         2 * N_Z * n_s * wide * hidden,
         3 * 10**6,
         in_specs=[scalar] + [array] * 5,
+        vmem=12,
     )(my_z, feat_in, *sources)
     look = after(look, w_part)
     w_part = lax.all_to_all(w_part, plane, split_axis=0, concat_axis=0, tiled=True)
@@ -424,9 +428,14 @@
         shape((n_plane, n_rows, E), BF),
         15 * 10**9,
         4 * 10**7,
-        scratch_shapes=[pltpu.VMEM((2, n_plane, seg, E), F32)],
+        out_specs=pl.BlockSpec(memory_space=pltpu.HBM),
+        scratch_shapes=[
+            pltpu.VMEM((2, n_plane, seg, E), F32),
+            pltpu.VMEM((n_plane, n_rows, E), BF),
+            pltpu.SemaphoreType.DMA((n_plane,)),
+        ],
         vmem=28,
-    )(look, slots, labels, group, bias)
+    )(look, slots, down, bias)
 
     w_part = after(w_part, chunks)
     w_own = jnp.sum(w_part.astype(F32), axis=0).astype(BF)
@@ -434,7 +443,6 @@
 
     w_two = jnp.concatenate([w_own, swap(w_own, "tz", 2)], axis=0)
     w_four = jnp.concatenate([w_two, swap(w_two, "tz", 1)], axis=0)
-    w_four = after(w_four, chunks)
     sides = [w_four[:, : hidden // 2], w_four[:, hidden // 2 :]]
     over_y = [("ty", k) for k in doubling(n_y)]
     over_x = [("x", k) for k in doubling(n_dp // n_core)]
@@ -448,17 +456,16 @@
             outs if table == 0 else outs[:1],
             4 * 10**9,
             4 * 10**6,
-            vmem=40,
+            vmem=28,
         )(chunks)
 
-    q_grad, b_grad, adm_grad = sums(0, after(chunks, w_four))
     for i, steps in enumerate(zip(over_y + over_x, over_x + over_y)):
         moved = [swap(side, *step) for side, step in zip(sides, steps)]
-        if i == 0:
-            moved = [after(part, q_grad) for part in moved]
         sides = [jnp.concatenate(pair, axis=0) for pair in zip(sides, moved)]
         last = sides if i == len(over_x + over_y) - 2 else last
-    (r_grad,) = sums(1, after(chunks, *last))
+    chunks = after(chunks, *last)
+    q_grad, b_grad, adm_grad = sums(0, chunks)
+    (r_grad,) = sums(1, after(chunks, q_grad))
     sides = [after(side, r_grad) for side in sides]
     others = [swap(side, "core", 1) for side in sides]
     at = jnp.stack([lax.axis_index(name) for name in ("x", "core", "tz", "ty")]).astype(jnp.int32)

time: 134 us -> 131 us (0.978)
  local copies, waits for them, and re-layouts: 7.73 us -> 3.56 us
  other arithmetic: 2.91 us -> 5.69 us
    all_to_all x1, waiting for transfers between devices: 5.21 us -> 0.01 us  [local(): lax.all_to_all(chunks, plane, split_axis=0, concat_axis=0, tiled=True)]
    unnamed x20 -> x12, local copies, waits for them, and re-layouts: 7.69 us -> 3.52 us
    concatenate x4, other arithmetic: 0.21 us -> 3.89 us  [local(): sides = [jnp.concatenate(pair, axis=0) for pair in zip(sides, moved)]]
    ppermute x14, waiting for transfers between devices: 44.5 us -> 48.1 us  [swap(): return lax.ppermute(x, axis, [(i, i ^ k) for i in range(n)])]
    pallas_call x1, Pallas kernels: 2.97 us -> 0.87 us  [local(): call(functools.partial(slots_kernel, n_plane, cap), 'slots', (shape((3, N...]
    pallas_call x1, Pallas kernels: 9.44 us -> 11.1 us  [local(): call(functools.partial(bucket_kernel, n_plane, cap), 'buckets', shape((n_...]
  transfers between devices with their start and end apart: 17 -> 17, of which waited for: 12 -> 10; matrix products, arithmetic and copies ran while one was open for 1% -> 2% of each run, Pallas kernels for 22% -> 26%
where the time goes in v9:
time: 131 us; the launch traced here: 130 us
  waiting for transfers between devices  51.5 us (39%)
  Pallas kernels  38.9 us (30%)
  starting transfers between devices  29.6 us (23%)
  other arithmetic  5.69 us (4%)
  local copies, waits for them, and re-layouts  3.56 us (3%)
    ppermute x14, waiting for transfers between devices, swap(): return lax.ppermute(x, axis, [(i, i ^ k) for i in range(n)])  48.1 us
    ppermute x14, starting transfers between devices, swap(): return lax.ppermute(x, axis, [(i, i ^ k) for i in range(n)])  18.5 us
    pallas_call x1, Pallas kernels, local(): call(functools.partial(bucket_kernel, n_plane, cap), 'buckets', shape((n_...  11.1 us
    pallas_call x2, Pallas kernels, sums(): call(functools.partial(sums_kernel, n_plane, seg, n_bias, table), ('q_sum...  10.8 us
    pallas_call x2, Pallas kernels, widen(): call(functools.partial(widen_kernel, n_x, n_y, share), 'widen', jax.Shape...  6.32 us
    pallas_call x1, Pallas kernels, local(): call(dpre_kernel, 'dpre', shape((n_s, hidden), BF), 2 * n_s * width * hid...  4.77 us
    concatenate x4, other arithmetic, local(): sides = [jnp.concatenate(pair, axis=0) for pair in zip(sides, moved)]  3.89 us
    all_to_all x1, starting transfers between devices, local(): lax.all_to_all(w_part, plane, split_axis=0, concat_axis=0, tiled=True)  3.88 us
  transfers between devices with their start and end apart: 17, of which 10 were waited for; matrix products, arithmetic and copies ran while one was open for 2% of the time, Pallas kernels for 26%

profile of v9, /device:TPU:0, one launch (start us, length us, event | category | flops | bytes accessed | tf_op | source)
XLA Modules:
  0.0 130.2 jit_solution(1735524579948673086)
XLA Ops:
  2.2 4.1 %collective-permute-start = (bf16[2,128,128]{2,1,0:T(8,128)(2,1)S(1)}, bf16[2,128,128]{2,1,0:T(8,128)(2,1)S(1)}, u32[]{:S(2)}, u32[]{:S(2)}) collective-permute-start(bf16[2,128,128]{2,1,0:T(8,128)(2,1)S(1)} %get-tuple-element.33), channel_id=1, source_target_pairs={{0,4},{2,6},{4,0},{6,2},{1,5},{3,7},{5,1},{7,3},{8,12},{10,14},{12... | collective-permute-start | bytes 196616 | tf_op jit(solution)/shard_map/ppermute | solution.py:267
  6.3 1.6 %collective-permute-start.1 = (bf16[128,128]{1,0:T(8,128)(2,1)S(1)}, bf16[128,128]{1,0:T(8,128)(2,1)S(1)}, u32[]{:S(2)}, u32[]{:S(2)}) collective-permute-start(bf16[128,128]{1,0:T(8,128)(2,1)S(1)} %get-tuple-element.34), channel_id=1, source_target_pairs={{0,2},{2,0},{4,6},{6,4},{1,3},{3,1},{5,7},{7,5},{8,10},{10,8},{12,... | collective-permute-start | bytes 98312 | tf_op jit(solution)/shard_map/ppermute | solution.py:267
  7.8 4.8 %dpre.1.d0_ref = bf16[128,1024]{1,0:T(8,128)(2,1)} custom-call(bf16[128,2048]{1,0:T(8,128)(2,1)} %x_ref.1, bf16[2048,1024]{1,0:T(8,128)(2,1)} %w_ref.3, f32[1,1024]{1,0:T(1,128)} %bitcast.38, bf16[128,1024]{1,0:T(8,128)(2,1)} %g_ref.1), custom_call_target="tpu_custom_call" | custom-call | flops 536870912 | bytes 6000000 | tf_op jit(solution)/shard_map/dpre/pallas_call | solution.py:364
  15.9 9.8 %collective-permute-done.4.last_ref = bf16[128,128]{1,0:T(8,128)(2,1)S(1)} collective-permute-done((bf16[128,128]{1,0:T(8,128)(2,1)S(1)}, bf16[128,128]{1,0:T(8,128)(2,1)S(1)}, u32[]{:S(2)}, u32[]{:S(2)}) %collective-permute-start.4) | collective-permute-done | bytes 32800 | tf_op jit(solution)/shard_map/ppermute | solution.py:267
  27.1 3.5 %all-to-all-start = ((bf16[4,128,512]{2,1,0:T(8,128)(2,1)}), bf16[4,128,512]{2,1,0:T(8,128)(2,1)S(1)}, u32[]{:S(2)}, u32[]{:S(2)}) async-start(bf16[4,128,512]{2,1,0:T(8,128)(2,1)} %cut.1), calls=%async_computation | async-start | bytes 1048576 | tf_op jit(solution)/shard_map/all_to_all | solution.py:399
  30.6 2.0 %collective-permute-start.5 = (bf16[128,1024]{1,0:T(8,128)(2,1)S(1)}, bf16[128,1024]{1,0:T(8,128)(2,1)S(1)}, u32[]{:S(2)}, u32[]{:S(2)}) collective-permute-start(bf16[128,1024]{1,0:T(8,128)(2,1)S(1)} %collective-permute-done.2.d2_ref), channel_id=1, source_target_pairs={{0,2},{2,0},{4,6},{6,4},{1,3},{3,1},{5,7},{7,5},{8,10},{10,8},{12,... | collective-permute-start | bytes 786440 | tf_op jit(solution)/shard_map/ppermute | solution.py:267
  32.6 13.0 %collective-permute-done.5.d3_ref = bf16[128,1024]{1,0:T(8,128)(2,1)S(1)} collective-permute-done((bf16[128,1024]{1,0:T(8,128)(2,1)S(1)}, bf16[128,1024]{1,0:T(8,128)(2,1)S(1)}, u32[]{:S(2)}, u32[]{:S(2)}) %collective-permute-start.5) | collective-permute-done | bytes 262176 | tf_op jit(solution)/shard_map/ppermute | solution.py:267
  45.6 2.2 %copy-done = bf16[2048,1024]{1,0:T(8,128)(2,1)S(1)} copy-done((bf16[2048,1024]{1,0:T(8,128)(2,1)S(1)}, bf16[2048,1024]{1,0:T(8,128)(2,1)}, u32[]{:S(2)}) %copy-start) | copy-done | bytes 4194328
  47.8 2.4 %lookups.1 = (bf16[4,2048,128]{2,1,0:T(8,128)(2,1)S(1)}, bf16[16,128]{1,0:T(8,128)(2,1)S(1)}) custom-call(bf16[128,1024]{1,0:T(8,128)(2,1)S(1)} %copy-done.2, bf16[128,1024]{1,0:T(8,128)(2,1)S(1)} %collective-permute-done.3.d1_ref, bf16[128,1024]{1,0:T(8,128)(2,1)S(1)} %collective-permute-done.2.d2_ref, bf16[128,1024]{1,0:T(8,128)(2,1)S(1)} %collective-permute-done.5.d3_ref, ...), custom_call_target="tpu_custom_call" | custom-call | flops 2147483648 | bytes 7000000 | tf_op jit(solution)/shard_map/lookups/pallas_call | solution.py:401
  51.5 1.7 %w_part.1 = bf16[8,64,1024]{2,1,0:T(8,128)(2,1)} custom-call(s32[1]{0:T(128)} %bitcast.2.z_ref, bf16[4,128,512]{2,1,0:T(8,128)(2,1)S(1)} %all-to-all-done.x_ref, bf16[128,1024]{1,0:T(8,128)(2,1)S(1)} %copy-done.2, bf16[128,1024]{1,0:T(8,128)(2,1)S(1)} %collective-permute-done.3.d1_ref, bf16[128,1024]{1,0:T(8,128)(2,1)S(1)} %collective-permute-done.2.d2_ref, ...), custom_call_target="tpu_custom_call" | custom-call | flops 536870912 | bytes 3000000 | tf_op jit(solution)/shard_map/w_part/pallas_call | solution.py:412
  53.2 3.9 %all-to-all-start.1 = ((bf16[8,64,1024]{2,1,0:T(8,128)(2,1)}), bf16[8,64,1024]{2,1,0:T(8,128)(2,1)S(1)}, u32[]{:S(2)}, u32[]{:S(2)}) async-start(bf16[8,64,1024]{2,1,0:T(8,128)(2,1)} %w_part.1), calls=%async_computation.1 | async-start | bytes 2097152 | tf_op jit(solution)/shard_map/all_to_all | solution.py:422
  57.1 11.1 %buckets.1 = bf16[8,928,128]{2,1,0:T(8,128)(2,1)} custom-call(bf16[4,2048,128]{2,1,0:T(8,128)(2,1)S(1)} %copy-done.4, s32[3,4,16,128]{3,2,1,0:T(8,128)S(1)} %get-tuple-element.39.slot_ref, f32[4,128,128]{2,1,0:T(8,128)S(1)} %get-tuple-element.45.down_ref, bf16[16,128]{1,0:T(8,128)(2,1)S(1)} %get-tuple-element.46.bias_ref), custom_call_target="tpu_custom_call" | custom-call | flops 15000000512 | bytes 40000000 | tf_op jit(solution)/shard_map/buckets/pallas_call | solution.py:425
  68.2 3.4 %all-to-all-done.1 = bf16[8,64,1024]{2,1,0:T(8,128)(2,1)S(1)} async-done(((bf16[8,64,1024]{2,1,0:T(8,128)(2,1)}), bf16[8,64,1024]{2,1,0:T(8,128)(2,1)S(1)}, u32[]{:S(2)}, u32[]{:S(2)}) %all-to-all-start.1) | async-done | bytes 1048608 | tf_op jit(solution)/shard_map/all_to_all | solution.py:422
  71.6 3.8 %all-to-all-start.2 = ((bf16[8,928,128]{2,1,0:T(8,128)(2,1)}), bf16[8,928,128]{2,1,0:T(8,128)(2,1)S(1)}, u32[]{:S(2)}, u32[]{:S(2)}) async-start(bf16[8,928,128]{2,1,0:T(8,128)(2,1)} %buckets.1), calls=%async_computation.2 | async-start | bytes 3801088 | tf_op jit(solution)/shard_map/all_to_all | solution.py:442
  75.6 2.5 %collective-permute-start.6 = (bf16[64,1024]{1,0:T(8,128)(2,1)S(1)}, bf16[64,1024]{1,0:T(8,128)(2,1)S(1)}, u32[]{:S(2)}, u32[]{:S(2)}) collective-permute-start(bf16[64,1024]{1,0:T(8,128)(2,1)S(1)} %reduce_sum.12), channel_id=1, source_target_pairs={{0,4},{2,6},{4,0},{6,2},{1,5},{3,7},{5,1},{7,3},{8,12},{10,14},{12... | collective-permute-start | bytes 393224 | tf_op jit(solution)/shard_map/ppermute | solution.py:267
  78.1 6.6 %collective-permute-done.6 = bf16[64,1024]{1,0:T(8,128)(2,1)S(1)} collective-permute-done((bf16[64,1024]{1,0:T(8,128)(2,1)S(1)}, bf16[64,1024]{1,0:T(8,128)(2,1)S(1)}, u32[]{:S(2)}, u32[]{:S(2)}) %collective-permute-start.6) | collective-permute-done | bytes 131104 | tf_op jit(solution)/shard_map/ppermute | solution.py:267
  84.9 8.2 %collective-permute-done.7 = bf16[128,1024]{1,0:T(8,128)(2,1)S(1)} collective-permute-done((bf16[128,1024]{1,0:T(8,128)(2,1)S(1)}, bf16[128,1024]{1,0:T(8,128)(2,1)S(1)}, u32[]{:S(2)}, u32[]{:S(2)}) %collective-permute-start.7) | collective-permute-done | bytes 262176 | tf_op jit(solution)/shard_map/ppermute | solution.py:267
  93.2 1.7 %collective-permute-start.10 = (bf16[256,512]{1,0:T(8,128)(2,1)S(1)}, bf16[256,512]{1,0:T(8,128)(2,1)S(1)}, u32[]{:S(2)}, u32[]{:S(2)}) collective-permute-start(bf16[256,512]{1,0:T(8,128)(2,1)S(1)} %get-tuple-element.61), channel_id=1, source_target_pairs={{0,16},{16,0},{1,17},{17,1},{2,18},{18,2},{3,19},{19,3},{4,20},{20... | collective-permute-start | bytes 786440 | tf_op jit(solution)/shard_map/ppermute | solution.py:267
  94.9 1.5 %collective-permute-start.8 = (bf16[256,512]{1,0:T(8,128)(2,1)S(1)}, bf16[256,512]{1,0:T(8,128)(2,1)S(1)}, u32[]{:S(2)}, u32[]{:S(2)}) collective-permute-start(bf16[256,512]{1,0:T(8,128)(2,1)S(1)} %get-tuple-element.62), channel_id=1, source_target_pairs={{0,1},{1,0},{2,3},{3,2},{4,5},{5,4},{6,7},{7,6},{8,9},{9,8},{10,11... | collective-permute-start | bytes 786440 | tf_op jit(solution)/shard_map/ppermute | solution.py:267
  96.4 8.0 %collective-permute-done.10 = bf16[256,512]{1,0:T(8,128)(2,1)S(1)} collective-permute-done((bf16[256,512]{1,0:T(8,128)(2,1)S(1)}, bf16[256,512]{1,0:T(8,128)(2,1)S(1)}, u32[]{:S(2)}, u32[]{:S(2)}) %collective-permute-start.10) | collective-permute-done | bytes 262176 | tf_op jit(solution)/shard_map/ppermute | solution.py:267
  108.1 5.4 %q_sums.1 = (f32[4096,128]{1,0:T(8,128)}, f32[8,128]{1,0:T(8,128)}, f32[128,128]{1,0:T(8,128)}) custom-call(bf16[8,928,128]{2,1,0:T(8,128)(2,1)S(1)} %all-to-all-done.2.in_ref), custom_call_target="tpu_custom_call" | custom-call | flops 4000000000 | bytes 4000000 | tf_op jit(solution)/shard_map/q_sums/pallas_call | solution.py:453
  113.5 5.4 %r_sums.1 = f32[4096,128]{1,0:T(8,128)} custom-call(bf16[8,928,128]{2,1,0:T(8,128)(2,1)S(1)} %all-to-all-done.2.in_ref), custom_call_target="tpu_custom_call" | custom-call | flops 4000000000 | bytes 4000000 | tf_op jit(solution)/shard_map/r_sums/pallas_call | solution.py:453
  122.8 2.8 %widen.2.refs_0_ = f32[2048,1024]{1,0:T(8,128)} custom-call(s32[4]{0:T(128)S(1)} %get-tuple-element.60.at_ref, bf16[1024,512]{1,0:T(8,128)(2,1)S(1)} %pad_maximum_fusion.a_ref, bf16[1024,512]{1,0:T(8,128)(2,1)S(1)} %pad_maximum_fusion.1.b_ref), custom_call_target="tpu_custom_call" | custom-call | flops 1048576 | bytes 6291456 | tf_op jit(solution)/shard_map/widen/pallas_call | solution.py:297
  126.5 3.5 %widen.3 = f32[2048,1024]{1,0:T(8,128)} custom-call(s32[4]{0:T(128)S(1)} %get-tuple-element.59.at_ref, bf16[1024,512]{1,0:T(8,128)(2,1)S(1)} %collective-permute-done.11.a_ref, bf16[1024,512]{1,0:T(8,128)(2,1)} %collective-permute-done.13.b_ref, f32[2048,1024]{1,0:T(8,128)} %widen.2.refs_0_), custom_call_target="tpu_custom_call", output_to_operand_aliasing={{}: (3, {})} | custom-call | flops 1048576 | bytes 6291456 | tf_op jit(solution)/shard_map/widen/pallas_call | solution.py:297
  (45 shorter events, 16.3 us)
Async XLA Ops:
  2.2 10.5 %collective-permute-start = (bf16[2,128,128]{2,1,0:T(8,128)(2,1)S(1)}, bf16[2,128,128]{2,1,0:T(8,128)(2,1)S(1)}, u32[]{:S(2)}, u32[]{:S(2)}) collective-permute-start(bf16[2,128,128]{2,1,0:T(8,128)(2,1)S(1)} %get-tuple-element.33), channel_id=1, source_target_pairs={{0,4},{2,6},{4,0},{6,2},{1,5},{3,7},{5,1},{7,3},{8,12},{10,14},{12... | collective-permute-start | bytes 196616 | tf_op jit(solution)/shard_map/ppermute | solution.py:267
  6.3 6.4 %collective-permute-start.1 = (bf16[128,128]{1,0:T(8,128)(2,1)S(1)}, bf16[128,128]{1,0:T(8,128)(2,1)S(1)}, u32[]{:S(2)}, u32[]{:S(2)}) collective-permute-start(bf16[128,128]{1,0:T(8,128)(2,1)S(1)} %get-tuple-element.34), channel_id=1, source_target_pairs={{0,2},{2,0},{4,6},{6,4},{1,3},{3,1},{5,7},{7,5},{8,10},{10,8},{12,... | collective-permute-start | bytes 98312 | tf_op jit(solution)/shard_map/ppermute | solution.py:267
  7.8 7.2 %copy-start.1 = (bf16[128,2048]{1,0:T(8,128)(2,1)S(1)}, bf16[128,2048]{1,0:T(8,128)(2,1)}, u32[]{:S(2)}) copy-start(bf16[128,2048]{1,0:T(8,128)(2,1)} %x_ref.1) | copy-start | bytes 1572868
  12.6 14.0 %collective-permute-start.3 = (bf16[128,1024]{1,0:T(8,128)(2,1)}, bf16[128,1024]{1,0:T(8,128)(2,1)S(1)}, u32[]{:S(2)}, u32[]{:S(2)}) collective-permute-start(bf16[128,1024]{1,0:T(8,128)(2,1)} %dpre.1.d0_ref), channel_id=1, source_target_pairs={{0,2},{2,0},{4,6},{6,4},{1,3},{3,1},{5,7},{7,5},{8,10},{10,8},{12,... | collective-permute-start | bytes 786440 | tf_op jit(solution)/shard_map/ppermute | solution.py:267
  13.1 14.0 %collective-permute-start.2 = (bf16[128,1024]{1,0:T(8,128)(2,1)}, bf16[128,1024]{1,0:T(8,128)(2,1)S(1)}, u32[]{:S(2)}, u32[]{:S(2)}) collective-permute-start(bf16[128,1024]{1,0:T(8,128)(2,1)} %dpre.1.d0_ref), channel_id=1, source_target_pairs={{0,4},{2,6},{4,0},{6,2},{1,5},{3,7},{5,1},{7,3},{8,12},{10,14},{12... | collective-permute-start | bytes 786440 | tf_op jit(solution)/shard_map/ppermute | solution.py:267
  13.9 11.9 %collective-permute-start.4 = (bf16[128,128]{1,0:T(8,128)(2,1)S(1)}, bf16[128,128]{1,0:T(8,128)(2,1)S(1)}, u32[]{:S(2)}, u32[]{:S(2)}) collective-permute-start(bf16[128,128]{1,0:T(8,128)(2,1)S(1)} %slice_bitcast_fusion), channel_id=1, source_target_pairs={{0,2},{2,0},{4,6},{6,4},{1,3},{3,1},{5,7},{7,5},{8,10},{10,8},{12,... | collective-permute-start | bytes 98312 | tf_op jit(solution)/shard_map/ppermute | solution.py:267
  15.9 29.6 %copy-start.2 = (bf16[128,1024]{1,0:T(8,128)(2,1)S(1)}, bf16[128,1024]{1,0:T(8,128)(2,1)}, u32[]{:S(2)}) copy-start(bf16[128,1024]{1,0:T(8,128)(2,1)} %dpre.1.d0_ref) | copy-start | bytes 786436
  27.1 24.3 %all-to-all-start = ((bf16[4,128,512]{2,1,0:T(8,128)(2,1)}), bf16[4,128,512]{2,1,0:T(8,128)(2,1)S(1)}, u32[]{:S(2)}, u32[]{:S(2)}) async-start(bf16[4,128,512]{2,1,0:T(8,128)(2,1)} %cut.1), calls=%async_computation | async-start | bytes 1048576 | tf_op jit(solution)/shard_map/all_to_all | solution.py:399
  30.6 15.0 %collective-permute-start.5 = (bf16[128,1024]{1,0:T(8,128)(2,1)S(1)}, bf16[128,1024]{1,0:T(8,128)(2,1)S(1)}, u32[]{:S(2)}, u32[]{:S(2)}) collective-permute-start(bf16[128,1024]{1,0:T(8,128)(2,1)S(1)} %collective-permute-done.2.d2_ref), channel_id=1, source_target_pairs={{0,2},{2,0},{4,6},{6,4},{1,3},{3,1},{5,7},{7,5},{8,10},{10,8},{12,... | collective-permute-start | bytes 786440 | tf_op jit(solution)/shard_map/ppermute | solution.py:267
  45.6 2.2 %copy-start = (bf16[2048,1024]{1,0:T(8,128)(2,1)S(1)}, bf16[2048,1024]{1,0:T(8,128)(2,1)}, u32[]{:S(2)}) copy-start(bf16[2048,1024]{1,0:T(8,128)(2,1)} %w_ref.3) | copy-start | bytes 12582916
  50.1 1.3 %copy-start.3 = (bf16[4,2048,128]{2,1,0:T(8,128)(2,1)}, bf16[4,2048,128]{2,1,0:T(8,128)(2,1)S(1)}, u32[]{:S(2)}) copy-start(bf16[4,2048,128]{2,1,0:T(8,128)(2,1)S(1)} %get-tuple-element.44.look_ref) | copy-start | bytes 6291460
  53.2 3.9 %copy-start.4 = (bf16[4,2048,128]{2,1,0:T(8,128)(2,1)S(1)}, bf16[4,2048,128]{2,1,0:T(8,128)(2,1)}, u32[]{:S(2)}) copy-start(bf16[4,2048,128]{2,1,0:T(8,128)(2,1)} %copy-done.3) | copy-start | bytes 6291460
  53.2 18.4 %all-to-all-start.1 = ((bf16[8,64,1024]{2,1,0:T(8,128)(2,1)}), bf16[8,64,1024]{2,1,0:T(8,128)(2,1)S(1)}, u32[]{:S(2)}, u32[]{:S(2)}) async-start(bf16[8,64,1024]{2,1,0:T(8,128)(2,1)} %w_part.1), calls=%async_computation.1 | async-start | bytes 2097152 | tf_op jit(solution)/shard_map/all_to_all | solution.py:422
  71.6 36.5 %all-to-all-start.2 = ((bf16[8,928,128]{2,1,0:T(8,128)(2,1)}), bf16[8,928,128]{2,1,0:T(8,128)(2,1)S(1)}, u32[]{:S(2)}, u32[]{:S(2)}) async-start(bf16[8,928,128]{2,1,0:T(8,128)(2,1)} %buckets.1), calls=%async_computation.2 | async-start | bytes 3801088 | tf_op jit(solution)/shard_map/all_to_all | solution.py:442
  75.6 9.1 %collective-permute-start.6 = (bf16[64,1024]{1,0:T(8,128)(2,1)S(1)}, bf16[64,1024]{1,0:T(8,128)(2,1)S(1)}, u32[]{:S(2)}, u32[]{:S(2)}) collective-permute-start(bf16[64,1024]{1,0:T(8,128)(2,1)S(1)} %reduce_sum.12), channel_id=1, source_target_pairs={{0,4},{2,6},{4,0},{6,2},{1,5},{3,7},{5,1},{7,3},{8,12},{10,14},{12... | collective-permute-start | bytes 393224 | tf_op jit(solution)/shard_map/ppermute | solution.py:267
  84.8 8.3 %collective-permute-start.7 = (bf16[128,1024]{1,0:T(8,128)(2,1)S(1)}, bf16[128,1024]{1,0:T(8,128)(2,1)S(1)}, u32[]{:S(2)}, u32[]{:S(2)}) collective-permute-start(bf16[128,1024]{1,0:T(8,128)(2,1)S(1)} %pad_maximum_fusion.5), channel_id=1, source_target_pairs={{0,2},{2,0},{4,6},{6,4},{1,3},{3,1},{5,7},{7,5},{8,10},{10,8},{12,... | collective-permute-start | bytes 786440 | tf_op jit(solution)/shard_map/ppermute | solution.py:267
  93.2 11.3 %collective-permute-start.10 = (bf16[256,512]{1,0:T(8,128)(2,1)S(1)}, bf16[256,512]{1,0:T(8,128)(2,1)S(1)}, u32[]{:S(2)}, u32[]{:S(2)}) collective-permute-start(bf16[256,512]{1,0:T(8,128)(2,1)S(1)} %get-tuple-element.61), channel_id=1, source_target_pairs={{0,16},{16,0},{1,17},{17,1},{2,18},{18,2},{3,19},{19,3},{4,20},{20... | collective-permute-start | bytes 786440 | tf_op jit(solution)/shard_map/ppermute | solution.py:267
  94.9 11.8 %collective-permute-start.8 = (bf16[256,512]{1,0:T(8,128)(2,1)S(1)}, bf16[256,512]{1,0:T(8,128)(2,1)S(1)}, u32[]{:S(2)}, u32[]{:S(2)}) collective-permute-start(bf16[256,512]{1,0:T(8,128)(2,1)S(1)} %get-tuple-element.62), channel_id=1, source_target_pairs={{0,1},{1,0},{2,3},{3,2},{4,5},{5,4},{6,7},{7,6},{8,9},{9,8},{10,11... | collective-permute-start | bytes 786440 | tf_op jit(solution)/shard_map/ppermute | solution.py:267
  105.3 13.8 %collective-permute-start.12 = (bf16[512,512]{1,0:T(8,128)(2,1)}, bf16[512,512]{1,0:T(8,128)(2,1)}, u32[]{:S(2)}, u32[]{:S(2)}) collective-permute-start(bf16[512,512]{1,0:T(8,128)(2,1)} %pad_maximum_fusion.4), channel_id=1, source_target_pairs={{0,1},{1,0},{2,3},{3,2},{4,5},{5,4},{6,7},{7,6},{8,9},{9,8},{10,11... | collective-permute-start | bytes 1572872 | tf_op jit(solution)/shard_map/ppermute | solution.py:267
  107.6 13.5 %collective-permute-start.9 = (bf16[512,512]{1,0:T(8,128)(2,1)}, bf16[512,512]{1,0:T(8,128)(2,1)}, u32[]{:S(2)}, u32[]{:S(2)}) collective-permute-start(bf16[512,512]{1,0:T(8,128)(2,1)} %pad_maximum_fusion.3), channel_id=1, source_target_pairs={{0,16},{16,0},{1,17},{17,1},{2,18},{18,2},{3,19},{19,3},{4,20},{20... | collective-permute-start | bytes 1572872 | tf_op jit(solution)/shard_map/ppermute | solution.py:267
  118.9 3.8 %copy-start.5 = (s32[4]{0:T(128)S(1)}, s32[4]{0:T(128)}, u32[]{:S(2)}) copy-start(s32[4]{0:T(128)} %constant.30.clone) | copy-start | bytes 52
  122.2 3.5 %collective-permute-start.11 = (bf16[1024,512]{1,0:T(8,128)(2,1)S(1)}, bf16[1024,512]{1,0:T(8,128)(2,1)S(1)}, u32[]{:S(2)}, u32[]{:S(2)}) collective-permute-start(bf16[1024,512]{1,0:T(8,128)(2,1)S(1)} %pad_maximum_fusion.a_ref), channel_id=1, source_target_pairs={{0,8},{8,0},{1,9},{9,1},{2,10},{10,2},{3,11},{11,3},{4,12},{12,4},... | collective-permute-start | bytes 3145736 | tf_op jit(solution)/shard_map/ppermute | solution.py:267
  122.3 4.3 %collective-permute-start.13 = (bf16[1024,512]{1,0:T(8,128)(2,1)S(1)}, bf16[1024,512]{1,0:T(8,128)(2,1)}, u32[]{:S(2)}, u32[]{:S(2)}) collective-permute-start(bf16[1024,512]{1,0:T(8,128)(2,1)S(1)} %pad_maximum_fusion.1.b_ref), channel_id=1, source_target_pairs={{0,8},{8,0},{1,9},{9,1},{2,10},{10,2},{3,11},{11,3},{4,12},{12,4},... | collective-permute-start | bytes 3145736 | tf_op jit(solution)/shard_map/ppermute | solution.py:267

commit v10 on v9

--- a/solution.py
+++ b/solution.py
@@ -267,40 +267,46 @@
     return lax.ppermute(x, axis, [(i, i ^ k) for i in range(n)])
 
 
-def widen_kernel(n_x, n_y, share, at_ref, a_ref, b_ref, *refs):
+def widen_kernel(n_x, n_y, share, at_ref, *refs):
+    n = n_x * n_y
     out_ref, held_ref, sems = refs[-3:]
-    half = a_ref.shape[1]
+    half = refs[0].shape[1]
+    tall = N_Z * share
     copies = []
-    for b in range(a_ref.shape[0] // share):
-        z = at_ref[2] ^ (((b & 1) << 1) | ((b >> 1) & 1))
-        rest = b >> 2
-        rows = slice(b * share, (b + 1) * share)
-        for side, ref in enumerate((a_ref, b_ref)):
-            y, x = (rest % n_y, rest // n_y) if side == 0 else (rest // n_x, rest % n_x)
-            row = ((((at_ref[0] ^ x) * 2 + at_ref[1]) * N_Z + z) * n_y + (at_ref[3] ^ y)) * share
+    for piece in range(n):
+        for side in range(2):
             cols = slice(side * half, (side + 1) * half)
-            held_ref[rows, cols] = ref[rows, :].astype(F32)
-            copy = pltpu.make_async_copy(
-                held_ref.at[rows, cols], out_ref.at[pl.ds(pl.multiple_of(row, share), share), cols], sems.at[len(copies)]
-            )
-            copy.start()
-            copies.append(copy)
+            held_ref[piece * tall : (piece + 1) * tall, cols] = refs[side * n + piece][...].astype(F32)
+            x, y = at_ref[0] ^ (piece // n_y), at_ref[3] ^ (piece % n_y)
+            for b in range(N_Z):
+                z = at_ref[2] ^ (((b & 1) << 1) | (b >> 1))
+                row = (((x * 2 + at_ref[1]) * N_Z + z) * n_y + y) * share
+                copy = pltpu.make_async_copy(
+                    held_ref.at[piece * tall + b * share : piece * tall + (b + 1) * share, cols],
+                    out_ref.at[pl.ds(pl.multiple_of(row, share), share), cols],
+                    sems.at[len(copies)],
+                )
+                copy.start()
+                copies.append(copy)
     for copy in copies:
         copy.wait()
 
 
-def widen(n_x, n_y, share, at, sides, so_far):
-    rows, half = sides[0].shape
+def widen(n_x, n_y, share, at, pieces, so_far):
+    tall, half = pieces[0].shape
+    rows = n_x * n_y * tall
     array = pl.BlockSpec(memory_space=pltpu.VMEM)
     more = () if so_far is None else (so_far,)
-    alias = {} if so_far is None else {"input_output_aliases": {3: 0}}
+    alias = {} if so_far is None else {"input_output_aliases": {1 + len(pieces): 0}}
     return call(
         functools.partial(widen_kernel, n_x, n_y, share),
         "widen",
         jax.ShapeDtypeStruct((2 * rows, 2 * half), F32),
         rows * half * 2,
         rows * half * 12,
-        in_specs=[pl.BlockSpec(memory_space=pltpu.SMEM), array, array] + [pl.BlockSpec(memory_space=pltpu.HBM)] * len(more),
+        in_specs=[pl.BlockSpec(memory_space=pltpu.SMEM)]
+        + [array] * len(pieces)
+        + [pl.BlockSpec(memory_space=pltpu.HBM)] * len(more),
         out_specs=pl.BlockSpec(memory_space=pltpu.HBM),
         scratch_shapes=[
             pltpu.VMEM((rows, 2 * half), F32),
@@ -308,7 +314,7 @@
         ],
         vmem=16,
         **alias,
-    )(at, *sides, *more)
+    )(at, *pieces, *more)
 
 
 def after(x, *others):
@@ -398,17 +404,6 @@
     )(after(features, dpre))
     feat_in = lax.all_to_all(after(cut, far), "tz", split_axis=0, concat_axis=0, tiled=True)
 
-    look, bias = call(
-        lookup_kernel,
-        "lookups",
-        (shape((N_Z, count, E), BF), shape((2 * n_bias, E), BF)),
-        2 * N_Z * n_s * width * hidden,
-        7 * 10**6,
-        scratch_shapes=[pltpu.VMEM((N_Z * n_s, hidden), BF)],
-        vmem=16,
-    )(*sources, w_first)
-    feat_in = after(feat_in, look)
-
     w_part = call(
         functools.partial(w_kernel, n_plane),
         "w_part",
@@ -418,7 +413,15 @@
         in_specs=[scalar] + [array] * 5,
         vmem=12,
     )(my_z, feat_in, *sources)
-    look = after(look, w_part)
+    look, bias = call(
+        lookup_kernel,
+        "lookups",
+        (shape((N_Z, count, E), BF), shape((2 * n_bias, E), BF)),
+        2 * N_Z * n_s * width * hidden,
+        7 * 10**6,
+        scratch_shapes=[pltpu.VMEM((N_Z * n_s, hidden), BF)],
+        vmem=16,
+    )(*sources[:3], after(sources[3], w_part), w_first)
     w_part = lax.all_to_all(w_part, plane, split_axis=0, concat_axis=0, tiled=True)
 
     n_rows = 2 * seg + ADM_DEV + 16 + 2 * n_bias
@@ -441,12 +444,20 @@
     w_own = jnp.sum(w_part.astype(F32), axis=0).astype(BF)
     chunks = lax.all_to_all(chunks, plane, split_axis=0, concat_axis=0, tiled=True)
 
-    w_two = jnp.concatenate([w_own, swap(w_own, "tz", 2)], axis=0)
-    w_four = jnp.concatenate([w_two, swap(w_two, "tz", 1)], axis=0)
-    sides = [w_four[:, : hidden // 2], w_four[:, hidden // 2 :]]
-    over_y = [("ty", k) for k in doubling(n_y)]
-    over_x = [("x", k) for k in doubling(n_dp // n_core)]
-    last = sides
+    w_far, w_near = swap(w_own, "tz", 2), swap(w_own, "tz", 1)
+    w_four = jnp.concatenate([w_own, w_far, w_near, swap(w_far, "tz", 1)], axis=0)
+    n_x = n_dp // n_core
+    over_y = [("ty", 1, k) for k in doubling(n_y)]
+    over_x = [("x", n_y, k) for k in doubling(n_x)]
+    side = hidden // 2
+    halves = []
+    for own, steps in ((w_four[:, :side], over_y + over_x), (w_four[:, side:], over_x + over_y)):
+        pieces = {0: own}
+        for axis, stride, k in steps:
+            pieces.update({key ^ (k * stride): swap(piece, axis, k) for key, piece in pieces.items()})
+        halves.append(pieces)
+    late = n_x * n_y - 1
+    through = [halves[0][n_y - 1], halves[1][late + 1 - n_y]]
 
     def sums(table, chunks):
         outs = (shape((QROWS_DEV, E), F32), shape((n_bias, E), F32), shape((ADM_DEV, E), F32))
@@ -459,20 +470,18 @@
             vmem=28,
         )(chunks)
 
-    for i, steps in enumerate(zip(over_y + over_x, over_x + over_y)):
-        moved = [swap(side, *step) for side, step in zip(sides, steps)]
-        sides = [jnp.concatenate(pair, axis=0) for pair in zip(sides, moved)]
-        last = sides if i == len(over_x + over_y) - 2 else last
-    chunks = after(chunks, *last)
+    chunks = after(chunks, *through)
     q_grad, b_grad, adm_grad = sums(0, chunks)
-    (r_grad,) = sums(1, after(chunks, q_grad))
-    sides = [after(side, r_grad) for side in sides]
-    others = [swap(side, "core", 1) for side in sides]
+    others = [{key: swap(piece, "core", 1) for key, piece in pieces.items() if key != late} for pieces in halves]
+    early = [piece for other in others for piece in other.values()] + [pieces[late] for pieces in halves]
+    (r_grad,) = sums(1, after(chunks, q_grad, *early))
+    for pieces, other in zip(halves, others):
+        other[late] = after(swap(pieces[late], "core", 1), r_grad)
     at = jnp.stack([lax.axis_index(name) for name in ("x", "core", "tz", "ty")]).astype(jnp.int32)
-    n_x = n_dp // n_core
-    w_grad = widen(n_x, n_y, share, at, [after(side, r_grad) for side in sides], None)
+    order = range(n_x * n_y)
+    w_grad = widen(n_x, n_y, share, at, [pieces[i] for pieces in halves for i in order], None)
     flip = at ^ jnp.array([0, 1, 0, 0], jnp.int32)
-    w_grad = widen(n_x, n_y, share, flip, others, w_grad)
+    w_grad = widen(n_x, n_y, share, flip, [other[i] for other in others for i in order], w_grad)
     return (w_grad, b_grad.reshape(hidden), adm_grad, q_grad, r_grad)
 
 

time: 131 us -> 131 us (level)
  other arithmetic: 5.69 us -> 1.78 us
  starting transfers between devices: 29.6 us -> 31.9 us
  Pallas kernels: 38.9 us -> 40.5 us
    concatenate x6 -> x1, other arithmetic: 3.94 us -> 0.03 us  [local(): jnp.concatenate([w_own, w_far, w_near, swap(w_far, 'tz', 1)], axis=0)]
    ppermute x14 -> x23, waiting for transfers between devices: 48.1 us -> 51.9 us  [swap(): return lax.ppermute(x, axis, [(i, i ^ k) for i in range(n)])]
    all_to_all x1, waiting for transfers between devices: 3.41 us -> 0.01 us  [local(): lax.all_to_all(w_part, plane, split_axis=0, concat_axis=0, tiled=True)]
    ppermute x14 -> x23, starting transfers between devices: 18.5 us -> 20.4 us  [swap(): return lax.ppermute(x, axis, [(i, i ^ k) for i in range(n)])]
    pallas_call x1, Pallas kernels: 11.1 us -> 12.7 us  [local(): call(functools.partial(bucket_kernel, n_plane, cap), 'buckets', shape((n_...]
    unnamed x12 -> x10, local copies, waits for them, and re-layouts: 3.52 us -> 3.44 us
  transfers between devices with their start and end apart: 17 -> 26, of which waited for: 10 -> 11; matrix products, arithmetic and copies ran while one was open for 2% -> 0% of each run, Pallas kernels for 26% -> 28%
where the time goes in v10:
time: 131 us; the launch traced here: 130 us
  waiting for transfers between devices  51.9 us (40%)
  Pallas kernels  40.5 us (31%)
  starting transfers between devices  31.9 us (24%)
  local copies, waits for them, and re-layouts  3.48 us (3%)
  other arithmetic  1.78 us (1%)
    ppermute x23, waiting for transfers between devices, swap(): return lax.ppermute(x, axis, [(i, i ^ k) for i in range(n)])  51.9 us
    ppermute x23, starting transfers between devices, swap(): return lax.ppermute(x, axis, [(i, i ^ k) for i in range(n)])  20.4 us
    pallas_call x1, Pallas kernels, local(): call(functools.partial(bucket_kernel, n_plane, cap), 'buckets', shape((n_...  12.7 us
    pallas_call x2, Pallas kernels, sums(): call(functools.partial(sums_kernel, n_plane, seg, n_bias, table), ('q_sum...  10.8 us
    pallas_call x2, Pallas kernels, widen(): call(functools.partial(widen_kernel, n_x, n_y, share), 'widen', jax.Shape...  6.33 us
    pallas_call x1, Pallas kernels, local(): call(dpre_kernel, 'dpre', shape((n_s, hidden), BF), 2 * n_s * width * hid...  4.77 us
    all_to_all x1, starting transfers between devices, local(): lax.all_to_all(chunks, plane, split_axis=0, concat_axis=0, tiled=True)  4.2 us
    all_to_all x1, starting transfers between devices, local(): lax.all_to_all(w_part, plane, split_axis=0, concat_axis=0, tiled=True)  3.75 us
  transfers between devices with their start and end apart: 26, of which 11 were waited for; matrix products, arithmetic and copies ran while one was open for 0% of the time, Pallas kernels for 28%

profile of v10, /device:TPU:0, one launch (start us, length us, event | category | flops | bytes accessed | tf_op | source)
XLA Modules:
  0.0 130.5 jit_solution(11177134549884258032)
XLA Ops:
  2.2 4.1 %collective-permute-start = (bf16[2,128,128]{2,1,0:T(8,128)(2,1)S(1)}, bf16[2,128,128]{2,1,0:T(8,128)(2,1)S(1)}, u32[]{:S(2)}, u32[]{:S(2)}) collective-permute-start(bf16[2,128,128]{2,1,0:T(8,128)(2,1)S(1)} %get-tuple-element.30), channel_id=1, source_target_pairs={{0,4},{2,6},{4,0},{6,2},{1,5},{3,7},{5,1},{7,3},{8,12},{10,14},{12... | collective-permute-start | bytes 196616 | tf_op jit(solution)/shard_map/ppermute | solution.py:267
  6.3 1.6 %collective-permute-start.1 = (bf16[128,128]{1,0:T(8,128)(2,1)S(1)}, bf16[128,128]{1,0:T(8,128)(2,1)S(1)}, u32[]{:S(2)}, u32[]{:S(2)}) collective-permute-start(bf16[128,128]{1,0:T(8,128)(2,1)S(1)} %get-tuple-element.31), channel_id=1, source_target_pairs={{0,2},{2,0},{4,6},{6,4},{1,3},{3,1},{5,7},{7,5},{8,10},{10,8},{12,... | collective-permute-start | bytes 98312 | tf_op jit(solution)/shard_map/ppermute | solution.py:267
  7.8 4.8 %dpre.1.d0_ref = bf16[128,1024]{1,0:T(8,128)(2,1)} custom-call(bf16[128,2048]{1,0:T(8,128)(2,1)} %x_ref.1, bf16[2048,1024]{1,0:T(8,128)(2,1)} %w_ref.3, f32[1,1024]{1,0:T(1,128)} %bitcast.38, bf16[128,1024]{1,0:T(8,128)(2,1)} %g_ref.1), custom_call_target="tpu_custom_call" | custom-call | flops 536870912 | bytes 6000000 | tf_op jit(solution)/shard_map/dpre/pallas_call | solution.py:370
  15.9 9.8 %collective-permute-done.4.last_ref = bf16[128,128]{1,0:T(8,128)(2,1)S(1)} collective-permute-done((bf16[128,128]{1,0:T(8,128)(2,1)S(1)}, bf16[128,128]{1,0:T(8,128)(2,1)S(1)}, u32[]{:S(2)}, u32[]{:S(2)}) %collective-permute-start.4) | collective-permute-done | bytes 32800 | tf_op jit(solution)/shard_map/ppermute | solution.py:267
  27.1 3.5 %all-to-all-start = ((bf16[4,128,512]{2,1,0:T(8,128)(2,1)}), bf16[4,128,512]{2,1,0:T(8,128)(2,1)S(1)}, u32[]{:S(2)}, u32[]{:S(2)}) async-start(bf16[4,128,512]{2,1,0:T(8,128)(2,1)} %cut.1), calls=%async_computation | async-start | bytes 1048576 | tf_op jit(solution)/shard_map/all_to_all | solution.py:405
  30.6 2.0 %collective-permute-start.5 = (bf16[128,1024]{1,0:T(8,128)(2,1)S(1)}, bf16[128,1024]{1,0:T(8,128)(2,1)S(1)}, u32[]{:S(2)}, u32[]{:S(2)}) collective-permute-start(bf16[128,1024]{1,0:T(8,128)(2,1)S(1)} %collective-permute-done.2.d2_ref), channel_id=1, source_target_pairs={{0,2},{2,0},{4,6},{6,4},{1,3},{3,1},{5,7},{7,5},{8,10},{10,8},{12,... | collective-permute-start | bytes 786440 | tf_op jit(solution)/shard_map/ppermute | solution.py:267
  32.6 13.0 %collective-permute-done.5.d3_ref = bf16[128,1024]{1,0:T(8,128)(2,1)S(1)} collective-permute-done((bf16[128,1024]{1,0:T(8,128)(2,1)S(1)}, bf16[128,1024]{1,0:T(8,128)(2,1)S(1)}, u32[]{:S(2)}, u32[]{:S(2)}) %collective-permute-start.5) | collective-permute-done | bytes 262176 | tf_op jit(solution)/shard_map/ppermute | solution.py:267
  45.6 1.7 %w_part.1 = bf16[8,64,1024]{2,1,0:T(8,128)(2,1)} custom-call(s32[1]{0:T(128)} %bitcast.2.z_ref, bf16[4,128,512]{2,1,0:T(8,128)(2,1)S(1)} %all-to-all-done.x_ref, bf16[128,1024]{1,0:T(8,128)(2,1)S(1)} %copy-done.3, bf16[128,1024]{1,0:T(8,128)(2,1)S(1)} %collective-permute-done.3.d1_ref, bf16[128,1024]{1,0:T(8,128)(2,1)S(1)} %collective-permute-done.2.d2_ref, ...), custom_call_target="tpu_custom_call" | custom-call | flops 536870912 | bytes 3000000 | tf_op jit(solution)/shard_map/w_part/pallas_call | solution.py:407
  47.3 3.7 %all-to-all-start.1 = ((bf16[8,64,1024]{2,1,0:T(8,128)(2,1)}), bf16[8,64,1024]{2,1,0:T(8,128)(2,1)S(1)}, u32[]{:S(2)}, u32[]{:S(2)}) async-start(bf16[8,64,1024]{2,1,0:T(8,128)(2,1)} %w_part.1), calls=%async_computation.1 | async-start | bytes 2097152 | tf_op jit(solution)/shard_map/all_to_all | solution.py:425
  51.1 2.2 %copy-done = bf16[2048,1024]{1,0:T(8,128)(2,1)S(1)} copy-done((bf16[2048,1024]{1,0:T(8,128)(2,1)S(1)}, bf16[2048,1024]{1,0:T(8,128)(2,1)}, u32[]{:S(2)}) %copy-start) | copy-done | bytes 4194328
  53.2 2.4 %lookups.1 = (bf16[4,2048,128]{2,1,0:T(8,128)(2,1)S(1)}, bf16[16,128]{1,0:T(8,128)(2,1)S(1)}) custom-call(bf16[128,1024]{1,0:T(8,128)(2,1)S(1)} %copy-done.3, bf16[128,1024]{1,0:T(8,128)(2,1)S(1)} %collective-permute-done.3.d1_ref, bf16[128,1024]{1,0:T(8,128)(2,1)S(1)} %collective-permute-done.2.d2_ref, bf16[128,1024]{1,0:T(8,128)(2,1)S(1)} %collective-permute-done.5.d3_ref, ...), custom_call_target="tpu_custom_call" | custom-call | flops 2147483648 | bytes 7000000 | tf_op jit(solution)/shard_map/lookups/pallas_call | solution.py:416
  55.6 12.7 %buckets.1 = bf16[8,928,128]{2,1,0:T(8,128)(2,1)S(1)} custom-call(bf16[4,2048,128]{2,1,0:T(8,128)(2,1)S(1)} %get-tuple-element.40.look_ref, s32[3,4,16,128]{3,2,1,0:T(8,128)S(1)} %get-tuple-element.36.slot_ref, f32[4,128,128]{2,1,0:T(8,128)S(1)} %get-tuple-element.41.down_ref, bf16[16,128]{1,0:T(8,128)(2,1)S(1)} %get-tuple-element.42.bias_ref), custom_call_target="tpu_custom_call" | custom-call | flops 15000000512 | bytes 40000000 | tf_op jit(solution)/shard_map/buckets/pallas_call | solution.py:428
  69.6 4.2 %all-to-all-start.2 = ((bf16[8,928,128]{2,1,0:T(8,128)(2,1)}), bf16[8,928,128]{2,1,0:T(8,128)(2,1)S(1)}, u32[]{:S(2)}, u32[]{:S(2)}) async-start(bf16[8,928,128]{2,1,0:T(8,128)(2,1)} %copy-done.2), calls=%async_computation.2 | async-start | bytes 3801088 | tf_op jit(solution)/shard_map/all_to_all | solution.py:445
  74.0 2.5 %collective-permute-start.6 = (bf16[64,1024]{1,0:T(8,128)(2,1)S(1)}, bf16[64,1024]{1,0:T(8,128)(2,1)S(1)}, u32[]{:S(2)}, u32[]{:S(2)}) collective-permute-start(bf16[64,1024]{1,0:T(8,128)(2,1)S(1)} %reduce_sum.12), channel_id=1, source_target_pairs={{0,4},{2,6},{4,0},{6,2},{1,5},{3,7},{5,1},{7,3},{8,12},{10,14},{12... | collective-permute-start | bytes 393224 | tf_op jit(solution)/shard_map/ppermute | solution.py:267
  77.0 6.6 %collective-permute-done.6 = bf16[64,1024]{1,0:T(8,128)(2,1)S(1)} collective-permute-done((bf16[64,1024]{1,0:T(8,128)(2,1)S(1)}, bf16[64,1024]{1,0:T(8,128)(2,1)S(1)}, u32[]{:S(2)}, u32[]{:S(2)}) %collective-permute-start.6) | collective-permute-done | bytes 131104 | tf_op jit(solution)/shard_map/ppermute | solution.py:267
  84.8 4.1 %collective-permute-done.8 = bf16[64,1024]{1,0:T(8,128)(2,1)S(1)} collective-permute-done((bf16[64,1024]{1,0:T(8,128)(2,1)S(1)}, bf16[64,1024]{1,0:T(8,128)(2,1)S(1)}, u32[]{:S(2)}, u32[]{:S(2)}) %collective-permute-start.8) | collective-permute-done | bytes 131104 | tf_op jit(solution)/shard_map/ppermute | solution.py:267
  89.0 1.7 %collective-permute-start.19 = (bf16[256,512]{1,0:T(8,128)(2,1)S(1)}, bf16[256,512]{1,0:T(8,128)(2,1)S(1)}, u32[]{:S(2)}, u32[]{:S(2)}) collective-permute-start(bf16[256,512]{1,0:T(8,128)(2,1)S(1)} %get-tuple-element.55.refs_4_), channel_id=1, source_target_pairs={{0,1},{1,0},{2,3},{3,2},{4,5},{5,4},{6,7},{7,6},{8,9},{9,8},{10,11... | collective-permute-start | bytes 786440 | tf_op jit(solution)/shard_map/ppermute | solution.py:267
  93.2 10.3 %collective-permute-done.19.refs_5_ = bf16[256,512]{1,0:T(8,128)(2,1)S(1)} collective-permute-done((bf16[256,512]{1,0:T(8,128)(2,1)S(1)}, bf16[256,512]{1,0:T(8,128)(2,1)S(1)}, u32[]{:S(2)}, u32[]{:S(2)}) %collective-permute-start.19) | collective-permute-done | bytes 262176 | tf_op jit(solution)/shard_map/ppermute | solution.py:267
  104.1 4.7 %collective-permute-done.10.refs_1_ = bf16[256,512]{1,0:T(8,128)(2,1)} collective-permute-done((bf16[256,512]{1,0:T(8,128)(2,1)S(1)}, bf16[256,512]{1,0:T(8,128)(2,1)}, u32[]{:S(2)}, u32[]{:S(2)}) %collective-permute-start.10) | collective-permute-done | bytes 262176 | tf_op jit(solution)/shard_map/ppermute | solution.py:267
  109.1 1.5 %collective-permute-start.14 = (bf16[256,512]{1,0:T(8,128)(2,1)}, bf16[256,512]{1,0:T(8,128)(2,1)S(1)}, u32[]{:S(2)}, u32[]{:S(2)}) collective-permute-start(bf16[256,512]{1,0:T(8,128)(2,1)} %collective-permute-done.10.refs_1_), channel_id=1, source_target_pairs={{0,16},{16,0},{1,17},{17,1},{2,18},{18,2},{3,19},{19,3},{4,20},{20... | collective-permute-start | bytes 786440 | tf_op jit(solution)/shard_map/ppermute | solution.py:267
  111.2 5.4 %q_sums.1 = (f32[4096,128]{1,0:T(8,128)}, f32[8,128]{1,0:T(8,128)}, f32[128,128]{1,0:T(8,128)}) custom-call(bf16[8,928,128]{2,1,0:T(8,128)(2,1)S(1)} %all-to-all-done.2.in_ref), custom_call_target="tpu_custom_call" | custom-call | flops 4000000000 | bytes 4000000 | tf_op jit(solution)/shard_map/q_sums/pallas_call | solution.py:464
  118.6 3.5 %widen.2.refs_8_ = f32[2048,1024]{1,0:T(8,128)} custom-call(s32[4]{0:T(128)S(1)} %get-tuple-element.54.at_ref, bf16[256,512]{1,0:T(8,128)(2,1)S(1)} %get-tuple-element.56.refs_0_, bf16[256,512]{1,0:T(8,128)(2,1)} %collective-permute-done.10.refs_1_, bf16[256,512]{1,0:T(8,128)(2,1)} %collective-permute-done.12.refs_2_, ...), custom_call_target="tpu_custom_call" | custom-call | flops 1048576 | bytes 6291456 | tf_op jit(solution)/shard_map/widen/pallas_call | solution.py:301
  122.1 5.4 %r_sums.1 = f32[4096,128]{1,0:T(8,128)} custom-call(bf16[8,928,128]{2,1,0:T(8,128)(2,1)S(1)} %all-to-all-done.2.in_ref), custom_call_target="tpu_custom_call" | custom-call | flops 4000000000 | bytes 4000000 | tf_op jit(solution)/shard_map/r_sums/pallas_call | solution.py:464
  127.5 2.8 %widen.3 = f32[2048,1024]{1,0:T(8,128)} custom-call(s32[4]{0:T(128)S(1)} %get-tuple-element.53.at_ref, bf16[256,512]{1,0:T(8,128)(2,1)S(1)} %collective-permute-done.9.refs_0_, bf16[256,512]{1,0:T(8,128)(2,1)S(1)} %collective-permute-done.11.refs_1_, bf16[256,512]{1,0:T(8,128)(2,1)S(1)} %collective-permute-done.13.refs_2_, ...), custom_call_target="tpu_custom_call", output_to_operand_aliasing={{}: (9, {})} | custom-call | flops 1048576 | bytes 6291456 | tf_op jit(solution)/shard_map/widen/pallas_call | solution.py:301
  (56 shorter events, 15.3 us)
Async XLA Ops:
  2.2 10.5 %collective-permute-start = (bf16[2,128,128]{2,1,0:T(8,128)(2,1)S(1)}, bf16[2,128,128]{2,1,0:T(8,128)(2,1)S(1)}, u32[]{:S(2)}, u32[]{:S(2)}) collective-permute-start(bf16[2,128,128]{2,1,0:T(8,128)(2,1)S(1)} %get-tuple-element.30), channel_id=1, source_target_pairs={{0,4},{2,6},{4,0},{6,2},{1,5},{3,7},{5,1},{7,3},{8,12},{10,14},{12... | collective-permute-start | bytes 196616 | tf_op jit(solution)/shard_map/ppermute | solution.py:267
  6.3 6.4 %collective-permute-start.1 = (bf16[128,128]{1,0:T(8,128)(2,1)S(1)}, bf16[128,128]{1,0:T(8,128)(2,1)S(1)}, u32[]{:S(2)}, u32[]{:S(2)}) collective-permute-start(bf16[128,128]{1,0:T(8,128)(2,1)S(1)} %get-tuple-element.31), channel_id=1, source_target_pairs={{0,2},{2,0},{4,6},{6,4},{1,3},{3,1},{5,7},{7,5},{8,10},{10,8},{12,... | collective-permute-start | bytes 98312 | tf_op jit(solution)/shard_map/ppermute | solution.py:267
  12.6 14.0 %collective-permute-start.3 = (bf16[128,1024]{1,0:T(8,128)(2,1)}, bf16[128,1024]{1,0:T(8,128)(2,1)S(1)}, u32[]{:S(2)}, u32[]{:S(2)}) collective-permute-start(bf16[128,1024]{1,0:T(8,128)(2,1)} %dpre.1.d0_ref), channel_id=1, source_target_pairs={{0,2},{2,0},{4,6},{6,4},{1,3},{3,1},{5,7},{7,5},{8,10},{10,8},{12,... | collective-permute-start | bytes 786440 | tf_op jit(solution)/shard_map/ppermute | solution.py:267
  13.1 14.0 %collective-permute-start.2 = (bf16[128,1024]{1,0:T(8,128)(2,1)}, bf16[128,1024]{1,0:T(8,128)(2,1)S(1)}, u32[]{:S(2)}, u32[]{:S(2)}) collective-permute-start(bf16[128,1024]{1,0:T(8,128)(2,1)} %dpre.1.d0_ref), channel_id=1, source_target_pairs={{0,4},{2,6},{4,0},{6,2},{1,5},{3,7},{5,1},{7,3},{8,12},{10,14},{12... | collective-permute-start | bytes 786440 | tf_op jit(solution)/shard_map/ppermute | solution.py:267
  13.9 11.9 %collective-permute-start.4 = (bf16[128,128]{1,0:T(8,128)(2,1)S(1)}, bf16[128,128]{1,0:T(8,128)(2,1)S(1)}, u32[]{:S(2)}, u32[]{:S(2)}) collective-permute-start(bf16[128,128]{1,0:T(8,128)(2,1)S(1)} %slice_bitcast_fusion), channel_id=1, source_target_pairs={{0,2},{2,0},{4,6},{6,4},{1,3},{3,1},{5,7},{7,5},{8,10},{10,8},{12,... | collective-permute-start | bytes 98312 | tf_op jit(solution)/shard_map/ppermute | solution.py:267
  27.1 18.5 %all-to-all-start = ((bf16[4,128,512]{2,1,0:T(8,128)(2,1)}), bf16[4,128,512]{2,1,0:T(8,128)(2,1)S(1)}, u32[]{:S(2)}, u32[]{:S(2)}) async-start(bf16[4,128,512]{2,1,0:T(8,128)(2,1)} %cut.1), calls=%async_computation | async-start | bytes 1048576 | tf_op jit(solution)/shard_map/all_to_all | solution.py:405
  30.6 15.0 %collective-permute-start.5 = (bf16[128,1024]{1,0:T(8,128)(2,1)S(1)}, bf16[128,1024]{1,0:T(8,128)(2,1)S(1)}, u32[]{:S(2)}, u32[]{:S(2)}) collective-permute-start(bf16[128,1024]{1,0:T(8,128)(2,1)S(1)} %collective-permute-done.2.d2_ref), channel_id=1, source_target_pairs={{0,2},{2,0},{4,6},{6,4},{1,3},{3,1},{5,7},{7,5},{8,10},{10,8},{12,... | collective-permute-start | bytes 786440 | tf_op jit(solution)/shard_map/ppermute | solution.py:267
  47.3 22.3 %all-to-all-start.1 = ((bf16[8,64,1024]{2,1,0:T(8,128)(2,1)}), bf16[8,64,1024]{2,1,0:T(8,128)(2,1)S(1)}, u32[]{:S(2)}, u32[]{:S(2)}) async-start(bf16[8,64,1024]{2,1,0:T(8,128)(2,1)} %w_part.1), calls=%async_computation.1 | async-start | bytes 2097152 | tf_op jit(solution)/shard_map/all_to_all | solution.py:425
  69.6 39.5 %all-to-all-start.2 = ((bf16[8,928,128]{2,1,0:T(8,128)(2,1)}), bf16[8,928,128]{2,1,0:T(8,128)(2,1)S(1)}, u32[]{:S(2)}, u32[]{:S(2)}) async-start(bf16[8,928,128]{2,1,0:T(8,128)(2,1)} %copy-done.2), calls=%async_computation.2 | async-start | bytes 3801088 | tf_op jit(solution)/shard_map/all_to_all | solution.py:445
  74.0 9.6 %collective-permute-start.6 = (bf16[64,1024]{1,0:T(8,128)(2,1)S(1)}, bf16[64,1024]{1,0:T(8,128)(2,1)S(1)}, u32[]{:S(2)}, u32[]{:S(2)}) collective-permute-start(bf16[64,1024]{1,0:T(8,128)(2,1)S(1)} %reduce_sum.12), channel_id=1, source_target_pairs={{0,4},{2,6},{4,0},{6,2},{1,5},{3,7},{5,1},{7,3},{8,12},{10,14},{12... | collective-permute-start | bytes 393224 | tf_op jit(solution)/shard_map/ppermute | solution.py:267
  76.5 8.3 %collective-permute-start.7 = (bf16[64,1024]{1,0:T(8,128)(2,1)S(1)}, bf16[64,1024]{1,0:T(8,128)(2,1)S(1)}, u32[]{:S(2)}, u32[]{:S(2)}) collective-permute-start(bf16[64,1024]{1,0:T(8,128)(2,1)S(1)} %reduce_sum.12), channel_id=1, source_target_pairs={{0,2},{2,0},{4,6},{6,4},{1,3},{3,1},{5,7},{7,5},{8,10},{10,8},{12,... | collective-permute-start | bytes 393224 | tf_op jit(solution)/shard_map/ppermute | solution.py:267
  89.0 14.4 %collective-permute-start.19 = (bf16[256,512]{1,0:T(8,128)(2,1)S(1)}, bf16[256,512]{1,0:T(8,128)(2,1)S(1)}, u32[]{:S(2)}, u32[]{:S(2)}) collective-permute-start(bf16[256,512]{1,0:T(8,128)(2,1)S(1)} %get-tuple-element.55.refs_4_), channel_id=1, source_target_pairs={{0,1},{1,0},{2,3},{3,2},{4,5},{5,4},{6,7},{7,6},{8,9},{9,8},{10,11... | collective-permute-start | bytes 786440 | tf_op jit(solution)/shard_map/ppermute | solution.py:267
  90.7 12.9 %collective-permute-start.16 = (bf16[256,512]{1,0:T(8,128)(2,1)S(1)}, bf16[256,512]{1,0:T(8,128)(2,1)}, u32[]{:S(2)}, u32[]{:S(2)}) collective-permute-start(bf16[256,512]{1,0:T(8,128)(2,1)S(1)} %get-tuple-element.55.refs_4_), channel_id=1, source_target_pairs={{0,16},{16,0},{1,17},{17,1},{2,18},{18,2},{3,19},{19,3},{4,20},{20... | collective-permute-start | bytes 786440 | tf_op jit(solution)/shard_map/ppermute | solution.py:267
  92.2 16.5 %collective-permute-start.10 = (bf16[256,512]{1,0:T(8,128)(2,1)S(1)}, bf16[256,512]{1,0:T(8,128)(2,1)}, u32[]{:S(2)}, u32[]{:S(2)}) collective-permute-start(bf16[256,512]{1,0:T(8,128)(2,1)S(1)} %get-tuple-element.56.refs_0_), channel_id=1, source_target_pairs={{0,1},{1,0},{2,3},{3,2},{4,5},{5,4},{6,7},{7,6},{8,9},{9,8},{10,11... | collective-permute-start | bytes 786440 | tf_op jit(solution)/shard_map/ppermute | solution.py:267
  92.8 16.3 %collective-permute-start.17 = (bf16[256,512]{1,0:T(8,128)(2,1)S(1)}, bf16[256,512]{1,0:T(8,128)(2,1)S(1)}, u32[]{:S(2)}, u32[]{:S(2)}) collective-permute-start(bf16[256,512]{1,0:T(8,128)(2,1)S(1)} %get-tuple-element.55.refs_4_), channel_id=1, source_target_pairs={{0,8},{8,0},{1,9},{9,1},{2,10},{10,2},{3,11},{11,3},{4,12},{12,4},... | collective-permute-start | bytes 786440 | tf_op jit(solution)/shard_map/ppermute | solution.py:267
  92.8 16.3 %collective-permute-start.12 = (bf16[256,512]{1,0:T(8,128)(2,1)S(1)}, bf16[256,512]{1,0:T(8,128)(2,1)}, u32[]{:S(2)}, u32[]{:S(2)}) collective-permute-start(bf16[256,512]{1,0:T(8,128)(2,1)S(1)} %get-tuple-element.56.refs_0_), channel_id=1, source_target_pairs={{0,16},{16,0},{1,17},{17,1},{2,18},{18,2},{3,19},{19,3},{4,20},{20... | collective-permute-start | bytes 786440 | tf_op jit(solution)/shard_map/ppermute | solution.py:267
  103.5 7.2 %collective-permute-start.9 = (bf16[256,512]{1,0:T(8,128)(2,1)S(1)}, bf16[256,512]{1,0:T(8,128)(2,1)S(1)}, u32[]{:S(2)}, u32[]{:S(2)}) collective-permute-start(bf16[256,512]{1,0:T(8,128)(2,1)S(1)} %get-tuple-element.56.refs_0_), channel_id=1, source_target_pairs={{0,8},{8,0},{1,9},{9,1},{2,10},{10,2},{3,11},{11,3},{4,12},{12,4},... | collective-permute-start | bytes 786440 | tf_op jit(solution)/shard_map/ppermute | solution.py:267
  103.7 7.1 %collective-permute-start.20 = (bf16[256,512]{1,0:T(8,128)(2,1)S(1)}, bf16[256,512]{1,0:T(8,128)(2,1)S(1)}, u32[]{:S(2)}, u32[]{:S(2)}) collective-permute-start(bf16[256,512]{1,0:T(8,128)(2,1)S(1)} %collective-permute-done.19.refs_5_), channel_id=1, source_target_pairs={{0,8},{8,0},{1,9},{9,1},{2,10},{10,2},{3,11},{11,3},{4,12},{12,4},... | collective-permute-start | bytes 786440 | tf_op jit(solution)/shard_map/ppermute | solution.py:267
  108.7 8.2 %collective-permute-start.21 = (bf16[256,512]{1,0:T(8,128)(2,1)}, bf16[256,512]{1,0:T(8,128)(2,1)}, u32[]{:S(2)}, u32[]{:S(2)}) collective-permute-start(bf16[256,512]{1,0:T(8,128)(2,1)} %collective-permute-done.16.refs_6_), channel_id=1, source_target_pairs={{0,1},{1,0},{2,3},{3,2},{4,5},{5,4},{6,7},{7,6},{8,9},{9,8},{10,11... | collective-permute-start | bytes 786440 | tf_op jit(solution)/shard_map/ppermute | solution.py:267
  109.1 7.8 %collective-permute-start.18 = (bf16[256,512]{1,0:T(8,128)(2,1)}, bf16[256,512]{1,0:T(8,128)(2,1)S(1)}, u32[]{:S(2)}, u32[]{:S(2)}) collective-permute-start(bf16[256,512]{1,0:T(8,128)(2,1)} %collective-permute-done.16.refs_6_), channel_id=1, source_target_pairs={{0,8},{8,0},{1,9},{9,1},{2,10},{10,2},{3,11},{11,3},{4,12},{12,4},... | collective-permute-start | bytes 786440 | tf_op jit(solution)/shard_map/ppermute | solution.py:267
  109.1 8.9 %collective-permute-start.14 = (bf16[256,512]{1,0:T(8,128)(2,1)}, bf16[256,512]{1,0:T(8,128)(2,1)S(1)}, u32[]{:S(2)}, u32[]{:S(2)}) collective-permute-start(bf16[256,512]{1,0:T(8,128)(2,1)} %collective-permute-done.10.refs_1_), channel_id=1, source_target_pairs={{0,16},{16,0},{1,17},{17,1},{2,18},{18,2},{3,19},{19,3},{4,20},{20... | collective-permute-start | bytes 786440 | tf_op jit(solution)/shard_map/ppermute | solution.py:267
  110.6 7.4 %collective-permute-start.11 = (bf16[256,512]{1,0:T(8,128)(2,1)}, bf16[256,512]{1,0:T(8,128)(2,1)S(1)}, u32[]{:S(2)}, u32[]{:S(2)}) collective-permute-start(bf16[256,512]{1,0:T(8,128)(2,1)} %collective-permute-done.10.refs_1_), channel_id=1, source_target_pairs={{0,8},{8,0},{1,9},{9,1},{2,10},{10,2},{3,11},{11,3},{4,12},{12,4},... | collective-permute-start | bytes 786440 | tf_op jit(solution)/shard_map/ppermute | solution.py:267
  118.1 9.4 %collective-permute-start.22 = (bf16[256,512]{1,0:T(8,128)(2,1)}, bf16[256,512]{1,0:T(8,128)(2,1)S(1)}, u32[]{:S(2)}, u32[]{:S(2)}) collective-permute-start(bf16[256,512]{1,0:T(8,128)(2,1)} %collective-permute-done.21.refs_7_), channel_id=1, source_target_pairs={{0,8},{8,0},{1,9},{9,1},{2,10},{10,2},{3,11},{11,3},{4,12},{12,4},... | collective-permute-start | bytes 786440 | tf_op jit(solution)/shard_map/ppermute | solution.py:267
  118.1 9.4 %collective-permute-start.15 = (bf16[256,512]{1,0:T(8,128)(2,1)S(1)}, bf16[256,512]{1,0:T(8,128)(2,1)S(1)}, u32[]{:S(2)}, u32[]{:S(2)}) collective-permute-start(bf16[256,512]{1,0:T(8,128)(2,1)S(1)} %collective-permute-done.14.refs_3_), channel_id=1, source_target_pairs={{0,8},{8,0},{1,9},{9,1},{2,10},{10,2},{3,11},{11,3},{4,12},{12,4},... | collective-permute-start | bytes 786440 | tf_op jit(solution)/shard_map/ppermute | solution.py:267
  (7 other events, 82.0 us)

commit v11 on v10

--- a/solution.py
+++ b/solution.py
@@ -158,7 +158,7 @@
     ).astype(BF)
 
 
-def bucket_kernel(n_dest, cap, look_ref, slot_ref, down_ref, bias_ref, all_ref, mark_ref, out_ref, sems):
+def bucket_kernel(n_dest, cap, look_ref, slot_ref, down_ref, bias_ref, out_ref, mark_ref):
     n_feat, n_s = slot_ref.shape[2:]
     seg = N_Z * cap
     n_mark = -(-seg // E)
@@ -202,7 +202,6 @@
 
     lane = iota((seg, E), 1) & 3
     rows = iota((16, E), 0) >> 2
-    copies = []
     for d in range(n_dest):
         mixed = jnp.where(lane < 2, mark_ref[0, d], mark_ref[1, d])
         if seg % E:
@@ -213,10 +212,6 @@
             marks = jnp.where(rows == j, across[0:16, :], marks)
         out_ref[d, at_mark : at_mark + 16, :] = marks.astype(BF)
         out_ref[d, at_mark + 16 : at_mark + 16 + bias_ref.shape[0], :] = bias_ref[...]
-        copies.append(pltpu.make_async_copy(out_ref.at[d], all_ref.at[d], sems.at[d]))
-        copies[-1].start()
-    for copy in copies:
-        copy.wait()
 
 
 def sums_kernel(n_src, seg, n_bias, table, in_ref, *outs):
@@ -345,27 +340,6 @@
     scalar = pl.BlockSpec(memory_space=pltpu.SMEM)
     array = pl.BlockSpec(memory_space=pltpu.VMEM)
 
-    admit, owner, adm_row, q_shard, q_local, r_shard, r_local = [
-        a.reshape(n_s, n_feat).T for a in (admit, owner, adm_row, q_shard, q_local, r_shard, r_local)
-    ]
-    n_code = N_CODE * n_feat
-    own_codes, near_codes, far_codes = call(
-        functools.partial(codes_kernel, n_y, n_table),
-        "codes",
-        (shape((n_code, n_s), BF), shape((n_code, n_s), BF), shape((2, n_code, n_s), BF)),
-        10**6,
-        2 * 10**5,
-        in_specs=[scalar] + [array] * 3,
-    )(
-        my_z,
-        jnp.where(admit == 0, q_shard * QROWS_DEV + q_local, -1),
-        jnp.where(admit == 0, r_shard * QROWS_DEV + r_local, -1),
-        jnp.where(admit == 1, owner * (ADM_DEV * n_table) + adm_row, -1),
-    )
-    far_codes = swap(far_codes, "tz", 2)
-    near_codes = swap(near_codes, "tz", 1)
-    last_codes = swap(after(far_codes[1], near_codes), "tz", 1)
-
     block = width // 4
     dpre = call(
         dpre_kernel,
@@ -383,11 +357,31 @@
         out_specs=pl.BlockSpec((n_s, hidden), lambda i: (0, 0)),
         scratch_shapes=[pltpu.VMEM((n_s, hidden), F32)],
         vmem=56,
-    )(after(features, own_codes), w_first, b_first.reshape(1, hidden), grad_out)
-    dpre = after(dpre, far_codes, near_codes)
+    )(features, w_first, b_first.reshape(1, hidden), grad_out)
 
     far = swap(dpre, "tz", 2)
     near = swap(dpre, "tz", 1)
+    admit, owner, adm_row, q_shard, q_local, r_shard, r_local = [
+        a.reshape(n_s, n_feat).T for a in (admit, owner, adm_row, q_shard, q_local, r_shard, r_local)
+    ]
+    n_code = N_CODE * n_feat
+    own_codes, near_codes, far_codes = call(
+        functools.partial(codes_kernel, n_y, n_table),
+        "codes",
+        (shape((n_code, n_s), BF), shape((n_code, n_s), BF), shape((2, n_code, n_s), BF)),
+        10**6,
+        2 * 10**5,
+        in_specs=[scalar] + [array] * 3,
+    )(
+        after(my_z, dpre),
+        jnp.where(admit == 0, q_shard * QROWS_DEV + q_local, -1),
+        jnp.where(admit == 0, r_shard * QROWS_DEV + r_local, -1),
+        jnp.where(admit == 1, owner * (ADM_DEV * n_table) + adm_row, -1),
+    )
+    far_codes = swap(far_codes, "tz", 2)
+    near_codes = swap(near_codes, "tz", 1)
+    last_codes = swap(after(far_codes[1], near_codes), "tz", 1)
+
     slots, down = call(
         functools.partial(slots_kernel, n_plane, cap),
         "slots",
@@ -395,14 +389,16 @@
         10**9,
         10**6,
         vmem=12,
-    )(after(own_codes, dpre), near_codes, far_codes, last_codes)
-    far = after(far, near, slots)
+    )(own_codes, near_codes, far_codes, last_codes)
+    far = after(far, near)
     sources = [dpre, near, far, swap(far, "tz", 1)]
 
     cut = call(
         functools.partial(cut_kernel, n_dp), "cut", shape((N_Z, n_s, wide), BF), 10**6, 2 * 10**6, vmem=8
     )(after(features, dpre))
-    feat_in = lax.all_to_all(after(cut, far), "tz", split_axis=0, concat_axis=0, tiled=True)
+    feat_in = lax.all_to_all(after(cut, far, far_codes, near_codes), "tz", split_axis=0, concat_axis=0, tiled=True)
+
+    feat_in = after(feat_in, slots)
 
     w_part = call(
         functools.partial(w_kernel, n_plane),
@@ -431,12 +427,7 @@
         shape((n_plane, n_rows, E), BF),
         15 * 10**9,
         4 * 10**7,
-        out_specs=pl.BlockSpec(memory_space=pltpu.HBM),
-        scratch_shapes=[
-            pltpu.VMEM((2, n_plane, seg, E), F32),
-            pltpu.VMEM((n_plane, n_rows, E), BF),
-            pltpu.SemaphoreType.DMA((n_plane,)),
-        ],
+        scratch_shapes=[pltpu.VMEM((2, n_plane, seg, E), F32)],
         vmem=28,
     )(look, slots, down, bias)
 
@@ -450,15 +441,6 @@
     over_y = [("ty", 1, k) for k in doubling(n_y)]
     over_x = [("x", n_y, k) for k in doubling(n_x)]
     side = hidden // 2
-    halves = []
-    for own, steps in ((w_four[:, :side], over_y + over_x), (w_four[:, side:], over_x + over_y)):
-        pieces = {0: own}
-        for axis, stride, k in steps:
-            pieces.update({key ^ (k * stride): swap(piece, axis, k) for key, piece in pieces.items()})
-        halves.append(pieces)
-    late = n_x * n_y - 1
-    through = [halves[0][n_y - 1], halves[1][late + 1 - n_y]]
-
     def sums(table, chunks):
         outs = (shape((QROWS_DEV, E), F32), shape((n_bias, E), F32), shape((ADM_DEV, E), F32))
         return call(
@@ -470,13 +452,24 @@
             vmem=28,
         )(chunks)
 
-    chunks = after(chunks, *through)
     q_grad, b_grad, adm_grad = sums(0, chunks)
+    late = n_x * n_y - 1
+    halves, through = [], []
+    for own, steps in ((w_four[:, :side], over_y + over_x), (w_four[:, side:], over_x + over_y)):
+        pieces = {0: own}
+        for axis, stride, k in steps:
+            last = late ^ (k * stride)
+            if last in pieces:
+                pieces[last] = after(pieces[last], q_grad)
+            pieces.update({key ^ (k * stride): swap(piece, axis, k) for key, piece in pieces.items()})
+        pieces.update({key: after(piece, q_grad) for key, piece in pieces.items() if key not in (0, late)})
+        through += [piece for key, piece in pieces.items() if key != late]
+        halves.append(pieces)
+    (r_grad,) = sums(1, after(chunks, q_grad, *through))
     others = [{key: swap(piece, "core", 1) for key, piece in pieces.items() if key != late} for pieces in halves]
-    early = [piece for other in others for piece in other.values()] + [pieces[late] for pieces in halves]
-    (r_grad,) = sums(1, after(chunks, q_grad, *early))
     for pieces, other in zip(halves, others):
-        other[late] = after(swap(pieces[late], "core", 1), r_grad)
+        pieces[late] = after(pieces[late], r_grad)
+        other[late] = swap(pieces[late], "core", 1)
     at = jnp.stack([lax.axis_index(name) for name in ("x", "core", "tz", "ty")]).astype(jnp.int32)
     order = range(n_x * n_y)
     w_grad = widen(n_x, n_y, share, at, [pieces[i] for pieces in halves for i in order], None)

time: 131 us -> 125 us (0.954)
  Pallas kernels: 40.5 us -> 37.7 us
  starting transfers between devices: 31.9 us -> 30 us
  other arithmetic: 1.78 us -> 0.31 us
    all_to_all x1, waiting for transfers between devices: 0.01 us -> 4.75 us  [local(): lax.all_to_all(chunks, plane, split_axis=0, concat_axis=0, tiled=True)]
    ppermute x23, waiting for transfers between devices: 51.9 us -> 47.3 us  [swap(): return lax.ppermute(x, axis, [(i, i ^ k) for i in range(n)])]
    pallas_call x1, Pallas kernels: 12.7 us -> 9.75 us  [local(): call(functools.partial(bucket_kernel, n_plane, cap), 'buckets', shape((n_...]
    ppermute x23, starting transfers between devices: 20.4 us -> 18.4 us  [swap(): return lax.ppermute(x, axis, [(i, i ^ k) for i in range(n)])]
    unnamed x10 -> x24, local copies, waits for them, and re-layouts: 3.44 us -> 3.47 us
  transfers between devices with their start and end apart: 26 -> 26, of which waited for: 11 -> 11; matrix products, arithmetic and copies ran while one was open for 0% -> 0% of each run, Pallas kernels for 28% -> 23%
where the time goes in v11:
time: 125 us
  waiting for transfers between devices  52 us (42%)
  Pallas kernels  37.7 us (30%)
  starting transfers between devices  30 us (24%)
  local copies, waits for them, and re-layouts  3.51 us (3%)
    ppermute x23, waiting for transfers between devices, swap(): return lax.ppermute(x, axis, [(i, i ^ k) for i in range(n)])  47.3 us
    ppermute x23, starting transfers between devices, swap(): return lax.ppermute(x, axis, [(i, i ^ k) for i in range(n)])  18.4 us
    pallas_call x2, Pallas kernels, sums(): call(functools.partial(sums_kernel, n_plane, seg, n_bias, table), ('q_sum...  10.8 us
    pallas_call x1, Pallas kernels, local(): call(functools.partial(bucket_kernel, n_plane, cap), 'buckets', shape((n_...  9.75 us
    pallas_call x2, Pallas kernels, widen(): call(functools.partial(widen_kernel, n_x, n_y, share), 'widen', jax.Shape...  6.41 us
    pallas_call x1, Pallas kernels, local(): call(dpre_kernel, 'dpre', shape((n_s, hidden), BF), 2 * n_s * width * hid...  4.82 us
    all_to_all x1, waiting for transfers between devices, local(): lax.all_to_all(chunks, plane, split_axis=0, concat_axis=0, tiled=True)  4.75 us
    all_to_all x1, starting transfers between devices, local(): lax.all_to_all(chunks, plane, split_axis=0, concat_axis=0, tiled=True)  4.18 us
  transfers between devices with their start and end apart: 26, of which 11 were waited for; matrix products, arithmetic and copies ran while one was open for 0% of the time, Pallas kernels for 23%

profile of v11, /device:TPU:0, one launch (start us, length us, event | category | flops | bytes accessed | tf_op | source)
XLA Modules:
  0.0 124.7 jit_solution(7496642331448670816)
XLA Ops:
  0.7 4.8 %dpre.1.d0_ref = bf16[128,1024]{1,0:T(8,128)(2,1)} custom-call(bf16[128,2048]{1,0:T(8,128)(2,1)} %x_ref.2, bf16[2048,1024]{1,0:T(8,128)(2,1)} %w_ref.3, f32[1,1024]{1,0:T(1,128)} %bitcast.38, bf16[128,1024]{1,0:T(8,128)(2,1)} %g_ref.1), custom_call_target="tpu_custom_call" | custom-call | flops 536870912 | bytes 6000000 | tf_op jit(solution)/shard_map/dpre/pallas_call | solution.py:344
  5.5 3.0 %collective-permute-start.1 = (bf16[128,1024]{1,0:T(8,128)(2,1)}, bf16[128,1024]{1,0:T(8,128)(2,1)S(1)}, u32[]{:S(2)}, u32[]{:S(2)}) collective-permute-start(bf16[128,1024]{1,0:T(8,128)(2,1)} %dpre.1.d0_ref), channel_id=1, source_target_pairs={{0,2},{2,0},{4,6},{6,4},{1,3},{3,1},{5,7},{7,5},{8,10},{10,8},{12,... | collective-permute-start | bytes 786440 | tf_op jit(solution)/shard_map/ppermute | solution.py:262
  8.6 2.6 %collective-permute-start = (bf16[128,1024]{1,0:T(8,128)(2,1)}, bf16[128,1024]{1,0:T(8,128)(2,1)S(1)}, u32[]{:S(2)}, u32[]{:S(2)}) collective-permute-start(bf16[128,1024]{1,0:T(8,128)(2,1)} %dpre.1.d0_ref), channel_id=1, source_target_pairs={{0,4},{2,6},{4,0},{6,2},{1,5},{3,7},{5,1},{7,3},{8,12},{10,14},{12... | collective-permute-start | bytes 786440 | tf_op jit(solution)/shard_map/ppermute | solution.py:262
  12.7 8.2 %collective-permute-done.1.d1_ref = bf16[128,1024]{1,0:T(8,128)(2,1)S(1)} collective-permute-done((bf16[128,1024]{1,0:T(8,128)(2,1)}, bf16[128,1024]{1,0:T(8,128)(2,1)S(1)}, u32[]{:S(2)}, u32[]{:S(2)}) %collective-permute-start.1) | collective-permute-done | bytes 262176 | tf_op jit(solution)/shard_map/ppermute | solution.py:262
  20.9 4.3 %collective-permute-done.d2_ref = bf16[128,1024]{1,0:T(8,128)(2,1)S(1)} collective-permute-done((bf16[128,1024]{1,0:T(8,128)(2,1)}, bf16[128,1024]{1,0:T(8,128)(2,1)S(1)}, u32[]{:S(2)}, u32[]{:S(2)}) %collective-permute-start) | collective-permute-done | bytes 262176 | tf_op jit(solution)/shard_map/ppermute | solution.py:262
  25.9 3.7 %all-to-all-start = ((bf16[4,128,512]{2,1,0:T(8,128)(2,1)}), bf16[4,128,512]{2,1,0:T(8,128)(2,1)S(1)}, u32[]{:S(2)}, u32[]{:S(2)}) async-start(bf16[4,128,512]{2,1,0:T(8,128)(2,1)} %cut.1), calls=%async_computation | async-start | bytes 1048576 | tf_op jit(solution)/shard_map/all_to_all | solution.py:399
  29.7 2.0 %collective-permute-start.5 = (bf16[128,1024]{1,0:T(8,128)(2,1)S(1)}, bf16[128,1024]{1,0:T(8,128)(2,1)S(1)}, u32[]{:S(2)}, u32[]{:S(2)}) collective-permute-start(bf16[128,1024]{1,0:T(8,128)(2,1)S(1)} %collective-permute-done.d2_ref), channel_id=1, source_target_pairs={{0,2},{2,0},{4,6},{6,4},{1,3},{3,1},{5,7},{7,5},{8,10},{10,8},{12,... | collective-permute-start | bytes 786440 | tf_op jit(solution)/shard_map/ppermute | solution.py:262
  31.8 13.9 %collective-permute-done.4.last_ref = bf16[128,128]{1,0:T(8,128)(2,1)S(1)} collective-permute-done((bf16[128,128]{1,0:T(8,128)(2,1)S(1)}, bf16[128,128]{1,0:T(8,128)(2,1)S(1)}, u32[]{:S(2)}, u32[]{:S(2)}) %collective-permute-start.4) | collective-permute-done | bytes 32800 | tf_op jit(solution)/shard_map/ppermute | solution.py:262
  46.5 1.7 %w_part.1 = bf16[8,64,1024]{2,1,0:T(8,128)(2,1)} custom-call(s32[1]{0:T(128)} %bitcast.2.z_ref, bf16[4,128,512]{2,1,0:T(8,128)(2,1)S(1)} %all-to-all-done.x_ref, bf16[128,1024]{1,0:T(8,128)(2,1)S(1)} %copy-done.3, bf16[128,1024]{1,0:T(8,128)(2,1)S(1)} %collective-permute-done.1.d1_ref, bf16[128,1024]{1,0:T(8,128)(2,1)S(1)} %collective-permute-done.d2_ref, ...), custom_call_target="tpu_custom_call" | custom-call | flops 536870912 | bytes 3000000 | tf_op jit(solution)/shard_map/w_part/pallas_call | solution.py:403
  48.2 3.7 %all-to-all-start.1 = ((bf16[8,64,1024]{2,1,0:T(8,128)(2,1)}), bf16[8,64,1024]{2,1,0:T(8,128)(2,1)S(1)}, u32[]{:S(2)}, u32[]{:S(2)}) async-start(bf16[8,64,1024]{2,1,0:T(8,128)(2,1)} %w_part.1), calls=%async_computation.1 | async-start | bytes 2097152 | tf_op jit(solution)/shard_map/all_to_all | solution.py:421
  52.0 2.2 %copy-done = bf16[2048,1024]{1,0:T(8,128)(2,1)S(1)} copy-done((bf16[2048,1024]{1,0:T(8,128)(2,1)S(1)}, bf16[2048,1024]{1,0:T(8,128)(2,1)}, u32[]{:S(2)}) %copy-start) | copy-done | bytes 4194328
  54.2 2.4 %lookups.1 = (bf16[4,2048,128]{2,1,0:T(8,128)(2,1)S(1)}, bf16[16,128]{1,0:T(8,128)(2,1)S(1)}) custom-call(bf16[128,1024]{1,0:T(8,128)(2,1)S(1)} %copy-done.3, bf16[128,1024]{1,0:T(8,128)(2,1)S(1)} %collective-permute-done.1.d1_ref, bf16[128,1024]{1,0:T(8,128)(2,1)S(1)} %collective-permute-done.d2_ref, bf16[128,1024]{1,0:T(8,128)(2,1)S(1)} %collective-permute-done.5.d3_ref, ...), custom_call_target="tpu_custom_call" | custom-call | flops 2147483648 | bytes 7000000 | tf_op jit(solution)/shard_map/lookups/pallas_call | solution.py:412
  56.5 9.8 %buckets.1 = bf16[8,928,128]{2,1,0:T(8,128)(2,1)S(1)} custom-call(bf16[4,2048,128]{2,1,0:T(8,128)(2,1)S(1)} %get-tuple-element.43.look_ref, s32[3,4,16,128]{3,2,1,0:T(8,128)S(1)} %get-tuple-element.40.slot_ref, f32[4,128,128]{2,1,0:T(8,128)S(1)} %get-tuple-element.44.down_ref, bf16[16,128]{1,0:T(8,128)(2,1)S(1)} %get-tuple-element.45.bias_ref), custom_call_target="tpu_custom_call" | custom-call | flops 15000000512 | bytes 40000000 | tf_op jit(solution)/shard_map/buckets/pallas_call | solution.py:424
  67.6 4.2 %all-to-all-start.2 = ((bf16[8,928,128]{2,1,0:T(8,128)(2,1)}), bf16[8,928,128]{2,1,0:T(8,128)(2,1)S(1)}, u32[]{:S(2)}, u32[]{:S(2)}) async-start(bf16[8,928,128]{2,1,0:T(8,128)(2,1)} %copy-done.2), calls=%async_computation.2 | async-start | bytes 3801088 | tf_op jit(solution)/shard_map/all_to_all | solution.py:436
  71.9 2.5 %collective-permute-start.6 = (bf16[64,1024]{1,0:T(8,128)(2,1)S(1)}, bf16[64,1024]{1,0:T(8,128)(2,1)S(1)}, u32[]{:S(2)}, u32[]{:S(2)}) collective-permute-start(bf16[64,1024]{1,0:T(8,128)(2,1)S(1)} %reduce_sum.12), channel_id=1, source_target_pairs={{0,4},{2,6},{4,0},{6,2},{1,5},{3,7},{5,1},{7,3},{8,12},{10,14},{12... | collective-permute-start | bytes 393224 | tf_op jit(solution)/shard_map/ppermute | solution.py:262
  74.9 6.5 %collective-permute-done.6 = bf16[64,1024]{1,0:T(8,128)(2,1)S(1)} collective-permute-done((bf16[64,1024]{1,0:T(8,128)(2,1)S(1)}, bf16[64,1024]{1,0:T(8,128)(2,1)S(1)}, u32[]{:S(2)}, u32[]{:S(2)}) %collective-permute-start.6) | collective-permute-done | bytes 131104 | tf_op jit(solution)/shard_map/ppermute | solution.py:262
  82.8 4.1 %collective-permute-done.8 = bf16[64,1024]{1,0:T(8,128)(2,1)S(1)} collective-permute-done((bf16[64,1024]{1,0:T(8,128)(2,1)S(1)}, bf16[64,1024]{1,0:T(8,128)(2,1)S(1)}, u32[]{:S(2)}, u32[]{:S(2)}) %collective-permute-start.8) | collective-permute-done | bytes 131104 | tf_op jit(solution)/shard_map/ppermute | solution.py:262
  91.1 4.8 %all-to-all-done.2.in_ref = bf16[8,928,128]{2,1,0:T(8,128)(2,1)S(1)} async-done(((bf16[8,928,128]{2,1,0:T(8,128)(2,1)}), bf16[8,928,128]{2,1,0:T(8,128)(2,1)S(1)}, u32[]{:S(2)}, u32[]{:S(2)}) %all-to-all-start.2) | async-done | bytes 1900576 | tf_op jit(solution)/shard_map/all_to_all | solution.py:436
  95.9 5.4 %q_sums.1 = (f32[4096,128]{1,0:T(8,128)}, f32[8,128]{1,0:T(8,128)}, f32[128,128]{1,0:T(8,128)}) custom-call(bf16[8,928,128]{2,1,0:T(8,128)(2,1)S(1)} %all-to-all-done.2.in_ref), custom_call_target="tpu_custom_call" | custom-call | flops 4000000000 | bytes 4000000 | tf_op jit(solution)/shard_map/q_sums/pallas_call | solution.py:446
  101.3 5.4 %collective-permute-done.10.refs_1_ = bf16[256,512]{1,0:T(8,128)(2,1)} collective-permute-done((bf16[256,512]{1,0:T(8,128)(2,1)S(1)}, bf16[256,512]{1,0:T(8,128)(2,1)}, u32[]{:S(2)}, u32[]{:S(2)}) %collective-permute-start.10) | collective-permute-done | bytes 262176 | tf_op jit(solution)/shard_map/ppermute | solution.py:262
  108.6 5.4 %r_sums.1 = f32[4096,128]{1,0:T(8,128)} custom-call(bf16[8,928,128]{2,1,0:T(8,128)(2,1)S(1)} %all-to-all-done.2.in_ref), custom_call_target="tpu_custom_call" | custom-call | flops 4000000000 | bytes 4000000 | tf_op jit(solution)/shard_map/r_sums/pallas_call | solution.py:446
  114.0 1.7 %collective-permute-done.14.refs_3_ = bf16[256,512]{1,0:T(8,128)(2,1)} collective-permute-done((bf16[256,512]{1,0:T(8,128)(2,1)}, bf16[256,512]{1,0:T(8,128)(2,1)}, u32[]{:S(2)}, u32[]{:S(2)}) %collective-permute-start.14) | collective-permute-done | bytes 262176 | tf_op jit(solution)/shard_map/ppermute | solution.py:262
  118.0 3.6 %widen.2.refs_8_ = f32[2048,1024]{1,0:T(8,128)} custom-call(s32[4]{0:T(128)S(1)} %get-tuple-element.62.at_ref, bf16[256,512]{1,0:T(8,128)(2,1)S(1)} %get-tuple-element.64.refs_0_, bf16[256,512]{1,0:T(8,128)(2,1)} %collective-permute-done.10.refs_1_, bf16[256,512]{1,0:T(8,128)(2,1)} %collective-permute-done.12.refs_2_, ...), custom_call_target="tpu_custom_call" | custom-call | flops 1048576 | bytes 6291456 | tf_op jit(solution)/shard_map/widen/pallas_call | solution.py:296
  121.6 2.8 %widen.3 = f32[2048,1024]{1,0:T(8,128)} custom-call(s32[4]{0:T(128)S(1)} %get-tuple-element.61.at_ref, bf16[256,512]{1,0:T(8,128)(2,1)S(1)} %collective-permute-done.9.refs_0_, bf16[256,512]{1,0:T(8,128)(2,1)S(1)} %collective-permute-done.11.refs_1_, bf16[256,512]{1,0:T(8,128)(2,1)S(1)} %collective-permute-done.13.refs_2_, ...), custom_call_target="tpu_custom_call", output_to_operand_aliasing={{}: (9, {})} | custom-call | flops 1048576 | bytes 6291456 | tf_op jit(solution)/shard_map/widen/pallas_call | solution.py:296
  (70 shorter events, 14.9 us)
Async XLA Ops:
  5.5 15.4 %collective-permute-start.1 = (bf16[128,1024]{1,0:T(8,128)(2,1)}, bf16[128,1024]{1,0:T(8,128)(2,1)S(1)}, u32[]{:S(2)}, u32[]{:S(2)}) collective-permute-start(bf16[128,1024]{1,0:T(8,128)(2,1)} %dpre.1.d0_ref), channel_id=1, source_target_pairs={{0,2},{2,0},{4,6},{6,4},{1,3},{3,1},{5,7},{7,5},{8,10},{10,8},{12,... | collective-permute-start | bytes 786440 | tf_op jit(solution)/shard_map/ppermute | solution.py:262
  8.6 16.7 %collective-permute-start = (bf16[128,1024]{1,0:T(8,128)(2,1)}, bf16[128,1024]{1,0:T(8,128)(2,1)S(1)}, u32[]{:S(2)}, u32[]{:S(2)}) collective-permute-start(bf16[128,1024]{1,0:T(8,128)(2,1)} %dpre.1.d0_ref), channel_id=1, source_target_pairs={{0,4},{2,6},{4,0},{6,2},{1,5},{3,7},{5,1},{7,3},{8,12},{10,14},{12... | collective-permute-start | bytes 786440 | tf_op jit(solution)/shard_map/ppermute | solution.py:262
  11.3 14.7 %collective-permute-start.2 = (bf16[2,128,128]{2,1,0:T(8,128)(2,1)S(1)}, bf16[2,128,128]{2,1,0:T(8,128)(2,1)S(1)}, u32[]{:S(2)}, u32[]{:S(2)}) collective-permute-start(bf16[2,128,128]{2,1,0:T(8,128)(2,1)S(1)} %get-tuple-element.35), channel_id=1, source_target_pairs={{0,4},{2,6},{4,0},{6,2},{1,5},{3,7},{5,1},{7,3},{8,12},{10,14},{12... | collective-permute-start | bytes 196616 | tf_op jit(solution)/shard_map/ppermute | solution.py:262
  11.7 13.6 %collective-permute-start.3 = (bf16[128,128]{1,0:T(8,128)(2,1)S(1)}, bf16[128,128]{1,0:T(8,128)(2,1)S(1)}, u32[]{:S(2)}, u32[]{:S(2)}) collective-permute-start(bf16[128,128]{1,0:T(8,128)(2,1)S(1)} %get-tuple-element.36), channel_id=1, source_target_pairs={{0,2},{2,0},{4,6},{6,4},{1,3},{3,1},{5,7},{7,5},{8,10},{10,8},{12,... | collective-permute-start | bytes 98312 | tf_op jit(solution)/shard_map/ppermute | solution.py:262
  25.9 20.6 %all-to-all-start = ((bf16[4,128,512]{2,1,0:T(8,128)(2,1)}), bf16[4,128,512]{2,1,0:T(8,128)(2,1)S(1)}, u32[]{:S(2)}, u32[]{:S(2)}) async-start(bf16[4,128,512]{2,1,0:T(8,128)(2,1)} %cut.1), calls=%async_computation | async-start | bytes 1048576 | tf_op jit(solution)/shard_map/all_to_all | solution.py:399
  29.7 16.8 %collective-permute-start.5 = (bf16[128,1024]{1,0:T(8,128)(2,1)S(1)}, bf16[128,1024]{1,0:T(8,128)(2,1)S(1)}, u32[]{:S(2)}, u32[]{:S(2)}) collective-permute-start(bf16[128,1024]{1,0:T(8,128)(2,1)S(1)} %collective-permute-done.d2_ref), channel_id=1, source_target_pairs={{0,2},{2,0},{4,6},{6,4},{1,3},{3,1},{5,7},{7,5},{8,10},{10,8},{12,... | collective-permute-start | bytes 786440 | tf_op jit(solution)/shard_map/ppermute | solution.py:262
  31.7 13.9 %collective-permute-start.4 = (bf16[128,128]{1,0:T(8,128)(2,1)S(1)}, bf16[128,128]{1,0:T(8,128)(2,1)S(1)}, u32[]{:S(2)}, u32[]{:S(2)}) collective-permute-start(bf16[128,128]{1,0:T(8,128)(2,1)S(1)} %slice_bitcast_fusion), channel_id=1, source_target_pairs={{0,2},{2,0},{4,6},{6,4},{1,3},{3,1},{5,7},{7,5},{8,10},{10,8},{12,... | collective-permute-start | bytes 98312 | tf_op jit(solution)/shard_map/ppermute | solution.py:262
  48.2 19.3 %all-to-all-start.1 = ((bf16[8,64,1024]{2,1,0:T(8,128)(2,1)}), bf16[8,64,1024]{2,1,0:T(8,128)(2,1)S(1)}, u32[]{:S(2)}, u32[]{:S(2)}) async-start(bf16[8,64,1024]{2,1,0:T(8,128)(2,1)} %w_part.1), calls=%async_computation.1 | async-start | bytes 2097152 | tf_op jit(solution)/shard_map/all_to_all | solution.py:421
  67.6 28.3 %all-to-all-start.2 = ((bf16[8,928,128]{2,1,0:T(8,128)(2,1)}), bf16[8,928,128]{2,1,0:T(8,128)(2,1)S(1)}, u32[]{:S(2)}, u32[]{:S(2)}) async-start(bf16[8,928,128]{2,1,0:T(8,128)(2,1)} %copy-done.2), calls=%async_computation.2 | async-start | bytes 3801088 | tf_op jit(solution)/shard_map/all_to_all | solution.py:436
  71.9 9.5 %collective-permute-start.6 = (bf16[64,1024]{1,0:T(8,128)(2,1)S(1)}, bf16[64,1024]{1,0:T(8,128)(2,1)S(1)}, u32[]{:S(2)}, u32[]{:S(2)}) collective-permute-start(bf16[64,1024]{1,0:T(8,128)(2,1)S(1)} %reduce_sum.12), channel_id=1, source_target_pairs={{0,4},{2,6},{4,0},{6,2},{1,5},{3,7},{5,1},{7,3},{8,12},{10,14},{12... | collective-permute-start | bytes 393224 | tf_op jit(solution)/shard_map/ppermute | solution.py:262
  74.4 8.3 %collective-permute-start.7 = (bf16[64,1024]{1,0:T(8,128)(2,1)S(1)}, bf16[64,1024]{1,0:T(8,128)(2,1)S(1)}, u32[]{:S(2)}, u32[]{:S(2)}) collective-permute-start(bf16[64,1024]{1,0:T(8,128)(2,1)S(1)} %reduce_sum.12), channel_id=1, source_target_pairs={{0,2},{2,0},{4,6},{6,4},{1,3},{3,1},{5,7},{7,5},{8,10},{10,8},{12,... | collective-permute-start | bytes 393224 | tf_op jit(solution)/shard_map/ppermute | solution.py:262
  81.4 5.4 %collective-permute-start.8 = (bf16[64,1024]{1,0:T(8,128)(2,1)S(1)}, bf16[64,1024]{1,0:T(8,128)(2,1)S(1)}, u32[]{:S(2)}, u32[]{:S(2)}) collective-permute-start(bf16[64,1024]{1,0:T(8,128)(2,1)S(1)} %collective-permute-done.6), channel_id=1, source_target_pairs={{0,2},{2,0},{4,6},{6,4},{1,3},{3,1},{5,7},{7,5},{8,10},{10,8},{12,... | collective-permute-start | bytes 393224 | tf_op jit(solution)/shard_map/ppermute | solution.py:262
  86.9 30.0 %collective-permute-start.18 = (bf16[256,512]{1,0:T(8,128)(2,1)S(1)}, bf16[256,512]{1,0:T(8,128)(2,1)S(1)}, u32[]{:S(2)}, u32[]{:S(2)}) collective-permute-start(bf16[256,512]{1,0:T(8,128)(2,1)S(1)} %get-tuple-element.63.refs_4_), channel_id=1, source_target_pairs={{0,8},{8,0},{1,9},{9,1},{2,10},{10,2},{3,11},{11,3},{4,12},{12,4},... | collective-permute-start | bytes 786440 | tf_op jit(solution)/shard_map/ppermute | solution.py:262
  87.0 21.2 %collective-permute-start.16 = (bf16[256,512]{1,0:T(8,128)(2,1)S(1)}, bf16[256,512]{1,0:T(8,128)(2,1)S(1)}, u32[]{:S(2)}, u32[]{:S(2)}) collective-permute-start(bf16[256,512]{1,0:T(8,128)(2,1)S(1)} %get-tuple-element.63.refs_4_), channel_id=1, source_target_pairs={{0,1},{1,0},{2,3},{3,2},{4,5},{5,4},{6,7},{7,6},{8,9},{9,8},{10,11... | collective-permute-start | bytes 786440 | tf_op jit(solution)/shard_map/ppermute | solution.py:262
  88.7 18.0 %collective-permute-start.15 = (bf16[256,512]{1,0:T(8,128)(2,1)S(1)}, bf16[256,512]{1,0:T(8,128)(2,1)}, u32[]{:S(2)}, u32[]{:S(2)}) collective-permute-start(bf16[256,512]{1,0:T(8,128)(2,1)S(1)} %get-tuple-element.63.refs_4_), channel_id=1, source_target_pairs={{0,16},{16,0},{1,17},{17,1},{2,18},{18,2},{3,19},{19,3},{4,20},{20... | collective-permute-start | bytes 786440 | tf_op jit(solution)/shard_map/ppermute | solution.py:262
  90.2 18.4 %collective-permute-start.12 = (bf16[256,512]{1,0:T(8,128)(2,1)S(1)}, bf16[256,512]{1,0:T(8,128)(2,1)}, u32[]{:S(2)}, u32[]{:S(2)}) collective-permute-start(bf16[256,512]{1,0:T(8,128)(2,1)S(1)} %get-tuple-element.64.refs_0_), channel_id=1, source_target_pairs={{0,16},{16,0},{1,17},{17,1},{2,18},{18,2},{3,19},{19,3},{4,20},{20... | collective-permute-start | bytes 786440 | tf_op jit(solution)/shard_map/ppermute | solution.py:262
  90.7 15.9 %collective-permute-start.10 = (bf16[256,512]{1,0:T(8,128)(2,1)S(1)}, bf16[256,512]{1,0:T(8,128)(2,1)}, u32[]{:S(2)}, u32[]{:S(2)}) collective-permute-start(bf16[256,512]{1,0:T(8,128)(2,1)S(1)} %get-tuple-element.64.refs_0_), channel_id=1, source_target_pairs={{0,1},{1,0},{2,3},{3,2},{4,5},{5,4},{6,7},{7,6},{8,9},{9,8},{10,11... | collective-permute-start | bytes 786440 | tf_op jit(solution)/shard_map/ppermute | solution.py:262
  106.7 10.7 %collective-permute-start.9 = (bf16[256,512]{1,0:T(8,128)(2,1)S(1)}, bf16[256,512]{1,0:T(8,128)(2,1)S(1)}, u32[]{:S(2)}, u32[]{:S(2)}) collective-permute-start(bf16[256,512]{1,0:T(8,128)(2,1)S(1)} %get-tuple-element.64.refs_0_), channel_id=1, source_target_pairs={{0,8},{8,0},{1,9},{9,1},{2,10},{10,2},{3,11},{11,3},{4,12},{12,4},... | collective-permute-start | bytes 786440 | tf_op jit(solution)/shard_map/ppermute | solution.py:262
  106.7 9.0 %collective-permute-start.14 = (bf16[256,512]{1,0:T(8,128)(2,1)}, bf16[256,512]{1,0:T(8,128)(2,1)}, u32[]{:S(2)}, u32[]{:S(2)}) collective-permute-start(bf16[256,512]{1,0:T(8,128)(2,1)} %collective-permute-done.10.refs_1_), channel_id=1, source_target_pairs={{0,16},{16,0},{1,17},{17,1},{2,18},{18,2},{3,19},{19,3},{4,20},{20... | collective-permute-start | bytes 786440 | tf_op jit(solution)/shard_map/ppermute | solution.py:262
  108.2 8.7 %collective-permute-start.21 = (bf16[256,512]{1,0:T(8,128)(2,1)}, bf16[256,512]{1,0:T(8,128)(2,1)}, u32[]{:S(2)}, u32[]{:S(2)}) collective-permute-start(bf16[256,512]{1,0:T(8,128)(2,1)} %collective-permute-done.15.refs_6_), channel_id=1, source_target_pairs={{0,1},{1,0},{2,3},{3,2},{4,5},{5,4},{6,7},{7,6},{8,9},{9,8},{10,11... | collective-permute-start | bytes 786440 | tf_op jit(solution)/shard_map/ppermute | solution.py:262
  108.6 8.9 %collective-permute-start.11 = (bf16[256,512]{1,0:T(8,128)(2,1)}, bf16[256,512]{1,0:T(8,128)(2,1)S(1)}, u32[]{:S(2)}, u32[]{:S(2)}) collective-permute-start(bf16[256,512]{1,0:T(8,128)(2,1)} %collective-permute-done.10.refs_1_), channel_id=1, source_target_pairs={{0,8},{8,0},{1,9},{9,1},{2,10},{10,2},{3,11},{11,3},{4,12},{12,4},... | collective-permute-start | bytes 786440 | tf_op jit(solution)/shard_map/ppermute | solution.py:262
  115.7 5.9 %collective-permute-start.13 = (bf16[256,512]{1,0:T(8,128)(2,1)}, bf16[256,512]{1,0:T(8,128)(2,1)S(1)}, u32[]{:S(2)}, u32[]{:S(2)}) collective-permute-start(bf16[256,512]{1,0:T(8,128)(2,1)} %collective-permute-done.12.refs_2_), channel_id=1, source_target_pairs={{0,8},{8,0},{1,9},{9,1},{2,10},{10,2},{3,11},{11,3},{4,12},{12,4},... | collective-permute-start | bytes 786440 | tf_op jit(solution)/shard_map/ppermute | solution.py:262
  116.9 4.7 %collective-permute-start.20 = (bf16[256,512]{1,0:T(8,128)(2,1)}, bf16[256,512]{1,0:T(8,128)(2,1)S(1)}, u32[]{:S(2)}, u32[]{:S(2)}) collective-permute-start(bf16[256,512]{1,0:T(8,128)(2,1)} %collective-permute-done.15.refs_6_), channel_id=1, source_target_pairs={{0,8},{8,0},{1,9},{9,1},{2,10},{10,2},{3,11},{11,3},{4,12},{12,4},... | collective-permute-start | bytes 786440 | tf_op jit(solution)/shard_map/ppermute | solution.py:262
  116.9 4.7 %collective-permute-start.19 = (bf16[256,512]{1,0:T(8,128)(2,1)S(1)}, bf16[256,512]{1,0:T(8,128)(2,1)S(1)}, u32[]{:S(2)}, u32[]{:S(2)}) collective-permute-start(bf16[256,512]{1,0:T(8,128)(2,1)S(1)} %collective-permute-done.16.refs_5_), channel_id=1, source_target_pairs={{0,8},{8,0},{1,9},{9,1},{2,10},{10,2},{3,11},{11,3},{4,12},{12,4},... | collective-permute-start | bytes 786440 | tf_op jit(solution)/shard_map/ppermute | solution.py:262
  (14 other events, 124.6 us)

commit v12 on v11

--- a/solution.py
+++ b/solution.py
@@ -262,52 +262,48 @@
     return lax.ppermute(x, axis, [(i, i ^ k) for i in range(n)])
 
 
-def widen_kernel(n_x, n_y, share, at_ref, *refs):
-    n = n_x * n_y
+def widen_kernel(n_y, share, places, at_ref, *refs):
     out_ref, held_ref, sems = refs[-3:]
     half = refs[0].shape[1]
     tall = N_Z * share
     copies = []
-    for piece in range(n):
-        for side in range(2):
-            cols = slice(side * half, (side + 1) * half)
-            held_ref[piece * tall : (piece + 1) * tall, cols] = refs[side * n + piece][...].astype(F32)
-            x, y = at_ref[0] ^ (piece // n_y), at_ref[3] ^ (piece % n_y)
-            for b in range(N_Z):
-                z = at_ref[2] ^ (((b & 1) << 1) | (b >> 1))
-                row = (((x * 2 + at_ref[1]) * N_Z + z) * n_y + y) * share
-                copy = pltpu.make_async_copy(
-                    held_ref.at[piece * tall + b * share : piece * tall + (b + 1) * share, cols],
-                    out_ref.at[pl.ds(pl.multiple_of(row, share), share), cols],
-                    sems.at[len(copies)],
-                )
-                copy.start()
-                copies.append(copy)
+    for i, (key, side, flip) in enumerate(places):
+        held_ref[i * tall : (i + 1) * tall, :] = refs[i][...].astype(F32)
+        x, y = at_ref[0] ^ (key // n_y), at_ref[3] ^ (key % n_y)
+        for b in range(N_Z):
+            z = at_ref[2] ^ (((b & 1) << 1) | (b >> 1))
+            row = (((x * 2 + (at_ref[1] ^ flip)) * N_Z + z) * n_y + y) * share
+            copy = pltpu.make_async_copy(
+                held_ref.at[i * tall + b * share : i * tall + (b + 1) * share, :],
+                out_ref.at[pl.ds(pl.multiple_of(row, share), share), side * half : (side + 1) * half],
+                sems.at[len(copies)],
+            )
+            copy.start()
+            copies.append(copy)
     for copy in copies:
         copy.wait()
 
 
-def widen(n_x, n_y, share, at, pieces, so_far):
+def widen(n_y, share, rows, at, parts, so_far):
+    places, pieces = tuple(parts), list(parts.values())
     tall, half = pieces[0].shape
-    rows = n_x * n_y * tall
     array = pl.BlockSpec(memory_space=pltpu.VMEM)
     more = () if so_far is None else (so_far,)
     alias = {} if so_far is None else {"input_output_aliases": {1 + len(pieces): 0}}
     return call(
-        functools.partial(widen_kernel, n_x, n_y, share),
+        functools.partial(widen_kernel, n_y, share, places),
         "widen",
-        jax.ShapeDtypeStruct((2 * rows, 2 * half), F32),
-        rows * half * 2,
-        rows * half * 12,
+        jax.ShapeDtypeStruct((rows, 2 * half), F32),
+        len(pieces) * tall * half,
+        len(pieces) * tall * half * 6,
         in_specs=[pl.BlockSpec(memory_space=pltpu.SMEM)]
         + [array] * len(pieces)
         + [pl.BlockSpec(memory_space=pltpu.HBM)] * len(more),
         out_specs=pl.BlockSpec(memory_space=pltpu.HBM),
         scratch_shapes=[
-            pltpu.VMEM((rows, 2 * half), F32),
-            pltpu.SemaphoreType.DMA((2 * (rows // share),)),
+            pltpu.VMEM((len(pieces) * tall, half), F32),
+            pltpu.SemaphoreType.DMA((len(pieces) * N_Z,)),
         ],
-        vmem=16,
         **alias,
     )(at, *pieces, *more)
 
@@ -452,29 +448,28 @@
             vmem=28,
         )(chunks)
 
-    q_grad, b_grad, adm_grad = sums(0, chunks)
+    q_grad, b_grad, adm_grad = sums(0, after(chunks, w_four))
     late = n_x * n_y - 1
-    halves, through = [], []
-    for own, steps in ((w_four[:, :side], over_y + over_x), (w_four[:, side:], over_x + over_y)):
+    (r_grad,) = sums(1, after(chunks, q_grad))
+    early, mine, theirs = {}, {}, {}
+    for h, steps in enumerate((over_y + over_x, over_x + over_y)):
+        own = w_four[:, h * side : (h + 1) * side]
         pieces = {0: own}
         for axis, stride, k in steps:
             last = late ^ (k * stride)
             if last in pieces:
-                pieces[last] = after(pieces[last], q_grad)
+                pieces[last] = after(pieces[last], r_grad)
             pieces.update({key ^ (k * stride): swap(piece, axis, k) for key, piece in pieces.items()})
-        pieces.update({key: after(piece, q_grad) for key, piece in pieces.items() if key not in (0, late)})
-        through += [piece for key, piece in pieces.items() if key != late]
-        halves.append(pieces)
-    (r_grad,) = sums(1, after(chunks, q_grad, *through))
-    others = [{key: swap(piece, "core", 1) for key, piece in pieces.items() if key != late} for pieces in halves]
-    for pieces, other in zip(halves, others):
-        pieces[late] = after(pieces[late], r_grad)
-        other[late] = swap(pieces[late], "core", 1)
+        mine[late, h, 0] = pieces.pop(late)
+        pieces.update({key: after(piece, r_grad) for key, piece in pieces.items() if key > 0})
+        early.update({(key, h, 0): piece for key, piece in pieces.items()})
+        early.update({(key, h, 1): swap(piece, "core", 1) for key, piece in pieces.items()})
     at = jnp.stack([lax.axis_index(name) for name in ("x", "core", "tz", "ty")]).astype(jnp.int32)
-    order = range(n_x * n_y)
-    w_grad = widen(n_x, n_y, share, at, [pieces[i] for pieces in halves for i in order], None)
-    flip = at ^ jnp.array([0, 1, 0, 0], jnp.int32)
-    w_grad = widen(n_x, n_y, share, flip, [other[i] for other in others for i in order], w_grad)
+    w_grad = widen(n_y, share, width, at, early, None)
+    mine = {key: after(piece, w_grad) for key, piece in mine.items()}
+    theirs = {(key, h, 1): swap(piece, "core", 1) for (key, h, _), piece in mine.items()}
+    w_grad = widen(n_y, share, width, at, mine, w_grad)
+    w_grad = widen(n_y, share, width, at, theirs, w_grad)
     return (w_grad, b_grad.reshape(hidden), adm_grad, q_grad, r_grad)
 
 

time: 125 us -> 122 us (0.976)
  waiting for transfers between devices: 52 us -> 47.5 us
  Pallas kernels: 37.7 us -> 39.8 us
  local copies, waits for them, and re-layouts: 3.51 us -> 2.26 us
    ppermute x23, waiting for transfers between devices: 47.3 us -> 42.8 us  [swap(): return lax.ppermute(x, axis, [(i, i ^ k) for i in range(n)])]
    pallas_call x1, Pallas kernels: 9.75 us -> 11 us  [local(): call(functools.partial(bucket_kernel, n_plane, cap), 'buckets', shape((n_...]
    unnamed x24 -> x20, local copies, waits for them, and re-layouts: 3.47 us -> 2.22 us
    pallas_call x2 -> x3, Pallas kernels: 6.41 us -> 7.23 us  [widen(): call(functools.partial(widen_kernel, n_y, share, places), 'widen', jax.Sh...]
  transfers between devices with their start and end apart: 26 -> 26, of which waited for: 11 -> 11; matrix products, arithmetic and copies ran while one was open for 0% -> 0% of each run, Pallas kernels for 23% -> 26%
where the time goes in v12:
time: 122 us
  waiting for transfers between devices  47.5 us (39%)
  Pallas kernels  39.8 us (33%)
  starting transfers between devices  30.8 us (25%)
  local copies, waits for them, and re-layouts  2.26 us (2%)
    ppermute x23, waiting for transfers between devices, swap(): return lax.ppermute(x, axis, [(i, i ^ k) for i in range(n)])  42.8 us
    ppermute x23, starting transfers between devices, swap(): return lax.ppermute(x, axis, [(i, i ^ k) for i in range(n)])  19.1 us
    pallas_call x1, Pallas kernels, local(): call(functools.partial(bucket_kernel, n_plane, cap), 'buckets', shape((n_...  11 us
    pallas_call x2, Pallas kernels, sums(): call(functools.partial(sums_kernel, n_plane, seg, n_bias, table), ('q_sum...  10.8 us
    pallas_call x3, Pallas kernels, widen(): call(functools.partial(widen_kernel, n_y, share, places), 'widen', jax.Sh...  7.23 us
    pallas_call x1, Pallas kernels, local(): call(dpre_kernel, 'dpre', shape((n_s, hidden), BF), 2 * n_s * width * hid...  4.82 us
    all_to_all x1, waiting for transfers between devices, local(): lax.all_to_all(chunks, plane, split_axis=0, concat_axis=0, tiled=True)  4.75 us
    all_to_all x1, starting transfers between devices, local(): lax.all_to_all(chunks, plane, split_axis=0, concat_axis=0, tiled=True)  4.18 us
  transfers between devices with their start and end apart: 26, of which 11 were waited for; matrix products, arithmetic and copies ran while one was open for 0% of the time, Pallas kernels for 26%

profile of v12, /device:TPU:0, one launch (start us, length us, event | category | flops | bytes accessed | tf_op | source)
XLA Modules:
  0.0 121.7 jit_solution(4966847965905573459)
XLA Ops:
  0.7 4.8 %dpre.1.d0_ref = bf16[128,1024]{1,0:T(8,128)(2,1)} custom-call(bf16[128,2048]{1,0:T(8,128)(2,1)} %x_ref.2, bf16[2048,1024]{1,0:T(8,128)(2,1)} %w_ref.3, f32[1,1024]{1,0:T(1,128)} %bitcast.38, bf16[128,1024]{1,0:T(8,128)(2,1)} %g_ref.1), custom_call_target="tpu_custom_call" | custom-call | flops 536870912 | bytes 6000000 | tf_op jit(solution)/shard_map/dpre/pallas_call | solution.py:340
  5.5 3.0 %collective-permute-start.1 = (bf16[128,1024]{1,0:T(8,128)(2,1)}, bf16[128,1024]{1,0:T(8,128)(2,1)S(1)}, u32[]{:S(2)}, u32[]{:S(2)}) collective-permute-start(bf16[128,1024]{1,0:T(8,128)(2,1)} %dpre.1.d0_ref), channel_id=1, source_target_pairs={{0,2},{2,0},{4,6},{6,4},{1,3},{3,1},{5,7},{7,5},{8,10},{10,8},{12,... | collective-permute-start | bytes 786440 | tf_op jit(solution)/shard_map/ppermute | solution.py:262
  8.6 2.6 %collective-permute-start = (bf16[128,1024]{1,0:T(8,128)(2,1)}, bf16[128,1024]{1,0:T(8,128)(2,1)S(1)}, u32[]{:S(2)}, u32[]{:S(2)}) collective-permute-start(bf16[128,1024]{1,0:T(8,128)(2,1)} %dpre.1.d0_ref), channel_id=1, source_target_pairs={{0,4},{2,6},{4,0},{6,2},{1,5},{3,7},{5,1},{7,3},{8,12},{10,14},{12... | collective-permute-start | bytes 786440 | tf_op jit(solution)/shard_map/ppermute | solution.py:262
  12.7 8.2 %collective-permute-done.1.d1_ref = bf16[128,1024]{1,0:T(8,128)(2,1)S(1)} collective-permute-done((bf16[128,1024]{1,0:T(8,128)(2,1)}, bf16[128,1024]{1,0:T(8,128)(2,1)S(1)}, u32[]{:S(2)}, u32[]{:S(2)}) %collective-permute-start.1) | collective-permute-done | bytes 262176 | tf_op jit(solution)/shard_map/ppermute | solution.py:262
  20.9 4.3 %collective-permute-done.d2_ref = bf16[128,1024]{1,0:T(8,128)(2,1)S(1)} collective-permute-done((bf16[128,1024]{1,0:T(8,128)(2,1)}, bf16[128,1024]{1,0:T(8,128)(2,1)S(1)}, u32[]{:S(2)}, u32[]{:S(2)}) %collective-permute-start) | collective-permute-done | bytes 262176 | tf_op jit(solution)/shard_map/ppermute | solution.py:262
  25.9 3.7 %all-to-all-start = ((bf16[4,128,512]{2,1,0:T(8,128)(2,1)}), bf16[4,128,512]{2,1,0:T(8,128)(2,1)S(1)}, u32[]{:S(2)}, u32[]{:S(2)}) async-start(bf16[4,128,512]{2,1,0:T(8,128)(2,1)} %cut.1), calls=%async_computation | async-start | bytes 1048576 | tf_op jit(solution)/shard_map/all_to_all | solution.py:395
  29.7 2.0 %collective-permute-start.5 = (bf16[128,1024]{1,0:T(8,128)(2,1)S(1)}, bf16[128,1024]{1,0:T(8,128)(2,1)S(1)}, u32[]{:S(2)}, u32[]{:S(2)}) collective-permute-start(bf16[128,1024]{1,0:T(8,128)(2,1)S(1)} %collective-permute-done.d2_ref), channel_id=1, source_target_pairs={{0,2},{2,0},{4,6},{6,4},{1,3},{3,1},{5,7},{7,5},{8,10},{10,8},{12,... | collective-permute-start | bytes 786440 | tf_op jit(solution)/shard_map/ppermute | solution.py:262
  31.8 13.9 %collective-permute-done.4.last_ref = bf16[128,128]{1,0:T(8,128)(2,1)S(1)} collective-permute-done((bf16[128,128]{1,0:T(8,128)(2,1)S(1)}, bf16[128,128]{1,0:T(8,128)(2,1)S(1)}, u32[]{:S(2)}, u32[]{:S(2)}) %collective-permute-start.4) | collective-permute-done | bytes 32800 | tf_op jit(solution)/shard_map/ppermute | solution.py:262
  46.5 1.7 %w_part.1 = bf16[8,64,1024]{2,1,0:T(8,128)(2,1)} custom-call(s32[1]{0:T(128)} %bitcast.2.z_ref, bf16[4,128,512]{2,1,0:T(8,128)(2,1)S(1)} %all-to-all-done.x_ref, bf16[128,1024]{1,0:T(8,128)(2,1)S(1)} %copy-done.2, bf16[128,1024]{1,0:T(8,128)(2,1)S(1)} %collective-permute-done.1.d1_ref, bf16[128,1024]{1,0:T(8,128)(2,1)S(1)} %collective-permute-done.d2_ref, ...), custom_call_target="tpu_custom_call" | custom-call | flops 536870912 | bytes 3000000 | tf_op jit(solution)/shard_map/w_part/pallas_call | solution.py:399
  48.2 3.7 %all-to-all-start.1 = ((bf16[8,64,1024]{2,1,0:T(8,128)(2,1)}), bf16[8,64,1024]{2,1,0:T(8,128)(2,1)S(1)}, u32[]{:S(2)}, u32[]{:S(2)}) async-start(bf16[8,64,1024]{2,1,0:T(8,128)(2,1)} %w_part.1), calls=%async_computation.1 | async-start | bytes 2097152 | tf_op jit(solution)/shard_map/all_to_all | solution.py:417
  52.0 2.2 %copy-done = bf16[2048,1024]{1,0:T(8,128)(2,1)S(1)} copy-done((bf16[2048,1024]{1,0:T(8,128)(2,1)S(1)}, bf16[2048,1024]{1,0:T(8,128)(2,1)}, u32[]{:S(2)}) %copy-start) | copy-done | bytes 4194328
  54.2 2.4 %lookups.1 = (bf16[4,2048,128]{2,1,0:T(8,128)(2,1)S(1)}, bf16[16,128]{1,0:T(8,128)(2,1)S(1)}) custom-call(bf16[128,1024]{1,0:T(8,128)(2,1)S(1)} %copy-done.2, bf16[128,1024]{1,0:T(8,128)(2,1)S(1)} %collective-permute-done.1.d1_ref, bf16[128,1024]{1,0:T(8,128)(2,1)S(1)} %collective-permute-done.d2_ref, bf16[128,1024]{1,0:T(8,128)(2,1)S(1)} %collective-permute-done.5.d3_ref, ...), custom_call_target="tpu_custom_call" | custom-call | flops 2147483648 | bytes 7000000 | tf_op jit(solution)/shard_map/lookups/pallas_call | solution.py:408
  56.5 11.0 %buckets.1 = bf16[8,928,128]{2,1,0:T(8,128)(2,1)} custom-call(bf16[4,2048,128]{2,1,0:T(8,128)(2,1)S(1)} %get-tuple-element.44.look_ref, s32[3,4,16,128]{3,2,1,0:T(8,128)S(1)} %get-tuple-element.41.slot_ref, f32[4,128,128]{2,1,0:T(8,128)S(1)} %get-tuple-element.45.down_ref, bf16[16,128]{1,0:T(8,128)(2,1)S(1)} %get-tuple-element.46.bias_ref), custom_call_target="tpu_custom_call" | custom-call | flops 15000000512 | bytes 40000000 | tf_op jit(solution)/shard_map/buckets/pallas_call | solution.py:420
  67.6 4.2 %all-to-all-start.2 = ((bf16[8,928,128]{2,1,0:T(8,128)(2,1)}), bf16[8,928,128]{2,1,0:T(8,128)(2,1)S(1)}, u32[]{:S(2)}, u32[]{:S(2)}) async-start(bf16[8,928,128]{2,1,0:T(8,128)(2,1)} %buckets.1), calls=%async_computation.2 | async-start | bytes 3801088 | tf_op jit(solution)/shard_map/all_to_all | solution.py:432
  71.9 2.5 %collective-permute-start.6 = (bf16[64,1024]{1,0:T(8,128)(2,1)S(1)}, bf16[64,1024]{1,0:T(8,128)(2,1)S(1)}, u32[]{:S(2)}, u32[]{:S(2)}) collective-permute-start(bf16[64,1024]{1,0:T(8,128)(2,1)S(1)} %reduce_sum.12), channel_id=1, source_target_pairs={{0,4},{2,6},{4,0},{6,2},{1,5},{3,7},{5,1},{7,3},{8,12},{10,14},{12... | collective-permute-start | bytes 393224 | tf_op jit(solution)/shard_map/ppermute | solution.py:262
  74.9 6.5 %collective-permute-done.6 = bf16[64,1024]{1,0:T(8,128)(2,1)S(1)} collective-permute-done((bf16[64,1024]{1,0:T(8,128)(2,1)S(1)}, bf16[64,1024]{1,0:T(8,128)(2,1)S(1)}, u32[]{:S(2)}, u32[]{:S(2)}) %collective-permute-start.6) | collective-permute-done | bytes 131104 | tf_op jit(solution)/shard_map/ppermute | solution.py:262
  82.8 4.1 %collective-permute-done.8 = bf16[64,1024]{1,0:T(8,128)(2,1)S(1)} collective-permute-done((bf16[64,1024]{1,0:T(8,128)(2,1)S(1)}, bf16[64,1024]{1,0:T(8,128)(2,1)S(1)}, u32[]{:S(2)}, u32[]{:S(2)}) %collective-permute-start.8) | collective-permute-done | bytes 131104 | tf_op jit(solution)/shard_map/ppermute | solution.py:262
  87.0 1.7 %collective-permute-start.16 = (bf16[256,512]{1,0:T(8,128)(2,1)S(1)}, bf16[256,512]{1,0:T(8,128)(2,1)S(1)}, u32[]{:S(2)}, u32[]{:S(2)}) collective-permute-start(bf16[256,512]{1,0:T(8,128)(2,1)S(1)} %get-tuple-element.63.refs_6_), channel_id=1, source_target_pairs={{0,1},{1,0},{2,3},{3,2},{4,5},{5,4},{6,7},{7,6},{8,9},{9,8},{10,11... | collective-permute-start | bytes 786440 | tf_op jit(solution)/shard_map/ppermute | solution.py:262
  91.1 4.8 %all-to-all-done.2.in_ref = bf16[8,928,128]{2,1,0:T(8,128)(2,1)S(1)} async-done(((bf16[8,928,128]{2,1,0:T(8,128)(2,1)}), bf16[8,928,128]{2,1,0:T(8,128)(2,1)S(1)}, u32[]{:S(2)}, u32[]{:S(2)}) %all-to-all-start.2) | async-done | bytes 1900576 | tf_op jit(solution)/shard_map/all_to_all | solution.py:432
  95.9 5.4 %q_sums.1 = (f32[4096,128]{1,0:T(8,128)}, f32[8,128]{1,0:T(8,128)}, f32[128,128]{1,0:T(8,128)}) custom-call(bf16[8,928,128]{2,1,0:T(8,128)(2,1)S(1)} %all-to-all-done.2.in_ref), custom_call_target="tpu_custom_call" | custom-call | flops 4000000000 | bytes 4000000 | tf_op jit(solution)/shard_map/q_sums/pallas_call | solution.py:442
  101.3 5.4 %r_sums.1 = f32[4096,128]{1,0:T(8,128)} custom-call(bf16[8,928,128]{2,1,0:T(8,128)(2,1)S(1)} %all-to-all-done.2.in_ref), custom_call_target="tpu_custom_call" | custom-call | flops 4000000000 | bytes 4000000 | tf_op jit(solution)/shard_map/r_sums/pallas_call | solution.py:442
  110.4 4.0 %widen.3.refs_2_ = f32[2048,1024]{1,0:T(8,128)} custom-call(s32[4]{0:T(128)S(1)} %pad_add_fusion.at_ref, bf16[256,512]{1,0:T(8,128)(2,1)S(1)} %get-tuple-element.64.refs_0_, bf16[256,512]{1,0:T(8,128)(2,1)S(1)} %collective-permute-done.9.refs_1_, bf16[256,512]{1,0:T(8,128)(2,1)} %collective-permute-done.11.refs_2_, ...), custom_call_target="tpu_custom_call" | custom-call | flops 1572864 | bytes 9437184 | tf_op jit(solution)/shard_map/widen/pallas_call | solution.py:293
  114.4 2.2 %collective-permute-done.21.refs_1_ = bf16[256,512]{1,0:T(8,128)(2,1)S(1)} collective-permute-done((bf16[256,512]{1,0:T(8,128)(2,1)S(1)}, bf16[256,512]{1,0:T(8,128)(2,1)S(1)}, u32[]{:S(2)}, u32[]{:S(2)}) %collective-permute-start.21) | collective-permute-done | bytes 262176 | tf_op jit(solution)/shard_map/ppermute | solution.py:262
  119.9 1.6 %widen.5 = f32[2048,1024]{1,0:T(8,128)} custom-call(s32[4]{0:T(128)S(1)} %pad_add_fusion.at_ref, bf16[256,512]{1,0:T(8,128)(2,1)S(1)} %collective-permute-done.20.refs_0_, bf16[256,512]{1,0:T(8,128)(2,1)S(1)} %collective-permute-done.22.refs_1_, f32[2048,1024]{1,0:T(8,128)} %widen.4.refs_2_), custom_call_target="tpu_custom_call", output_to_operand_aliasing={{}: (3, {})} | custom-call | flops 262144 | bytes 1572864 | tf_op jit(solution)/shard_map/widen/pallas_call | solution.py:293
  (67 shorter events, 14.7 us)
Async XLA Ops:
  5.5 15.4 %collective-permute-start.1 = (bf16[128,1024]{1,0:T(8,128)(2,1)}, bf16[128,1024]{1,0:T(8,128)(2,1)S(1)}, u32[]{:S(2)}, u32[]{:S(2)}) collective-permute-start(bf16[128,1024]{1,0:T(8,128)(2,1)} %dpre.1.d0_ref), channel_id=1, source_target_pairs={{0,2},{2,0},{4,6},{6,4},{1,3},{3,1},{5,7},{7,5},{8,10},{10,8},{12,... | collective-permute-start | bytes 786440 | tf_op jit(solution)/shard_map/ppermute | solution.py:262
  8.6 16.7 %collective-permute-start = (bf16[128,1024]{1,0:T(8,128)(2,1)}, bf16[128,1024]{1,0:T(8,128)(2,1)S(1)}, u32[]{:S(2)}, u32[]{:S(2)}) collective-permute-start(bf16[128,1024]{1,0:T(8,128)(2,1)} %dpre.1.d0_ref), channel_id=1, source_target_pairs={{0,4},{2,6},{4,0},{6,2},{1,5},{3,7},{5,1},{7,3},{8,12},{10,14},{12... | collective-permute-start | bytes 786440 | tf_op jit(solution)/shard_map/ppermute | solution.py:262
  11.3 14.7 %collective-permute-start.2 = (bf16[2,128,128]{2,1,0:T(8,128)(2,1)S(1)}, bf16[2,128,128]{2,1,0:T(8,128)(2,1)S(1)}, u32[]{:S(2)}, u32[]{:S(2)}) collective-permute-start(bf16[2,128,128]{2,1,0:T(8,128)(2,1)S(1)} %get-tuple-element.36), channel_id=1, source_target_pairs={{0,4},{2,6},{4,0},{6,2},{1,5},{3,7},{5,1},{7,3},{8,12},{10,14},{12... | collective-permute-start | bytes 196616 | tf_op jit(solution)/shard_map/ppermute | solution.py:262
  11.7 13.6 %collective-permute-start.3 = (bf16[128,128]{1,0:T(8,128)(2,1)S(1)}, bf16[128,128]{1,0:T(8,128)(2,1)S(1)}, u32[]{:S(2)}, u32[]{:S(2)}) collective-permute-start(bf16[128,128]{1,0:T(8,128)(2,1)S(1)} %get-tuple-element.37), channel_id=1, source_target_pairs={{0,2},{2,0},{4,6},{6,4},{1,3},{3,1},{5,7},{7,5},{8,10},{10,8},{12,... | collective-permute-start | bytes 98312 | tf_op jit(solution)/shard_map/ppermute | solution.py:262
  25.9 20.6 %all-to-all-start = ((bf16[4,128,512]{2,1,0:T(8,128)(2,1)}), bf16[4,128,512]{2,1,0:T(8,128)(2,1)S(1)}, u32[]{:S(2)}, u32[]{:S(2)}) async-start(bf16[4,128,512]{2,1,0:T(8,128)(2,1)} %cut.1), calls=%async_computation | async-start | bytes 1048576 | tf_op jit(solution)/shard_map/all_to_all | solution.py:395
  29.7 16.8 %collective-permute-start.5 = (bf16[128,1024]{1,0:T(8,128)(2,1)S(1)}, bf16[128,1024]{1,0:T(8,128)(2,1)S(1)}, u32[]{:S(2)}, u32[]{:S(2)}) collective-permute-start(bf16[128,1024]{1,0:T(8,128)(2,1)S(1)} %collective-permute-done.d2_ref), channel_id=1, source_target_pairs={{0,2},{2,0},{4,6},{6,4},{1,3},{3,1},{5,7},{7,5},{8,10},{10,8},{12,... | collective-permute-start | bytes 786440 | tf_op jit(solution)/shard_map/ppermute | solution.py:262
  31.7 13.9 %collective-permute-start.4 = (bf16[128,128]{1,0:T(8,128)(2,1)S(1)}, bf16[128,128]{1,0:T(8,128)(2,1)S(1)}, u32[]{:S(2)}, u32[]{:S(2)}) collective-permute-start(bf16[128,128]{1,0:T(8,128)(2,1)S(1)} %slice_bitcast_fusion), channel_id=1, source_target_pairs={{0,2},{2,0},{4,6},{6,4},{1,3},{3,1},{5,7},{7,5},{8,10},{10,8},{12,... | collective-permute-start | bytes 98312 | tf_op jit(solution)/shard_map/ppermute | solution.py:262
  48.2 19.3 %all-to-all-start.1 = ((bf16[8,64,1024]{2,1,0:T(8,128)(2,1)}), bf16[8,64,1024]{2,1,0:T(8,128)(2,1)S(1)}, u32[]{:S(2)}, u32[]{:S(2)}) async-start(bf16[8,64,1024]{2,1,0:T(8,128)(2,1)} %w_part.1), calls=%async_computation.1 | async-start | bytes 2097152 | tf_op jit(solution)/shard_map/all_to_all | solution.py:417
  67.6 28.3 %all-to-all-start.2 = ((bf16[8,928,128]{2,1,0:T(8,128)(2,1)}), bf16[8,928,128]{2,1,0:T(8,128)(2,1)S(1)}, u32[]{:S(2)}, u32[]{:S(2)}) async-start(bf16[8,928,128]{2,1,0:T(8,128)(2,1)} %buckets.1), calls=%async_computation.2 | async-start | bytes 3801088 | tf_op jit(solution)/shard_map/all_to_all | solution.py:432
  71.9 9.5 %collective-permute-start.6 = (bf16[64,1024]{1,0:T(8,128)(2,1)S(1)}, bf16[64,1024]{1,0:T(8,128)(2,1)S(1)}, u32[]{:S(2)}, u32[]{:S(2)}) collective-permute-start(bf16[64,1024]{1,0:T(8,128)(2,1)S(1)} %reduce_sum.12), channel_id=1, source_target_pairs={{0,4},{2,6},{4,0},{6,2},{1,5},{3,7},{5,1},{7,3},{8,12},{10,14},{12... | collective-permute-start | bytes 393224 | tf_op jit(solution)/shard_map/ppermute | solution.py:262
  74.4 8.3 %collective-permute-start.7 = (bf16[64,1024]{1,0:T(8,128)(2,1)S(1)}, bf16[64,1024]{1,0:T(8,128)(2,1)S(1)}, u32[]{:S(2)}, u32[]{:S(2)}) collective-permute-start(bf16[64,1024]{1,0:T(8,128)(2,1)S(1)} %reduce_sum.12), channel_id=1, source_target_pairs={{0,2},{2,0},{4,6},{6,4},{1,3},{3,1},{5,7},{7,5},{8,10},{10,8},{12,... | collective-permute-start | bytes 393224 | tf_op jit(solution)/shard_map/ppermute | solution.py:262
  81.4 5.4 %collective-permute-start.8 = (bf16[64,1024]{1,0:T(8,128)(2,1)S(1)}, bf16[64,1024]{1,0:T(8,128)(2,1)S(1)}, u32[]{:S(2)}, u32[]{:S(2)}) collective-permute-start(bf16[64,1024]{1,0:T(8,128)(2,1)S(1)} %collective-permute-done.6), channel_id=1, source_target_pairs={{0,2},{2,0},{4,6},{6,4},{1,3},{3,1},{5,7},{7,5},{8,10},{10,8},{12,... | collective-permute-start | bytes 393224 | tf_op jit(solution)/shard_map/ppermute | solution.py:262
  86.9 20.8 %collective-permute-start.17 = (bf16[256,512]{1,0:T(8,128)(2,1)S(1)}, bf16[256,512]{1,0:T(8,128)(2,1)S(1)}, u32[]{:S(2)}, u32[]{:S(2)}) collective-permute-start(bf16[256,512]{1,0:T(8,128)(2,1)S(1)} %get-tuple-element.63.refs_6_), channel_id=1, source_target_pairs={{0,8},{8,0},{1,9},{9,1},{2,10},{10,2},{3,11},{11,3},{4,12},{12,4},... | collective-permute-start | bytes 786440 | tf_op jit(solution)/shard_map/ppermute | solution.py:262
  87.0 19.7 %collective-permute-start.16 = (bf16[256,512]{1,0:T(8,128)(2,1)S(1)}, bf16[256,512]{1,0:T(8,128)(2,1)S(1)}, u32[]{:S(2)}, u32[]{:S(2)}) collective-permute-start(bf16[256,512]{1,0:T(8,128)(2,1)S(1)} %get-tuple-element.63.refs_6_), channel_id=1, source_target_pairs={{0,1},{1,0},{2,3},{3,2},{4,5},{5,4},{6,7},{7,6},{8,9},{9,8},{10,11... | collective-permute-start | bytes 786440 | tf_op jit(solution)/shard_map/ppermute | solution.py:262
  88.7 18.5 %collective-permute-start.15 = (bf16[256,512]{1,0:T(8,128)(2,1)S(1)}, bf16[256,512]{1,0:T(8,128)(2,1)S(1)}, u32[]{:S(2)}, u32[]{:S(2)}) collective-permute-start(bf16[256,512]{1,0:T(8,128)(2,1)S(1)} %get-tuple-element.63.refs_6_), channel_id=1, source_target_pairs={{0,16},{16,0},{1,17},{17,1},{2,18},{18,2},{3,19},{19,3},{4,20},{20... | collective-permute-start | bytes 786440 | tf_op jit(solution)/shard_map/ppermute | solution.py:262
  90.2 17.1 %collective-permute-start.11 = (bf16[256,512]{1,0:T(8,128)(2,1)S(1)}, bf16[256,512]{1,0:T(8,128)(2,1)}, u32[]{:S(2)}, u32[]{:S(2)}) collective-permute-start(bf16[256,512]{1,0:T(8,128)(2,1)S(1)} %get-tuple-element.64.refs_0_), channel_id=1, source_target_pairs={{0,16},{16,0},{1,17},{17,1},{2,18},{18,2},{3,19},{19,3},{4,20},{20... | collective-permute-start | bytes 786440 | tf_op jit(solution)/shard_map/ppermute | solution.py:262
  90.7 16.0 %collective-permute-start.9 = (bf16[256,512]{1,0:T(8,128)(2,1)S(1)}, bf16[256,512]{1,0:T(8,128)(2,1)S(1)}, u32[]{:S(2)}, u32[]{:S(2)}) collective-permute-start(bf16[256,512]{1,0:T(8,128)(2,1)S(1)} %get-tuple-element.64.refs_0_), channel_id=1, source_target_pairs={{0,1},{1,0},{2,3},{3,2},{4,5},{5,4},{6,7},{7,6},{8,9},{9,8},{10,11... | collective-permute-start | bytes 786440 | tf_op jit(solution)/shard_map/ppermute | solution.py:262
  106.7 3.0 %collective-permute-start.13 = (bf16[256,512]{1,0:T(8,128)(2,1)S(1)}, bf16[256,512]{1,0:T(8,128)(2,1)S(1)}, u32[]{:S(2)}, u32[]{:S(2)}) collective-permute-start(bf16[256,512]{1,0:T(8,128)(2,1)S(1)} %collective-permute-done.9.refs_1_), channel_id=1, source_target_pairs={{0,8},{8,0},{1,9},{9,1},{2,10},{10,2},{3,11},{11,3},{4,12},{12,4},... | collective-permute-start | bytes 786440 | tf_op jit(solution)/shard_map/ppermute | solution.py:262
  107.2 3.1 %collective-permute-start.14 = (bf16[256,512]{1,0:T(8,128)(2,1)}, bf16[256,512]{1,0:T(8,128)(2,1)S(1)}, u32[]{:S(2)}, u32[]{:S(2)}) collective-permute-start(bf16[256,512]{1,0:T(8,128)(2,1)} %collective-permute-done.11.refs_2_), channel_id=1, source_target_pairs={{0,8},{8,0},{1,9},{9,1},{2,10},{10,2},{3,11},{11,3},{4,12},{12,4},... | collective-permute-start | bytes 786440 | tf_op jit(solution)/shard_map/ppermute | solution.py:262
  107.3 3.0 %collective-permute-start.18 = (bf16[256,512]{1,0:T(8,128)(2,1)S(1)}, bf16[256,512]{1,0:T(8,128)(2,1)S(1)}, u32[]{:S(2)}, u32[]{:S(2)}) collective-permute-start(bf16[256,512]{1,0:T(8,128)(2,1)S(1)} %collective-permute-done.15.refs_7_), channel_id=1, source_target_pairs={{0,8},{8,0},{1,9},{9,1},{2,10},{10,2},{3,11},{11,3},{4,12},{12,4},... | collective-permute-start | bytes 786440 | tf_op jit(solution)/shard_map/ppermute | solution.py:262
  107.7 2.6 %collective-permute-start.19 = (bf16[256,512]{1,0:T(8,128)(2,1)S(1)}, bf16[256,512]{1,0:T(8,128)(2,1)S(1)}, u32[]{:S(2)}, u32[]{:S(2)}) collective-permute-start(bf16[256,512]{1,0:T(8,128)(2,1)S(1)} %collective-permute-done.16.refs_8_), channel_id=1, source_target_pairs={{0,8},{8,0},{1,9},{9,1},{2,10},{10,2},{3,11},{11,3},{4,12},{12,4},... | collective-permute-start | bytes 786440 | tf_op jit(solution)/shard_map/ppermute | solution.py:262
  108.2 8.3 %collective-permute-start.21 = (bf16[256,512]{1,0:T(8,128)(2,1)S(1)}, bf16[256,512]{1,0:T(8,128)(2,1)S(1)}, u32[]{:S(2)}, u32[]{:S(2)}) collective-permute-start(bf16[256,512]{1,0:T(8,128)(2,1)S(1)} %collective-permute-done.15.refs_7_), channel_id=1, source_target_pairs={{0,1},{1,0},{2,3},{3,2},{4,5},{5,4},{6,7},{7,6},{8,9},{9,8},{10,11... | collective-permute-start | bytes 786440 | tf_op jit(solution)/shard_map/ppermute | solution.py:262
  109.7 8.1 %collective-permute-start.10 = (bf16[256,512]{1,0:T(8,128)(2,1)S(1)}, bf16[256,512]{1,0:T(8,128)(2,1)S(1)}, u32[]{:S(2)}, u32[]{:S(2)}) collective-permute-start(bf16[256,512]{1,0:T(8,128)(2,1)S(1)} %collective-permute-done.9.refs_1_), channel_id=1, source_target_pairs={{0,16},{16,0},{1,17},{17,1},{2,18},{18,2},{3,19},{19,3},{4,20},{20... | collective-permute-start | bytes 786440 | tf_op jit(solution)/shard_map/ppermute | solution.py:262
  117.8 2.1 %collective-permute-start.22 = (bf16[256,512]{1,0:T(8,128)(2,1)S(1)}, bf16[256,512]{1,0:T(8,128)(2,1)S(1)}, u32[]{:S(2)}, u32[]{:S(2)}) collective-permute-start(bf16[256,512]{1,0:T(8,128)(2,1)S(1)} %collective-permute-done.21.refs_1_), channel_id=1, source_target_pairs={{0,8},{8,0},{1,9},{9,1},{2,10},{10,2},{3,11},{11,3},{4,12},{12,4},... | collective-permute-start | bytes 786440 | tf_op jit(solution)/shard_map/ppermute | solution.py:262
  (12 other events, 107.4 us)

commit v13 on v12

--- a/solution.py
+++ b/solution.py
@@ -140,17 +140,23 @@
         out_ref[p] = res[p * share : (p + 1) * share, :]
 
 
-def lookup_kernel(d0_ref, d1_ref, d2_ref, d3_ref, w_ref, out_ref, bias_ref, d_ref):
-    n_s, depth = d0_ref.shape
-    for z, ref in enumerate((d0_ref, d1_ref, d2_ref, d3_ref)):
+def lookup_kernel(n_src, *refs):
+    sources, w_ref, so_far = refs[:n_src], refs[n_src], refs[n_src + 1 : -3]
+    out_ref, bias_ref, d_ref = refs[-3:]
+    n_s, depth = sources[0].shape
+    for z, ref in enumerate(sources):
         d_ref[z * n_s : (z + 1) * n_s, :] = ref[...]
     for step in range(w_ref.shape[0] // (2 * E)):
         res = dot(d_ref[...], w_ref[step * 2 * E : (step + 1) * 2 * E, :], ((1,), (1,))).astype(BF)
-        for z in range(N_Z):
+        for z in range(n_src):
             for h in range(2):
                 row = (step * 2 + h) * n_s
                 out_ref[z, row : row + n_s, :] = res[z * n_s : (z + 1) * n_s, h * E : (h + 1) * E]
     bias = jnp.sum(d_ref[...].astype(F32), axis=0, keepdims=True)
+    if not so_far:
+        bias_ref[...] = bias
+        return
+    bias = bias + so_far[0][...]
     high = bias.astype(BF)
     low = (bias - high.astype(F32)).astype(BF)
     bias_ref[...] = jnp.concatenate(
@@ -158,11 +164,12 @@
     ).astype(BF)
 
 
-def bucket_kernel(n_dest, cap, look_ref, slot_ref, down_ref, bias_ref, out_ref, mark_ref):
+def bucket_kernel(n_dest, cap, first_ref, last_ref, slot_ref, down_ref, bias_ref, out_ref, mark_ref):
     n_feat, n_s = slot_ref.shape[2:]
     seg = N_Z * cap
     n_mark = -(-seg // E)
     half = n_dest // 2
+    look = [first_ref.at[z] for z in range(N_Z - 1)] + [last_ref.at[0]]
 
     slots = n_dest * cap
     wanted = rows_from(slots)
@@ -173,7 +180,7 @@
             col = [down_ref[z, :, i * n_feat + f : i * n_feat + f + 1] for i in (1, 2, 4, 5)]
             one = jnp.where(kind < 2, jnp.where(kind == 0, col[0], col[1]), jnp.where(kind == 2, col[2], col[3]))
             labels.append(one.astype(BF))
-        values = jnp.concatenate([look_ref[z], jnp.concatenate(labels, axis=0)], axis=1)
+        values = jnp.concatenate([look[z][...], jnp.concatenate(labels, axis=0)], axis=1)
         for which in range(2):
             hits = [one_hot(wanted, slot_ref[which, z, f : f + 1, :]) for f in range(n_feat)]
             o = dot(jnp.concatenate(hits, axis=1), values)
@@ -190,7 +197,7 @@
         sides = []
         for f in range(n_feat):
             upper = down_ref[z, :, 6 * n_feat + f : 6 * n_feat + f + 1] >= half
-            v = look_ref[z, f * n_s : (f + 1) * n_s, :].astype(F32)
+            v = look[z][f * n_s : (f + 1) * n_s, :].astype(F32)
             sides.append(jnp.concatenate([jnp.where(upper, 0.0, v), jnp.where(upper, v, 0.0)], axis=1).astype(BF))
         o = o + dot(jnp.concatenate(hits, axis=1), jnp.concatenate(sides, axis=0))
     for d in range(n_dest):
@@ -394,6 +401,19 @@
     )(after(features, dpre))
     feat_in = lax.all_to_all(after(cut, far, far_codes, near_codes), "tz", split_axis=0, concat_axis=0, tiled=True)
 
+    def lookups(n_src, summed, *args):
+        return call(
+            functools.partial(lookup_kernel, n_src),
+            "lookups",
+            (shape((n_src, count, E), BF), summed),
+            2 * n_src * n_s * width * hidden,
+            7 * 10**6,
+            scratch_shapes=[pltpu.VMEM((n_src * n_s, hidden), BF)],
+            vmem=16,
+        )(*args)
+
+    look, sum_so_far = lookups(3, shape((1, hidden), F32), *sources[:3], w_first)
+    sources[3] = after(sources[3], look)
     feat_in = after(feat_in, slots)
 
     w_part = call(
@@ -405,15 +425,7 @@
         in_specs=[scalar] + [array] * 5,
         vmem=12,
     )(my_z, feat_in, *sources)
-    look, bias = call(
-        lookup_kernel,
-        "lookups",
-        (shape((N_Z, count, E), BF), shape((2 * n_bias, E), BF)),
-        2 * N_Z * n_s * width * hidden,
-        7 * 10**6,
-        scratch_shapes=[pltpu.VMEM((N_Z * n_s, hidden), BF)],
-        vmem=16,
-    )(*sources[:3], after(sources[3], w_part), w_first)
+    last_look, bias = lookups(1, shape((2 * n_bias, E), BF), after(sources[3], w_part), w_first, sum_so_far)
     w_part = lax.all_to_all(w_part, plane, split_axis=0, concat_axis=0, tiled=True)
 
     n_rows = 2 * seg + ADM_DEV + 16 + 2 * n_bias
@@ -425,7 +437,7 @@
         4 * 10**7,
         scratch_shapes=[pltpu.VMEM((2, n_plane, seg, E), F32)],
         vmem=28,
-    )(look, slots, down, bias)
+    )(look, last_look, slots, down, bias)
 
     w_part = after(w_part, chunks)
     w_own = jnp.sum(w_part.astype(F32), axis=0).astype(BF)

time: 122 us -> 122 us (level)
  waiting for transfers between devices: 47.5 us -> 42.1 us
  local copies, waits for them, and re-layouts: 2.26 us -> 4.44 us
  other arithmetic: 0.3 us -> 1.53 us
    ppermute x23, waiting for transfers between devices: 42.8 us -> 39.2 us  [swap(): return lax.ppermute(x, axis, [(i, i ^ k) for i in range(n)])]
    unnamed x20 -> x22, local copies, waits for them, and re-layouts: 2.22 us -> 4.4 us
    all_to_all x1, waiting for transfers between devices: 4.75 us -> 2.92 us  [local(): lax.all_to_all(chunks, plane, split_axis=0, concat_axis=0, tiled=True)]
    reduce_sum x1, other arithmetic: 0.18 us -> 1.41 us  [local(): w_own = jnp.sum(w_part.astype(F32), axis=0).astype(BF)]
    pallas_call x1 -> x2, Pallas kernels: 2.37 us -> 3.32 us  [lookups(): call(functools.partial(lookup_kernel, n_src), 'lookups', (shape((n_src, c...]
  transfers between devices with their start and end apart: 26 -> 26, of which waited for: 11 -> 11; matrix products, arithmetic and copies ran while one was open for 0% -> 1% of each run, Pallas kernels for 26% -> 27%
where the time goes in v13:
time: 122 us
  waiting for transfers between devices  42.1 us (35%)
  Pallas kernels  40.8 us (33%)
  starting transfers between devices  31.5 us (26%)
  local copies, waits for them, and re-layouts  4.44 us (4%)
  other arithmetic  1.53 us (1%)
    ppermute x23, waiting for transfers between devices, swap(): return lax.ppermute(x, axis, [(i, i ^ k) for i in range(n)])  39.2 us
    ppermute x23, starting transfers between devices, swap(): return lax.ppermute(x, axis, [(i, i ^ k) for i in range(n)])  19.4 us
    pallas_call x1, Pallas kernels, local(): call(functools.partial(bucket_kernel, n_plane, cap), 'buckets', shape((n_...  11.1 us
    pallas_call x2, Pallas kernels, sums(): call(functools.partial(sums_kernel, n_plane, seg, n_bias, table), ('q_sum...  10.8 us
    pallas_call x3, Pallas kernels, widen(): call(functools.partial(widen_kernel, n_y, share, places), 'widen', jax.Sh...  7.23 us
    pallas_call x1, Pallas kernels, local(): call(dpre_kernel, 'dpre', shape((n_s, hidden), BF), 2 * n_s * width * hid...  4.82 us
    all_to_all x1, starting transfers between devices, local(): lax.all_to_all(w_part, plane, split_axis=0, concat_axis=0, tiled=True)  4.43 us
    unnamed x22, local copies, waits for them, and re-layouts  4.4 us
  transfers between devices with their start and end apart: 26, of which 11 were waited for; matrix products, arithmetic and copies ran while one was open for 1% of the time, Pallas kernels for 27%

profile of v13, /device:TPU:0, one launch (start us, length us, event | category | flops | bytes accessed | tf_op | source)
XLA Modules:
  0.0 121.5 jit_solution(14089222434970152234)
XLA Ops:
  0.7 4.8 %dpre.1.refs_0_.d0_ref = bf16[128,1024]{1,0:T(8,128)(2,1)} custom-call(bf16[128,2048]{1,0:T(8,128)(2,1)} %x_ref.2, bf16[2048,1024]{1,0:T(8,128)(2,1)} %refs_1_.1, f32[1,1024]{1,0:T(1,128)} %bitcast.38, bf16[128,1024]{1,0:T(8,128)(2,1)} %g_ref.1), custom_call_target="tpu_custom_call" | custom-call | flops 536870912 | bytes 6000000 | tf_op jit(solution)/shard_map/dpre/pallas_call | solution.py:347
  5.5 3.0 %collective-permute-start.1 = (bf16[128,1024]{1,0:T(8,128)(2,1)}, bf16[128,1024]{1,0:T(8,128)(2,1)S(1)}, u32[]{:S(2)}, u32[]{:S(2)}) collective-permute-start(bf16[128,1024]{1,0:T(8,128)(2,1)} %dpre.1.refs_0_.d0_ref), channel_id=1, source_target_pairs={{0,2},{2,0},{4,6},{6,4},{1,3},{3,1},{5,7},{7,5},{8,10},{10,8},{12,... | collective-permute-start | bytes 786440 | tf_op jit(solution)/shard_map/ppermute | solution.py:269
  8.6 2.6 %collective-permute-start = (bf16[128,1024]{1,0:T(8,128)(2,1)}, bf16[128,1024]{1,0:T(8,128)(2,1)S(1)}, u32[]{:S(2)}, u32[]{:S(2)}) collective-permute-start(bf16[128,1024]{1,0:T(8,128)(2,1)} %dpre.1.refs_0_.d0_ref), channel_id=1, source_target_pairs={{0,4},{2,6},{4,0},{6,2},{1,5},{3,7},{5,1},{7,3},{8,12},{10,14},{12... | collective-permute-start | bytes 786440 | tf_op jit(solution)/shard_map/ppermute | solution.py:269
  12.7 8.2 %collective-permute-done.1.refs_1_.d1_ref = bf16[128,1024]{1,0:T(8,128)(2,1)S(1)} collective-permute-done((bf16[128,1024]{1,0:T(8,128)(2,1)}, bf16[128,1024]{1,0:T(8,128)(2,1)S(1)}, u32[]{:S(2)}, u32[]{:S(2)}) %collective-permute-start.1) | collective-permute-done | bytes 262176 | tf_op jit(solution)/shard_map/ppermute | solution.py:269
  20.9 4.3 %collective-permute-done.refs_2_.d2_ref = bf16[128,1024]{1,0:T(8,128)(2,1)S(1)} collective-permute-done((bf16[128,1024]{1,0:T(8,128)(2,1)}, bf16[128,1024]{1,0:T(8,128)(2,1)S(1)}, u32[]{:S(2)}, u32[]{:S(2)}) %collective-permute-start) | collective-permute-done | bytes 262176 | tf_op jit(solution)/shard_map/ppermute | solution.py:269
  25.9 3.7 %all-to-all-start = ((bf16[4,128,512]{2,1,0:T(8,128)(2,1)}), bf16[4,128,512]{2,1,0:T(8,128)(2,1)S(1)}, u32[]{:S(2)}, u32[]{:S(2)}) async-start(bf16[4,128,512]{2,1,0:T(8,128)(2,1)} %cut.1), calls=%async_computation | async-start | bytes 1048576 | tf_op jit(solution)/shard_map/all_to_all | solution.py:402
  29.7 2.0 %collective-permute-start.4 = (bf16[128,128]{1,0:T(8,128)(2,1)S(1)}, bf16[128,128]{1,0:T(8,128)(2,1)S(1)}, u32[]{:S(2)}, u32[]{:S(2)}) collective-permute-start(bf16[128,128]{1,0:T(8,128)(2,1)S(1)} %slice_bitcast_fusion), channel_id=1, source_target_pairs={{0,2},{2,0},{4,6},{6,4},{1,3},{3,1},{5,7},{7,5},{8,10},{10,8},{12,... | collective-permute-start | bytes 98312 | tf_op jit(solution)/shard_map/ppermute | solution.py:269
  31.8 10.0 %collective-permute-done.4.last_ref = bf16[128,128]{1,0:T(8,128)(2,1)S(1)} collective-permute-done((bf16[128,128]{1,0:T(8,128)(2,1)S(1)}, bf16[128,128]{1,0:T(8,128)(2,1)S(1)}, u32[]{:S(2)}, u32[]{:S(2)}) %collective-permute-start.4) | collective-permute-done | bytes 32800 | tf_op jit(solution)/shard_map/ppermute | solution.py:269
  42.7 2.2 %copy-done = bf16[2048,1024]{1,0:T(8,128)(2,1)S(1)} copy-done((bf16[2048,1024]{1,0:T(8,128)(2,1)S(1)}, bf16[2048,1024]{1,0:T(8,128)(2,1)}, u32[]{:S(2)}) %copy-start) | copy-done | bytes 4194328
  44.8 1.8 %lookups.2 = (bf16[3,2048,128]{2,1,0:T(8,128)(2,1)S(1)}, f32[1,1024]{1,0:T(1,128)S(1)}) custom-call(bf16[128,1024]{1,0:T(8,128)(2,1)S(1)} %copy-done.3, bf16[128,1024]{1,0:T(8,128)(2,1)S(1)} %collective-permute-done.1.refs_1_.d1_ref, bf16[128,1024]{1,0:T(8,128)(2,1)S(1)} %collective-permute-done.refs_2_.d2_ref, bf16[2048,1024]{1,0:T(8,128)(2,1)S(1)} %copy-done), custom_call_target="tpu_custom_call" | custom-call | flops 1610612736 | bytes 7000000 | tf_op jit(solution)/shard_map/lookups/pallas_call | solution.py:405
  46.7 1.7 %w_part.1 = bf16[8,64,1024]{2,1,0:T(8,128)(2,1)} custom-call(s32[1]{0:T(128)} %bitcast.2.z_ref, bf16[4,128,512]{2,1,0:T(8,128)(2,1)S(1)} %all-to-all-done.x_ref, bf16[128,1024]{1,0:T(8,128)(2,1)S(1)} %copy-done.3, bf16[128,1024]{1,0:T(8,128)(2,1)S(1)} %collective-permute-done.1.refs_1_.d1_ref, bf16[128,1024]{1,0:T(8,128)(2,1)S(1)} %collective-permute-done.refs_2_.d2_ref, ...), custom_call_target="tpu_custom_call" | custom-call | flops 536870912 | bytes 3000000 | tf_op jit(solution)/shard_map/w_part/pallas_call | solution.py:419
  48.4 4.4 %all-to-all-start.1 = ((bf16[8,64,1024]{2,1,0:T(8,128)(2,1)}), bf16[8,64,1024]{2,1,0:T(8,128)(2,1)}, u32[]{:S(2)}, u32[]{:S(2)}) async-start(bf16[8,64,1024]{2,1,0:T(8,128)(2,1)} %w_part.1), calls=%async_computation.1 | async-start | bytes 2097152 | tf_op jit(solution)/shard_map/all_to_all | solution.py:429
  52.9 2.2 %copy-done.1 = bf16[2048,1024]{1,0:T(8,128)(2,1)S(1)} copy-done((bf16[2048,1024]{1,0:T(8,128)(2,1)S(1)}, bf16[2048,1024]{1,0:T(8,128)(2,1)}, u32[]{:S(2)}) %copy-start.1) | copy-done | bytes 4194328
  56.5 11.1 %buckets.1 = bf16[8,928,128]{2,1,0:T(8,128)(2,1)} custom-call(bf16[3,2048,128]{2,1,0:T(8,128)(2,1)S(1)} %get-tuple-element.46.first_ref, bf16[1,2048,128]{2,1,0:T(8,128)(2,1)S(1)} %get-tuple-element.50.last_ref, s32[3,4,16,128]{3,2,1,0:T(8,128)S(1)} %get-tuple-element.44.slot_ref, f32[4,128,128]{2,1,0:T(8,128)S(1)} %get-tuple-element.51.down_ref, ...), custom_call_target="tpu_custom_call" | custom-call | flops 15000000512 | bytes 40000000 | tf_op jit(solution)/shard_map/buckets/pallas_call | solution.py:432
  67.6 3.9 %all-to-all-start.2 = ((bf16[8,928,128]{2,1,0:T(8,128)(2,1)}), bf16[8,928,128]{2,1,0:T(8,128)(2,1)S(1)}, u32[]{:S(2)}, u32[]{:S(2)}) async-start(bf16[8,928,128]{2,1,0:T(8,128)(2,1)} %buckets.1), calls=%async_computation.2 | async-start | bytes 3801088 | tf_op jit(solution)/shard_map/all_to_all | solution.py:444
  73.0 3.3 %collective-permute-start.6 = (bf16[64,1024]{1,0:T(8,128)(2,1)S(1)}, bf16[64,1024]{1,0:T(8,128)(2,1)S(1)}, u32[]{:S(2)}, u32[]{:S(2)}) collective-permute-start(bf16[64,1024]{1,0:T(8,128)(2,1)S(1)} %reduce_sum.12), channel_id=1, source_target_pairs={{0,4},{2,6},{4,0},{6,2},{1,5},{3,7},{5,1},{7,3},{8,12},{10,14},{12... | collective-permute-start | bytes 393224 | tf_op jit(solution)/shard_map/ppermute | solution.py:269
  76.3 6.8 %collective-permute-done.6 = bf16[64,1024]{1,0:T(8,128)(2,1)S(1)} collective-permute-done((bf16[64,1024]{1,0:T(8,128)(2,1)S(1)}, bf16[64,1024]{1,0:T(8,128)(2,1)S(1)}, u32[]{:S(2)}, u32[]{:S(2)}) %collective-permute-start.6) | collective-permute-done | bytes 131104 | tf_op jit(solution)/shard_map/ppermute | solution.py:269
  84.6 3.9 %collective-permute-done.8 = bf16[64,1024]{1,0:T(8,128)(2,1)S(1)} collective-permute-done((bf16[64,1024]{1,0:T(8,128)(2,1)S(1)}, bf16[64,1024]{1,0:T(8,128)(2,1)S(1)}, u32[]{:S(2)}, u32[]{:S(2)}) %collective-permute-start.8) | collective-permute-done | bytes 131104 | tf_op jit(solution)/shard_map/ppermute | solution.py:269
  88.7 1.7 %collective-permute-start.16 = (bf16[256,512]{1,0:T(8,128)(2,1)S(1)}, bf16[256,512]{1,0:T(8,128)(2,1)S(1)}, u32[]{:S(2)}, u32[]{:S(2)}) collective-permute-start(bf16[256,512]{1,0:T(8,128)(2,1)S(1)} %get-tuple-element.69.refs_6_), channel_id=1, source_target_pairs={{0,1},{1,0},{2,3},{3,2},{4,5},{5,4},{6,7},{7,6},{8,9},{9,8},{10,11... | collective-permute-start | bytes 786440 | tf_op jit(solution)/shard_map/ppermute | solution.py:269
  92.8 2.9 %all-to-all-done.2.in_ref = bf16[8,928,128]{2,1,0:T(8,128)(2,1)S(1)} async-done(((bf16[8,928,128]{2,1,0:T(8,128)(2,1)}), bf16[8,928,128]{2,1,0:T(8,128)(2,1)S(1)}, u32[]{:S(2)}, u32[]{:S(2)}) %all-to-all-start.2) | async-done | bytes 1900576 | tf_op jit(solution)/shard_map/all_to_all | solution.py:444
  95.7 5.4 %q_sums.1 = (f32[4096,128]{1,0:T(8,128)}, f32[8,128]{1,0:T(8,128)}, f32[128,128]{1,0:T(8,128)}) custom-call(bf16[8,928,128]{2,1,0:T(8,128)(2,1)S(1)} %all-to-all-done.2.in_ref), custom_call_target="tpu_custom_call" | custom-call | flops 4000000000 | bytes 4000000 | tf_op jit(solution)/shard_map/q_sums/pallas_call | solution.py:454
  101.1 5.4 %r_sums.1 = f32[4096,128]{1,0:T(8,128)} custom-call(bf16[8,928,128]{2,1,0:T(8,128)(2,1)S(1)} %all-to-all-done.2.in_ref), custom_call_target="tpu_custom_call" | custom-call | flops 4000000000 | bytes 4000000 | tf_op jit(solution)/shard_map/r_sums/pallas_call | solution.py:454
  110.2 4.0 %widen.3.refs_2_ = f32[2048,1024]{1,0:T(8,128)} custom-call(s32[4]{0:T(128)S(1)} %pad_add_fusion.at_ref, bf16[256,512]{1,0:T(8,128)(2,1)S(1)} %get-tuple-element.70.refs_0_, bf16[256,512]{1,0:T(8,128)(2,1)S(1)} %collective-permute-done.9.refs_1_, bf16[256,512]{1,0:T(8,128)(2,1)} %collective-permute-done.11.refs_2_, ...), custom_call_target="tpu_custom_call" | custom-call | flops 1572864 | bytes 9437184 | tf_op jit(solution)/shard_map/widen/pallas_call | solution.py:300
  114.2 2.2 %collective-permute-done.21.refs_1_ = bf16[256,512]{1,0:T(8,128)(2,1)S(1)} collective-permute-done((bf16[256,512]{1,0:T(8,128)(2,1)S(1)}, bf16[256,512]{1,0:T(8,128)(2,1)S(1)}, u32[]{:S(2)}, u32[]{:S(2)}) %collective-permute-start.21) | collective-permute-done | bytes 262176 | tf_op jit(solution)/shard_map/ppermute | solution.py:269
  (70 shorter events, 18.8 us)
Async XLA Ops:
  5.5 15.4 %collective-permute-start.1 = (bf16[128,1024]{1,0:T(8,128)(2,1)}, bf16[128,1024]{1,0:T(8,128)(2,1)S(1)}, u32[]{:S(2)}, u32[]{:S(2)}) collective-permute-start(bf16[128,1024]{1,0:T(8,128)(2,1)} %dpre.1.refs_0_.d0_ref), channel_id=1, source_target_pairs={{0,2},{2,0},{4,6},{6,4},{1,3},{3,1},{5,7},{7,5},{8,10},{10,8},{12,... | collective-permute-start | bytes 786440 | tf_op jit(solution)/shard_map/ppermute | solution.py:269
  8.6 16.7 %collective-permute-start = (bf16[128,1024]{1,0:T(8,128)(2,1)}, bf16[128,1024]{1,0:T(8,128)(2,1)S(1)}, u32[]{:S(2)}, u32[]{:S(2)}) collective-permute-start(bf16[128,1024]{1,0:T(8,128)(2,1)} %dpre.1.refs_0_.d0_ref), channel_id=1, source_target_pairs={{0,4},{2,6},{4,0},{6,2},{1,5},{3,7},{5,1},{7,3},{8,12},{10,14},{12... | collective-permute-start | bytes 786440 | tf_op jit(solution)/shard_map/ppermute | solution.py:269
  11.3 14.7 %collective-permute-start.2 = (bf16[2,128,128]{2,1,0:T(8,128)(2,1)S(1)}, bf16[2,128,128]{2,1,0:T(8,128)(2,1)S(1)}, u32[]{:S(2)}, u32[]{:S(2)}) collective-permute-start(bf16[2,128,128]{2,1,0:T(8,128)(2,1)S(1)} %get-tuple-element.39), channel_id=1, source_target_pairs={{0,4},{2,6},{4,0},{6,2},{1,5},{3,7},{5,1},{7,3},{8,12},{10,14},{12... | collective-permute-start | bytes 196616 | tf_op jit(solution)/shard_map/ppermute | solution.py:269
  11.7 13.6 %collective-permute-start.3 = (bf16[128,128]{1,0:T(8,128)(2,1)S(1)}, bf16[128,128]{1,0:T(8,128)(2,1)S(1)}, u32[]{:S(2)}, u32[]{:S(2)}) collective-permute-start(bf16[128,128]{1,0:T(8,128)(2,1)S(1)} %get-tuple-element.40), channel_id=1, source_target_pairs={{0,2},{2,0},{4,6},{6,4},{1,3},{3,1},{5,7},{7,5},{8,10},{10,8},{12,... | collective-permute-start | bytes 98312 | tf_op jit(solution)/shard_map/ppermute | solution.py:269
  25.9 20.8 %all-to-all-start = ((bf16[4,128,512]{2,1,0:T(8,128)(2,1)}), bf16[4,128,512]{2,1,0:T(8,128)(2,1)S(1)}, u32[]{:S(2)}, u32[]{:S(2)}) async-start(bf16[4,128,512]{2,1,0:T(8,128)(2,1)} %cut.1), calls=%async_computation | async-start | bytes 1048576 | tf_op jit(solution)/shard_map/all_to_all | solution.py:402
  29.7 12.1 %collective-permute-start.4 = (bf16[128,128]{1,0:T(8,128)(2,1)S(1)}, bf16[128,128]{1,0:T(8,128)(2,1)S(1)}, u32[]{:S(2)}, u32[]{:S(2)}) collective-permute-start(bf16[128,128]{1,0:T(8,128)(2,1)S(1)} %slice_bitcast_fusion), channel_id=1, source_target_pairs={{0,2},{2,0},{4,6},{6,4},{1,3},{3,1},{5,7},{7,5},{8,10},{10,8},{12,... | collective-permute-start | bytes 98312 | tf_op jit(solution)/shard_map/ppermute | solution.py:269
  31.7 15.0 %collective-permute-start.5 = (bf16[128,1024]{1,0:T(8,128)(2,1)S(1)}, bf16[128,1024]{1,0:T(8,128)(2,1)S(1)}, u32[]{:S(2)}, u32[]{:S(2)}) collective-permute-start(bf16[128,1024]{1,0:T(8,128)(2,1)S(1)} %collective-permute-done.refs_2_.d2_ref), channel_id=1, source_target_pairs={{0,2},{2,0},{4,6},{6,4},{1,3},{3,1},{5,7},{7,5},{8,10},{10,8},{12,... | collective-permute-start | bytes 786440 | tf_op jit(solution)/shard_map/ppermute | solution.py:269
  48.4 19.2 %all-to-all-start.1 = ((bf16[8,64,1024]{2,1,0:T(8,128)(2,1)}), bf16[8,64,1024]{2,1,0:T(8,128)(2,1)}, u32[]{:S(2)}, u32[]{:S(2)}) async-start(bf16[8,64,1024]{2,1,0:T(8,128)(2,1)} %w_part.1), calls=%async_computation.1 | async-start | bytes 2097152 | tf_op jit(solution)/shard_map/all_to_all | solution.py:429
  67.6 28.1 %all-to-all-start.2 = ((bf16[8,928,128]{2,1,0:T(8,128)(2,1)}), bf16[8,928,128]{2,1,0:T(8,128)(2,1)S(1)}, u32[]{:S(2)}, u32[]{:S(2)}) async-start(bf16[8,928,128]{2,1,0:T(8,128)(2,1)} %buckets.1), calls=%async_computation.2 | async-start | bytes 3801088 | tf_op jit(solution)/shard_map/all_to_all | solution.py:444
  73.0 10.1 %collective-permute-start.6 = (bf16[64,1024]{1,0:T(8,128)(2,1)S(1)}, bf16[64,1024]{1,0:T(8,128)(2,1)S(1)}, u32[]{:S(2)}, u32[]{:S(2)}) collective-permute-start(bf16[64,1024]{1,0:T(8,128)(2,1)S(1)} %reduce_sum.12), channel_id=1, source_target_pairs={{0,4},{2,6},{4,0},{6,2},{1,5},{3,7},{5,1},{7,3},{8,12},{10,14},{12... | collective-permute-start | bytes 393224 | tf_op jit(solution)/shard_map/ppermute | solution.py:269
  76.3 8.3 %collective-permute-start.7 = (bf16[64,1024]{1,0:T(8,128)(2,1)S(1)}, bf16[64,1024]{1,0:T(8,128)(2,1)S(1)}, u32[]{:S(2)}, u32[]{:S(2)}) collective-permute-start(bf16[64,1024]{1,0:T(8,128)(2,1)S(1)} %reduce_sum.12), channel_id=1, source_target_pairs={{0,2},{2,0},{4,6},{6,4},{1,3},{3,1},{5,7},{7,5},{8,10},{10,8},{12,... | collective-permute-start | bytes 393224 | tf_op jit(solution)/shard_map/ppermute | solution.py:269
  83.1 5.4 %collective-permute-start.8 = (bf16[64,1024]{1,0:T(8,128)(2,1)S(1)}, bf16[64,1024]{1,0:T(8,128)(2,1)S(1)}, u32[]{:S(2)}, u32[]{:S(2)}) collective-permute-start(bf16[64,1024]{1,0:T(8,128)(2,1)S(1)} %collective-permute-done.6), channel_id=1, source_target_pairs={{0,2},{2,0},{4,6},{6,4},{1,3},{3,1},{5,7},{7,5},{8,10},{10,8},{12,... | collective-permute-start | bytes 393224 | tf_op jit(solution)/shard_map/ppermute | solution.py:269
  88.6 19.0 %collective-permute-start.17 = (bf16[256,512]{1,0:T(8,128)(2,1)S(1)}, bf16[256,512]{1,0:T(8,128)(2,1)S(1)}, u32[]{:S(2)}, u32[]{:S(2)}) collective-permute-start(bf16[256,512]{1,0:T(8,128)(2,1)S(1)} %get-tuple-element.69.refs_6_), channel_id=1, source_target_pairs={{0,8},{8,0},{1,9},{9,1},{2,10},{10,2},{3,11},{11,3},{4,12},{12,4},... | collective-permute-start | bytes 786440 | tf_op jit(solution)/shard_map/ppermute | solution.py:269
  88.7 17.9 %collective-permute-start.16 = (bf16[256,512]{1,0:T(8,128)(2,1)S(1)}, bf16[256,512]{1,0:T(8,128)(2,1)S(1)}, u32[]{:S(2)}, u32[]{:S(2)}) collective-permute-start(bf16[256,512]{1,0:T(8,128)(2,1)S(1)} %get-tuple-element.69.refs_6_), channel_id=1, source_target_pairs={{0,1},{1,0},{2,3},{3,2},{4,5},{5,4},{6,7},{7,6},{8,9},{9,8},{10,11... | collective-permute-start | bytes 786440 | tf_op jit(solution)/shard_map/ppermute | solution.py:269
  90.4 16.7 %collective-permute-start.15 = (bf16[256,512]{1,0:T(8,128)(2,1)S(1)}, bf16[256,512]{1,0:T(8,128)(2,1)S(1)}, u32[]{:S(2)}, u32[]{:S(2)}) collective-permute-start(bf16[256,512]{1,0:T(8,128)(2,1)S(1)} %get-tuple-element.69.refs_6_), channel_id=1, source_target_pairs={{0,16},{16,0},{1,17},{17,1},{2,18},{18,2},{3,19},{19,3},{4,20},{20... | collective-permute-start | bytes 786440 | tf_op jit(solution)/shard_map/ppermute | solution.py:269
  91.8 15.2 %collective-permute-start.11 = (bf16[256,512]{1,0:T(8,128)(2,1)S(1)}, bf16[256,512]{1,0:T(8,128)(2,1)}, u32[]{:S(2)}, u32[]{:S(2)}) collective-permute-start(bf16[256,512]{1,0:T(8,128)(2,1)S(1)} %get-tuple-element.70.refs_0_), channel_id=1, source_target_pairs={{0,16},{16,0},{1,17},{17,1},{2,18},{18,2},{3,19},{19,3},{4,20},{20... | collective-permute-start | bytes 786440 | tf_op jit(solution)/shard_map/ppermute | solution.py:269
  92.4 14.1 %collective-permute-start.9 = (bf16[256,512]{1,0:T(8,128)(2,1)S(1)}, bf16[256,512]{1,0:T(8,128)(2,1)S(1)}, u32[]{:S(2)}, u32[]{:S(2)}) collective-permute-start(bf16[256,512]{1,0:T(8,128)(2,1)S(1)} %get-tuple-element.70.refs_0_), channel_id=1, source_target_pairs={{0,1},{1,0},{2,3},{3,2},{4,5},{5,4},{6,7},{7,6},{8,9},{9,8},{10,11... | collective-permute-start | bytes 786440 | tf_op jit(solution)/shard_map/ppermute | solution.py:269
  106.6 3.0 %collective-permute-start.13 = (bf16[256,512]{1,0:T(8,128)(2,1)S(1)}, bf16[256,512]{1,0:T(8,128)(2,1)S(1)}, u32[]{:S(2)}, u32[]{:S(2)}) collective-permute-start(bf16[256,512]{1,0:T(8,128)(2,1)S(1)} %collective-permute-done.9.refs_1_), channel_id=1, source_target_pairs={{0,8},{8,0},{1,9},{9,1},{2,10},{10,2},{3,11},{11,3},{4,12},{12,4},... | collective-permute-start | bytes 786440 | tf_op jit(solution)/shard_map/ppermute | solution.py:269
  107.1 3.1 %collective-permute-start.14 = (bf16[256,512]{1,0:T(8,128)(2,1)}, bf16[256,512]{1,0:T(8,128)(2,1)S(1)}, u32[]{:S(2)}, u32[]{:S(2)}) collective-permute-start(bf16[256,512]{1,0:T(8,128)(2,1)} %collective-permute-done.11.refs_2_), channel_id=1, source_target_pairs={{0,8},{8,0},{1,9},{9,1},{2,10},{10,2},{3,11},{11,3},{4,12},{12,4},... | collective-permute-start | bytes 786440 | tf_op jit(solution)/shard_map/ppermute | solution.py:269
  107.1 3.0 %collective-permute-start.18 = (bf16[256,512]{1,0:T(8,128)(2,1)S(1)}, bf16[256,512]{1,0:T(8,128)(2,1)S(1)}, u32[]{:S(2)}, u32[]{:S(2)}) collective-permute-start(bf16[256,512]{1,0:T(8,128)(2,1)S(1)} %collective-permute-done.15.refs_7_), channel_id=1, source_target_pairs={{0,8},{8,0},{1,9},{9,1},{2,10},{10,2},{3,11},{11,3},{4,12},{12,4},... | collective-permute-start | bytes 786440 | tf_op jit(solution)/shard_map/ppermute | solution.py:269
  107.6 2.6 %collective-permute-start.19 = (bf16[256,512]{1,0:T(8,128)(2,1)S(1)}, bf16[256,512]{1,0:T(8,128)(2,1)S(1)}, u32[]{:S(2)}, u32[]{:S(2)}) collective-permute-start(bf16[256,512]{1,0:T(8,128)(2,1)S(1)} %collective-permute-done.16.refs_8_), channel_id=1, source_target_pairs={{0,8},{8,0},{1,9},{9,1},{2,10},{10,2},{3,11},{11,3},{4,12},{12,4},... | collective-permute-start | bytes 786440 | tf_op jit(solution)/shard_map/ppermute | solution.py:269
  108.1 8.3 %collective-permute-start.21 = (bf16[256,512]{1,0:T(8,128)(2,1)S(1)}, bf16[256,512]{1,0:T(8,128)(2,1)S(1)}, u32[]{:S(2)}, u32[]{:S(2)}) collective-permute-start(bf16[256,512]{1,0:T(8,128)(2,1)S(1)} %collective-permute-done.15.refs_7_), channel_id=1, source_target_pairs={{0,1},{1,0},{2,3},{3,2},{4,5},{5,4},{6,7},{7,6},{8,9},{9,8},{10,11... | collective-permute-start | bytes 786440 | tf_op jit(solution)/shard_map/ppermute | solution.py:269
  109.5 8.1 %collective-permute-start.10 = (bf16[256,512]{1,0:T(8,128)(2,1)S(1)}, bf16[256,512]{1,0:T(8,128)(2,1)S(1)}, u32[]{:S(2)}, u32[]{:S(2)}) collective-permute-start(bf16[256,512]{1,0:T(8,128)(2,1)S(1)} %collective-permute-done.9.refs_1_), channel_id=1, source_target_pairs={{0,16},{16,0},{1,17},{17,1},{2,18},{18,2},{3,19},{19,3},{4,20},{20... | collective-permute-start | bytes 786440 | tf_op jit(solution)/shard_map/ppermute | solution.py:269
  117.6 2.1 %collective-permute-start.22 = (bf16[256,512]{1,0:T(8,128)(2,1)S(1)}, bf16[256,512]{1,0:T(8,128)(2,1)S(1)}, u32[]{:S(2)}, u32[]{:S(2)}) collective-permute-start(bf16[256,512]{1,0:T(8,128)(2,1)S(1)} %collective-permute-done.21.refs_1_), channel_id=1, source_target_pairs={{0,8},{8,0},{1,9},{9,1},{2,10},{10,2},{3,11},{11,3},{4,12},{12,4},... | collective-permute-start | bytes 786440 | tf_op jit(solution)/shard_map/ppermute | solution.py:269
  (13 other events, 105.7 us)
